TPU v7x, 32 devices: a whole 2x2x4 slice. The times are simulated.
32 devices in a mesh: expert: 8 (over z, x), shard: 4 (over y, core).
Axes of the slice: x: 2, y: 2, z: 4, core: 2. Of those that a mesh axis runs over, the one named last changes fastest.
Arguments:
- tokens: bfloat16 [8192, 1536], P(('expert', 'shard')), may hold values from -6 to 6
- lengths: int32 [8, 4], P('expert'), may hold values from 1 to 770, 1024 in all within a row
- routes: int32 [8192, 4], P(('expert', 'shard')), may hold values from 0 to 7, all different within a row
- slot_order: int32 [32, 1024], P(('expert', 'shard')), may hold values from 0 to 1023, each once within a row
- cotangent: bfloat16 [8192, 1536], P(('expert', 'shard')), may hold values from -6 to 6
- q_weight: bfloat16 [2, 1536, 1536], P(None, 'shard'), may hold values from -0.15625 to 0.15625
- key_matrix: bfloat16 [2, 1536, 256], P(None, 'shard'), may hold values from -0.15625 to 0.15625
- value_matrix: bfloat16 [2, 1536, 256], P(None, 'shard'), may hold values from -0.15625 to 0.15625
- out_weight: bfloat16 [2, 1536, 1536], P(None, 'shard'), may hold values from -2.5 to 2.5
- router_weight: bfloat16 [2, 1536, 8], P(None, 'shard'), may hold values from -0.078125 to 0.078125
- attn_gain: bfloat16 [2, 1536], P(None, 'shard'), may hold values from 0.099609375 to 1.8984375
- ffn_gain: bfloat16 [2, 1536], P(None, 'shard'), may hold values from 0.099609375 to 1.8984375
- gate_weight: bfloat16 [2, 8, 1536, 768], P(None, 'expert'), may hold values from -0.15625 to 0.15625
- up_weight: bfloat16 [2, 8, 1536, 768], P(None, 'expert'), may hold values from -0.15625 to 0.15625
- down_weight: bfloat16 [2, 8, 768, 1536], P(None, 'expert'), may hold values from -0.21875 to 0.21875
Outputs:
- output: bfloat16 [8192, 1536], P(('expert', 'shard'))
- input_grad: bfloat16 [8192, 1536], P(('expert', 'shard'))
- q_grad: float32 [2, 1536, 1536], P(None, 'shard')
- key_grad: float32 [2, 1536, 256], P(None, 'shard')
- value_grad: float32 [2, 1536, 256], P(None, 'shard')
- out_grad: float32 [2, 1536, 1536], P(None, 'shard')
- router_grad: float32 [2, 1536, 8], P(None, 'shard')
- attn_gain_grad: float32 [2, 1536], P(None, 'shard')
- ffn_gain_grad: float32 [2, 1536], P(None, 'shard')
- gate_grad: float32 [2, 8, 1536, 768], P(None, 'expert', 'shard')
- up_grad: float32 [2, 8, 1536, 768], P(None, 'expert', 'shard')
- down_grad: float32 [2, 8, 768, 1536], P(None, 'expert', 'shard')
Inputs may be any that keep to these rules, and one draw needn't show every extreme that they name: `routes`: each row names 4 different experts. `slot_order`: each row orders the 1024 pairs of one device, each once. Row s gives the lengths of the 4 documents of sequence s in order; they sum to 1024.
All inputs are finite; a program needn't handle non-finite values.
Results may differ from a plain program's by a relative error of at most 0.025.
Values may be sent and summed in bfloat16 or wider, within the bound.
No kernel may reach another device: no remote copies, remote signals or barrier semaphores. Data moves between devices by JAX's collectives and lax.ppermute only.
A program may use at most 320 MiB of HBM per device.

v0:
```python
import jax
import jax.numpy as jnp
from jax import lax
from jax.sharding import PartitionSpec as P

MODEL_WIDTH = 1536
QUERY_HEADS = 12
KEY_VALUE_HEADS = 2
HEAD_SIZE = 128
LAYER_COUNT = 2


norm_eps = 1e-06
rope_base = 10000.0
masked_score = -1e30


def norm_rows(values, norm_gain):
    inverse = lax.rsqrt(jnp.mean(values * values, axis=-1, keepdims=True) + norm_eps)
    return values * inverse * norm_gain


def rotary_apply(values, position, head_count, direction):
    head_width = values.shape[1] // head_count
    half_width = head_width // 2
    frequency = rope_base ** (-(jnp.arange(half_width).astype(jnp.float32) * 2.0 / head_width))
    angles = position.astype(jnp.float32)[:, None] * frequency[None, :]
    cosine = jnp.cos(angles)[:, None, :]
    sine_part = direction * jnp.sin(angles)[:, None, :]
    split_rows = values.reshape(values.shape[0], head_count, head_width)
    first_half = split_rows[:, :, :half_width]
    second_half = split_rows[:, :, half_width:]
    turned = jnp.concatenate(
        [
            first_half * cosine - second_half * sine_part,
            second_half * cosine + first_half * sine_part,
        ],
        axis=-1,
    )
    return turned.reshape(values.shape[0], head_count * head_width)


def documents(lengths_row, position):
    doc_ends = jnp.cumsum(lengths_row)
    doc_starts = doc_ends - lengths_row
    document_index = jnp.sum((position[:, None] >= doc_ends[None, :]).astype(jnp.int32), axis=1)
    doc_first = jnp.max(
        jnp.where(doc_starts[None, :] <= position[:, None], doc_starts[None, :], 0), axis=1
    )
    return (document_index, position - doc_first)


def router_gates(logits, route_rows, experts):
    probability = jax.nn.softmax(logits, axis=-1)
    picked = (route_rows[:, :, None] == jnp.arange(experts, dtype=jnp.int32)[None, None, :]).astype(
        logits.dtype
    )
    chosen = jnp.sum(probability[:, None, :] * picked, axis=-1)
    return chosen / jnp.sum(chosen, axis=-1, keepdims=True)


def gated_unit(gate_pre, up_pre):
    return jax.nn.gelu(gate_pre, approximate=True) * up_pre


def route_slots(route_flat, order_row, experts, capacity):
    ranked = route_flat[order_row]
    matches = (ranked[:, None] == jnp.arange(experts, dtype=jnp.int32)[None, :]).astype(jnp.int32)
    before = jnp.cumsum(matches, axis=0) - matches
    slot_index = jnp.sum(before * matches, axis=1)
    target = jnp.where(slot_index < capacity, ranked * capacity + slot_index, experts * capacity)
    return jnp.zeros_like(route_flat).at[order_row].set(target)


def per_device(
    tokens,
    lengths,
    routes,
    slot_order,
    cotangent,
    q_weight,
    key_matrix,
    value_matrix,
    out_weight,
    router_weight,
    attn_gain,
    ffn_gain,
    gate_weight,
    up_weight,
    down_weight,
):
    shard_count = lax.axis_size("shard")
    expert_count = lax.axis_size("expert")
    token_rows = tokens.shape[0]
    top_count = routes.shape[1]
    pair_count = token_rows * top_count
    local_experts = gate_weight.shape[1]
    experts = local_experts * expert_count
    capacity = (pair_count * 5 + 4 * experts - 1) // (4 * experts)
    sequence_length = token_rows * shard_count
    group_width = QUERY_HEADS // KEY_VALUE_HEADS
    score_scale = HEAD_SIZE ** (-0.5)
    position = lax.axis_index("shard") * token_rows + jnp.arange(token_rows, dtype=jnp.int32)
    key_position = jnp.arange(sequence_length, dtype=jnp.int32)
    query_doc, query_position = documents(lengths[0], position)
    key_doc = documents(lengths[0], key_position)[0]
    visible = (query_doc[:, None] == key_doc[None, :]) & (
        key_position[None, :] <= position[:, None]
    )
    target = route_slots(routes.reshape(pair_count), slot_order[0], experts, capacity)
    pair_of_slot = (
        jnp.full((experts * capacity,), pair_count, jnp.int32)
        .at[target]
        .set(jnp.arange(pair_count, dtype=jnp.int32), mode="drop")
    )
    token_of_slot = pair_of_slot // top_count
    zero_row = jnp.zeros((1, MODEL_WIDTH), jnp.bfloat16)
    stream = tokens.astype(jnp.float32)
    stored = []
    for layer_index in range(LAYER_COUNT):
        shard_parts = (
            q_weight[layer_index],
            key_matrix[layer_index],
            value_matrix[layer_index],
            out_weight[layer_index],
            router_weight[layer_index],
            attn_gain[layer_index],
            ffn_gain[layer_index],
        )
        gathered = (
            lax.all_gather(shard_parts[0], "shard", axis=0, tiled=True),
            lax.all_gather(shard_parts[1], "shard", axis=0, tiled=True),
            lax.all_gather(shard_parts[2], "shard", axis=0, tiled=True),
            lax.all_gather(shard_parts[3], "shard", axis=0, tiled=True),
            lax.all_gather(shard_parts[4], "shard", axis=0, tiled=True),
            lax.all_gather(shard_parts[5], "shard", axis=0, tiled=True),
            lax.all_gather(shard_parts[6], "shard", axis=0, tiled=True),
        )
        w_query, w_key, w_value, w_out, w_router, gain_attn, gain_ffn = gathered
        normed, attn_norm_pull = jax.vjp(norm_rows, stream, gain_attn.astype(jnp.float32))
        hidden = normed.astype(jnp.bfloat16)
        q_pre = jnp.dot(hidden, w_query, preferred_element_type=jnp.float32)
        key_before_rotation = jnp.dot(hidden, w_key, preferred_element_type=jnp.float32)
        value_rows = jnp.dot(hidden, w_value, preferred_element_type=jnp.float32).astype(
            jnp.bfloat16
        )
        query_rotated = rotary_apply(q_pre, query_position, QUERY_HEADS, 1.0).astype(jnp.bfloat16)
        key_rotated = rotary_apply(
            key_before_rotation, query_position, KEY_VALUE_HEADS, 1.0
        ).astype(jnp.bfloat16)
        every_key, every_value = (
            lax.all_gather(key_rotated, "shard", axis=0, tiled=True),
            lax.all_gather(value_rows, "shard", axis=0, tiled=True),
        )
        query_head_rows = query_rotated.reshape(token_rows, KEY_VALUE_HEADS, group_width, HEAD_SIZE)
        key_head_rows = every_key.reshape(sequence_length, KEY_VALUE_HEADS, HEAD_SIZE)
        value_head_rows = every_value.reshape(sequence_length, KEY_VALUE_HEADS, HEAD_SIZE)
        raw_scores = jnp.einsum(
            "qhgd,khd->hgqk", query_head_rows, key_head_rows, preferred_element_type=jnp.float32
        )
        scores = jnp.where(visible, raw_scores * score_scale, masked_score)
        row_peak = jnp.max(scores, axis=-1, keepdims=True)
        exponent = jnp.exp(scores - row_peak)
        row_total = jnp.sum(exponent, axis=-1, keepdims=True)
        probs_low = (exponent / row_total).astype(jnp.bfloat16)
        log_total = row_peak + jnp.log(row_total)
        mixed_heads = (
            jnp.einsum(
                "hgqk,khd->qhgd", probs_low, value_head_rows, preferred_element_type=jnp.float32
            )
            .reshape(token_rows, QUERY_HEADS * HEAD_SIZE)
            .astype(jnp.bfloat16)
        )
        stream = stream + jnp.dot(mixed_heads, w_out, preferred_element_type=jnp.float32)
        normed_ffn, ffn_norm_pull = jax.vjp(norm_rows, stream, gain_ffn.astype(jnp.float32))
        routed = normed_ffn.astype(jnp.bfloat16)
        logits = jnp.dot(routed, w_router, preferred_element_type=jnp.float32)
        gate_values, gate_pull = jax.vjp(
            lambda logit_rows: router_gates(logit_rows, routes, experts), logits
        )
        padded = jnp.concatenate([routed, zero_row], axis=0)
        sending = padded[token_of_slot].reshape(experts, capacity, MODEL_WIDTH)
        arrived = lax.all_to_all(sending, "expert", split_axis=0, concat_axis=1, tiled=True)
        w_gate = gate_weight[layer_index]
        w_up = up_weight[layer_index]
        w_down = down_weight[layer_index]
        gate_pre = jnp.einsum("erd,edf->erf", arrived, w_gate, preferred_element_type=jnp.float32)
        up_pre = jnp.einsum("erd,edf->erf", arrived, w_up, preferred_element_type=jnp.float32)
        active, unit_pull = jax.vjp(gated_unit, gate_pre, up_pre)
        active_low = active.astype(jnp.bfloat16)
        produced = jnp.einsum(
            "erf,efd->erd", active_low, w_down, preferred_element_type=jnp.float32
        ).astype(jnp.bfloat16)
        returned = lax.all_to_all(produced, "expert", split_axis=1, concat_axis=0, tiled=True)
        flat_back = jnp.concatenate(
            [returned.reshape(experts * capacity, MODEL_WIDTH), zero_row], axis=0
        )
        per_pair = flat_back[target].reshape(token_rows, top_count, MODEL_WIDTH)
        stream = stream + jnp.sum(gate_values[:, :, None] * per_pair.astype(jnp.float32), axis=1)
        stored.append(
            {
                "gathered": gathered,
                "attn_norm_pull": attn_norm_pull,
                "hidden": hidden,
                "query_heads": query_head_rows,
                "key_heads": key_head_rows,
                "value_heads": value_head_rows,
                "log_total": log_total,
                "mixed_heads": mixed_heads,
                "ffn_norm_pull": ffn_norm_pull,
                "routed": routed,
                "gate_pull": gate_pull,
                "gate_values": gate_values,
                "arrived": arrived,
                "unit_pull": unit_pull,
                "active_low": active_low,
                "per_pair": per_pair,
            }
        )
    output = stream.astype(jnp.bfloat16)
    upstream = cotangent.astype(jnp.float32)
    layer_grads = [None] * LAYER_COUNT
    expert_parts = [None] * LAYER_COUNT
    for layer_index in reversed(range(LAYER_COUNT)):
        saved_layer = stored[layer_index]
        shard_parts = (
            q_weight[layer_index],
            key_matrix[layer_index],
            value_matrix[layer_index],
            out_weight[layer_index],
            router_weight[layer_index],
            attn_gain[layer_index],
            ffn_gain[layer_index],
        )
        gathered = (
            lax.all_gather(shard_parts[0], "shard", axis=0, tiled=True),
            lax.all_gather(shard_parts[1], "shard", axis=0, tiled=True),
            lax.all_gather(shard_parts[2], "shard", axis=0, tiled=True),
            lax.all_gather(shard_parts[3], "shard", axis=0, tiled=True),
            lax.all_gather(shard_parts[4], "shard", axis=0, tiled=True),
            lax.all_gather(shard_parts[5], "shard", axis=0, tiled=True),
            lax.all_gather(shard_parts[6], "shard", axis=0, tiled=True),
        )
        w_query, w_key, w_value, w_out, w_router, gain_attn, gain_ffn = gathered
        w_gate = gate_weight[layer_index]
        w_up = up_weight[layer_index]
        w_down = down_weight[layer_index]
        per_pair = saved_layer["per_pair"]
        gate_values = saved_layer["gate_values"]
        d_gates = jnp.sum(upstream[:, None, :] * per_pair.astype(jnp.float32), axis=-1)
        d_pairs = (
            (gate_values[:, :, None] * upstream[:, None, :])
            .astype(jnp.bfloat16)
            .reshape(pair_count, MODEL_WIDTH)
        )
        d_padded = jnp.concatenate([d_pairs, zero_row], axis=0)
        d_sending = d_padded[pair_of_slot].reshape(experts, capacity, MODEL_WIDTH)
        d_arrived = lax.all_to_all(d_sending, "expert", split_axis=0, concat_axis=1, tiled=True)
        d_active = jnp.einsum(
            "erd,efd->erf", d_arrived, w_down, preferred_element_type=jnp.float32
        ).astype(jnp.bfloat16)
        d_gate_pre, d_up_pre = saved_layer["unit_pull"](d_active.astype(jnp.float32))
        d_gate_low = d_gate_pre.astype(jnp.bfloat16)
        d_up_low = d_up_pre.astype(jnp.bfloat16)
        arrived = saved_layer["arrived"]
        grad_down = jnp.einsum(
            "erf,erd->efd", saved_layer["active_low"], d_arrived, preferred_element_type=jnp.float32
        )
        grad_gate = jnp.einsum(
            "erd,erf->edf", arrived, d_gate_low, preferred_element_type=jnp.float32
        )
        grad_up = jnp.einsum("erd,erf->edf", arrived, d_up_low, preferred_element_type=jnp.float32)
        d_slot_rows = jnp.einsum(
            "erf,edf->erd", d_gate_low, w_gate, preferred_element_type=jnp.float32
        )
        d_slot_rows = (
            d_slot_rows
            + jnp.einsum("erf,edf->erd", d_up_low, w_up, preferred_element_type=jnp.float32)
        ).astype(jnp.bfloat16)
        d_returned = lax.all_to_all(d_slot_rows, "expert", split_axis=1, concat_axis=0, tiled=True)
        d_flat = jnp.concatenate(
            [d_returned.reshape(experts * capacity, MODEL_WIDTH), zero_row], axis=0
        )
        d_routed = jnp.sum(
            d_flat[target].reshape(token_rows, top_count, MODEL_WIDTH).astype(jnp.float32), axis=1
        )
        d_logits = saved_layer["gate_pull"](d_gates)[0].astype(jnp.bfloat16)
        routed = saved_layer["routed"]
        d_routed = d_routed + jnp.einsum(
            "te,de->td", d_logits, w_router, preferred_element_type=jnp.float32
        )
        d_stream, grad_ffn_gain = saved_layer["ffn_norm_pull"](d_routed)
        upstream = upstream + d_stream
        expert_parts[layer_index] = (
            lax.psum_scatter(
                grad_gate.astype(jnp.bfloat16), "shard", scatter_dimension=1, tiled=True
            ).astype(jnp.float32),
            lax.psum_scatter(
                grad_up.astype(jnp.bfloat16), "shard", scatter_dimension=1, tiled=True
            ).astype(jnp.float32),
            lax.psum_scatter(
                grad_down.astype(jnp.bfloat16), "shard", scatter_dimension=1, tiled=True
            ).astype(jnp.float32),
        )
        d_branch = upstream.astype(jnp.bfloat16)
        mixed_heads = saved_layer["mixed_heads"]
        d_mixed = (
            jnp.einsum("td,qd->tq", d_branch, w_out, preferred_element_type=jnp.float32)
            .astype(jnp.bfloat16)
            .reshape(token_rows, KEY_VALUE_HEADS, group_width, HEAD_SIZE)
        )
        query_head_rows = saved_layer["query_heads"]
        key_head_rows = saved_layer["key_heads"]
        value_head_rows = saved_layer["value_heads"]
        raw_scores = jnp.einsum(
            "qhgd,khd->hgqk", query_head_rows, key_head_rows, preferred_element_type=jnp.float32
        )
        scores = jnp.where(visible, raw_scores * score_scale, masked_score)
        probs_full = jnp.exp(scores - saved_layer["log_total"])
        d_probs = jnp.einsum(
            "qhgd,khd->hgqk", d_mixed, value_head_rows, preferred_element_type=jnp.float32
        )
        d_scores = (
            probs_full * (d_probs - jnp.sum(probs_full * d_probs, axis=-1, keepdims=True))
        ).astype(jnp.bfloat16)
        probs_low = probs_full.astype(jnp.bfloat16)
        d_value_all = jnp.einsum(
            "hgqk,qhgd->khd", probs_low, d_mixed, preferred_element_type=jnp.float32
        ).reshape(sequence_length, KEY_VALUE_HEADS * HEAD_SIZE)
        d_key_all = (
            jnp.einsum(
                "hgqk,qhgd->khd", d_scores, query_head_rows, preferred_element_type=jnp.float32
            )
            * score_scale
        ).reshape(sequence_length, KEY_VALUE_HEADS * HEAD_SIZE)
        d_query = (
            jnp.einsum(
                "hgqk,khd->qhgd", d_scores, key_head_rows, preferred_element_type=jnp.float32
            )
            * score_scale
        ).reshape(token_rows, QUERY_HEADS * HEAD_SIZE)
        key_gradient, d_value = (
            lax.psum_scatter(
                d_key_all.astype(jnp.bfloat16), "shard", scatter_dimension=0, tiled=True
            ).astype(jnp.float32),
            lax.psum_scatter(
                d_value_all.astype(jnp.bfloat16), "shard", scatter_dimension=0, tiled=True
            ).astype(jnp.float32),
        )
        d_q_low = rotary_apply(d_query, query_position, QUERY_HEADS, -1.0).astype(jnp.bfloat16)
        key_low_gradient = rotary_apply(key_gradient, query_position, KEY_VALUE_HEADS, -1.0).astype(
            jnp.bfloat16
        )
        d_v_low = d_value.astype(jnp.bfloat16)
        hidden = saved_layer["hidden"]
        d_hidden = jnp.einsum("tq,nq->tn", d_q_low, w_query, preferred_element_type=jnp.float32)
        d_hidden = d_hidden + jnp.einsum(
            "tq,nq->tn", key_low_gradient, w_key, preferred_element_type=jnp.float32
        )
        d_hidden = d_hidden + jnp.einsum(
            "tq,nq->tn", d_v_low, w_value, preferred_element_type=jnp.float32
        )
        d_stream, grad_attn_gain = saved_layer["attn_norm_pull"](d_hidden)
        upstream = upstream + d_stream
        grad_out = jnp.einsum(
            "tq,td->qd", mixed_heads, d_branch, preferred_element_type=jnp.float32
        )
        grad_router = jnp.einsum("td,te->de", routed, d_logits, preferred_element_type=jnp.float32)
        grad_query = jnp.einsum("tn,tq->nq", hidden, d_q_low, preferred_element_type=jnp.float32)
        grad_key = jnp.einsum(
            "tn,tq->nq", hidden, key_low_gradient, preferred_element_type=jnp.float32
        )
        grad_value = jnp.einsum("tn,tq->nq", hidden, d_v_low, preferred_element_type=jnp.float32)
        attn_terms = (
            grad_query,
            grad_key,
            grad_value,
            grad_out,
            grad_router,
            grad_attn_gain,
            grad_ffn_gain,
        )
        owned = (
            lax.psum_scatter(
                attn_terms[0].astype(jnp.bfloat16), "shard", scatter_dimension=0, tiled=True
            ).astype(jnp.float32),
            lax.psum_scatter(
                attn_terms[1].astype(jnp.bfloat16), "shard", scatter_dimension=0, tiled=True
            ).astype(jnp.float32),
            lax.psum_scatter(
                attn_terms[2].astype(jnp.bfloat16), "shard", scatter_dimension=0, tiled=True
            ).astype(jnp.float32),
            lax.psum_scatter(
                attn_terms[3].astype(jnp.bfloat16), "shard", scatter_dimension=0, tiled=True
            ).astype(jnp.float32),
            lax.psum_scatter(
                attn_terms[4].astype(jnp.bfloat16), "shard", scatter_dimension=0, tiled=True
            ).astype(jnp.float32),
            lax.psum_scatter(
                attn_terms[5].astype(jnp.bfloat16), "shard", scatter_dimension=0, tiled=True
            ).astype(jnp.float32),
            lax.psum_scatter(
                attn_terms[6].astype(jnp.bfloat16), "shard", scatter_dimension=0, tiled=True
            ).astype(jnp.float32),
        )
        owned = (
            lax.psum(owned[0].astype(jnp.bfloat16), "expert").astype(jnp.float32),
            lax.psum(owned[1].astype(jnp.bfloat16), "expert").astype(jnp.float32),
            lax.psum(owned[2].astype(jnp.bfloat16), "expert").astype(jnp.float32),
            lax.psum(owned[3].astype(jnp.bfloat16), "expert").astype(jnp.float32),
            lax.psum(owned[4].astype(jnp.bfloat16), "expert").astype(jnp.float32),
            lax.psum(owned[5].astype(jnp.bfloat16), "expert").astype(jnp.float32),
            lax.psum(owned[6].astype(jnp.bfloat16), "expert").astype(jnp.float32),
        )
        layer_grads[layer_index] = owned
    input_grad = upstream.astype(jnp.bfloat16)
    stacked = [
        jnp.stack([layer_grads[index][member] for index in range(LAYER_COUNT)], axis=0)
        for member in range(7)
    ]
    expert_stacked = [
        jnp.stack([expert_parts[index][member] for index in range(LAYER_COUNT)], axis=0)
        for member in range(3)
    ]
    return (
        output,
        input_grad,
        stacked[0],
        stacked[1],
        stacked[2],
        stacked[3],
        stacked[4],
        stacked[5],
        stacked[6],
        expert_stacked[0],
        expert_stacked[1],
        expert_stacked[2],
    )


def solution(mesh):
    placed = (
        P(("expert", "shard"), None),
        P("expert", None),
        P(("expert", "shard"), None),
        P(("expert", "shard"), None),
        P(("expert", "shard"), None),
        P(None, "shard", None),
        P(None, "shard", None),
        P(None, "shard", None),
        P(None, "shard", None),
        P(None, "shard", None),
        P(None, "shard"),
        P(None, "shard"),
        P(None, "expert", None, None),
        P(None, "expert", None, None),
        P(None, "expert", None, None),
    )
    return jax.shard_map(
        per_device,
        mesh=mesh,
        in_specs=placed,
        out_specs=(
            P(("expert", "shard"), None),
            P(("expert", "shard"), None),
            P(None, "shard", None),
            P(None, "shard", None),
            P(None, "shard", None),
            P(None, "shard", None),
            P(None, "shard", None),
            P(None, "shard"),
            P(None, "shard"),
            P(None, "expert", "shard", None),
            P(None, "expert", "shard", None),
            P(None, "expert", "shard", None),
        ),
        check_vma=False,
    )
```

profile of v0, /device:TPU:0, one launch (start us, length us, event | category | flops | bytes accessed | tf_op | source)
XLA Modules:
  0.0 2280.0 jit_solution(953837687002703200)
XLA Ops:
  36.4 13.6 all-gather.1
  66.1 13.3 all-gather.2
  80.3 10.6 all_gather.68
  123.5 87.4 %all-to-all-done = bf16[8,160,1536]{2,1,0:T(8,128)(2,1)} async-done(((bf16[8,160,1536]{2,1,0:T(8,128)(2,1)}), bf16[8,160,1536]{2,1,0:T(8,128)(2,1)}, u32[]{:S(2)}, u32[]{:S(2)}) %all-to-all-start) | async-done | bytes 3932192 | tf_op jit(solution)/shard_map/all_to_all | solution.py:183
  217.2 9.3 multiply_convert_fusion.3
  230.1 43.7 %copy.300 = bf16[1,1280,1536]{2,0,1:T(2,128)(2,1)} copy(bf16[1,1280,1536]{2,1,0:T(8,128)(2,1)S(1)} %fusion.12) | data formatting | bytes 7864320 | tf_op jit(solution)/shard_map/convert_element_type | solution.py:193
  274.2 26.9 %reduce.20 = bf16[1280,1536]{1,0:T(8,128)(2,1)} reduce(bf16[1280,1,1536]{2,1,0:T(2,128)(2,1)} %bitcast.438, bf16[]{:T(256)} %broadcast.611), dimensions={1}, to_apply=%bitcast.432.reduce_sub_computation | reduce | bytes 7864322
  317.4 7.8 mul.935
  346.2 13.1 all-gather.8
  359.3 9.2 all-gather.9
  369.5 31.1 %all-to-all-done.1 = bf16[8,2,122880]{2,1,0:T(2,128)(2,1)} async-done(((bf16[8,2,122880]{2,1,0:T(2,128)(2,1)}), bf16[8,2,122880]{2,1,0:T(2,128)(2,1)}, u32[]{:S(2)}, u32[]{:S(2)}) %all-to-all-start.1) | async-done | bytes 3932192 | tf_op jit(solution)/shard_map/all_to_all | solution.py:194
  400.6 8.7 reshape.905
  415.8 9.9 gather_fusion.2
  454.6 7.7 all_gather.77
  499.9 82.9 %all-to-all-done.4 = bf16[8,160,1536]{2,1,0:T(8,128)(2,1)} async-done(((bf16[8,160,1536]{2,1,0:T(8,128)(2,1)}), bf16[8,160,1536]{2,1,0:T(8,128)(2,1)}, u32[]{:S(2)}, u32[]{:S(2)}) %all-to-all-start.4) | async-done | bytes 3932192 | tf_op jit(solution)/shard_map/all_to_all | solution.py:258
  594.9 80.1 %all-to-all-done.2 = bf16[8,160,1536]{2,1,0:T(8,128)(2,1)} async-done(((bf16[8,160,1536]{2,1,0:T(8,128)(2,1)}), bf16[8,160,1536]{2,1,0:T(8,128)(2,1)}, u32[]{:S(2)}, u32[]{:S(2)}) %all-to-all-start.2) | async-done | bytes 3932192 | tf_op jit(solution)/shard_map/all_to_all | solution.py:183
  681.3 9.6 fusion.57
  694.3 43.7 %copy.299 = bf16[1,1280,1536]{2,0,1:T(2,128)(2,1)} copy(bf16[1,1280,1536]{2,1,0:T(8,128)(2,1)S(1)} %fusion.13) | data formatting | bytes 7864320 | tf_op jit(solution)/shard_map/convert_element_type | solution.py:193
  738.0 26.9 %reduce.22 = bf16[1280,1536]{1,0:T(8,128)(2,1)} reduce(bf16[1280,1,1536]{2,1,0:T(2,128)(2,1)} %bitcast.441, bf16[]{:T(256)} %broadcast.611), dimensions={1}, to_apply=%bitcast.431.reduce_sub_computation | reduce | bytes 7864322
  764.9 7.6 reshape.906
  789.4 43.7 %copy.298 = bf16[1,1280,1536]{2,0,1:T(2,128)(2,1)} copy(bf16[1,1280,1536]{2,1,0:T(8,128)(2,1)S(1)} %fusion.15) | data formatting | bytes 7864320 | tf_op jit(solution)/shard_map/convert_element_type | solution.py:279
  833.1 26.9 %reduce.21 = bf16[1280,1536]{1,0:T(8,128)(2,1)} reduce(bf16[1280,1,1536]{2,1,0:T(2,128)(2,1)} %bitcast.442, bf16[]{:T(256)} %broadcast.611), dimensions={1}, to_apply=%bitcast.430.reduce_sub_computation | reduce | bytes 7864322
  875.6 8.5 reshape.907
  890.6 9.3 gather_fusion.4
  903.7 9.6 multiply_reduce_fusion.1
  913.5 46.6 %all-to-all-done.5 = bf16[8,2,122880]{2,1,0:T(2,128)(2,1)} async-done(((bf16[8,2,122880]{2,1,0:T(2,128)(2,1)}), bf16[8,2,122880]{2,1,0:T(2,128)(2,1)}, u32[]{:S(2)}, u32[]{:S(2)}) %all-to-all-start.5) | async-done | bytes 3932192 | tf_op jit(solution)/shard_map/all_to_all | solution.py:280
  960.1 8.5 reshape.909
  975.1 9.3 gather_fusion.6
  1004.8 11.2 fusion.3
  1034.2 9.0 fusion.129
  1055.7 18.7 reduce-scatter.27.cloned.1.call-done
  1082.8 7.8 mul.990
  1099.9 93.7 %all_to_all.32 = bf16[8,160,1536]{2,1,0:T(8,128)(2,1)S(1)} all-to-all(bf16[8,160,1536]{2,1,0:T(8,128)(2,1)} %bitcast.453), channel_id=1, replica_groups=mesh['expert'=8,'shard'=4] {'expert'}, dimensions={0} | all-to-all | bytes 7864320 | tf_op jit(solution)/shard_map/all_to_all | solution.py:258
  1193.6 11.0 fusion.50
  1215.4 43.7 %copy.297 = bf16[1,1280,1536]{2,0,1:T(2,128)(2,1)} copy(bf16[1,1280,1536]{2,1,0:T(8,128)(2,1)S(1)} %fusion.14) | data formatting | bytes 7864320 | tf_op jit(solution)/shard_map/convert_element_type | solution.py:279
  1259.0 27.1 %reduce.23 = bf16[1280,1536]{1,0:T(8,128)(2,1)} reduce(bf16[1280,1,1536]{2,1,0:T(2,128)(2,1)} %bitcast.439, bf16[]{:T(256)} %broadcast.611), dimensions={1}, to_apply=%bitcast.429.reduce_sub_computation | reduce | bytes 7864322
  1303.1 82.0 %all-to-all-done.7 = bf16[8,2,122880]{2,1,0:T(2,128)(2,1)} async-done(((bf16[8,2,122880]{2,1,0:T(2,128)(2,1)}), bf16[8,2,122880]{2,1,0:T(2,128)(2,1)}, u32[]{:S(2)}, u32[]{:S(2)}) %all-to-all-start.7) | async-done | bytes 3932192 | tf_op jit(solution)/shard_map/all_to_all | solution.py:280
  1385.1 8.5 reshape.911
  1400.1 9.9 gather_fusion.8
  1416.9 7.8 reduce_sum.414
  1432.3 8.8 fusion.126
  1441.1 9.4 fusion
  1450.6 10.3 fusion.2
  1481.3 14.1 reduce-scatter.29.cloned.1.call-done
  1530.8 8.9 fusion.61
  1540.0 8.8 fusion.60
  1556.4 8.3 fusion.62
  1565.0 33.1 %reduce-scatter.47.cloned.1.call-done = bf16[384,1536]{1,0:T(8,128)(2,1)} async-done(((bf16[1536,1536]{1,0:T(8,128)(2,1)}), bf16[384,1536]{1,0:T(8,128)(2,1)}) %reduce-scatter.47.cloned.1.call-update) | async-done | bytes 1179664 | tf_op jit(solution)/shard_map/reduce_scatter | solution.py:393
  1598.1 51.0 %reduce-scatter.35.cloned.1.call-done = bf16[384,1536]{1,0:T(8,128)(2,1)} async-done(((bf16[1536,1536]{1,0:T(8,128)(2,1)}), bf16[384,1536]{1,0:T(8,128)(2,1)}) %reduce-scatter.35.cloned.1.call-update) | async-done | bytes 1179664 | tf_op jit(solution)/shard_map/reduce_scatter | solution.py:384
  1649.2 25.8 %reduce-scatter.41.cloned.1.call-done = bf16[384,256]{1,0:T(8,128)(2,1)} async-done(((bf16[1536,256]{1,0:T(8,128)(2,1)}), bf16[384,256]{1,0:T(8,128)(2,1)}) %reduce-scatter.41.cloned.1.call-update) | async-done | bytes 196624 | tf_op jit(solution)/shard_map/reduce_scatter | solution.py:390
  1675.0 25.9 %reduce-scatter.37.cloned.1.call-done = bf16[384,256]{1,0:T(8,128)(2,1)} async-done(((bf16[1536,256]{1,0:T(8,128)(2,1)}), bf16[384,256]{1,0:T(8,128)(2,1)}) %reduce-scatter.37.cloned.1.call-update) | async-done | bytes 196624 | tf_op jit(solution)/shard_map/reduce_scatter | solution.py:387
  1700.9 50.3 %reduce-scatter.45.cloned.1.call-done = bf16[384,1536]{1,0:T(8,128)(2,1)} async-done(((bf16[1536,1536]{1,0:T(8,128)(2,1)}), bf16[384,1536]{1,0:T(8,128)(2,1)}) %reduce-scatter.45.cloned.1.call-update) | async-done | bytes 1179664 | tf_op jit(solution)/shard_map/reduce_scatter | solution.py:393
  1751.1 51.0 %reduce-scatter.33.cloned.1.call-done = bf16[384,1536]{1,0:T(8,128)(2,1)} async-done(((bf16[1536,1536]{1,0:T(8,128)(2,1)}), bf16[384,1536]{1,0:T(8,128)(2,1)}) %reduce-scatter.33.cloned.1.call-update) | async-done | bytes 1179664 | tf_op jit(solution)/shard_map/reduce_scatter | solution.py:384
  1803.4 22.5 reduce-scatter.63.cloned.1.call-done
  1826.9 22.3 reduce-scatter.61.cloned.1.call-done
  1850.1 35.2 %reduce-scatter.51.cloned.1.call-done = bf16[1,384,768]{2,1,0:T(8,128)(2,1)} async-done(((bf16[1,1536,768]{2,1,0:T(8,128)(2,1)}), bf16[1,384,768]{2,1,0:T(8,128)(2,1)}) %reduce-scatter.51.cloned.1.call-update) | async-done | bytes 589840 | tf_op jit(solution)/shard_map/reduce_scatter | solution.py:295
  1885.3 36.2 %reduce-scatter.49.cloned.1.call-done = bf16[1,384,768]{2,1,0:T(8,128)(2,1)} async-done(((bf16[1,1536,768]{2,1,0:T(8,128)(2,1)}), bf16[1,384,768]{2,1,0:T(8,128)(2,1)}) %reduce-scatter.49.cloned.1.call-update) | async-done | bytes 589840 | tf_op jit(solution)/shard_map/reduce_scatter | solution.py:295
  1924.3 32.8 %reduce-scatter.55.cloned.1.call-done = bf16[1,384,768]{2,1,0:T(8,128)(2,1)} async-done(((bf16[1,1536,768]{2,1,0:T(8,128)(2,1)}), bf16[1,384,768]{2,1,0:T(8,128)(2,1)}) %reduce-scatter.55.cloned.1.call-update) | async-done | bytes 589840 | tf_op jit(solution)/shard_map/reduce_scatter | solution.py:298
  1957.2 35.8 %reduce-scatter.53.cloned.1.call-done = bf16[1,384,768]{2,1,0:T(8,128)(2,1)} async-done(((bf16[1,1536,768]{2,1,0:T(8,128)(2,1)}), bf16[1,384,768]{2,1,0:T(8,128)(2,1)}) %reduce-scatter.53.cloned.1.call-update) | async-done | bytes 589840 | tf_op jit(solution)/shard_map/reduce_scatter | solution.py:298
  1995.7 32.8 %reduce-scatter.59.cloned.1.call-done = bf16[1,192,1536]{2,1,0:T(8,128)(2,1)} async-done(((bf16[1,768,1536]{2,1,0:T(8,128)(2,1)}), bf16[1,192,1536]{2,1,0:T(8,128)(2,1)}) %reduce-scatter.59.cloned.1.call-update) | async-done | bytes 589840 | tf_op jit(solution)/shard_map/reduce_scatter | solution.py:301
  2028.6 35.6 %reduce-scatter.57.cloned.1.call-done = bf16[1,192,1536]{2,1,0:T(8,128)(2,1)} async-done(((bf16[1,768,1536]{2,1,0:T(8,128)(2,1)}), bf16[1,192,1536]{2,1,0:T(8,128)(2,1)}) %reduce-scatter.57.cloned.1.call-update) | async-done | bytes 589840 | tf_op jit(solution)/shard_map/reduce_scatter | solution.py:301
  2073.9 10.9 all-reduce.14
  2085.2 39.3 %all-reduce.12 = (bf16[1,384,8]{1,2,0:T(8,128)(2,1)S(1)}, bf16[1,384,8]{1,2,0:T(8,128)(2,1)S(1)}, bf16[1,384]{1,0:T(2,128)(2,1)S(1)}, bf16[1,384]{1,0:T(2,128)(2...) all-reduce(bf16[1,384,8]{1,2,0:T(8,128)(2,1)S(1)} %bitcast.513, ...), channel_id=1, replica_groups=mesh['expert'=8,'shard'=4] {'expert'}, use_global_device_ids=true, to_apply=%region_66.67 | all-reduce | flops 7680 | bytes 30720 | tf_op jit(solution)/shard_map/psum | solution.py:411
  2129.0 133.6 %all-reduce.17.cloned.1.call-done = (bf16[1,384,1536]{2,1,0:T(8,128)(2,1)}, bf16[1,384,1536]{2,1,0:T(8,128)(2,1)}, bf16[1,384,256]{2,1,0:T(8,128)(2,1)}, bf16[1,...) async-done(((bf16[1,384,1536]{2,1,0:T(8,128)(2,1)}, ...) | async-done | bytes 5505040 | tf_op jit(solution)/shard_map/psum | solution.py:407
  (613 shorter events, 484.1 us)
Async XLA Ops:
  7.2 84.0 %all-gather.19.cloned.1.call-start = ((), (), s32[]{:S(2)}) async-start(), calls=%async_computation.46 | async-start | bytes 5898240 | tf_op jit(solution)/shard_map/all_gather | solution.py:131
  10.6 95.7 %all-gather.21.cloned.1.call-start = ((), (), s32[]{:S(2)}) async-start(), calls=%async_computation.47 | async-start | bytes 5898240 | tf_op jit(solution)/shard_map/all_gather | solution.py:134
  12.5 78.7 %copy-start.100 = (f32[256]{0:T(256)}, f32[256]{0:T(256)S(1)}, u32[]{:S(2)}) copy-start(f32[256]{0:T(256)S(1)} %fusion.176) | copy-start | bytes 3076
  19.3 71.9 %copy-start.78 = (f32[1536]{0:T(1024)}, f32[1536]{0:T(1024)S(1)}, u32[]{:S(2)}) copy-start(f32[1536]{0:T(1024)S(1)} %convert_reduce_fusion.4) | copy-start | bytes 18436
  19.6 39.1 %copy-start.131 = (s32[1,4]{1,0:T(1,128)S(1)}, s32[1,4]{1,0:T(1,128)}, u32[]{:S(2)}) copy-start(s32[1,4]{1,0:T(1,128)} %param.16) | copy-start | bytes 52
  24.2 41.2 %copy-start.77 = (bf16[2,384,256]{2,1,0:T(8,128)(2,1)S(1)}, bf16[2,384,256]{2,1,0:T(8,128)(2,1)}, u32[]{:S(2)}) copy-start(bf16[2,384,256]{2,1,0:T(8,128)(2,1)} %param.21) | copy-start | bytes 1179652
  59.0 41.8 %copy-start.61 = (bf16[1024,2,128]{2,1,0:T(2,128)(2,1)}, bf16[1024,2,128]{2,1,0:T(2,128)(2,1)S(1)}, u32[]{:S(2)}) copy-start(bf16[1024,2,128]{2,1,0:T(2,128)(2,1)S(1)} %reshape.716) | copy-start | bytes 1572868
  64.2 420.0 %copy-start.92 = (s32[2048]{0:T(1024)}, s32[2048]{0:T(1024)S(1)}, u32[]{:S(2)}) copy-start(s32[2048]{0:T(1024)S(1)} %get-tuple-element.114) | copy-start | bytes 24580
  64.2 46.3 %copy-start.86 = (f32[1536]{0:T(1024)}, f32[1536]{0:T(1024)S(1)}, u32[]{:S(2)}) copy-start(f32[1536]{0:T(1024)S(1)} %convert_reduce_fusion.3) | copy-start | bytes 18436
  65.4 30.4 %copy-start.67 = (f32[256,64]{0,1:T(8,128)}, f32[256,64]{0,1:T(8,128)S(1)}, u32[]{:S(2)}) copy-start(f32[256,64]{0,1:T(8,128)S(1)} %get-tuple-element.83) | copy-start | bytes 196612
  65.4 388.9 %copy-start.41 = (f32[256,64]{0,1:T(8,128)}, f32[256,64]{0,1:T(8,128)S(1)}, u32[]{:S(2)}) copy-start(f32[256,64]{0,1:T(8,128)S(1)} %get-tuple-element.84) | copy-start | bytes 196612
  91.2 375.8 %copy-start.4 = (pred[256,1024]{0,1:T(8,128)(4,1)}, pred[256,1024]{0,1:T(8,128)(4,1)S(1)}, u32[]{:S(2)}) copy-start(pred[256,1024]{0,1:T(8,128)(4,1)S(1)} %fusion.134) | copy-start | bytes 786436
  110.5 329.3 %copy-start.6 = (f32[256,1536]{1,0:T(8,128)}, f32[256,1536]{1,0:T(8,128)S(1)}, u32[]{:S(2)}) copy-start(f32[256,1536]{1,0:T(8,128)S(1)} %get-tuple-element.92) | copy-start | bytes 4718596
  111.2 257.2 %copy-start.23 = (bf16[256,1536]{1,0:T(8,128)(2,1)}, bf16[256,1536]{1,0:T(8,128)(2,1)S(1)}, u32[]{:S(2)}) copy-start(bf16[256,1536]{1,0:T(8,128)(2,1)S(1)} %multiply_convert_fusion.6) | copy-start | bytes 2359300
  116.7 100.5 %slice-start.11 = ((s8[4718592]{0:T(1024)(128)(4,1)}), s8[524288]{0:T(1024)(128)(4,1)S(1)}, s32[]{:S(2)}) async-start(s8[4718592]{0:T(1024)(128)(4,1)} %bitcast.528), calls=%async_computation.64 | async-start | bytes 1048576
  116.7 94.2 %all-to-all-start = ((bf16[8,160,1536]{2,1,0:T(8,128)(2,1)}), bf16[8,160,1536]{2,1,0:T(8,128)(2,1)}, u32[]{:S(2)}, u32[]{:S(2)}) async-start(bf16[8,160,1536]{2,1,0:T(8,128)(2,1)} %bitcast.450), calls=%async_computation | async-start | bytes 7864320 | tf_op jit(solution)/shard_map/all_to_all | solution.py:183
  122.7 327.2 %all-gather.23.cloned.1.call-start = ((), (), s32[]{:S(2)}) async-start(), calls=%async_computation.48 | async-start | bytes 5898240 | tf_op jit(solution)/shard_map/all_gather | solution.py:131
  308.7 91.9 %all-to-all-start.1 = ((bf16[8,2,122880]{2,1,0:T(2,128)(2,1)}), bf16[8,2,122880]{2,1,0:T(2,128)(2,1)}, u32[]{:S(2)}, u32[]{:S(2)}) async-start(bf16[8,2,122880]{2,1,0:T(2,128)(2,1)} %reshape.904), calls=%async_computation.1 | async-start | bytes 7864320 | tf_op jit(solution)/shard_map/all_to_all | solution.py:194
  313.4 159.2 %all-gather.25.cloned.1.call-start = ((), (), s32[]{:S(2)}) async-start(), calls=%async_computation.49 | async-start | bytes 5898240 | tf_op jit(solution)/shard_map/all_gather | solution.py:134
  317.4 28.7 %copy-start.73 = (bf16[1,384,256]{2,1,0:T(8,128)(2,1)S(1)}, bf16[1,384,256]{2,1,0:T(8,128)(2,1)}, u32[]{:S(2)}) copy-start(bf16[1,384,256]{2,1,0:T(8,128)(2,1)} %get-tuple-element.68) | copy-start | bytes 589828
  317.4 41.8 %copy-start.74 = (bf16[1,384,256]{2,1,0:T(8,128)(2,1)S(1)}, bf16[1,384,256]{2,1,0:T(8,128)(2,1)}, u32[]{:S(2)}) copy-start(bf16[1,384,256]{2,1,0:T(8,128)(2,1)} %get-tuple-element.72) | copy-start | bytes 589828
  346.1 63.2 %copy-start.80 = (bf16[1,1536,8]{1,2,0:T(8,128)(2,1)}, bf16[1,1536,8]{1,2,0:T(8,128)(2,1)S(1)}, u32[]{:S(2)}) copy-start(bf16[1,1536,8]{1,2,0:T(8,128)(2,1)S(1)} %all-gather.6) | copy-start | bytes 73732
  346.2 94.0 %copy-start.88 = (f32[1536]{0:T(1024)}, f32[1536]{0:T(1024)S(1)}, u32[]{:S(2)}) copy-start(f32[1536]{0:T(1024)S(1)} %convert_reduce_fusion.2) | copy-start | bytes 18436
  368.8 40.5 %copy-start.82 = (f32[256,8]{0,1:T(8,128)}, f32[256,8]{0,1:T(8,128)S(1)}, u32[]{:S(2)}) copy-start(f32[256,8]{0,1:T(8,128)S(1)} %get-tuple-element.96) | copy-start | bytes 24580
  369.3 40.0 %copy-start.108 = (f32[256]{0:T(256)}, f32[256]{0:T(256)S(1)}, u32[]{:S(2)}) copy-start(f32[256]{0:T(256)S(1)} %fusion.168) | copy-start | bytes 3076
  369.4 39.9 %copy-start.96 = (f32[256,4]{0,1:T(4,128)}, f32[256,4]{0,1:T(4,128)S(1)}, u32[]{:S(2)}) copy-start(f32[256,4]{0,1:T(4,128)S(1)} %get-tuple-element.25) | copy-start | bytes 12292
  369.4 39.9 %copy-start.110 = (f32[256]{0:T(256)}, f32[256]{0:T(256)S(1)}, u32[]{:S(2)}) copy-start(f32[256]{0:T(256)S(1)} %get-tuple-element.24) | copy-start | bytes 3076
  489.7 93.0 %all-to-all-start.4 = ((bf16[8,160,1536]{2,1,0:T(8,128)(2,1)}), bf16[8,160,1536]{2,1,0:T(8,128)(2,1)}, u32[]{:S(2)}, u32[]{:S(2)}) async-start(bf16[8,160,1536]{2,1,0:T(8,128)(2,1)} %bitcast.452), calls=%async_computation.4 | async-start | bytes 7864320 | tf_op jit(solution)/shard_map/all_to_all | solution.py:258
  582.7 92.2 %all-to-all-start.2 = ((bf16[8,160,1536]{2,1,0:T(8,128)(2,1)}), bf16[8,160,1536]{2,1,0:T(8,128)(2,1)}, u32[]{:S(2)}, u32[]{:S(2)}) async-start(bf16[8,160,1536]{2,1,0:T(8,128)(2,1)} %bitcast.451), calls=%async_computation.2 | async-start | bytes 7864320 | tf_op jit(solution)/shard_map/all_to_all | solution.py:183
  587.4 93.8 %slice-start.7 = ((s8[4718592]{0:T(1024)(128)(4,1)}), s8[524288]{0:T(1024)(128)(4,1)S(1)}, s32[]{:S(2)}) async-start(s8[4718592]{0:T(1024)(128)(4,1)} %bitcast.524), calls=%async_computation.60 | async-start | bytes 1048576
  772.5 95.0 %all-to-all-start.3 = ((bf16[8,2,122880]{2,1,0:T(2,128)(2,1)}), bf16[8,2,122880]{2,1,0:T(2,128)(2,1)}, u32[]{:S(2)}, u32[]{:S(2)}) async-start(bf16[8,2,122880]{2,1,0:T(2,128)(2,1)} %reshape.906), calls=%async_computation.3 | async-start | bytes 7864320 | tf_op jit(solution)/shard_map/all_to_all | solution.py:194
  867.6 92.6 %all-to-all-start.5 = ((bf16[8,2,122880]{2,1,0:T(2,128)(2,1)}), bf16[8,2,122880]{2,1,0:T(2,128)(2,1)}, u32[]{:S(2)}, u32[]{:S(2)}) async-start(bf16[8,2,122880]{2,1,0:T(2,128)(2,1)} %reshape.908), calls=%async_computation.5 | async-start | bytes 7864320 | tf_op jit(solution)/shard_map/all_to_all | solution.py:280
  873.7 176.6 %reduce-scatter.25.cloned.1.call-start = ((), (), s32[]{:S(2)}) async-start(), calls=%async_computation.28 | async-start | bytes 655360 | tf_op jit(solution)/shard_map/reduce_scatter | solution.py:343
  913.5 81.5 %copy-start.98 = (bf16[256,8]{0,1:T(8,128)(2,1)}, bf16[256,8]{0,1:T(8,128)(2,1)S(1)}, u32[]{:S(2)}) copy-start(bf16[256,8]{0,1:T(8,128)(2,1)S(1)} %multiply_convert_fusion.8) | copy-start | bytes 12292
  1030.1 44.4 %reduce-scatter.27.cloned.1.call-start = ((), (), s32[]{:S(2)}) async-start(), calls=%async_computation.29 | async-start | bytes 655360 | tf_op jit(solution)/shard_map/reduce_scatter | solution.py:346
  1049.4 25.1 %copy-start.14 = (f32[256,1536]{1,0:T(8,128)S(1)}, f32[256,1536]{1,0:T(8,128)}, u32[]{:S(2)}) copy-start(f32[256,1536]{1,0:T(8,128)} %copy-done.12) | copy-start | bytes 4718596
  1049.4 25.1 %copy-start.39 = (bf16[1,1536,256]{2,1,0:T(8,128)(2,1)S(1)}, bf16[1,1536,256]{2,1,0:T(8,128)(2,1)}, u32[]{:S(2)}) copy-start(bf16[1,1536,256]{2,1,0:T(8,128)(2,1)} %all-gather.8) | copy-start | bytes 2359300
  1049.4 25.1 %copy-start.89 = (f32[1536]{0:T(1024)S(1)}, f32[1536]{0:T(1024)}, u32[]{:S(2)}) copy-start(f32[1536]{0:T(1024)} %copy-done.88) | copy-start | bytes 18436
  1049.4 25.1 %copy-start.107 = (f32[256]{0:T(256)S(1)}, f32[256]{0:T(256)}, u32[]{:S(2)}) copy-start(f32[256]{0:T(256)} %copy-done.106) | copy-start | bytes 3076
  1099.9 104.8 %slice-start.9 = ((s8[4718592]{0:T(1024)(128)(4,1)}), s8[4194304]{0:T(1024)(128)(4,1)S(1)}, s32[]{:S(2)}) async-start(s8[4718592]{0:T(1024)(128)(4,1)} %bitcast.526), calls=%async_computation.62 | async-start | bytes 8388608
  1099.9 109.8 %slice-start.15 = ((s8[4718592]{0:T(1024)(128)(4,1)}), s8[4194304]{0:T(1024)(128)(4,1)S(1)}, s32[]{:S(2)}) async-start(s8[4718592]{0:T(1024)(128)(4,1)} %bitcast.532), calls=%async_computation.68 | async-start | bytes 8388608
  1293.7 91.4 %all-to-all-start.7 = ((bf16[8,2,122880]{2,1,0:T(2,128)(2,1)}), bf16[8,2,122880]{2,1,0:T(2,128)(2,1)}, u32[]{:S(2)}, u32[]{:S(2)}) async-start(bf16[8,2,122880]{2,1,0:T(2,128)(2,1)} %reshape.910), calls=%async_computation.9 | async-start | bytes 7864320 | tf_op jit(solution)/shard_map/all_to_all | solution.py:280
  1298.4 179.5 %reduce-scatter.31.cloned.1.call-start = ((), (), s32[]{:S(2)}) async-start(), calls=%async_computation.31 | async-start | bytes 655360 | tf_op jit(solution)/shard_map/reduce_scatter | solution.py:346
  1450.5 44.9 %reduce-scatter.29.cloned.1.call-start = ((), (), s32[]{:S(2)}) async-start(), calls=%async_computation.30 | async-start | bytes 655360 | tf_op jit(solution)/shard_map/reduce_scatter | solution.py:343
  1466.5 98.5 %reduce-scatter.43.cloned.1.call-start = ((), (), s32[]{:S(2)}) async-start(), calls=%async_computation.37 | async-start | bytes 983040 | tf_op jit(solution)/shard_map/reduce_scatter | solution.py:390
  1468.0 97.0 %reduce-scatter.39.cloned.1.call-start = ((), (), s32[]{:S(2)}) async-start(), calls=%async_computation.35 | async-start | bytes 983040 | tf_op jit(solution)/shard_map/reduce_scatter | solution.py:387
  1469.4 128.8 %reduce-scatter.47.cloned.1.call-start = ((), (), s32[]{:S(2)}) async-start(), calls=%async_computation.39 | async-start | bytes 5898240 | tf_op jit(solution)/shard_map/reduce_scatter | solution.py:393
  1473.0 176.1 %reduce-scatter.35.cloned.1.call-start = ((), (), s32[]{:S(2)}) async-start(), calls=%async_computation.33 | async-start | bytes 5898240 | tf_op jit(solution)/shard_map/reduce_scatter | solution.py:384
  1477.8 197.2 %reduce-scatter.41.cloned.1.call-start = ((), (), s32[]{:S(2)}) async-start(), calls=%async_computation.36 | async-start | bytes 983040 | tf_op jit(solution)/shard_map/reduce_scatter | solution.py:390
  1481.3 219.6 %reduce-scatter.37.cloned.1.call-start = ((), (), s32[]{:S(2)}) async-start(), calls=%async_computation.34 | async-start | bytes 983040 | tf_op jit(solution)/shard_map/reduce_scatter | solution.py:387
  1497.8 253.3 %reduce-scatter.45.cloned.1.call-start = ((), (), s32[]{:S(2)}) async-start(), calls=%async_computation.38 | async-start | bytes 5898240 | tf_op jit(solution)/shard_map/reduce_scatter | solution.py:393
  1501.4 300.7 %reduce-scatter.33.cloned.1.call-start = ((), (), s32[]{:S(2)}) async-start(), calls=%async_computation.32 | async-start | bytes 5898240 | tf_op jit(solution)/shard_map/reduce_scatter | solution.py:384
  1511.4 314.5 %reduce-scatter.63.cloned.1.call-start = ((), (), s32[]{:S(2)}) async-start(), calls=%async_computation.51 | async-start | bytes 491520
  1514.3 334.8 %reduce-scatter.61.cloned.1.call-start = ((), (), s32[]{:S(2)}) async-start(), calls=%async_computation.50 | async-start | bytes 491520
  1515.6 369.8 %reduce-scatter.51.cloned.1.call-start = ((), (), s32[]{:S(2)}) async-start(), calls=%async_computation.41 | async-start | bytes 2949120 | tf_op jit(solution)/shard_map/reduce_scatter | solution.py:295
  1523.3 398.3 %reduce-scatter.49.cloned.1.call-start = ((), (), s32[]{:S(2)}) async-start(), calls=%async_computation.40 | async-start | bytes 2949120 | tf_op jit(solution)/shard_map/reduce_scatter | solution.py:295
  1530.8 426.4 %reduce-scatter.55.cloned.1.call-start = ((), (), s32[]{:S(2)}) async-start(), calls=%async_computation.43 | async-start | bytes 2949120 | tf_op jit(solution)/shard_map/reduce_scatter | solution.py:298
  1539.7 453.2 %reduce-scatter.53.cloned.1.call-start = ((), (), s32[]{:S(2)}) async-start(), calls=%async_computation.42 | async-start | bytes 2949120 | tf_op jit(solution)/shard_map/reduce_scatter | solution.py:298
  1548.8 479.8 %reduce-scatter.59.cloned.1.call-start = ((), (), s32[]{:S(2)}) async-start(), calls=%async_computation.45 | async-start | bytes 2949120 | tf_op jit(solution)/shard_map/reduce_scatter | solution.py:301
  1556.3 507.9 %reduce-scatter.57.cloned.1.call-start = ((), (), s32[]{:S(2)}) async-start(), calls=%async_computation.44 | async-start | bytes 2949120 | tf_op jit(solution)/shard_map/reduce_scatter | solution.py:301
  1564.7 237.5 %copy-start.132 = (u32[32]{0:T(128)S(1)}, u32[32]{0:T(128)}, u32[]{:S(2)}) copy-start(u32[32]{0:T(128)} %constant.126) | copy-start | bytes 388
  1564.7 697.9 %all-reduce.17.cloned.1.call-start = ((), (), s32[]{:S(2)}) async-start(), calls=%async_computation.52 | async-start | bytes 11010048 | tf_op jit(solution)/shard_map/psum | solution.py:407
  1924.3 142.7 %copy-start.51 = (bf16[256,12,128]{0,2,1:T(8,128)(2,1)S(1)}, bf16[256,12,128]{0,2,1:T(8,128)(2,1)}, u32[]{:S(2)}) copy-start(bf16[256,12,128]{0,2,1:T(8,128)(2,1)} %copy-done.50) | copy-start | bytes 2359300
  2070.9 55.3 %copy-start.120 = (f32[256]{0:T(256)S(1)}, f32[256]{0:T(256)}, u32[]{:S(2)}) copy-start(f32[256]{0:T(256)} %copy-done.119) | copy-start | bytes 3076
  (124 other events, 749.8 us)
Sparse Core Ops, SparseCore 0:
  10.7 44.3 all-gather.18
  57.3 44.6 all-gather.20
  125.7 38.8 all-gather.22
  316.1 43.2 all-gather.24
  1030.2 20.0 reduce-scatter.24
  1052.8 21.6 reduce-scatter.26
  1450.7 19.7 reduce-scatter.30
  1473.7 21.6 reduce-scatter.28
  1498.0 23.2 reduce-scatter.42
  1524.4 23.2 reduce-scatter.38
  1550.3 47.8 reduce-scatter.46
  1601.3 47.8 reduce-scatter.34
  1651.7 23.2 reduce-scatter.40
  1677.6 23.2 reduce-scatter.36
  1703.2 47.8 reduce-scatter.44
  1754.3 47.8 reduce-scatter.32
  1805.0 20.8 reduce-scatter.62
  1828.3 20.8 reduce-scatter.60
  1852.2 33.0 reduce-scatter.50
  1888.5 33.0 reduce-scatter.48
  1924.1 33.0 reduce-scatter.54
  1959.9 33.0 reduce-scatter.52
  1995.5 33.0 reduce-scatter.58
  2031.1 33.0 reduce-scatter.56
  2068.7 193.8 all-reduce.16
where the time goes:
time: 2290 us; the launch traced here: 2280 us
  waiting for transfers between devices  1070 us (47%)
  local copies, waits for them, and re-layouts  425 us (19%)
  matrix products  262 us (11%)
  blocking collectives  258 us (11%)
  other arithmetic  210 us (9%)
  starting transfers between devices  38.4 us (2%)
    all_to_all x2, waiting for transfers between devices, per_device(): lax.all_to_all(sending, 'expert', split_axis=0, concat_axis=1, tiled=True)  168 us
    psum x1, waiting for transfers between devices, per_device(): lax.psum(owned[0].astype(jnp.bfloat16), 'expert').astype(jnp.float32)  134 us
    all_to_all x2, waiting for transfers between devices, per_device(): lax.all_to_all(d_slot_rows, 'expert', split_axis=1, concat_axis=0, tiled=...  129 us
    unnamed x335, local copies, waits for them, and re-layouts  114 us
    unnamed x13, other arithmetic  108 us
    reduce_scatter x2, waiting for transfers between devices, per_device(): lax.psum_scatter(attn_terms[0].astype(jnp.bfloat16), 'shard', scatter_dim...  102 us
    all_to_all x1, blocking collectives, per_device(): lax.all_to_all(d_sending, 'expert', split_axis=0, concat_axis=1, tiled=True)  93.7 us
    convert_element_type x2, local copies, waits for them, and re-layouts, per_device(): d_slot_rows = (d_slot_rows + jnp.einsum('erf,edf->erd', d_up_low, w_up, p...  87.3 us
  transfers between devices with their start and end apart: 32, of which 24 were waited for; matrix products, arithmetic and copies ran while one was open for 21% of the time, Pallas kernels for 0%

commit v1 on v0

v1 whole, which is shorter than its diff:
```python
import jax
import jax.numpy as jnp
from jax import lax
from jax.sharding import PartitionSpec as P

QUERY_HEADS = 12
KEY_VALUE_HEADS = 2
HEAD_SIZE = 128

norm_eps = 1e-06
rope_base = 10000.0
masked_score = -1e30

bf16 = jnp.bfloat16
f32 = jnp.float32


def mm(left, right):
    return jnp.dot(left, right, preferred_element_type=f32)


def mm_tn(left, right):
    return lax.dot_general(left, right, (((0,), (0,)), ((), ())), preferred_element_type=f32)


def mm_nt(left, right):
    return lax.dot_general(left, right, (((1,), (1,)), ((), ())), preferred_element_type=f32)


def norm_forward(values, gain):
    inverse = lax.rsqrt(jnp.mean(values * values, axis=-1, keepdims=True) + norm_eps)
    return values * inverse * gain, inverse


def norm_backward(values, inverse, gain, grad):
    scaled = grad * gain
    mean_part = jnp.mean(values * scaled, axis=-1, keepdims=True)
    d_values = inverse * scaled - values * (inverse * inverse * inverse * mean_part)
    d_gain = jnp.sum(grad * values * inverse, axis=0)
    return d_values, d_gain


def rotary_tables(position):
    half_width = HEAD_SIZE // 2
    frequency = rope_base ** (-(jnp.arange(half_width).astype(f32) * 2.0 / HEAD_SIZE))
    angles = position.astype(f32)[:, None] * frequency[None, :]
    return jnp.cos(angles)[:, None, :], jnp.sin(angles)[:, None, :]


def rotary_apply(values, tables, head_count, direction):
    cosine, sine = tables
    sine = direction * sine
    half_width = HEAD_SIZE // 2
    split_rows = values.reshape(values.shape[0], head_count, HEAD_SIZE)
    first_half = split_rows[:, :, :half_width]
    second_half = split_rows[:, :, half_width:]
    turned = jnp.concatenate(
        [first_half * cosine - second_half * sine, second_half * cosine + first_half * sine],
        axis=-1,
    )
    return turned.reshape(values.shape[0], head_count * HEAD_SIZE)


def documents(lengths_row, position):
    doc_ends = jnp.cumsum(lengths_row)
    doc_starts = doc_ends - lengths_row
    document_index = jnp.sum((position[:, None] >= doc_ends[None, :]).astype(jnp.int32), axis=1)
    doc_first = jnp.max(
        jnp.where(doc_starts[None, :] <= position[:, None], doc_starts[None, :], 0), axis=1
    )
    return (document_index, position - doc_first)


def slot_table(routes, order_row, experts, capacity):
    token_rows, top_count = routes.shape
    pair_count = token_rows * top_count
    pairs = jnp.arange(pair_count, dtype=jnp.int32)
    named = (order_row[:, None] == pairs[None, :]).astype(bf16)
    of_pair = (
        routes.reshape(pair_count)[:, None] == jnp.arange(experts, dtype=jnp.int32)[None, :]
    ).astype(bf16)
    ranked = mm(named, of_pair)
    earlier = (pairs[None, :] < pairs[:, None]).astype(bf16)
    before = mm(earlier, ranked.astype(bf16))
    code = jnp.where(before < capacity, before + 1.0, -1.0) * ranked
    back = mm_tn(code.astype(bf16), named)
    return jnp.sum(back.reshape(experts, token_rows, top_count), axis=2)


def chosen_softmax(logits, chosen):
    top = jnp.max(jnp.where(chosen, logits, masked_score), axis=-1, keepdims=True)
    weight = jnp.where(chosen, jnp.exp(jnp.where(chosen, logits - top, 0.0)), 0.0)
    total = jnp.sum(weight, axis=-1, keepdims=True)
    return weight / jnp.where(total > 0.0, total, 1.0)


class Lines:
    def __init__(self):
        self.experts = lax.axis_size("expert")
        self.count = self.experts // 2
        self.index = lax.axis_index("expert")
        self.line = self.index // 2
        self.side = self.index % 2

    def source(self, slot):
        count, line = self.count, self.line
        low = jnp.where(line + slot < count, line + slot, count - 1 - slot)
        mirror = count - 1 - line
        high = count - 1 - jnp.where(mirror + slot < count, mirror + slot, count - 1 - slot)
        return jnp.where(line < count // 2, low, high)

    def swap(self, values):
        return lax.ppermute(values, "expert", [(i, i ^ 1) for i in range(self.experts)])

    def shift(self, values, lines, delta):
        pairs = [(2 * i + k, 2 * (i + delta) + k) for i in lines for k in range(2)]
        return lax.ppermute(values, "expert", pairs)

    def gather(self, values):
        count = self.count
        above, below = {0: values}, {0: values}
        for step in range(1, count):
            below[step] = self.shift(below[step - 1], range(step - 1, count - 1), 1)
            above[step] = self.shift(above[step - 1], range(1, count - step + 1), -1)
        slots = [values]
        for slot in range(1, count):
            parts = {}
            for line in range(count):
                near = line if line < count // 2 else count - 1 - line
                toward = near + slot < count
                distance = slot if toward else near + slot + 1 - count
                up = toward == (line < count // 2)
                parts.setdefault((up, distance), []).append(line)
            chosen = None
            for (up, distance), lines in parts.items():
                block = above[distance] if up else below[distance]
                if chosen is None:
                    chosen = block
                else:
                    here = jnp.any(self.line == jnp.array(lines))
                    chosen = jnp.where(here, block, chosen)
            slots.append(chosen)
        return slots

    def reduce(self, blocks):
        count, line = self.count, self.line
        half = count // 2

        def pick(distance, up):
            near = {}
            for at in range(count):
                if up and at + distance >= count or not up and at - distance < 0:
                    continue
                if up:
                    slot = distance if at < half else at + distance
                else:
                    slot = distance if at >= half else count - 1 - at + distance
                near.setdefault(slot, []).append(at)
            value = None
            for slot, lines in near.items():
                if value is None:
                    value = blocks[slot]
                else:
                    value = jnp.where(jnp.any(line == jnp.array(lines)), blocks[slot], value)
            return value

        from_below = from_above = None
        for step in range(count - 1):
            distance = count - 1 - step
            up, down = pick(distance, True), pick(distance, False)
            if from_below is not None:
                up = up + from_below.astype(f32)
                down = down + from_above.astype(f32)
            from_below = self.shift(up.astype(bf16), range(0, step + 1), 1)
            from_above = self.shift(down.astype(bf16), range(count - 1 - step, count), -1)
        return blocks[0] + from_below.astype(f32) + from_above.astype(f32)


def core_swap(values):
    return lax.ppermute(values, "shard", [(i, i ^ 1) for i in range(lax.axis_size("shard"))])


def row_swap(values):
    return lax.ppermute(values, "shard", [(i, i ^ 2) for i in range(lax.axis_size("shard"))])


def gather_weight(shard_rows):
    mine = lax.axis_index("shard")
    rows = shard_rows.shape[0]
    across = row_swap(shard_rows)
    beside = core_swap(shard_rows)
    diagonal = core_swap(across)
    whole = jnp.zeros((4 * rows, shard_rows.shape[1]), shard_rows.dtype)
    for mask, block in ((0, shard_rows), (2, across), (1, beside), (3, diagonal)):
        whole = lax.dynamic_update_slice(whole, block, ((mine ^ mask) * rows, 0))
    return whole


def split_columns(values):
    mine = lax.axis_index("shard")
    width = values.shape[1] // 4
    return [
        lax.dynamic_slice(values, (0, (mine ^ mask) * width), (values.shape[0], width))
        for mask in range(4)
    ]


def scattered_product(columns, right):
    width = columns[0].shape[1]
    sent = mm_tn(jnp.concatenate([columns[3], columns[1]], axis=1), right).astype(bf16)
    arrived = core_swap(sent).astype(f32)
    across = mm_tn(columns[2], right) + arrived[:width]
    crossed = row_swap(across.astype(bf16)).astype(f32)
    return mm_tn(columns[0], right) + arrived[width:] + crossed


def sum_over_experts(lines, part):
    rows, width = part.shape
    half = rows // 2
    block = half // lines.count
    low = part.astype(bf16)
    given = lax.dynamic_slice(low, ((1 - lines.side) * half, 0), (half, width))
    kept = lax.dynamic_slice(part, (lines.side * half, 0), (half, width))
    kept = kept + lines.swap(given).astype(f32)
    blocks = [
        lax.dynamic_slice(kept, (lines.source(slot) * block, 0), (block, width))
        for slot in range(lines.count)
    ]
    own = lines.reduce(blocks).astype(bf16)
    slots = lines.gather(own)
    mine = jnp.zeros((half, width), bf16)
    for slot in range(lines.count):
        mine = lax.dynamic_update_slice(mine, slots[slot], (lines.source(slot) * block, 0))
    other = lines.swap(mine)
    whole = jnp.zeros((rows, width), bf16)
    whole = lax.dynamic_update_slice(whole, mine, (lines.side * half, 0))
    whole = lax.dynamic_update_slice(whole, other, ((1 - lines.side) * half, 0))
    return whole.astype(f32)


def per_device(
    tokens,
    lengths,
    routes,
    slot_order,
    cotangent,
    q_weight,
    key_matrix,
    value_matrix,
    out_weight,
    router_weight,
    attn_gain,
    ffn_gain,
    gate_weight,
    up_weight,
    down_weight,
):
    lines = Lines()
    layer_count = q_weight.shape[0]
    shard_count = lax.axis_size("shard")
    mine = lax.axis_index("shard")
    token_rows, model_width = tokens.shape
    top_count = routes.shape[1]
    pair_count = token_rows * top_count
    experts = router_weight.shape[2]
    assert shard_count == 4 and experts == lines.experts and gate_weight.shape[1] == 1
    hidden_units = gate_weight.shape[3]
    capacity = (pair_count * 5 + 4 * experts - 1) // (4 * experts)
    assert capacity < 256
    sequence_length = token_rows * shard_count
    group_width = QUERY_HEADS // KEY_VALUE_HEADS
    kv_width = KEY_VALUE_HEADS * HEAD_SIZE
    score_scale = HEAD_SIZE ** (-0.5)

    own_rows = jnp.arange(token_rows, dtype=jnp.int32)
    position = mine * token_rows + own_rows
    key_position = jnp.concatenate([(mine ^ mask) * token_rows + own_rows for mask in (0, 2, 1, 3)])
    query_doc, query_position = documents(lengths[0], position)
    key_doc = documents(lengths[0], key_position)[0]
    visible = (query_doc[:, None] == key_doc[None, :]) & (
        key_position[None, :] <= position[:, None]
    )
    tables = rotary_tables(query_position)

    qkv_shards = [
        (q_weight[i], jnp.concatenate([key_matrix[i], value_matrix[i]], axis=1))
        for i in range(layer_count)
    ]
    gathered = []
    for i in range(layer_count):
        if i == 0:
            w_kv, w_query = gather_weight(qkv_shards[i][1]), gather_weight(qkv_shards[i][0])
        else:
            w_kv = lax.all_gather(qkv_shards[i][1], "shard", axis=0, tiled=True)
            w_query = lax.all_gather(qkv_shards[i][0], "shard", axis=0, tiled=True)
        w_out = lax.all_gather(out_weight[i], "shard", axis=0, tiled=True)
        gathered.append((w_query, w_kv, w_out))
    small = jnp.concatenate(
        [
            router_weight.transpose(0, 2, 1),
            attn_gain[:, None, :],
            ffn_gain[:, None, :],
        ],
        axis=1,
    )
    small = lax.all_gather(small, "shard", axis=2, tiled=True)
    routers = [small[i, :experts] for i in range(layer_count)]
    attn_gains = [small[i, experts].astype(f32)[None, :] for i in range(layer_count)]
    ffn_gains = [small[i, experts + 1].astype(f32)[None, :] for i in range(layer_count)]

    own_table = slot_table(routes, slot_order[0], experts, capacity)
    chosen_here = own_table.T != 0.0
    all_tables = lax.all_gather(own_table, "expert", axis=0)
    slot_code = jnp.arange(1, capacity + 1, dtype=jnp.int32).astype(f32)[:, None]
    mates = []
    own_hot, mate_hot, row_chosen = [], [], []
    for column in range(2):
        for slot in range(lines.count):
            source = lines.source(slot) * 2 + (lines.side ^ column)
            at_source = lax.dynamic_index_in_dim(all_tables, source, 0, keepdims=False)
            for_own = lax.dynamic_index_in_dim(at_source, lines.index, 0, keepdims=True)
            hot = (for_own == slot_code).astype(bf16)
            row_chosen.append(mm_nt(hot, (at_source != 0.0).astype(bf16)))
            if column == 0:
                own_hot.append(hot)
                for_mate = lax.dynamic_index_in_dim(at_source, lines.index ^ 1, 0, keepdims=True)
                mate_hot.append((for_mate == slot_code).astype(bf16))
            mates.append((source, hot))
    row_chosen = jnp.concatenate(row_chosen, axis=0) > 0.5

    def dispatch(values):
        slots = lines.gather(values)
        far = [lines.swap(mm(mate_hot[j], slots[j]).astype(bf16)) for j in range(lines.count)]
        near = [mm(own_hot[j], slots[j]).astype(bf16) for j in range(lines.count)]
        return jnp.concatenate(near + far, axis=0)

    def give_back(rows):
        blocks = [rows[i * capacity : (i + 1) * capacity] for i in range(2 * lines.count)]
        parts = [None] * lines.count
        for j in reversed(range(lines.count)):
            arrived = lines.swap(blocks[lines.count + j])
            parts[j] = mm_tn(own_hot[j], blocks[j]) + mm_tn(mate_hot[j], arrived)
        return lines.reduce(parts)

    def gate_grads_back(row_values):
        blocks = row_values.reshape(2 * lines.count, capacity)
        spread = jnp.zeros((experts, token_rows), f32)
        for i, (source, hot) in enumerate(mates):
            dense = jnp.sum(hot.astype(f32) * blocks[i][:, None], axis=0, keepdims=True)
            spread = lax.dynamic_update_slice(spread, dense, (source, 0))
        return lax.all_to_all(spread, "expert", split_axis=0, concat_axis=0, tiled=True).T

    def expert_forward(i, arrived):
        logits = mm_nt(arrived, routers[i])
        gates = chosen_softmax(logits, row_chosen)
        own_gate = lax.dynamic_slice(gates, (0, lines.index), (gates.shape[0], 1))
        gate_pre = mm(arrived, gate_weight[i, 0])
        up_pre = mm(arrived, up_weight[i, 0])
        active = jax.nn.gelu(gate_pre, approximate=True) * up_pre
        gated = (own_gate * active).astype(bf16)
        produced = mm(gated, down_weight[i, 0]).astype(bf16)
        return produced, dict(gate=own_gate, gate_pre=gate_pre, up_pre=up_pre, gated=gated)

    def expert_backward(i, arrived, kept, d_arrived):
        du = mm_nt(d_arrived, down_weight[i, 0])
        unit, pull = jax.vjp(
            lambda a, b: jax.nn.gelu(a, approximate=True) * b, kept["gate_pre"], kept["up_pre"]
        )
        d_gate_rows = jnp.sum(du * unit, axis=1)
        d_active = (kept["gate"] * du).astype(bf16).astype(f32)
        d_gate_pre, d_up_pre = pull(d_active)
        d_both = jnp.concatenate([d_gate_pre.astype(bf16), d_up_pre.astype(bf16)], axis=1)
        both_weight = jnp.concatenate([gate_weight[i, 0], up_weight[i, 0]], axis=1)
        d_rows = mm_nt(d_both, both_weight).astype(bf16)
        both_grad = scattered_product(split_columns(arrived), d_both)
        down_grad = scattered_product(split_columns(kept["gated"]), d_arrived)
        return d_rows, d_gate_rows, both_grad, down_grad

    stream = tokens.astype(f32)
    stored = []
    d_arrived_last = dispatch(cotangent)
    for i in range(layer_count):
        w_query, w_kv, w_out = gathered[i]
        normed, attn_inverse = norm_forward(stream, attn_gains[i])
        hidden = normed.astype(bf16)
        kv_pre = mm(hidden, w_kv)
        keys = rotary_apply(kv_pre[:, :kv_width], tables, KEY_VALUE_HEADS, 1.0)
        kv_own = jnp.concatenate([keys, kv_pre[:, kv_width:]], axis=1).astype(bf16)
        kv_pair = jnp.concatenate([kv_own, row_swap(kv_own)], axis=0)
        kv_all = jnp.concatenate([kv_pair, core_swap(kv_pair)], axis=0)
        q_pre = mm(hidden, w_query)
        query_heads = rotary_apply(q_pre, tables, QUERY_HEADS, 1.0).astype(bf16)
        query_heads = query_heads.reshape(token_rows, KEY_VALUE_HEADS, group_width, HEAD_SIZE)
        key_heads = kv_all[:, :kv_width].reshape(sequence_length, KEY_VALUE_HEADS, HEAD_SIZE)
        value_heads = kv_all[:, kv_width:].reshape(sequence_length, KEY_VALUE_HEADS, HEAD_SIZE)
        raw_scores = jnp.einsum(
            "qhgd,khd->hgqk", query_heads, key_heads, preferred_element_type=f32
        )
        scores = jnp.where(visible, raw_scores * score_scale, masked_score)
        row_peak = jnp.max(scores, axis=-1, keepdims=True)
        exponent = jnp.exp(scores - row_peak)
        row_total = jnp.sum(exponent, axis=-1, keepdims=True)
        probs_low = (exponent / row_total).astype(bf16)
        log_total = row_peak + jnp.log(row_total)
        mixed = (
            jnp.einsum("hgqk,khd->qhgd", probs_low, value_heads, preferred_element_type=f32)
            .reshape(token_rows, QUERY_HEADS * HEAD_SIZE)
            .astype(bf16)
        )
        stream_mid = stream + mm(mixed, w_out)
        normed_ffn, ffn_inverse = norm_forward(stream_mid, ffn_gains[i])
        routed = normed_ffn.astype(bf16)
        gates = chosen_softmax(mm_nt(routed, routers[i]), chosen_here)
        arrived = dispatch(routed)
        produced, kept = expert_forward(i, arrived)
        stored.append(
            dict(
                stream=stream,
                attn_inverse=attn_inverse,
                hidden=hidden,
                query_heads=query_heads,
                key_heads=key_heads,
                value_heads=value_heads,
                log_total=log_total,
                mixed=mixed,
                stream_mid=stream_mid,
                ffn_inverse=ffn_inverse,
                routed=routed,
                gates=gates,
                arrived=arrived,
                kept=kept,
            )
        )
        stream = stream_mid + give_back(produced)
    output = stream.astype(bf16)

    upstream = cotangent.astype(f32)
    d_arrived = d_arrived_last
    grads = [None] * layer_count
    for i in reversed(range(layer_count)):
        w_query, w_kv, w_out = gathered[i]
        saved = stored[i]
        if i < layer_count - 1:
            d_arrived = dispatch(upstream.astype(bf16))
        d_rows, d_gate_rows, both_grad, down_grad = expert_backward(
            i, saved["arrived"], saved["kept"], d_arrived
        )
        d_gates = gate_grads_back(d_gate_rows)
        gates = saved["gates"]
        d_logits = gates * (d_gates - jnp.sum(gates * d_gates, axis=1, keepdims=True))
        d_logits = d_logits.astype(bf16)
        router_grad = mm_tn(d_logits, saved["routed"])
        d_routed = give_back(d_rows) + mm(d_logits, routers[i])
        d_stream, ffn_gain_grad = norm_backward(
            saved["stream_mid"], saved["ffn_inverse"], ffn_gains[i], d_routed
        )
        upstream = upstream + d_stream
        d_branch = upstream.astype(bf16)
        mixed = saved["mixed"]
        d_mixed = (
            mm_nt(d_branch, w_out)
            .astype(bf16)
            .reshape(token_rows, KEY_VALUE_HEADS, group_width, HEAD_SIZE)
        )
        out_grad = scattered_product(split_columns(mixed), d_branch)
        out_grad = sum_over_experts(lines, out_grad)
        query_heads, key_heads = saved["query_heads"], saved["key_heads"]
        value_heads = saved["value_heads"]
        raw_scores = jnp.einsum(
            "qhgd,khd->hgqk", query_heads, key_heads, preferred_element_type=f32
        )
        scores = jnp.where(visible, raw_scores * score_scale, masked_score)
        probs_full = jnp.exp(scores - saved["log_total"])
        d_probs = jnp.einsum("qhgd,khd->hgqk", d_mixed, value_heads, preferred_element_type=f32)
        d_scores = (
            probs_full * (d_probs - jnp.sum(probs_full * d_probs, axis=-1, keepdims=True))
        ).astype(bf16)
        probs_low = probs_full.astype(bf16)
        d_value_all = jnp.einsum(
            "hgqk,qhgd->khd", probs_low, d_mixed, preferred_element_type=f32
        ).reshape(sequence_length, kv_width)
        d_key_all = (
            jnp.einsum("hgqk,qhgd->khd", d_scores, query_heads, preferred_element_type=f32)
            * score_scale
        ).reshape(sequence_length, kv_width)
        d_kv = jnp.concatenate([d_key_all, d_value_all], axis=1)
        pair_rows = 2 * token_rows
        d_kv_pair = d_kv[:pair_rows] + core_swap(d_kv[pair_rows:].astype(bf16)).astype(f32)
        d_kv_own = d_kv_pair[:token_rows] + row_swap(d_kv_pair[token_rows:].astype(bf16)).astype(
            f32
        )
        d_query = (
            jnp.einsum("hgqk,khd->qhgd", d_scores, key_heads, preferred_element_type=f32)
            * score_scale
        ).reshape(token_rows, QUERY_HEADS * HEAD_SIZE)
        d_q_low = rotary_apply(d_query, tables, QUERY_HEADS, -1.0).astype(bf16)
        d_kv_low = jnp.concatenate(
            [
                rotary_apply(d_kv_own[:, :kv_width], tables, KEY_VALUE_HEADS, -1.0),
                d_kv_own[:, kv_width:],
            ],
            axis=1,
        ).astype(bf16)
        d_hidden = mm_nt(d_q_low, w_query) + mm_nt(d_kv_low, w_kv)
        d_stream, attn_gain_grad = norm_backward(
            saved["stream"], saved["attn_inverse"], attn_gains[i], d_hidden
        )
        upstream = upstream + d_stream
        hidden_columns = split_columns(saved["hidden"])
        q_grad = sum_over_experts(lines, scattered_product(hidden_columns, d_q_low))
        kv_grad = sum_over_experts(lines, scattered_product(hidden_columns, d_kv_low))
        small_grad = jnp.concatenate(
            [router_grad, attn_gain_grad[None, :], ffn_gain_grad[None, :]], axis=0
        )
        grads[i] = (
            q_grad,
            kv_grad[:, :kv_width],
            kv_grad[:, kv_width:],
            out_grad,
            small_grad,
            both_grad[:, :hidden_units],
            both_grad[:, hidden_units:],
            down_grad,
        )
    input_grad = upstream.astype(bf16)
    stacked = [jnp.stack([grads[i][k] for i in range(layer_count)], axis=0) for k in range(8)]
    small_sum = lax.psum(stacked[4], ("expert", "shard"))
    own_width = model_width // shard_count
    small_sum = lax.dynamic_slice(
        small_sum, (0, 0, mine * own_width), (layer_count, experts + 2, own_width)
    )
    return (
        output,
        input_grad,
        stacked[0],
        stacked[1],
        stacked[2],
        stacked[3],
        small_sum[:, :experts].transpose(0, 2, 1),
        small_sum[:, experts],
        small_sum[:, experts + 1],
        stacked[5][:, None],
        stacked[6][:, None],
        stacked[7][:, None],
    )


def solution(mesh):
    tokens_spec = P(("expert", "shard"), None)
    shard_spec = P(None, "shard", None)
    expert_spec = P(None, "expert", None, None)
    expert_grad_spec = P(None, "expert", "shard", None)
    return jax.shard_map(
        per_device,
        mesh=mesh,
        in_specs=(
            tokens_spec,
            P("expert", None),
            tokens_spec,
            tokens_spec,
            tokens_spec,
            shard_spec,
            shard_spec,
            shard_spec,
            shard_spec,
            shard_spec,
            P(None, "shard"),
            P(None, "shard"),
            expert_spec,
            expert_spec,
            expert_spec,
        ),
        out_specs=(
            tokens_spec,
            tokens_spec,
            shard_spec,
            shard_spec,
            shard_spec,
            shard_spec,
            shard_spec,
            P(None, "shard"),
            P(None, "shard"),
            expert_grad_spec,
            expert_grad_spec,
            expert_grad_spec,
        ),
        check_vma=False,
    )
```

time: 2290 us -> 1490 us (0.65)
  waiting for transfers between devices: 1070 us -> 525 us
  local copies, waits for them, and re-layouts: 425 us -> 115 us
  starting transfers between devices: 38.4 us -> 343 us
  blocking collectives: 258 us -> 48.2 us
  other arithmetic: 210 us -> 103 us
  matrix products: 262 us -> 319 us
    reduce_scatter x18 -> x0, waiting for transfers between devices: 479 us -> none  [the longest x2 102 us: per_device(): lax.psum_scatter(attn_terms[0].astype(jnp.bfloat16), 'shard', scatter_dim...]
    ppermute x0 -> x198, waiting for transfers between devices: none -> 433 us  [the longest x120 234 us: shift(): return lax.ppermute(values, 'expert', pairs)]
    all_to_all x7 -> x2, waiting for transfers between devices: 410 us -> 0.01 us  [gate_grads_back(): lax.all_to_all(spread, 'expert', split_axis=0, concat_axis=0, tiled=True)]
    ppermute x0 -> x198, starting transfers between devices: none -> 327 us  [the longest x120 250 us: shift(): return lax.ppermute(values, 'expert', pairs)]
    convert_element_type x10 -> x14, local copies, waits for them, and re-layouts: 198 us -> 4.77 us  [the longest x2 2.56 us: per_device(): d_mixed = mm_nt(d_branch, w_out).astype(bf16).reshape(token_rows, KEY_VAL...]
    unnamed x13 -> x18, other arithmetic: 108 us -> 4.68 us
    all_to_all x1 -> x0, blocking collectives: 93.7 us -> none  [per_device(): lax.all_to_all(d_sending, 'expert', split_axis=0, concat_axis=1, tiled=True)]
    unnamed x335 -> x625, local copies, waits for them, and re-layouts: 114 us -> 27.8 us
  transfers between devices with their start and end apart: 32 -> 205, of which waited for: 24 -> 74; matrix products, arithmetic and copies ran while one was open for 21% -> 32% of each run, Pallas kernels for 0% -> 0%
where the time goes in v1:
time: 1490 us; the launch traced here: 1470 us
  waiting for transfers between devices  525 us (35%)
  starting transfers between devices  343 us (23%)
  matrix products  319 us (21%)
  local copies, waits for them, and re-layouts  115 us (8%)
  other arithmetic  103 us (7%)
  blocking collectives  48.2 us (3%)
  between operations  21.2 us (1%)
    ppermute x120, starting transfers between devices, shift(): return lax.ppermute(values, 'expert', pairs)  250 us
    ppermute x120, waiting for transfers between devices, shift(): return lax.ppermute(values, 'expert', pairs)  234 us
    ppermute x44, waiting for transfers between devices, swap(): lax.ppermute(values, 'expert', [(i, i ^ 1) for i in range(self.experts)])  135 us
    dot_general x65, matrix products, mm_tn(): lax.dot_general(left, right, (((0,), (0,)), ((), ())), preferred_element_...  125 us
    psum x1, waiting for transfers between devices, per_device(): small_sum = lax.psum(stacked[4], ('expert', 'shard'))  91.9 us
    dot_general x47, matrix products, mm(): return jnp.dot(left, right, preferred_element_type=f32)  88.6 us
    ppermute x16, waiting for transfers between devices, row_swap(): lax.ppermute(values, 'shard', [(i, i ^ 2) for i in range(lax.axis_size('s...  64.3 us
    ppermute x44, starting transfers between devices, swap(): lax.ppermute(values, 'expert', [(i, i ^ 1) for i in range(self.experts)])  53.2 us
  transfers between devices with their start and end apart: 205, of which 74 were waited for; matrix products, arithmetic and copies ran while one was open for 32% of the time, Pallas kernels for 0%

profile of v1, /device:TPU:0, one launch (start us, length us, event | category | flops | bytes accessed | tf_op | source)
XLA Modules:
  0.0 1474.4 jit_solution(10589288701286235746)
XLA Ops:
  28.5 37.0 %all-gather.1 = f32[64,256]{1,0:T(8,128)S(1)} all-gather(f32[8,256]{1,0:T(8,128)S(1)} %copy.310), channel_id=3, replica_groups=mesh['expert'=8,'shard'=4] {'expert'}, dimensions={0}, use_global_device_ids=true | all-gather | bytes 73728 | tf_op jit(solution)/shard_map/all_gather | solution.py:313
  68.2 11.3 all_gather.21
  90.4 5.3 slice_bitcast_fusion.3
  125.7 8.1 collective-permute-done.51
  154.4 10.5 collective-permute-done.53
  194.2 15.0 %collective-permute-start.8 = (bf16[256,1536]{1,0:T(8,128)(2,1)S(1)}, bf16[256,1536]{1,0:T(8,128)(2,1)S(1)}, u32[]{:S(2)}, u32[]{:S(2)}) collective-permute-start(bf16[256,1536]{1,0:T(8,128)(2,1)S(1)} %multiply_convert_fusion.6), channel_id=1, source_target_pairs={{0,8},{4,12},{8,16},{12,20},{16,24},{20,28},{1,9},{5,13},{9,17},{1... | collective-permute-start | bytes 2359304 | tf_op jit(solution)/shard_map/ppermute | solution.py:117
  215.7 12.7 collective-permute-done.9
  233.8 12.9 collective-permute-done.11
  253.0 11.0 collective-permute-done.13
  268.7 9.5 collective-permute-done.16
  279.7 9.0 collective-permute-done.17
  294.2 6.1 multiply_convert_fusion.3
  300.3 5.9 convolution_convert_fusion.3
  309.5 5.7 collective-permute-done.19
  323.3 10.6 collective-permute-done.21
  339.6 8.0 collective-permute-done.23
  348.7 6.3 collective-permute-start.24
  356.8 5.1 fusion.115
  365.6 5.2 collective-permute-done.18
  419.8 13.8 collective-permute-done.30
  444.7 13.7 collective-permute-done.33
  465.1 13.0 collective-permute-done.35
  480.8 9.0 collective-permute-done.39
  491.0 5.4 fusion.615
  496.5 9.2 fusion.56
  505.7 6.6 convolution_convert_fusion.1
  543.8 5.3 convolution_convert_fusion.10
  551.0 5.7 convolution_convert_fusion.4
  565.4 8.6 collective-permute-done.61
  589.4 8.1 collective-permute-done.64
  602.7 5.6 collective-permute-done.43
  624.0 7.1 collective-permute-done.65
  634.4 11.9 collective-permute-done.45
  654.4 5.9 collective-permute-start.46
  680.1 9.3 fusion.12
  689.3 9.5 fusion.3
  698.9 7.1 fusion.5
  786.6 7.6 collective-permute-start.147
  823.8 7.8 collective-permute-done.154
  852.9 11.1 collective-permute-done.80
  864.0 8.8 collective-permute-done.175
  874.8 14.3 collective-permute-done.111
  891.4 9.5 fusion.49
  900.9 6.7 convolution_convert_fusion
  919.9 12.1 all-to-all-start.1
  932.0 5.1 convolution_convert_fusion.11
  937.2 5.7 convolution_convert_fusion.5
  959.4 11.1 collective-permute-done.83
  984.8 15.2 %collective-permute-done.178 = bf16[48,1536]{1,0:T(8,128)(2,1)S(1)} collective-permute-done((bf16[48,1536]{1,0:T(8,128)(2,1)S(1)}, bf16[48,1536]{1,0:T(8,128)(2,1)S(1)}, u32[]{:S(2)}, u32[]{:S(2)}) %collective-permute-start.178) | collective-permute-done | bytes 147488 | tf_op jit(solution)/shard_map/ppermute | solution.py:117
  1037.4 5.4 collective-permute-done.120
  1053.4 5.0 collective-permute-done.122
  1065.7 5.5 collective-permute-done.188
  1082.3 12.1 collective-permute-done.189
  1119.2 10.3 fusion
  1129.5 6.5 fusion.10
  1136.1 7.2 fusion.2
  1177.0 5.2 fusion.143
  1185.8 11.0 collective-permute-done.127
  1199.2 6.0 collective-permute-done.128
  1214.8 91.9 %all-reduce.2.cloned.1.call-done = f32[2,10,1536]{2,1,0:T(8,128)} async-done(((f32[2,10,1536]{2,1,0:T(8,128)}), f32[2,10,1536]{2,1,0:T(8,128)}) %all-reduce.2.cloned.1.call-update) | async-done | bytes 122896 | tf_op jit(solution)/shard_map/psum | solution.py:527
  1308.8 5.2 collective-permute-start.131
  1358.7 18.7 %collective-permute-done.95 = bf16[384,1536]{1,0:T(8,128)(2,1)S(1)} collective-permute-done((bf16[384,1536]{1,0:T(8,128)(2,1)S(1)}, bf16[384,1536]{1,0:T(8,128)(2,1)S(1)}, u32[]{:S(2)}, u32[]{:S(2)}) %collective-permute-start.95) | collective-permute-done | bytes 1179680 | tf_op jit(solution)/shard_map/ppermute | solution.py:184
  1411.9 5.2 collective-permute-start.99
  1453.4 5.2 collective-permute-done.173
  (1427 shorter events, 788.0 us)
Async XLA Ops:
  7.2 182.6 %all-gather.11.cloned.1.call-start = ((), (), s32[]{:S(2)}) async-start(), calls=%async_computation.4 | async-start | bytes 5898240 | tf_op jit(solution)/shard_map/all_gather | solution.py:296
  10.5 362.0 %all-gather.9.cloned.1.call-start = ((), (), s32[]{:S(2)}) async-start(), calls=%async_computation.2 | async-start | bytes 1966080 | tf_op jit(solution)/shard_map/all_gather | solution.py:294
  12.6 370.7 %all-gather.13.cloned.1.call-start = ((), (), s32[]{:S(2)}) async-start(), calls=%async_computation.5 | async-start | bytes 5898240 | tf_op jit(solution)/shard_map/all_gather | solution.py:295
  14.2 392.8 %all-gather.15.cloned.1.call-start = ((), (), s32[]{:S(2)}) async-start(), calls=%async_computation.6 | async-start | bytes 5898240 | tf_op jit(solution)/shard_map/all_gather | solution.py:296
  15.2 87.0 %collective-permute-start = (bf16[384,512]{1,0:T(8,128)(2,1)}, bf16[384,512]{1,0:T(8,128)(2,1)}, u32[]{:S(2)}, u32[]{:S(2)}) collective-permute-start(bf16[384,512]{1,0:T(8,128)(2,1)} %get-tuple-element.261), channel_id=1, source_target_pairs={{0,2},{1,3},{2,0},{3,1},{4,6},{5,7},{6,4},{7,5},{8,10},{9,11},{10,... | collective-permute-start | bytes 1179656 | tf_op jit(solution)/shard_map/ppermute | solution.py:184
  18.2 93.9 %collective-permute-start.1 = (bf16[384,512]{1,0:T(8,128)(2,1)}, bf16[384,512]{1,0:T(8,128)(2,1)}, u32[]{:S(2)}, u32[]{:S(2)}) collective-permute-start(bf16[384,512]{1,0:T(8,128)(2,1)} %get-tuple-element.261), channel_id=1, source_target_pairs={{0,1},{1,0},{2,3},{3,2},{4,5},{5,4},{6,7},{7,6},{8,9},{9,8},{10,11... | collective-permute-start | bytes 1179656 | tf_op jit(solution)/shard_map/ppermute | solution.py:180
  18.2 124.7 %collective-permute-start.5 = (bf16[384,1536]{1,0:T(8,128)(2,1)}, bf16[384,1536]{1,0:T(8,128)(2,1)}, u32[]{:S(2)}, u32[]{:S(2)}) collective-permute-start(bf16[384,1536]{1,0:T(8,128)(2,1)} %get-tuple-element.188), channel_id=1, source_target_pairs={{0,2},{1,3},{2,0},{3,1},{4,6},{5,7},{6,4},{7,5},{8,10},{9,11},{10,... | collective-permute-start | bytes 3538952 | tf_op jit(solution)/shard_map/ppermute | solution.py:184
  18.2 127.2 %collective-permute-start.6 = (bf16[384,1536]{1,0:T(8,128)(2,1)}, bf16[384,1536]{1,0:T(8,128)(2,1)}, u32[]{:S(2)}, u32[]{:S(2)}) collective-permute-start(bf16[384,1536]{1,0:T(8,128)(2,1)} %get-tuple-element.188), channel_id=1, source_target_pairs={{0,1},{1,0},{2,3},{3,2},{4,5},{5,4},{6,7},{7,6},{8,9},{9,8},{10,11... | collective-permute-start | bytes 3538952 | tf_op jit(solution)/shard_map/ppermute | solution.py:180
  18.7 105.4 %collective-permute-start.50 = (bf16[256,1536]{1,0:T(8,128)(2,1)S(1)}, bf16[256,1536]{1,0:T(8,128)(2,1)}, u32[]{:S(2)}, u32[]{:S(2)}) collective-permute-start(bf16[256,1536]{1,0:T(8,128)(2,1)S(1)} %copy-done.21), channel_id=1, source_target_pairs={{0,8},{4,12},{8,16},{12,20},{16,24},{20,28},{1,9},{5,13},{9,17},{1... | collective-permute-start | bytes 2359304 | tf_op jit(solution)/shard_map/ppermute | solution.py:117
  114.5 193.5 %collective-permute-start.56 = (bf16[160,1536]{1,0:T(8,128)(2,1)}, bf16[160,1536]{1,0:T(8,128)(2,1)}, u32[]{:S(2)}, u32[]{:S(2)}) collective-permute-start(bf16[160,1536]{1,0:T(8,128)(2,1)} %convolution_convert_fusion.23), channel_id=1, source_target_pairs={{0,4},{4,0},{8,12},{12,8},{16,20},{20,16},{24,28},{28,24},{1,5},{5... | collective-permute-start | bytes 1474568 | tf_op jit(solution)/shard_map/ppermute | solution.py:113
  141.3 23.5 %collective-permute-start.53 = (bf16[256,1536]{1,0:T(8,128)(2,1)}, bf16[256,1536]{1,0:T(8,128)(2,1)}, u32[]{:S(2)}, u32[]{:S(2)}) collective-permute-start(bf16[256,1536]{1,0:T(8,128)(2,1)} %collective-permute-done.51), channel_id=1, source_target_pairs={{8,0},{12,4},{16,8},{20,12},{9,1},{13,5},{17,9},{21,13},{10,2},{14... | collective-permute-start | bytes 2359304 | tf_op jit(solution)/shard_map/ppermute | solution.py:117
  145.4 26.9 %collective-permute-start.7 = (bf16[384,1536]{1,0:T(8,128)(2,1)}, bf16[384,1536]{1,0:T(8,128)(2,1)}, u32[]{:S(2)}, u32[]{:S(2)}) collective-permute-start(bf16[384,1536]{1,0:T(8,128)(2,1)} %collective-permute-done.5), channel_id=1, source_target_pairs={{0,1},{1,0},{2,3},{3,2},{4,5},{5,4},{6,7},{7,6},{8,9},{9,8},{10,11... | collective-permute-start | bytes 3538952 | tf_op jit(solution)/shard_map/ppermute | solution.py:180
  148.2 170.6 %collective-permute-start.57 = (bf16[160,1536]{1,0:T(8,128)(2,1)}, bf16[160,1536]{1,0:T(8,128)(2,1)}, u32[]{:S(2)}, u32[]{:S(2)}) collective-permute-start(bf16[160,1536]{1,0:T(8,128)(2,1)} %convolution_convert_fusion.22), channel_id=1, source_target_pairs={{0,4},{4,0},{8,12},{12,8},{16,20},{20,16},{24,28},{28,24},{1,5},{5... | collective-permute-start | bytes 1474568 | tf_op jit(solution)/shard_map/ppermute | solution.py:113
  152.8 56.4 %collective-permute-start.54 = (bf16[256,1536]{1,0:T(8,128)(2,1)}, bf16[256,1536]{1,0:T(8,128)(2,1)}, u32[]{:S(2)}, u32[]{:S(2)}) collective-permute-start(bf16[256,1536]{1,0:T(8,128)(2,1)} %collective-permute-done.52), channel_id=1, source_target_pairs={{16,24},{20,28},{17,25},{21,29},{18,26},{22,30},{19,27},{23,31}} | collective-permute-start | bytes 2359304 | tf_op jit(solution)/shard_map/ppermute | solution.py:117
  164.9 45.6 %collective-permute-start.55 = (bf16[256,1536]{1,0:T(8,128)(2,1)}, bf16[256,1536]{1,0:T(8,128)(2,1)}, u32[]{:S(2)}, u32[]{:S(2)}) collective-permute-start(bf16[256,1536]{1,0:T(8,128)(2,1)} %collective-permute-done.53), channel_id=1, source_target_pairs={{8,0},{12,4},{9,1},{13,5},{10,2},{14,6},{11,3},{15,7}} | collective-permute-start | bytes 2359304 | tf_op jit(solution)/shard_map/ppermute | solution.py:117
  230.0 36.4 %collective-permute-start.14 = (bf16[160,1536]{1,0:T(8,128)(2,1)S(1)}, bf16[160,1536]{1,0:T(8,128)(2,1)S(1)}, u32[]{:S(2)}, u32[]{:S(2)}) collective-permute-start(bf16[160,1536]{1,0:T(8,128)(2,1)S(1)} %convolution_convert_fusion.39), channel_id=1, source_target_pairs={{0,4},{4,0},{8,12},{12,8},{16,20},{20,16},{24,28},{28,24},{1,5},{5... | collective-permute-start | bytes 1474568 | tf_op jit(solution)/shard_map/ppermute | solution.py:113
  267.1 52.9 %collective-permute-start.58 = (bf16[160,1536]{1,0:T(8,128)(2,1)S(1)}, bf16[160,1536]{1,0:T(8,128)(2,1)S(1)}, u32[]{:S(2)}, u32[]{:S(2)}) collective-permute-start(bf16[160,1536]{1,0:T(8,128)(2,1)S(1)} %copy-done.138), channel_id=1, source_target_pairs={{0,4},{4,0},{8,12},{12,8},{16,20},{20,16},{24,28},{28,24},{1,5},{5... | collective-permute-start | bytes 1474568 | tf_op jit(solution)/shard_map/ppermute | solution.py:113
  278.2 58.7 %collective-permute-start.59 = (bf16[160,1536]{1,0:T(8,128)(2,1)S(1)}, bf16[160,1536]{1,0:T(8,128)(2,1)S(1)}, u32[]{:S(2)}, u32[]{:S(2)}) collective-permute-start(bf16[160,1536]{1,0:T(8,128)(2,1)S(1)} %convolution_convert_fusion.20), channel_id=1, source_target_pairs={{0,4},{4,0},{8,12},{12,8},{16,20},{20,16},{24,28},{28,24},{1,5},{5... | collective-permute-start | bytes 1474568 | tf_op jit(solution)/shard_map/ppermute | solution.py:113
  439.9 40.8 %collective-permute-start.36 = (bf16[160,1536]{1,0:T(8,128)(2,1)S(1)}, bf16[160,1536]{1,0:T(8,128)(2,1)S(1)}, u32[]{:S(2)}, u32[]{:S(2)}) collective-permute-start(bf16[160,1536]{1,0:T(8,128)(2,1)S(1)} %convolution_convert_fusion.31), channel_id=1, source_target_pairs={{0,4},{4,0},{8,12},{12,8},{16,20},{20,16},{24,28},{28,24},{1,5},{5... | collective-permute-start | bytes 1474568 | tf_op jit(solution)/shard_map/ppermute | solution.py:113
  443.5 37.2 %collective-permute-start.37 = (bf16[160,1536]{1,0:T(8,128)(2,1)S(1)}, bf16[160,1536]{1,0:T(8,128)(2,1)S(1)}, u32[]{:S(2)}, u32[]{:S(2)}) collective-permute-start(bf16[160,1536]{1,0:T(8,128)(2,1)S(1)} %convolution_convert_fusion.30), channel_id=1, source_target_pairs={{0,4},{4,0},{8,12},{12,8},{16,20},{20,16},{24,28},{28,24},{1,5},{5... | collective-permute-start | bytes 1474568 | tf_op jit(solution)/shard_map/ppermute | solution.py:113
  533.1 49.2 %collective-permute-start.62 = (bf16[160,1536]{1,0:T(8,128)(2,1)}, bf16[160,1536]{1,0:T(8,128)(2,1)}, u32[]{:S(2)}, u32[]{:S(2)}) collective-permute-start(bf16[160,1536]{1,0:T(8,128)(2,1)} %get-tuple-element.161), channel_id=1, source_target_pairs={{0,4},{4,0},{8,12},{12,8},{16,20},{20,16},{24,28},{28,24},{1,5},{5... | collective-permute-start | bytes 1474568 | tf_op jit(solution)/shard_map/ppermute | solution.py:113
  549.0 36.5 %collective-permute-start.196 = (bf16[384,1536]{1,0:T(8,128)(2,1)}, bf16[384,1536]{1,0:T(8,128)(2,1)}, u32[]{:S(2)}, u32[]{:S(2)}) collective-permute-start(bf16[384,1536]{1,0:T(8,128)(2,1)} %convolution_convert_fusion.10), channel_id=1, source_target_pairs={{0,1},{1,0},{2,3},{3,2},{4,5},{5,4},{6,7},{7,6},{8,9},{9,8},{10,11... | collective-permute-start | bytes 3538952 | tf_op jit(solution)/shard_map/ppermute | solution.py:180
  549.0 31.0 %collective-permute-start.41 = (bf16[160,1536]{1,0:T(8,128)(2,1)}, bf16[160,1536]{1,0:T(8,128)(2,1)}, u32[]{:S(2)}, u32[]{:S(2)}) collective-permute-start(bf16[160,1536]{1,0:T(8,128)(2,1)} %get-tuple-element.167), channel_id=1, source_target_pairs={{0,4},{4,0},{8,12},{12,8},{16,20},{20,16},{24,28},{28,24},{1,5},{5... | collective-permute-start | bytes 1474568 | tf_op jit(solution)/shard_map/ppermute | solution.py:113
  559.5 29.2 %collective-permute-start.63 = (bf16[160,1536]{1,0:T(8,128)(2,1)}, bf16[160,1536]{1,0:T(8,128)(2,1)}, u32[]{:S(2)}, u32[]{:S(2)}) collective-permute-start(bf16[160,1536]{1,0:T(8,128)(2,1)} %get-tuple-element.162), channel_id=1, source_target_pairs={{0,4},{4,0},{8,12},{12,8},{16,20},{20,16},{24,28},{28,24},{1,5},{5... | collective-permute-start | bytes 1474568 | tf_op jit(solution)/shard_map/ppermute | solution.py:113
  582.3 32.0 %collective-permute-start.44 = (bf16[256,1536]{1,0:T(8,128)(2,1)S(1)}, bf16[256,1536]{1,0:T(8,128)(2,1)S(1)}, u32[]{:S(2)}, u32[]{:S(2)}) collective-permute-start(bf16[256,1536]{1,0:T(8,128)(2,1)S(1)} %get-tuple-element.317), channel_id=1, source_target_pairs={{0,8},{4,12},{1,9},{5,13},{2,10},{6,14},{3,11},{7,15}} | collective-permute-start | bytes 2359304 | tf_op jit(solution)/shard_map/ppermute | solution.py:117
  599.1 55.2 %collective-permute-start.192 = (bf16[768,1536]{1,0:T(8,128)(2,1)S(1)}, bf16[768,1536]{1,0:T(8,128)(2,1)S(1)}, u32[]{:S(2)}, u32[]{:S(2)}) collective-permute-start(bf16[768,1536]{1,0:T(8,128)(2,1)S(1)} %copy-done.248), channel_id=1, source_target_pairs={{0,1},{1,0},{2,3},{3,2},{4,5},{5,4},{6,7},{7,6},{8,9},{9,8},{10,11... | collective-permute-start | bytes 7077896 | tf_op jit(solution)/shard_map/ppermute | solution.py:180
  608.3 22.8 %collective-permute-start.65 = (bf16[256,1536]{1,0:T(8,128)(2,1)S(1)}, bf16[256,1536]{1,0:T(8,128)(2,1)S(1)}, u32[]{:S(2)}, u32[]{:S(2)}) collective-permute-start(bf16[256,1536]{1,0:T(8,128)(2,1)S(1)} %get-tuple-element.203), channel_id=1, source_target_pairs={{0,8},{4,12},{8,16},{12,20},{1,9},{5,13},{9,17},{13,21},{2,10},{6,... | collective-permute-start | bytes 2359304 | tf_op jit(solution)/shard_map/ppermute | solution.py:117
  616.1 30.2 %collective-permute-start.45 = (bf16[256,1536]{1,0:T(8,128)(2,1)S(1)}, bf16[256,1536]{1,0:T(8,128)(2,1)S(1)}, u32[]{:S(2)}, u32[]{:S(2)}) collective-permute-start(bf16[256,1536]{1,0:T(8,128)(2,1)S(1)} %get-tuple-element.205), channel_id=1, source_target_pairs={{0,8},{4,12},{8,16},{12,20},{1,9},{5,13},{9,17},{13,21},{2,10},{6,... | collective-permute-start | bytes 2359304 | tf_op jit(solution)/shard_map/ppermute | solution.py:117
  621.2 29.5 %collective-permute-start.48 = (bf16[256,1536]{1,0:T(8,128)(2,1)S(1)}, bf16[256,1536]{1,0:T(8,128)(2,1)S(1)}, u32[]{:S(2)}, u32[]{:S(2)}) collective-permute-start(bf16[256,1536]{1,0:T(8,128)(2,1)S(1)} %get-tuple-element.206), channel_id=1, source_target_pairs={{16,8},{20,12},{24,16},{28,20},{17,9},{21,13},{25,17},{29,21},{18,... | collective-permute-start | bytes 2359304 | tf_op jit(solution)/shard_map/ppermute | solution.py:117
  631.1 34.8 %collective-permute-start.60 = (bf16[160,1536]{1,0:T(8,128)(2,1)S(1)}, bf16[160,1536]{1,0:T(8,128)(2,1)S(1)}, u32[]{:S(2)}, u32[]{:S(2)}) collective-permute-start(bf16[160,1536]{1,0:T(8,128)(2,1)S(1)} %copy-done.135), channel_id=1, source_target_pairs={{0,4},{4,0},{8,12},{12,8},{16,20},{20,16},{24,28},{28,24},{1,5},{5... | collective-permute-start | bytes 1474568 | tf_op jit(solution)/shard_map/ppermute | solution.py:113
  632.6 83.0 %collective-permute-start.40 = (bf16[160,1536]{1,0:T(8,128)(2,1)}, bf16[160,1536]{1,0:T(8,128)(2,1)}, u32[]{:S(2)}, u32[]{:S(2)}) collective-permute-start(bf16[160,1536]{1,0:T(8,128)(2,1)} %get-tuple-element.168), channel_id=1, source_target_pairs={{0,4},{4,0},{8,12},{12,8},{16,20},{20,16},{24,28},{28,24},{1,5},{5... | collective-permute-start | bytes 1474568 | tf_op jit(solution)/shard_map/ppermute | solution.py:113
  654.4 61.7 %collective-permute-start.46 = (bf16[256,1536]{1,0:T(8,128)(2,1)}, bf16[256,1536]{1,0:T(8,128)(2,1)}, u32[]{:S(2)}, u32[]{:S(2)}) collective-permute-start(bf16[256,1536]{1,0:T(8,128)(2,1)} %get-tuple-element.177), channel_id=1, source_target_pairs={{0,8},{4,12},{8,16},{12,20},{16,24},{20,28},{1,9},{5,13},{9,17},{1... | collective-permute-start | bytes 2359304 | tf_op jit(solution)/shard_map/ppermute | solution.py:117
  666.0 50.0 %collective-permute-start.49 = (bf16[256,1536]{1,0:T(8,128)(2,1)}, bf16[256,1536]{1,0:T(8,128)(2,1)}, u32[]{:S(2)}, u32[]{:S(2)}) collective-permute-start(bf16[256,1536]{1,0:T(8,128)(2,1)} %get-tuple-element.178), channel_id=1, source_target_pairs={{8,0},{12,4},{16,8},{20,12},{24,16},{28,20},{9,1},{13,5},{17,9},{2... | collective-permute-start | bytes 2359304 | tf_op jit(solution)/shard_map/ppermute | solution.py:117
  668.7 60.8 %collective-permute-start.193 = (bf16[384,1536]{1,0:T(8,128)(2,1)}, bf16[384,1536]{1,0:T(8,128)(2,1)}, u32[]{:S(2)}, u32[]{:S(2)}) collective-permute-start(bf16[384,1536]{1,0:T(8,128)(2,1)} %fusion.60), channel_id=1, source_target_pairs={{0,2},{1,3},{2,0},{3,1},{4,6},{5,7},{6,4},{7,5},{8,10},{9,11},{10,... | collective-permute-start | bytes 3538952 | tf_op jit(solution)/shard_map/ppermute | solution.py:184
  715.6 86.0 %collective-permute-start.174 = (bf16[768,1536]{1,0:T(8,128)(2,1)}, bf16[768,1536]{1,0:T(8,128)(2,1)}, u32[]{:S(2)}, u32[]{:S(2)}) collective-permute-start(bf16[768,1536]{1,0:T(8,128)(2,1)} %convolution_convert_fusion.6), channel_id=1, source_target_pairs={{0,1},{1,0},{2,3},{3,2},{4,5},{5,4},{6,7},{7,6},{8,9},{9,8},{10,11... | collective-permute-start | bytes 7077896 | tf_op jit(solution)/shard_map/ppermute | solution.py:180
  724.5 80.1 %collective-permute-start.110 = (bf16[768,1536]{1,0:T(8,128)(2,1)}, bf16[768,1536]{1,0:T(8,128)(2,1)}, u32[]{:S(2)}, u32[]{:S(2)}) collective-permute-start(bf16[768,1536]{1,0:T(8,128)(2,1)} %convolution_convert_fusion.8), channel_id=1, source_target_pairs={{0,1},{1,0},{2,3},{3,2},{4,5},{5,4},{6,7},{7,6},{8,9},{9,8},{10,11... | collective-permute-start | bytes 7077896 | tf_op jit(solution)/shard_map/ppermute | solution.py:180
  755.7 24.0 %collective-permute-start.72 = (bf16[256,1536]{1,0:T(8,128)(2,1)S(1)}, bf16[256,1536]{1,0:T(8,128)(2,1)S(1)}, u32[]{:S(2)}, u32[]{:S(2)}) collective-permute-start(bf16[256,1536]{1,0:T(8,128)(2,1)S(1)} %get-tuple-element.132), channel_id=1, source_target_pairs={{0,8},{4,12},{8,16},{12,20},{16,24},{20,28},{1,9},{5,13},{9,17},{1... | collective-permute-start | bytes 2359304 | tf_op jit(solution)/shard_map/ppermute | solution.py:117
  758.9 25.3 %collective-permute-start.73 = (bf16[256,1536]{1,0:T(8,128)(2,1)S(1)}, bf16[256,1536]{1,0:T(8,128)(2,1)S(1)}, u32[]{:S(2)}, u32[]{:S(2)}) collective-permute-start(bf16[256,1536]{1,0:T(8,128)(2,1)S(1)} %get-tuple-element.132), channel_id=1, source_target_pairs={{8,0},{12,4},{16,8},{20,12},{24,16},{28,20},{9,1},{13,5},{17,9},{2... | collective-permute-start | bytes 2359304 | tf_op jit(solution)/shard_map/ppermute | solution.py:117
  778.2 73.0 %collective-permute-start.78 = (bf16[160,1536]{1,0:T(8,128)(2,1)S(1)}, bf16[160,1536]{1,0:T(8,128)(2,1)S(1)}, u32[]{:S(2)}, u32[]{:S(2)}) collective-permute-start(bf16[160,1536]{1,0:T(8,128)(2,1)S(1)} %convolution_convert_fusion.15), channel_id=1, source_target_pairs={{0,4},{4,0},{8,12},{12,8},{16,20},{20,16},{24,28},{28,24},{1,5},{5... | collective-permute-start | bytes 1474568 | tf_op jit(solution)/shard_map/ppermute | solution.py:113
  801.6 51.2 %collective-permute-start.79 = (bf16[160,1536]{1,0:T(8,128)(2,1)S(1)}, bf16[160,1536]{1,0:T(8,128)(2,1)S(1)}, u32[]{:S(2)}, u32[]{:S(2)}) collective-permute-start(bf16[160,1536]{1,0:T(8,128)(2,1)S(1)} %convolution_convert_fusion.14), channel_id=1, source_target_pairs={{0,4},{4,0},{8,12},{12,8},{16,20},{20,16},{24,28},{28,24},{1,5},{5... | collective-permute-start | bytes 1474568 | tf_op jit(solution)/shard_map/ppermute | solution.py:113
  818.7 28.1 %collective-permute-start.76 = (bf16[256,1536]{1,0:T(8,128)(2,1)S(1)}, bf16[256,1536]{1,0:T(8,128)(2,1)S(1)}, u32[]{:S(2)}, u32[]{:S(2)}) collective-permute-start(bf16[256,1536]{1,0:T(8,128)(2,1)S(1)} %collective-permute-done.74), channel_id=1, source_target_pairs={{16,24},{20,28},{17,25},{21,29},{18,26},{22,30},{19,27},{23,31}} | collective-permute-start | bytes 2359304 | tf_op jit(solution)/shard_map/ppermute | solution.py:117
  843.9 28.9 %collective-permute-start.175 = (bf16[384,1536]{1,0:T(8,128)(2,1)S(1)}, bf16[384,1536]{1,0:T(8,128)(2,1)S(1)}, u32[]{:S(2)}, u32[]{:S(2)}) collective-permute-start(bf16[384,1536]{1,0:T(8,128)(2,1)S(1)} %fusion.107), channel_id=1, source_target_pairs={{0,2},{1,3},{2,0},{3,1},{4,6},{5,7},{6,4},{7,5},{8,10},{9,11},{10,... | collective-permute-start | bytes 3538952 | tf_op jit(solution)/shard_map/ppermute | solution.py:184
  846.7 42.4 %collective-permute-start.111 = (bf16[384,1536]{1,0:T(8,128)(2,1)S(1)}, bf16[384,1536]{1,0:T(8,128)(2,1)S(1)}, u32[]{:S(2)}, u32[]{:S(2)}) collective-permute-start(bf16[384,1536]{1,0:T(8,128)(2,1)S(1)} %fusion.111), channel_id=1, source_target_pairs={{0,2},{1,3},{2,0},{3,1},{4,6},{5,7},{6,4},{7,5},{8,10},{9,11},{10,... | collective-permute-start | bytes 3538952 | tf_op jit(solution)/shard_map/ppermute | solution.py:184
  851.2 40.0 %collective-permute-start.81 = (bf16[160,1536]{1,0:T(8,128)(2,1)S(1)}, bf16[160,1536]{1,0:T(8,128)(2,1)S(1)}, u32[]{:S(2)}, u32[]{:S(2)}) collective-permute-start(bf16[160,1536]{1,0:T(8,128)(2,1)S(1)} %convolution_convert_fusion.12), channel_id=1, source_target_pairs={{0,4},{4,0},{8,12},{12,8},{16,20},{20,16},{24,28},{28,24},{1,5},{5... | collective-permute-start | bytes 1474568 | tf_op jit(solution)/shard_map/ppermute | solution.py:113
  874.3 77.1 %collective-permute-start.176 = (bf16[192,1536]{1,0:T(8,128)(2,1)}, bf16[192,1536]{1,0:T(8,128)(2,1)}, u32[]{:S(2)}, u32[]{:S(2)}) collective-permute-start(bf16[192,1536]{1,0:T(8,128)(2,1)} %dynamic-slice_convert_fusion), channel_id=1, source_target_pairs={{0,4},{4,0},{8,12},{12,8},{16,20},{20,16},{24,28},{28,24},{1,5},{5... | collective-permute-start | bytes 1769480 | tf_op jit(solution)/shard_map/ppermute | solution.py:113
  890.7 64.0 %collective-permute-start.112 = (bf16[192,1536]{1,0:T(8,128)(2,1)}, bf16[192,1536]{1,0:T(8,128)(2,1)}, u32[]{:S(2)}, u32[]{:S(2)}) collective-permute-start(bf16[192,1536]{1,0:T(8,128)(2,1)} %dynamic-slice_convert_fusion.2), channel_id=1, source_target_pairs={{0,4},{4,0},{8,12},{12,8},{16,20},{20,16},{24,28},{28,24},{1,5},{5... | collective-permute-start | bytes 1769480 | tf_op jit(solution)/shard_map/ppermute | solution.py:113
  919.9 27.8 %all-to-all-start.1 = ((f32[8,1,256]{2,1,0:T(1,128)}), f32[8,1,256]{2,1,0:T(1,128)}, u32[]{:S(2)}, u32[]{:S(2)}) async-start(f32[8,1,256]{2,1,0:T(1,128)} %constant_dynamic-update-slice_fusion.26), calls=%async_computation.1 | async-start | bytes 16384 | tf_op jit(solution)/shard_map/all_to_all | solution.py:351
  932.0 374.8 %all-reduce.2.cloned.1.call-start = ((), (), s32[]{:S(2)}) async-start(), calls=%async_computation.3 | async-start | bytes 393216 | tf_op jit(solution)/shard_map/psum | solution.py:527
  945.6 98.6 %collective-permute-start.194 = (bf16[384,1536]{1,0:T(8,128)(2,1)}, bf16[384,1536]{1,0:T(8,128)(2,1)}, u32[]{:S(2)}, u32[]{:S(2)}) collective-permute-start(bf16[384,1536]{1,0:T(8,128)(2,1)} %convolution_convert_fusion.11), channel_id=1, source_target_pairs={{0,1},{1,0},{2,3},{3,2},{4,5},{5,4},{6,7},{7,6},{8,9},{9,8},{10,11... | collective-permute-start | bytes 3538952 | tf_op jit(solution)/shard_map/ppermute | solution.py:180
  945.6 27.6 %collective-permute-start.84 = (bf16[160,1536]{1,0:T(8,128)(2,1)}, bf16[160,1536]{1,0:T(8,128)(2,1)}, u32[]{:S(2)}, u32[]{:S(2)}) collective-permute-start(bf16[160,1536]{1,0:T(8,128)(2,1)} %get-tuple-element.157), channel_id=1, source_target_pairs={{0,4},{4,0},{8,12},{12,8},{16,20},{20,16},{24,28},{28,24},{1,5},{5... | collective-permute-start | bytes 1474568 | tf_op jit(solution)/shard_map/ppermute | solution.py:113
  947.6 23.0 %collective-permute-start.83 = (bf16[160,1536]{1,0:T(8,128)(2,1)}, bf16[160,1536]{1,0:T(8,128)(2,1)}, u32[]{:S(2)}, u32[]{:S(2)}) collective-permute-start(bf16[160,1536]{1,0:T(8,128)(2,1)} %get-tuple-element.159), channel_id=1, source_target_pairs={{0,4},{4,0},{8,12},{12,8},{16,20},{20,16},{24,28},{28,24},{1,5},{5... | collective-permute-start | bytes 1474568 | tf_op jit(solution)/shard_map/ppermute | solution.py:113
  951.4 109.3 %collective-permute-start.85 = (bf16[160,1536]{1,0:T(8,128)(2,1)S(1)}, bf16[160,1536]{1,0:T(8,128)(2,1)S(1)}, u32[]{:S(2)}, u32[]{:S(2)}) collective-permute-start(bf16[160,1536]{1,0:T(8,128)(2,1)S(1)} %copy-done.134), channel_id=1, source_target_pairs={{0,4},{4,0},{8,12},{12,8},{16,20},{20,16},{24,28},{28,24},{1,5},{5... | collective-permute-start | bytes 1474568 | tf_op jit(solution)/shard_map/ppermute | solution.py:113
  954.7 23.9 %collective-permute-start.177 = (bf16[48,1536]{1,0:T(8,128)(2,1)S(1)}, bf16[48,1536]{1,0:T(8,128)(2,1)S(1)}, u32[]{:S(2)}, u32[]{:S(2)}) collective-permute-start(bf16[48,1536]{1,0:T(8,128)(2,1)S(1)} %dynamic-slice_convert_fusion.6), channel_id=1, source_target_pairs={{0,8},{4,12},{1,9},{5,13},{2,10},{6,14},{3,11},{7,15}} | collective-permute-start | bytes 442376 | tf_op jit(solution)/shard_map/ppermute | solution.py:117
  979.3 83.1 %collective-permute-start.86 = (bf16[256,1536]{1,0:T(8,128)(2,1)S(1)}, bf16[256,1536]{1,0:T(8,128)(2,1)S(1)}, u32[]{:S(2)}, u32[]{:S(2)}) collective-permute-start(bf16[256,1536]{1,0:T(8,128)(2,1)S(1)} %get-tuple-element.327), channel_id=1, source_target_pairs={{0,8},{4,12},{1,9},{5,13},{2,10},{6,14},{3,11},{7,15}} | collective-permute-start | bytes 2359304 | tf_op jit(solution)/shard_map/ppermute | solution.py:117
  1036.7 26.3 %collective-permute-start.89 = (bf16[256,1536]{1,0:T(8,128)(2,1)S(1)}, bf16[256,1536]{1,0:T(8,128)(2,1)S(1)}, u32[]{:S(2)}, u32[]{:S(2)}) collective-permute-start(bf16[256,1536]{1,0:T(8,128)(2,1)S(1)} %get-tuple-element.327), channel_id=1, source_target_pairs={{24,16},{28,20},{25,17},{29,21},{26,18},{30,22},{27,19},{31,23}} | collective-permute-start | bytes 2359304 | tf_op jit(solution)/shard_map/ppermute | solution.py:117
  1053.3 51.1 %collective-permute-start.190 = (bf16[768,1536]{1,0:T(8,128)(2,1)S(1)}, bf16[768,1536]{1,0:T(8,128)(2,1)S(1)}, u32[]{:S(2)}, u32[]{:S(2)}) collective-permute-start(bf16[768,1536]{1,0:T(8,128)(2,1)S(1)} %copy-done.247), channel_id=1, source_target_pairs={{0,1},{1,0},{2,3},{3,2},{4,5},{5,4},{6,7},{7,6},{8,9},{9,8},{10,11... | collective-permute-start | bytes 7077896 | tf_op jit(solution)/shard_map/ppermute | solution.py:180
  1058.4 53.6 %collective-permute-start.82 = (bf16[160,1536]{1,0:T(8,128)(2,1)S(1)}, bf16[160,1536]{1,0:T(8,128)(2,1)S(1)}, u32[]{:S(2)}, u32[]{:S(2)}) collective-permute-start(bf16[160,1536]{1,0:T(8,128)(2,1)S(1)} %copy-done.133), channel_id=1, source_target_pairs={{0,4},{4,0},{8,12},{12,8},{16,20},{20,16},{24,28},{28,24},{1,5},{5... | collective-permute-start | bytes 1474568 | tf_op jit(solution)/shard_map/ppermute | solution.py:113
  1111.9 47.2 %collective-permute-start.191 = (bf16[384,1536]{1,0:T(8,128)(2,1)}, bf16[384,1536]{1,0:T(8,128)(2,1)}, u32[]{:S(2)}, u32[]{:S(2)}) collective-permute-start(bf16[384,1536]{1,0:T(8,128)(2,1)} %fusion.59), channel_id=1, source_target_pairs={{0,2},{1,3},{2,0},{3,1},{4,6},{5,7},{6,4},{7,5},{8,10},{9,11},{10,... | collective-permute-start | bytes 3538952 | tf_op jit(solution)/shard_map/ppermute | solution.py:184
  1149.8 174.1 %collective-permute-start.158 = (bf16[768,1536]{1,0:T(8,128)(2,1)}, bf16[768,1536]{1,0:T(8,128)(2,1)}, u32[]{:S(2)}, u32[]{:S(2)}) collective-permute-start(bf16[768,1536]{1,0:T(8,128)(2,1)} %convolution_convert_fusion.7), channel_id=1, source_target_pairs={{0,1},{1,0},{2,3},{3,2},{4,5},{5,4},{6,7},{7,6},{8,9},{9,8},{10,11... | collective-permute-start | bytes 7077896 | tf_op jit(solution)/shard_map/ppermute | solution.py:180
  1152.2 179.7 %collective-permute-start.94 = (bf16[768,1536]{1,0:T(8,128)(2,1)}, bf16[768,1536]{1,0:T(8,128)(2,1)}, u32[]{:S(2)}, u32[]{:S(2)}) collective-permute-start(bf16[768,1536]{1,0:T(8,128)(2,1)} %convolution_convert_fusion.9), channel_id=1, source_target_pairs={{0,1},{1,0},{2,3},{3,2},{4,5},{5,4},{6,7},{7,6},{8,9},{9,8},{10,11... | collective-permute-start | bytes 7077896 | tf_op jit(solution)/shard_map/ppermute | solution.py:180
  1210.8 97.3 %collective-permute-start.130 = (bf16[48,512]{1,0:T(8,128)(2,1)S(1)}, bf16[48,512]{1,0:T(8,128)(2,1)S(1)}, u32[]{:S(2)}, u32[]{:S(2)}) collective-permute-start(bf16[48,512]{1,0:T(8,128)(2,1)S(1)} %get-tuple-element.251), channel_id=1, source_target_pairs={{0,8},{4,12},{8,16},{12,20},{1,9},{5,13},{9,17},{13,21},{2,10},{6,... | collective-permute-start | bytes 147464 | tf_op jit(solution)/shard_map/ppermute | solution.py:117
  1214.1 94.0 %collective-permute-start.133 = (bf16[48,512]{1,0:T(8,128)(2,1)S(1)}, bf16[48,512]{1,0:T(8,128)(2,1)S(1)}, u32[]{:S(2)}, u32[]{:S(2)}) collective-permute-start(bf16[48,512]{1,0:T(8,128)(2,1)S(1)} %get-tuple-element.252), channel_id=1, source_target_pairs={{16,8},{20,12},{24,16},{28,20},{17,9},{21,13},{25,17},{29,21},{18,... | collective-permute-start | bytes 147464 | tf_op jit(solution)/shard_map/ppermute | solution.py:117
  1327.6 29.0 %collective-permute-start.159 = (bf16[384,1536]{1,0:T(8,128)(2,1)S(1)}, bf16[384,1536]{1,0:T(8,128)(2,1)S(1)}, u32[]{:S(2)}, u32[]{:S(2)}) collective-permute-start(bf16[384,1536]{1,0:T(8,128)(2,1)S(1)} %fusion.109), channel_id=1, source_target_pairs={{0,2},{1,3},{2,0},{3,1},{4,6},{5,7},{6,4},{7,5},{8,10},{9,11},{10,... | collective-permute-start | bytes 3538952 | tf_op jit(solution)/shard_map/ppermute | solution.py:184
  1346.3 31.1 %collective-permute-start.95 = (bf16[384,1536]{1,0:T(8,128)(2,1)S(1)}, bf16[384,1536]{1,0:T(8,128)(2,1)S(1)}, u32[]{:S(2)}, u32[]{:S(2)}) collective-permute-start(bf16[384,1536]{1,0:T(8,128)(2,1)S(1)} %fusion.113), channel_id=1, source_target_pairs={{0,2},{1,3},{2,0},{3,1},{4,6},{5,7},{6,4},{7,5},{8,10},{9,11},{10,... | collective-permute-start | bytes 3538952 | tf_op jit(solution)/shard_map/ppermute | solution.py:184
  (443 other events, 5886.3 us)
Sparse Core Ops, SparseCore 0:
  10.6 65.5 all-gather.10
  77.8 19.6 all-gather.8
  99.0 43.0 all-gather.12
  143.5 37.4 all-gather.14
  1185.9 120.7 all-reduce.1

commit v2 on v1

v2 whole, which is shorter than its diff:
```python
import jax
import jax.numpy as jnp
from jax import lax
from jax.experimental import pallas as pl
from jax.experimental.pallas import tpu as pltpu
from jax.sharding import PartitionSpec as P

QUERY_HEADS = 12
KEY_VALUE_HEADS = 2
HEAD_SIZE = 128

norm_eps = 1e-06
rope_base = 10000.0
masked_score = -1e30

bf16 = jnp.bfloat16
f32 = jnp.float32


def mm(left, right):
    return jnp.dot(left, right, preferred_element_type=f32)


def mm_tn(left, right):
    return lax.dot_general(left, right, (((0,), (0,)), ((), ())), preferred_element_type=f32)


def mm_nt(left, right):
    return lax.dot_general(left, right, (((1,), (1,)), ((), ())), preferred_element_type=f32)


def norm_forward(values, gain):
    inverse = lax.rsqrt(jnp.mean(values * values, axis=-1, keepdims=True) + norm_eps)
    return values * inverse * gain, inverse


def norm_backward(values, inverse, gain, grad):
    scaled = grad * gain
    mean_part = jnp.mean(values * scaled, axis=-1, keepdims=True)
    d_values = inverse * scaled - values * (inverse * inverse * inverse * mean_part)
    d_gain = jnp.sum(grad * values * inverse, axis=0)
    return d_values, d_gain


def sync(*values):
    return lax.optimization_barrier(values)


def rotary_tables(position):
    half_width = HEAD_SIZE // 2
    frequency = rope_base ** (-(jnp.arange(half_width).astype(f32) * 2.0 / HEAD_SIZE))
    angles = position.astype(f32)[:, None] * frequency[None, :]
    cosine, sine = jnp.cos(angles), jnp.sin(angles)
    return jnp.concatenate([cosine, cosine], axis=1), jnp.concatenate([-sine, sine], axis=1)


def turned(values, cosine, sine):
    return values * cosine + pltpu.roll(values, HEAD_SIZE // 2, 1) * sine


def kernel_params():
    return pltpu.CompilerParams(vmem_limit_bytes=40 * 1024 * 1024)


def project_kv(hidden, w_kv, tables):
    rows, width = hidden.shape[0], w_kv.shape[1]

    def kernel(hidden_ref, w_ref, cos_ref, sin_ref, out_ref):
        value = jnp.dot(hidden_ref[...], w_ref[...], preferred_element_type=f32)
        for at in range(0, width, HEAD_SIZE):
            part = value[:, at : at + HEAD_SIZE]
            if at // HEAD_SIZE % 2 == 0:
                part = turned(part, cos_ref[...], sin_ref[...])
            out_ref[:, at : at + HEAD_SIZE] = part.astype(bf16)

    return pl.pallas_call(
        kernel,
        out_shape=jax.ShapeDtypeStruct((rows, width), bf16),
        compiler_params=kernel_params(),
        cost_estimate=pl.CostEstimate(
            flops=2 * rows * width * hidden.shape[1],
            bytes_accessed=2 * hidden.size + 2 * w_kv.size,
            transcendentals=0,
        ),
    )(hidden, w_kv, *tables)


def turn_kv_back(first, second, tables):
    rows, width = first.shape

    def kernel(first_ref, second_ref, cos_ref, sin_ref, out_ref):
        for at in range(0, width, HEAD_SIZE):
            columns = slice(at, at + HEAD_SIZE)
            part = first_ref[:, columns].astype(f32) + second_ref[:, columns].astype(f32)
            if at // HEAD_SIZE % 2 == 0:
                part = turned(part, cos_ref[...], -sin_ref[...])
            out_ref[:, columns] = part.astype(bf16)

    return pl.pallas_call(
        kernel,
        out_shape=jax.ShapeDtypeStruct((rows, width), bf16),
        compiler_params=kernel_params(),
    )(first, second, *tables)


def attend(q_pre, kv_all, tables, query_marks, key_marks):
    rows, width = q_pre.shape
    keys = kv_all.shape[0]
    heads = width // HEAD_SIZE
    group = heads // KEY_VALUE_HEADS
    scale = HEAD_SIZE ** (-0.5)

    def kernel(
        q_ref, kv_ref, cos_ref, sin_ref, qd_ref, qp_ref, kd_ref, kp_ref, turned_ref, out_ref, bias
    ):
        @pl.when(pl.program_id(0) == 0)
        def _():
            seen = (qd_ref[...] == kd_ref[...]) & (kp_ref[...] <= qp_ref[...])
            bias[...] = jnp.where(seen, 0.0, masked_score)

        query = turned(q_ref[...], cos_ref[...], sin_ref[...]).astype(bf16)
        turned_ref[...] = query
        scores = mm_nt(query, kv_ref[:, :HEAD_SIZE]) * scale + bias[...]
        weight = jnp.exp(scores - jnp.max(scores, axis=1, keepdims=True))
        total = jnp.sum(weight, axis=1, keepdims=True)
        probs = (weight * (1.0 / total)).astype(bf16)
        out_ref[...] = mm(probs, kv_ref[:, HEAD_SIZE:]).astype(bf16)

    fixed = lambda shape: pl.BlockSpec(shape, lambda h: (0, 0))
    by_head = pl.BlockSpec((rows, HEAD_SIZE), lambda h: (0, h))
    return pl.pallas_call(
        kernel,
        grid=(heads,),
        in_specs=[
            by_head,
            pl.BlockSpec((keys, 2 * HEAD_SIZE), lambda h: (0, h // group)),
            fixed((rows, HEAD_SIZE)),
            fixed((rows, HEAD_SIZE)),
            fixed((rows, 1)),
            fixed((rows, 1)),
            fixed((1, keys)),
            fixed((1, keys)),
        ],
        out_specs=[by_head, by_head],
        out_shape=[jax.ShapeDtypeStruct((rows, width), bf16)] * 2,
        scratch_shapes=[pltpu.VMEM((rows, keys), f32)],
        compiler_params=kernel_params(),
        cost_estimate=pl.CostEstimate(
            flops=8 * rows * keys * width,
            bytes_accessed=8 * rows * width,
            transcendentals=rows * keys * heads,
        ),
    )(
        q_pre,
        kv_all,
        *tables,
        query_marks[0][:, None],
        query_marks[1][:, None],
        key_marks[0][None, :],
        key_marks[1][None, :],
    )


def attend_back(query, kv_all, d_mixed, tables, query_marks, key_marks):
    rows, width = query.shape
    keys = kv_all.shape[0]
    heads = width // HEAD_SIZE
    group = heads // KEY_VALUE_HEADS
    scale = HEAD_SIZE ** (-0.5)

    def kernel(
        q_ref, kv_ref, dm_ref, cos_ref, sin_ref, qd_ref, qp_ref, kd_ref, kp_ref, dq_ref, dkv_ref,
        bias, dkv,
    ):
        head = pl.program_id(0)

        @pl.when(head == 0)
        def _():
            seen = (qd_ref[...] == kd_ref[...]) & (kp_ref[...] <= qp_ref[...])
            bias[...] = jnp.where(seen, 0.0, masked_score)

        query, key, value = q_ref[...], kv_ref[:, :HEAD_SIZE], kv_ref[:, HEAD_SIZE:]
        d_out = dm_ref[...]
        scores = mm_nt(key, query) * scale + bias[...]
        weight = jnp.exp(scores - jnp.max(scores, axis=0, keepdims=True))
        probs = weight * (1.0 / jnp.sum(weight, axis=0, keepdims=True))
        d_probs = mm_nt(value, d_out)
        mean = jnp.sum(probs * d_probs, axis=0, keepdims=True)
        d_scores = (probs * (d_probs - mean)).astype(bf16)
        d_value = mm(probs.astype(bf16), d_out)
        d_key = mm(d_scores, query) * scale
        d_query = mm_tn(d_scores, key) * scale
        dq_ref[...] = turned(d_query, cos_ref[...], -sin_ref[...]).astype(bf16)

        @pl.when(head % group == 0)
        def _():
            dkv[:, :HEAD_SIZE] = d_key
            dkv[:, HEAD_SIZE:] = d_value

        @pl.when(head % group != 0)
        def _():
            dkv[:, :HEAD_SIZE] += d_key
            dkv[:, HEAD_SIZE:] += d_value

        @pl.when(head % group == group - 1)
        def _():
            dkv_ref[...] = dkv[...].astype(bf16)

    fixed = lambda shape: pl.BlockSpec(shape, lambda h: (0, 0))
    by_head = pl.BlockSpec((rows, HEAD_SIZE), lambda h: (0, h))
    by_group = pl.BlockSpec((keys, 2 * HEAD_SIZE), lambda h: (0, h // group))
    return pl.pallas_call(
        kernel,
        grid=(heads,),
        in_specs=[
            by_head,
            by_group,
            by_head,
            fixed((rows, HEAD_SIZE)),
            fixed((rows, HEAD_SIZE)),
            fixed((1, rows)),
            fixed((1, rows)),
            fixed((keys, 1)),
            fixed((keys, 1)),
        ],
        out_specs=[by_head, by_group],
        out_shape=[
            jax.ShapeDtypeStruct((rows, width), bf16),
            jax.ShapeDtypeStruct(kv_all.shape, bf16),
        ],
        scratch_shapes=[pltpu.VMEM((keys, rows), f32), pltpu.VMEM((keys, 2 * HEAD_SIZE), f32)],
        compiler_params=kernel_params(),
        cost_estimate=pl.CostEstimate(
            flops=20 * rows * keys * width,
            bytes_accessed=8 * rows * width,
            transcendentals=rows * keys * heads,
        ),
    )(
        query,
        kv_all,
        d_mixed,
        *tables,
        query_marks[0][None, :],
        query_marks[1][None, :],
        key_marks[0][:, None],
        key_marks[1][:, None],
    )


def documents(lengths_row, position):
    doc_ends = jnp.cumsum(lengths_row)
    doc_starts = doc_ends - lengths_row
    document_index = jnp.sum((position[:, None] >= doc_ends[None, :]).astype(jnp.int32), axis=1)
    doc_first = jnp.max(
        jnp.where(doc_starts[None, :] <= position[:, None], doc_starts[None, :], 0), axis=1
    )
    return (document_index, position - doc_first)


def slot_table(routes, order_row, experts, capacity):
    token_rows, top_count = routes.shape
    pair_count = token_rows * top_count
    pairs = jnp.arange(pair_count, dtype=jnp.int32)
    named = (order_row[:, None] == pairs[None, :]).astype(bf16)
    of_pair = (
        routes.reshape(pair_count)[:, None] == jnp.arange(experts, dtype=jnp.int32)[None, :]
    ).astype(bf16)
    ranked = mm(named, of_pair)
    earlier = (pairs[None, :] < pairs[:, None]).astype(bf16)
    before = mm(earlier, ranked.astype(bf16))
    code = jnp.where(before < capacity, before + 1.0, -1.0) * ranked
    back = mm_tn(code.astype(bf16), named)
    return jnp.sum(back.reshape(experts, token_rows, top_count), axis=2)


def chosen_softmax(logits, chosen):
    top = jnp.max(jnp.where(chosen, logits, masked_score), axis=-1, keepdims=True)
    weight = jnp.where(chosen, jnp.exp(jnp.where(chosen, logits - top, 0.0)), 0.0)
    total = jnp.sum(weight, axis=-1, keepdims=True)
    return weight / jnp.where(total > 0.0, total, 1.0)


class Lines:
    def __init__(self):
        self.experts = lax.axis_size("expert")
        self.count = self.experts // 2
        self.index = lax.axis_index("expert")
        self.line = self.index // 2
        self.side = self.index % 2

    def source(self, slot):
        count, line = self.count, self.line
        low = jnp.where(line + slot < count, line + slot, count - 1 - slot)
        mirror = count - 1 - line
        high = count - 1 - jnp.where(mirror + slot < count, mirror + slot, count - 1 - slot)
        return jnp.where(line < count // 2, low, high)

    def swap(self, values):
        return lax.ppermute(values, "expert", [(i, i ^ 1) for i in range(self.experts)])

    def even(self, values):
        return lax.ppermute(values, "expert", [(i, i ^ 2) for i in range(self.experts)])

    def odd(self, values):
        count, shards = self.count, lax.axis_size("shard")
        pairs = []
        for i in range(count):
            end = i in (0, count - 1)
            other = i if end else i + 1 if i % 2 else i - 1
            for k in range(2):
                for j in range(shards):
                    to = (2 * other + k) * shards + (j ^ 1 if end else j)
                    pairs.append(((2 * i + k) * shards + j, to))
        return lax.ppermute(values, ("expert", "shard"), pairs)

    def choose(self, table):
        value, seen = None, {}
        for line, array in table.items():
            seen.setdefault(id(array), (array, []))[1].append(line)
        for array, lines in seen.values():
            if value is None:
                value = array
            else:
                here = jnp.any(self.line == jnp.array(lines))
                value = jnp.where(here, array, value)
        return value

    def step_gather(self, held):
        last = len(held) == self.count - 1
        even, odd = held[-1]
        return held + [(self.even(odd), None if last else self.odd(even))]

    def slot(self, held, slot):
        count = self.count
        table = {}
        for line in range(count):
            near = line if line < count // 2 else count - 1 - line
            toward = near + slot < count
            distance = slot if toward else near + slot + 1 - count
            above = toward == (line < count // 2)
            table[line] = held[distance][0 if above == (line % 2 == 0) else 1]
        return self.choose(table)

    def pick(self, blocks, distance, even):
        count, half = self.count, self.count // 2
        table = {}
        for line in range(count):
            up = even == (line % 2 == 0)
            if not 0 <= (line + distance if up else line - distance) < count:
                continue
            if up:
                slot = distance if line < half else line + distance
            else:
                slot = distance if line >= half else count - 1 - line + distance
            table[line] = blocks[slot]
        return self.choose(table) if table else None

    def step_reduce(self, step, blocks, arrived):
        distance = self.count - 1 - step
        even, odd = self.pick(blocks, distance, True), self.pick(blocks, distance, False)
        if arrived is not None:
            from_even, from_odd = self.inward(arrived)
            even = even + from_odd
            odd = odd + from_even
        sent = None if odd is None else self.odd(odd.astype(bf16))
        return self.even(even.astype(bf16)), sent

    def inward(self, arrived):
        even, odd = arrived
        if odd is None:
            return even.astype(f32), 0.0
        end = (self.line == 0) | (self.line == self.count - 1)
        return even.astype(f32), jnp.where(end, 0.0, odd.astype(f32))

    def turn(self, values, steps):
        pairs = [
            (2 * i + k, 2 * ((i + steps) % self.count) + k)
            for i in range(self.count)
            for k in range(2)
        ]
        return lax.ppermute(values, "expert", pairs)


def core_swap(values):
    return lax.ppermute(values, "shard", [(i, i ^ 1) for i in range(lax.axis_size("shard"))])


def row_swap(values):
    return lax.ppermute(values, "shard", [(i, i ^ 2) for i in range(lax.axis_size("shard"))])


def column_units(lines):
    mine = lax.axis_index("shard")
    units = []
    for mask in (0, 1, 2, 3):
        first = lines.side if mask >= 2 else 0
        units += [(mine ^ mask) * 2 + first, (mine ^ mask) * 2 + 1 - first]
    return units


def ordered_columns(values, units):
    width = values.shape[1] // 8
    return jnp.concatenate(
        [lax.dynamic_slice(values, (0, unit * width), (values.shape[0], width)) for unit in units],
        axis=1,
    )


def ordered_small(blocks):
    mine = lax.axis_index("shard")
    shape = blocks[0].shape
    whole = jnp.zeros(shape[:-1] + (4 * shape[-1],), blocks[0].dtype)
    for mask, block in blocks.items():
        at = (0,) * (len(shape) - 1) + ((mine ^ mask) * shape[-1],)
        whole = lax.dynamic_update_slice(whole, block, at)
    return whole


def split_columns(values):
    mine = lax.axis_index("shard")
    width = values.shape[1] // 4
    return [
        lax.dynamic_slice(values, (0, (mine ^ mask) * width), (values.shape[0], width))
        for mask in range(4)
    ]


def shard_rows_of(values):
    return jnp.concatenate([values, row_swap(values)], axis=0)


def shard_rows_all(pair):
    return jnp.concatenate([pair, core_swap(pair)], axis=0)


def exchange_blocks(blocks):
    pairs = lambda mask: [(i, i ^ mask) for i in range(lax.axis_size("shard"))]
    return [blocks[0]] + [lax.ppermute(blocks[r], "shard", pairs(r)) for r in (2, 1, 3)]


def own_columns(values):
    return jnp.concatenate(exchange_blocks(split_columns(values)), axis=0)


class Summed:
    def __init__(self, lines, part):
        self.lines = lines
        self.part = part
        self.value = ()

    def side(self):
        part = self.part
        half = part.shape[0] // 2
        lines = self.lines
        given = lax.dynamic_slice(part, ((1 - lines.side) * half, 0), (half, part.shape[1]))
        self.kept = lax.dynamic_slice(part, (lines.side * half, 0), (half, part.shape[1]))
        self.value = lines.swap(given.astype(bf16))

    def place(self, steps):
        return (self.lines.line + steps) % self.lines.count

    def scatter(self):
        lines = self.lines
        part = (self.kept + self.value.astype(f32)).reshape(lines.count, -1, self.kept.shape[1])
        low = part.astype(bf16)
        take = lambda steps, x: lax.dynamic_index_in_dim(x, self.place(steps), 0, keepdims=False)
        self.kept = take(0, part)
        self.value = tuple(
            lines.turn(take(steps, low), steps) for steps in range(1, lines.count)
        )

    def spread(self):
        own = self.kept
        for came in self.value:
            own = own + came.astype(f32)
        self.kept = own.astype(bf16)
        self.value = tuple(
            self.lines.turn(self.kept, -steps) for steps in range(1, self.lines.count)
        )

    def join(self):
        lines = self.lines
        blocks = jnp.zeros((lines.count,) + self.kept.shape, bf16)
        for steps, block in enumerate((self.kept,) + self.value):
            blocks = lax.dynamic_update_slice(blocks, block[None], (self.place(steps), 0, 0))
        self.kept = blocks.reshape(-1, self.kept.shape[1])
        self.value = lines.swap(self.kept)

    def whole(self):
        low = self.lines.side == 0
        first = jnp.where(low, self.kept, self.value)
        second = jnp.where(low, self.value, self.kept)
        return jnp.concatenate([first, second], axis=0).astype(f32)


class Sent:
    def __init__(self, routing, values):
        self.routing = routing
        self.held = [(values, values)]
        rows = 2 * routing.lines.count * routing.capacity
        self.buffer = jnp.zeros((rows, values.shape[1]), values.dtype)
        self.far = None

    @property
    def value(self):
        return self.held[-1], self.buffer, self.far

    @value.setter
    def value(self, value):
        self.held[-1], self.buffer, self.far = value

    def step(self):
        self.held = self.routing.lines.step_gather(self.held)

    def put(self, rows, block):
        at = block * self.routing.capacity
        self.buffer = lax.dynamic_update_slice(self.buffer, rows, (at, 0))

    def pack(self, j):
        routing = self.routing
        block = routing.lines.slot(self.held, j)
        arrived = self.far
        self.far = routing.lines.swap(mm(routing.mate_hot[j], block).astype(bf16))
        if arrived is not None:
            self.put(arrived, routing.lines.count + j - 1)
        self.put(mm(routing.own_hot[j], block).astype(bf16), j)

    def total(self):
        if self.far is not None:
            self.put(self.far, 2 * self.routing.lines.count - 1)
            self.far = None
        return self.buffer


class Returned:
    def __init__(self, routing, rows):
        self.routing = routing
        count, capacity = routing.lines.count, routing.capacity
        self.blocks = [rows[i * capacity : (i + 1) * capacity] for i in range(2 * count)]
        self.parts = [None] * count
        self.round = 0
        self.value = (None, None)

    def spread(self, j):
        own, far = self.routing.own_hot[j], self.routing.mate_hot[j]
        self.parts[j] = mm_tn(own, self.blocks[j]) + mm_tn(far, self.value[0])

    def advance(self):
        lines = self.routing.lines
        j = lines.count - 1 - self.round
        arrived = self.value[1]
        if self.round > 0:
            self.spread(j + 1)
            arrived = lines.step_reduce(self.round - 1, self.parts, arrived)
        self.value = (lines.swap(self.blocks[lines.count + j]), arrived)
        self.round += 1

    def total(self):
        self.spread(0)
        from_even, from_odd = self.routing.lines.inward(self.value[1])
        return self.parts[0] + from_even + from_odd


def settle(moving, *values):
    arrived, values = sync([m.value for m in moving], values)
    for m, value in zip(moving, arrived, strict=True):
        m.value = value
    return values


class Routing:
    pass


def per_device(
    tokens,
    lengths,
    routes,
    slot_order,
    cotangent,
    q_weight,
    key_matrix,
    value_matrix,
    out_weight,
    router_weight,
    attn_gain,
    ffn_gain,
    gate_weight,
    up_weight,
    down_weight,
):
    lines = Lines()
    layer_count = q_weight.shape[0]
    shard_count = lax.axis_size("shard")
    mine = lax.axis_index("shard")
    token_rows, model_width = tokens.shape
    pair_count = token_rows * routes.shape[1]
    experts = router_weight.shape[2]
    assert shard_count == 4 and experts == lines.experts and gate_weight.shape[1] == 1
    hidden_units = gate_weight.shape[3]
    capacity = (pair_count * 5 + 4 * experts - 1) // (4 * experts)
    assert capacity < 256
    sequence_length = token_rows * shard_count
    kv_width = KEY_VALUE_HEADS * HEAD_SIZE

    own_rows = jnp.arange(token_rows, dtype=jnp.int32)
    position = mine * token_rows + own_rows
    key_position = jnp.concatenate([(mine ^ mask) * token_rows + own_rows for mask in (0, 2, 1, 3)])
    query_doc, query_position = documents(lengths[0], position)
    key_doc = documents(lengths[0], key_position)[0]
    tables = rotary_tables(query_position)
    query_marks, key_marks = (query_doc, position), (key_doc, key_position)

    def paired(i):
        parts = []
        for at in range(0, kv_width, HEAD_SIZE):
            parts += [key_matrix[i, :, at : at + HEAD_SIZE], value_matrix[i, :, at : at + HEAD_SIZE]]
        return jnp.concatenate(parts, axis=1)

    kv_shards = [paired(i) for i in range(layer_count)]
    small = jnp.concatenate(
        [router_weight.transpose(0, 2, 1), attn_gain[:, None, :], ffn_gain[:, None, :]], axis=1
    )
    routing = Routing()
    routing.lines, routing.capacity = lines, capacity
    late = Sent(routing, cotangent)
    units = column_units(lines)

    def side_half(shard):
        half = shard.shape[0] // 2
        return lax.dynamic_slice(shard, (lines.side * half, 0), (half, shard.shape[1]))

    def joined(shard, beside, across, crossed):
        far = jnp.concatenate([across, crossed], axis=0)
        return jnp.concatenate([shard, beside, far, core_swap(far)], axis=0)

    small_across, small_beside = row_swap(small), core_swap(small)
    kv_across, kv_beside = row_swap(side_half(kv_shards[0])), core_swap(kv_shards[0])
    own_table = slot_table(routes, slot_order[0], experts, capacity)
    first_query = q_weight[0]
    small_across, small_beside, kv_across, kv_beside, own_table, first_query = sync(
        small_across, small_beside, kv_across, kv_beside, own_table, first_query
    )

    query_across, query_beside = row_swap(side_half(first_query)), core_swap(first_query)
    kv_crossed = lines.swap(kv_across)
    late.step()
    small_diagonal = core_swap(small_across)
    small = ordered_small({0: small, 1: small_beside, 2: small_across, 3: small_diagonal})
    routers = [small[i, :experts] for i in range(layer_count)]
    attn_gains = [small[i, experts].astype(f32)[None, :] for i in range(layer_count)]
    ffn_gains = [small[i, experts + 1].astype(f32)[None, :] for i in range(layer_count)]
    stream = tokens.astype(f32)
    normed, attn_inverse = norm_forward(stream, attn_gains[0])
    hidden = normed.astype(bf16)
    matched = ordered_columns(hidden, units)
    first_out = out_weight[0]
    query_across, query_beside, kv_crossed, matched, own_table, first_out = settle(
        [late], query_across, query_beside, kv_crossed, matched, own_table, first_out
    )

    query_crossed = lines.swap(query_across)
    first_kv = joined(kv_shards[0], kv_beside, kv_across, kv_crossed)
    first_pair = shard_rows_of(project_kv(matched, first_kv, tables))
    held_tables = [(own_table, own_table)]
    for _ in range(lines.count - 1):
        held_tables = lines.step_gather(held_tables)
    near_tables = jnp.stack([lines.slot(held_tables, j) for j in range(lines.count)], axis=0)
    later = [q_weight[0], kv_shards[0]]
    for i in range(1, layer_count):
        later += [kv_shards[i], q_weight[i], out_weight[i]]
    query_crossed, first_pair, near_tables, later = sync(
        query_crossed, first_pair, near_tables, later
    )
    first_query = joined(first_query, query_beside, query_across, query_crossed)

    whole = [lax.all_gather(part, "shard", axis=0, tiled=True) for part in [first_out] + later]
    gathered = [(whole[1], whole[2], whole[0])]
    for i in range(1, layer_count):
        gathered.append((whole[3 * i + 1], whole[3 * i], whole[3 * i + 2]))

    chosen_here = own_table.T != 0.0
    far_tables = lines.swap(near_tables)
    slot_code = jnp.arange(1, capacity + 1, dtype=jnp.int32).astype(f32)[:, None]

    def hot_rows(codes, expert):
        code = lax.dynamic_index_in_dim(codes, expert, 1, keepdims=True)
        return (code == slot_code).astype(bf16)

    routing.own_hot = hot_rows(near_tables, lines.index)
    routing.mate_hot = hot_rows(near_tables, lines.index ^ 1)
    all_hot = jnp.concatenate([routing.own_hot, hot_rows(far_tables, lines.index)], axis=0)
    all_tables = jnp.concatenate([near_tables, far_tables], axis=0)
    row_chosen = jnp.einsum(
        "sct,set->sce", all_hot, (all_tables != 0.0).astype(bf16), preferred_element_type=f32
    ).reshape(2 * lines.count * capacity, experts)
    row_chosen = row_chosen > 0.5
    sources = [
        lines.source(slot) * 2 + (lines.side ^ column)
        for column in range(2)
        for slot in range(lines.count)
    ]

    def gate_grads_back(row_values):
        blocks = row_values.reshape(2 * lines.count, capacity)
        spread = jnp.zeros((experts, token_rows), f32)
        rows = jnp.sum(all_hot.astype(f32) * blocks[:, :, None], axis=1)
        for i, source in enumerate(sources):
            spread = lax.dynamic_update_slice(spread, rows[i : i + 1], (source, 0))
        return lax.all_to_all(spread, "expert", split_axis=0, concat_axis=0, tiled=True).T

    def expert_forward(i, arrived):
        gates = chosen_softmax(mm_nt(arrived, routers[i]), row_chosen)
        own_gate = lax.dynamic_slice(gates, (0, lines.index), (gates.shape[0], 1))
        gate_pre = mm(arrived, gate_weight[i, 0])
        up_pre = mm(arrived, up_weight[i, 0])
        active = jax.nn.gelu(gate_pre, approximate=True) * up_pre
        gated = (own_gate * active).astype(bf16)
        produced = mm(gated, down_weight[i, 0]).astype(bf16)
        return produced, dict(gate=own_gate, gate_pre=gate_pre, up_pre=up_pre, gated=gated)

    def expert_backward(i, kept, d_arrived):
        du = mm_nt(d_arrived, down_weight[i, 0])
        unit, pull = jax.vjp(
            lambda a, b: jax.nn.gelu(a, approximate=True) * b, kept["gate_pre"], kept["up_pre"]
        )
        d_gate_rows = jnp.sum(du * unit, axis=1)
        d_active = (kept["gate"] * du).astype(bf16).astype(f32)
        d_gate_pre, d_up_pre = pull(d_active)
        d_both = jnp.concatenate([d_gate_pre.astype(bf16), d_up_pre.astype(bf16)], axis=1)
        return d_gate_rows, d_both

    def expert_rows(i, d_both):
        d_rows = mm_nt(d_both[:, :hidden_units], gate_weight[i, 0])
        return (d_rows + mm_nt(d_both[:, hidden_units:], up_weight[i, 0])).astype(bf16)

    def shard_sum(part):
        return lax.psum_scatter(part, "shard", scatter_dimension=0, tiled=True)

    def small_sum(part):
        own = sum(exchange_blocks(split_columns(part)))
        return jnp.pad(own, ((0, -own.shape[0] % 128), (0, 0))).T

    last = layer_count - 1
    stored = []
    for i in range(layer_count):
        w_query, w_kv, w_out = gathered[i]
        if i == 0:
            late.step()
            late.pack(0)
            kv_pair = first_pair
            q_pre = mm(matched, first_query)
        else:
            if i == last:
                late.pack(2)
            normed, attn_inverse = norm_forward(stream, attn_gains[i])
            hidden = normed.astype(bf16)
            kv_pair = shard_rows_of(project_kv(hidden, w_kv, tables))
            q_pre = mm(hidden, w_query)
            kv_pair, q_pre = settle([late], kv_pair, q_pre)
            if i == last:
                late.pack(3)
        kv_all = shard_rows_all(kv_pair)
        query, mixed = attend(q_pre, kv_all, tables, query_marks, key_marks)
        stream_mid = stream + mm(mixed, w_out)
        normed_ffn, ffn_inverse = norm_forward(stream_mid, ffn_gains[i])
        routed = normed_ffn.astype(bf16)
        (routed,) = settle([late], routed)
        gates = chosen_softmax(mm_nt(routed, routers[i]), chosen_here)
        sent = Sent(routing, routed)
        for j in range(lines.count):
            if j < lines.count - 1:
                sent.step()
            sent.pack(j)
            if i == last and j == 0:
                late.total()
            hidden, mixed = settle([sent, late], hidden, mixed)
        columns = [own_columns(hidden), own_columns(mixed)]
        arrived = sent.total()
        if i == 0:
            (arrived,) = settle([late], arrived)
            late.step()
            late.pack(1)
        produced, kept = expert_forward(i, arrived)
        produced, kept = settle([late], produced, kept)
        stored.append(
            dict(
                stream=stream,
                attn_inverse=attn_inverse,
                hidden_columns=columns[0],
                query=query,
                kv_all=kv_all,
                mixed_columns=columns[1],
                stream_mid=stream_mid,
                ffn_inverse=ffn_inverse,
                routed=routed,
                gates=gates,
                arrived=arrived,
                kept=kept,
            )
        )
        back = Returned(routing, produced)
        if i < last:
            for _ in range(lines.count):
                back.advance()
                settle([back])
            stream = stream_mid + back.total()

    output_back = back
    output_back.advance()
    d_arrived = late.total()
    upstream = cotangent.astype(f32)
    grads = [None] * layer_count
    for i in reversed(range(layer_count)):
        w_query, w_kv, w_out = gathered[i]
        saved = stored[i]
        if i < last:
            sent = Sent(routing, upstream.astype(bf16))
            above = stored[i + 1]
            d_branch, d_query, d_kv_low = waiting
            for j in range(lines.count):
                if j < lines.count - 1:
                    sent.step()
                sent.pack(j)
                if j == 0:
                    d_branch = shard_rows_of(d_branch)
                    small_part = small_sum(small_grad)
                if j == 1:
                    d_query = shard_rows_of(d_query)
                    d_branch = shard_rows_all(d_branch)
                if j == 2:
                    out_part = mm_tn(above["mixed_columns"], d_branch).astype(bf16)
                    d_kv_low = shard_rows_of(d_kv_low)
                    d_query = shard_rows_all(d_query)
                if j == 3:
                    d_kv_low = shard_rows_all(d_kv_low)
                    q_part = mm_tn(above["hidden_columns"], d_query).astype(bf16)
                d_branch, d_query, d_kv_low = settle([sent], d_branch, d_query, d_kv_low)
            kv_part = mm_tn(above["hidden_columns"], d_kv_low).astype(bf16)
            part = jnp.concatenate([q_part, out_part, kv_part, small_part.astype(bf16)], axis=1)
            last_sum = Summed(lines, part)
            last_sum.side()
            last_experts = expert_grads
            d_arrived = sent.total()
        d_gate_rows, d_both = expert_backward(i, saved["kept"], d_arrived)
        if i == last:
            d_gate_rows, d_both = settle([output_back], d_gate_rows, d_both)
            output_back.advance()
            d_rows = expert_rows(i, d_both)
            d_rows, d_gate_rows, d_both = settle([output_back], d_rows, d_gate_rows, d_both)
        else:
            d_rows = expert_rows(i, d_both)
            d_rows, d_gate_rows, d_both = settle([last_sum], d_rows, d_gate_rows, d_both)
        d_gates = gate_grads_back(d_gate_rows)
        back = Returned(routing, d_rows)
        arrived, gated = saved["arrived"], saved["kept"]["gated"]
        for j in range(lines.count):
            back.advance()
            extra = ()
            if j == 0:
                extra = mm_tn(arrived, d_both).astype(bf16)
            if j == 1:
                extra = mm_tn(gated, d_arrived).astype(bf16)
            extra, d_gates, arrived, gated, d_both, d_arrived = settle(
                [back], extra, d_gates, arrived, gated, d_both, d_arrived
            )
            if j == 0:
                both_grad = shard_sum(extra).astype(f32)
            if j == 1:
                down_grad = shard_sum(extra).astype(f32)
        expert_grads = (both_grad, down_grad)
        gates = saved["gates"]
        d_logits = gates * (d_gates - jnp.sum(gates * d_gates, axis=1, keepdims=True))
        d_logits = d_logits.astype(bf16)
        router_grad = mm_tn(d_logits, saved["routed"])
        d_routed = back.total() + mm(d_logits, routers[i])
        d_stream, ffn_gain_grad = norm_backward(
            saved["stream_mid"], saved["ffn_inverse"], ffn_gains[i], d_routed
        )
        upstream = upstream + d_stream
        d_branch = upstream.astype(bf16)
        d_mixed = mm_nt(d_branch, w_out).astype(bf16)
        if i == last:
            output_back.advance()
            moving = [output_back]
            d_branch_all = ()
        else:
            last_sum.scatter()
            moving = [last_sum]
            d_branch_all = shard_rows_all(shard_rows_of(d_branch))
        d_query, d_kv = attend_back(
            saved["query"], saved["kv_all"], d_mixed, tables, query_marks, key_marks
        )
        d_query, d_kv, d_branch_all = settle(moving, d_query, d_kv, d_branch_all)
        if i == last:
            output_back.advance()
            sums = [output_back]
        else:
            out_sum = Summed(lines, mm_tn(saved["mixed_columns"], d_branch_all))
            out_sum.side()
            last_sum.spread()
            sums = [out_sum, last_sum]
        pair_rows = 2 * token_rows
        d_kv_pair = d_kv[:pair_rows].astype(f32) + core_swap(d_kv[pair_rows:]).astype(f32)
        d_hidden = mm_nt(d_query, w_query)
        d_kv_pair, d_hidden, d_query = sync(d_kv_pair, d_hidden, d_query)
        d_kv_crossed = row_swap(d_kv_pair[token_rows:].astype(bf16))
        if i < last:
            d_query_pair = shard_rows_of(d_query)
        d_kv_low = turn_kv_back(d_kv_pair[:token_rows], d_kv_crossed, tables)
        d_hidden = d_hidden + mm_nt(d_kv_low, w_kv)
        d_stream, attn_gain_grad = norm_backward(
            saved["stream"], saved["attn_inverse"], attn_gains[i], d_hidden
        )
        upstream = upstream + d_stream
        small_grad = jnp.concatenate(
            [router_grad, attn_gain_grad[None, :], ffn_gain_grad[None, :]], axis=0
        )
        if i == last:
            upstream, d_kv_low, small_grad = settle(sums, upstream, d_kv_low, small_grad)
            output = (saved["stream_mid"] + output_back.total()).astype(bf16)
            waiting = (d_branch, d_query, d_kv_low)
            upstream, output, waiting = sync(upstream, output, waiting)
        else:
            d_query_pair, d_kv_low, small_grad, upstream = settle(
                sums, d_query_pair, d_kv_low, small_grad, upstream
            )
            out_sum.scatter()
            d_kv_pair = shard_rows_of(d_kv_low)
            small_part = small_sum(small_grad)
            hidden_columns = saved["hidden_columns"]
            q_sum = Summed(lines, mm_tn(hidden_columns, shard_rows_all(d_query_pair)))
            q_sum.side()
            d_kv_pair, small_part = settle([q_sum, out_sum], d_kv_pair, small_part)
            kv_part = mm_tn(hidden_columns, shard_rows_all(d_kv_pair))
            kv_sum = Summed(lines, jnp.concatenate([kv_part, small_part], axis=1))
            for sends in (
                (q_sum.scatter, kv_sum.side, last_sum.join),
                (q_sum.spread, kv_sum.scatter, out_sum.spread),
                (q_sum.join, kv_sum.spread, out_sum.join),
                (kv_sum.join,),
            ):
                for send in sends:
                    send()
                settle([q_sum, kv_sum, out_sum, last_sum])
            grads[i] = (q_sum.whole(), kv_sum.whole(), out_sum.whole()) + expert_grads
            above = last_sum.whole()
            width = model_width
            grads[last] = (above[:, :width], above[:, 2 * width :], above[:, width : 2 * width])
            grads[last] += last_experts
    input_grad = upstream.astype(bf16)
    stacked = [jnp.stack([grads[i][k] for i in range(layer_count)], axis=0) for k in range(5)]
    q_grad, kv_grad, out_grad, both_grad, down_grad = stacked
    kv_parts = [kv_grad[:, :, at : at + HEAD_SIZE] for at in range(0, 2 * kv_width, HEAD_SIZE)]
    small_grad = kv_grad[:, :, 2 * kv_width :]
    return (
        output,
        input_grad,
        q_grad,
        jnp.concatenate(kv_parts[0::2], axis=2),
        jnp.concatenate(kv_parts[1::2], axis=2),
        out_grad,
        small_grad[:, :, :experts],
        small_grad[:, :, experts],
        small_grad[:, :, experts + 1],
        both_grad[:, None, :, :hidden_units],
        both_grad[:, None, :, hidden_units:],
        down_grad[:, None],
    )


def solution(mesh):
    tokens_spec = P(("expert", "shard"), None)
    shard_spec = P(None, "shard", None)
    expert_spec = P(None, "expert", None, None)
    expert_grad_spec = P(None, "expert", "shard", None)
    return jax.shard_map(
        per_device,
        mesh=mesh,
        in_specs=(
            tokens_spec,
            P("expert", None),
            tokens_spec,
            tokens_spec,
            tokens_spec,
            shard_spec,
            shard_spec,
            shard_spec,
            shard_spec,
            shard_spec,
            P(None, "shard"),
            P(None, "shard"),
            expert_spec,
            expert_spec,
            expert_spec,
        ),
        out_specs=(
            tokens_spec,
            tokens_spec,
            shard_spec,
            shard_spec,
            shard_spec,
            shard_spec,
            shard_spec,
            P(None, "shard"),
            P(None, "shard"),
            expert_grad_spec,
            expert_grad_spec,
            expert_grad_spec,
        ),
        check_vma=False,
    )
```

time: 1490 us -> 1150 us (0.77)
  starting transfers between devices: 343 us -> 173 us
  waiting for transfers between devices: 525 us -> 453 us
  Pallas kernels: 0 us -> 66.1 us
  matrix products: 319 us -> 255 us
  blocking collectives: 48.2 us -> 0 us
  other arithmetic: 103 us -> 75.3 us
  local copies, waits for them, and re-layouts: 115 us -> 98.7 us
    ppermute x120 -> x87, starting transfers between devices: 250 us -> 96.5 us  [the longest x27 43.4 us: even(): lax.ppermute(values, 'expert', [(i, i ^ 2) for i in range(self.experts)])]
    ppermute x120 -> x87, waiting for transfers between devices: 234 us -> 91.4 us  [the longest x27 59.7 us: even(): lax.ppermute(values, 'expert', [(i, i ^ 2) for i in range(self.experts)])]
    ppermute x44 -> x43, waiting for transfers between devices: 135 us -> 254 us  [swap(): lax.ppermute(values, 'expert', [(i, i ^ 1) for i in range(self.experts)])]
    psum x1 -> x0, waiting for transfers between devices: 91.9 us -> none  [per_device(): small_sum = lax.psum(stacked[4], ('expert', 'shard'))]
    pallas_call x0 -> x8, Pallas kernels: none -> 66.1 us  [the longest x2 42 us: attend_back(): pl.pallas_call(kernel, grid=(heads,), in_specs=[by_head, by_group, by_hea...]
    dot_general x12 -> x1, matrix products: 53.9 us -> 1.04 us  [per_device(): jnp.einsum('sct,set->sce', all_hot, (all_tables != 0.0).astype(bf16), pre...]
    all_gather x2 -> x0, blocking collectives: 48.2 us -> none  [the longest x1 37 us: per_device(): all_tables = lax.all_gather(own_table, 'expert', axis=0)]
    ppermute x16 -> x13, waiting for transfers between devices: 64.3 us -> 107 us  [row_swap(): lax.ppermute(values, 'shard', [(i, i ^ 2) for i in range(lax.axis_size('s...]
  transfers between devices with their start and end apart: 205 -> 171, of which waited for: 74 -> 67; matrix products, arithmetic and copies ran while one was open for 32% -> 34% of each run, Pallas kernels for 0% -> 6%
where the time goes in v2:
time: 1150 us; the launch traced here: 1140 us
  waiting for transfers between devices  453 us (39%)
  matrix products  255 us (22%)
  starting transfers between devices  173 us (15%)
  local copies, waits for them, and re-layouts  98.7 us (9%)
  other arithmetic  75.3 us (7%)
  Pallas kernels  66.1 us (6%)
  between operations  18.4 us (2%)
    ppermute x43, waiting for transfers between devices, swap(): lax.ppermute(values, 'expert', [(i, i ^ 1) for i in range(self.experts)])  254 us
    ppermute x13, waiting for transfers between devices, row_swap(): lax.ppermute(values, 'shard', [(i, i ^ 2) for i in range(lax.axis_size('s...  107 us
    dot_general x45, matrix products, mm_tn(): lax.dot_general(left, right, (((0,), (0,)), ((), ())), preferred_element_...  105 us
    dot_general x45, matrix products, mm(): return jnp.dot(left, right, preferred_element_type=f32)  84.9 us
    dot_general x16, matrix products, mm_nt(): lax.dot_general(left, right, (((1,), (1,)), ((), ())), preferred_element_...  64 us
    ppermute x27, waiting for transfers between devices, even(): lax.ppermute(values, 'expert', [(i, i ^ 2) for i in range(self.experts)])  59.7 us
    ppermute x43, starting transfers between devices, swap(): lax.ppermute(values, 'expert', [(i, i ^ 1) for i in range(self.experts)])  48.1 us
    ppermute x27, starting transfers between devices, even(): lax.ppermute(values, 'expert', [(i, i ^ 2) for i in range(self.experts)])  43.4 us
  transfers between devices with their start and end apart: 171, of which 67 were waited for; matrix products, arithmetic and copies ran while one was open for 34% of the time, Pallas kernels for 6%

profile of v2, /device:TPU:0, one launch (start us, length us, event | category | flops | bytes accessed | tf_op | source)
XLA Modules:
  0.0 1138.6 jit_solution(11748586920681893478)
XLA Ops:
  44.4 7.3 collective-permute-done.6
  70.4 11.3 collective-permute-done.14
  111.9 11.4 shard_map.410
  124.2 4.3 multiply_reduce_fusion.10
  134.9 9.3 collective-permute-done.25
  152.1 12.7 %collective-permute-done.28 = bf16[160,1536]{1,0:T(8,128)(2,1)S(1)} collective-permute-done((bf16[160,1536]{1,0:T(8,128)(2,1)S(1)}, bf16[160,1536]{1,0:T(8,128)(2,1)S(1)}, u32[]{:S(2)}, u32[]{:S(2)}) %collective-permute-start.28) | collective-permute-done | bytes 491552 | tf_op jit(solution)/shard_map/ppermute | solution.py:299
  170.8 8.5 collective-permute-done.30
  179.3 4.7 collective-permute-done.29
  187.2 8.4 collective-permute-done.31
  203.7 5.2 fusion.30
  220.3 8.3 collective-permute-done.37
  235.1 7.2 collective-permute-done.39
  242.3 4.8 collective-permute-done.40
  253.1 12.2 %collective-permute-done.38 = bf16[160,1536]{1,0:T(8,128)(2,1)} collective-permute-done((bf16[160,1536]{1,0:T(8,128)(2,1)}, bf16[160,1536]{1,0:T(8,128)(2,1)}, u32[]{:S(2)}, u32[]{:S(2)}) %collective-permute-start.38) | collective-permute-done | bytes 491552 | tf_op jit(solution)/shard_map/ppermute | solution.py:299
  279.2 18.7 %collective-permute-done.36 = bf16[160,1536]{1,0:T(8,128)(2,1)S(1)} collective-permute-done((bf16[160,1536]{1,0:T(8,128)(2,1)S(1)}, bf16[160,1536]{1,0:T(8,128)(2,1)S(1)}, u32[]{:S(2)}, u32[]{:S(2)}) %collective-permute-start.36) | collective-permute-done | bytes 491552 | tf_op jit(solution)/shard_map/ppermute | solution.py:299
  309.6 3.8 collective-permute-done.45
  320.5 11.1 shard_map.412
  333.4 4.3 multiply_reduce_fusion.8
  342.7 10.9 collective-permute-done.50
  353.5 5.4 collective-permute-done.48
  365.3 11.1 collective-permute-done.53
  382.2 9.5 collective-permute-done.55
  391.7 4.2 collective-permute-done.54
  398.3 9.3 collective-permute-done.56
  412.3 5.2 fusion.40
  417.5 3.9 convolution_convert_fusion.2
  426.5 10.0 fusion.13
  438.8 5.1 fusion.72
  447.8 4.9 fusion
  452.7 8.0 collective-permute-done.61
  474.4 10.1 convolution_convert_fusion.1
  492.3 7.4 convolution_convert_fusion.5
  512.7 10.3 collective-permute-done.66
  535.0 8.7 collective-permute-done.64
  553.0 21.0 %shard_map.413 = (bf16[256,1536]{1,0:T(8,128)(2,1)S(1)}, bf16[1024,512]{1,0:T(8,128)(2,1)S(1)}) custom-call(bf16[256,1536]{1,0:T(8,128)(2,1)S(1)} %copy-done.15, bf16[1024,512]{1,0:T(8,128)(2,1)S(1)} %copy-done.9, bf16[256,1536]{1,0:T(8,128)(2,1)S(1)} %convolution_convert_fusion.9.dm_ref, f32[256,128]{1,0:T(8,128)S(1)} %get-tuple-element.806.cos_ref, ...), custom_call_target="tpu_custom_call" | custom-call | flops 8053063680 | bytes 3145728 | tf_op jit(solution)/shard_map/pallas_call | solution.py:212
  576.9 3.7 fusion.264
  594.1 9.5 collective-permute-done.73
  613.0 11.1 collective-permute-done.86
  638.7 11.8 %collective-permute-done.91 = bf16[256,1536]{1,0:T(8,128)(2,1)S(1)} collective-permute-done((bf16[256,1536]{1,0:T(8,128)(2,1)S(1)}, bf16[256,1536]{1,0:T(8,128)(2,1)S(1)}, u32[]{:S(2)}, u32[]{:S(2)}) %collective-permute-start.91) | collective-permute-done | bytes 786464 | tf_op jit(solution)/shard_map/ppermute | solution.py:389
  654.4 3.8 pad_maximum_fusion.4
  664.7 7.3 collective-permute-done.96
  697.8 8.1 collective-permute-done.99
  706.0 9.2 multiply_reduce_fusion
  715.2 5.5 fusion.85
  728.2 5.1 fusion.1
  733.3 24.1 %collective-permute-done.104 = bf16[192,3712]{1,0:T(8,128)(2,1)S(1)} collective-permute-done((bf16[192,3712]{1,0:T(8,128)(2,1)S(1)}, bf16[192,3712]{1,0:T(8,128)(2,1)S(1)}, u32[]{:S(2)}, u32[]{:S(2)}) %collective-permute-start.104) | collective-permute-done | bytes 1425440 | tf_op jit(solution)/shard_map/ppermute | solution.py:299
  763.9 5.1 all-to-all-start.1
  773.6 10.1 convolution_convert_fusion
  791.2 4.6 convolution_convert_fusion.4
  795.8 5.2 collective-permute-done.111
  801.0 5.0 collective-permute-done.112
  812.2 12.9 %collective-permute-done.110 = bf16[160,1536]{1,0:T(8,128)(2,1)S(1)} collective-permute-done((bf16[160,1536]{1,0:T(8,128)(2,1)S(1)}, bf16[160,1536]{1,0:T(8,128)(2,1)S(1)}, u32[]{:S(2)}, u32[]{:S(2)}) %collective-permute-start.110) | collective-permute-done | bytes 491552 | tf_op jit(solution)/shard_map/ppermute | solution.py:299
  835.8 10.7 collective-permute-done.108
  857.9 26.1 %collective-permute-done.117 = bf16[256,1536]{1,0:T(8,128)(2,1)S(1)} collective-permute-done((bf16[256,1536]{1,0:T(8,128)(2,1)S(1)}, bf16[256,1536]{1,0:T(8,128)(2,1)S(1)}, u32[]{:S(2)}, u32[]{:S(2)}) %collective-permute-start.117) | collective-permute-done | bytes 786464 | tf_op jit(solution)/shard_map/ppermute | solution.py:389
  890.5 3.9 convolution_convert_fusion.8.dm_ref
  894.4 21.0 %shard_map.415 = (bf16[256,1536]{1,0:T(8,128)(2,1)S(1)}, bf16[1024,512]{1,0:T(8,128)(2,1)S(1)}) custom-call(bf16[256,1536]{1,0:T(8,128)(2,1)S(1)} %copy-done.13, bf16[1024,512]{1,0:T(8,128)(2,1)S(1)} %copy-done.7, bf16[256,1536]{1,0:T(8,128)(2,1)S(1)} %convolution_convert_fusion.8.dm_ref, f32[256,128]{1,0:T(8,128)S(1)} %get-tuple-element.806.cos_ref, ...), custom_call_target="tpu_custom_call" | custom-call | flops 8053063680 | bytes 3145728 | tf_op jit(solution)/shard_map/pallas_call | solution.py:212
  926.6 5.1 fusion.266
  938.2 10.1 collective-permute-done.125.second_ref
  953.7 20.7 %collective-permute-done.124 = bf16[256,1536]{1,0:T(8,128)(2,1)} collective-permute-done((bf16[256,1536]{1,0:T(8,128)(2,1)S(1)}, bf16[256,1536]{1,0:T(8,128)(2,1)}, u32[]{:S(2)}, u32[]{:S(2)}) %collective-permute-start.124) | collective-permute-done | bytes 786464 | tf_op jit(solution)/shard_map/ppermute | solution.py:389
  1000.2 5.0 collective-permute-done.132
  1017.8 18.4 %collective-permute-done.143 = bf16[192,3712]{1,0:T(8,128)(2,1)} collective-permute-done((bf16[192,3712]{1,0:T(8,128)(2,1)}, bf16[192,3712]{1,0:T(8,128)(2,1)}, u32[]{:S(2)}, u32[]{:S(2)}) %collective-permute-start.143) | collective-permute-done | bytes 1425440 | tf_op jit(solution)/shard_map/ppermute | solution.py:299
  1036.2 4.4 collective-permute-done.142
  1067.1 8.7 collective-permute-done.145
  1092.3 11.4 collective-permute-done.153
  (1038 shorter events, 534.1 us)
Async XLA Ops:
  7.2 117.0 %all-gather.7.cloned.1.call-start = ((), (), s32[]{:S(2)}) async-start(), calls=%async_computation.6 | async-start | bytes 5898240 | tf_op jit(solution)/shard_map/all_gather | solution.py:677
  9.4 23.7 %collective-permute-start.2 = (bf16[2,10,384]{2,1,0:T(8,128)(2,1)S(1)}, bf16[2,10,384]{2,1,0:T(8,128)(2,1)S(1)}, u32[]{:S(2)}, u32[]{:S(2)}) collective-permute-start(bf16[2,10,384]{2,1,0:T(8,128)(2,1)S(1)} %get-tuple-element.765), channel_id=1, source_target_pairs={{0,2},{1,3},{2,0},{3,1},{4,6},{5,7},{6,4},{7,5},{8,10},{9,11},{10,... | collective-permute-start | bytes 46088 | tf_op jit(solution)/shard_map/ppermute | solution.py:389
  12.5 20.7 %collective-permute-start.3 = (bf16[2,10,384]{2,1,0:T(8,128)(2,1)S(1)}, bf16[2,10,384]{2,1,0:T(8,128)(2,1)S(1)}, u32[]{:S(2)}, u32[]{:S(2)}) collective-permute-start(bf16[2,10,384]{2,1,0:T(8,128)(2,1)S(1)} %get-tuple-element.765), channel_id=1, source_target_pairs={{0,1},{1,0},{2,3},{3,2},{4,5},{5,4},{6,7},{7,6},{8,9},{9,8},{10,11... | collective-permute-start | bytes 46088 | tf_op jit(solution)/shard_map/ppermute | solution.py:385
  17.4 27.0 %collective-permute-start = (bf16[256,1536]{1,0:T(8,128)(2,1)S(1)}, bf16[256,1536]{1,0:T(8,128)(2,1)}, u32[]{:S(2)}, u32[]{:S(2)}) collective-permute-start(bf16[256,1536]{1,0:T(8,128)(2,1)S(1)} %copy-done.37), channel_id=1, source_target_pairs={{0,8},{4,12},{8,0},{12,4},{16,24},{20,28},{24,16},{28,20},{1,9},{5... | collective-permute-start | bytes 2359304 | tf_op jit(solution)/shard_map/ppermute | solution.py:302
  51.7 251.3 %all-gather.9.cloned.1.call-start = ((), (), s32[]{:S(2)}) async-start(), calls=%async_computation.7 | async-start | bytes 1966080 | tf_op jit(solution)/shard_map/all_gather | solution.py:677
  82.6 223.3 %all-gather.11.cloned.1.call-start = ((), (), s32[]{:S(2)}) async-start(), calls=%async_computation.8 | async-start | bytes 5898240 | tf_op jit(solution)/shard_map/all_gather | solution.py:677
  85.3 43.4 %collective-permute-start.10 = (bf16[256,1536]{1,0:T(8,128)(2,1)}, bf16[256,1536]{1,0:T(8,128)(2,1)}, u32[]{:S(2)}, u32[]{:S(2)}) collective-permute-start(bf16[256,1536]{1,0:T(8,128)(2,1)} %collective-permute-done.1), channel_id=1, source_target_pairs={{0,8},{4,12},{8,0},{12,4},{16,24},{20,28},{24,16},{28,20},{1,9},{5... | collective-permute-start | bytes 2359304 | tf_op jit(solution)/shard_map/ppermute | solution.py:302
  86.9 41.8 %collective-permute-start.11 = (bf16[256,1536]{1,0:T(8,128)(2,1)}, bf16[256,1536]{1,0:T(8,128)(2,1)}, u32[]{:S(2)}, u32[]{:S(2)}) collective-permute-start(bf16[256,1536]{1,0:T(8,128)(2,1)} %collective-permute-done), channel_id=1, source_target_pairs={{0,1},{1,0},{2,3},{3,2},{4,5},{5,4},{6,7},{7,6},{8,16},{9,17},{10,... | collective-permute-start | bytes 2359304 | tf_op jit(solution)/shard_map/ppermute | solution.py:314
  97.7 235.8 %all-gather.13.cloned.1.call-start = ((), (), s32[]{:S(2)}) async-start(), calls=%async_computation.9 | async-start | bytes 5898240 | tf_op jit(solution)/shard_map/all_gather | solution.py:677
  101.6 27.2 %collective-permute-start.20 = (bf16[160,1536]{1,0:T(8,128)(2,1)}, bf16[160,1536]{1,0:T(8,128)(2,1)}, u32[]{:S(2)}, u32[]{:S(2)}) collective-permute-start(bf16[160,1536]{1,0:T(8,128)(2,1)} %convolution_convert_fusion.40), channel_id=1, source_target_pairs={{0,4},{4,0},{8,12},{12,8},{16,20},{20,16},{24,28},{28,24},{1,5},{5... | collective-permute-start | bytes 1474568 | tf_op jit(solution)/shard_map/ppermute | solution.py:299
  128.8 19.1 %collective-permute-start.23 = (bf16[256,1536]{1,0:T(8,128)(2,1)S(1)}, bf16[256,1536]{1,0:T(8,128)(2,1)S(1)}, u32[]{:S(2)}, u32[]{:S(2)}) collective-permute-start(bf16[256,1536]{1,0:T(8,128)(2,1)S(1)} %multiply_convert_fusion.4), channel_id=1, source_target_pairs={{0,8},{4,12},{8,0},{12,4},{16,24},{20,28},{24,16},{28,20},{1,9},{5... | collective-permute-start | bytes 2359304 | tf_op jit(solution)/shard_map/ppermute | solution.py:302
  133.5 82.1 %collective-permute-start.33 = (bf16[160,1536]{1,0:T(8,128)(2,1)S(1)}, bf16[160,1536]{1,0:T(8,128)(2,1)S(1)}, u32[]{:S(2)}, u32[]{:S(2)}) collective-permute-start(bf16[160,1536]{1,0:T(8,128)(2,1)S(1)} %convolution_convert_fusion.30), channel_id=1, source_target_pairs={{0,4},{4,0},{8,12},{12,8},{16,20},{20,16},{24,28},{28,24},{1,5},{5... | collective-permute-start | bytes 1474568 | tf_op jit(solution)/shard_map/ppermute | solution.py:299
  195.7 19.9 %collective-permute-start.32 = (bf16[256,1536]{1,0:T(8,128)(2,1)}, bf16[256,1536]{1,0:T(8,128)(2,1)S(1)}, u32[]{:S(2)}, u32[]{:S(2)}) collective-permute-start(bf16[256,1536]{1,0:T(8,128)(2,1)} %collective-permute-done.11), channel_id=1, source_target_pairs={{0,8},{4,12},{8,0},{12,4},{16,24},{20,28},{24,16},{28,20},{1,9},{5... | collective-permute-start | bytes 2359304 | tf_op jit(solution)/shard_map/ppermute | solution.py:302
  220.3 706.3 %all-gather.15.cloned.1.call-start = ((), (), s32[]{:S(2)}) async-start(), calls=%async_computation.10 | async-start | bytes 5898240 | tf_op jit(solution)/shard_map/all_gather | solution.py:677
  269.2 28.8 %collective-permute-start.43 = (bf16[256,1536]{1,0:T(8,128)(2,1)S(1)}, bf16[256,1536]{1,0:T(8,128)(2,1)S(1)}, u32[]{:S(2)}, u32[]{:S(2)}) collective-permute-start(bf16[256,1536]{1,0:T(8,128)(2,1)S(1)} %get-tuple-element.701), channel_id=1, source_target_pairs={{0,8},{4,12},{8,0},{12,4},{16,24},{20,28},{24,16},{28,20},{1,9},{5... | collective-permute-start | bytes 2359304 | tf_op jit(solution)/shard_map/ppermute | solution.py:302
  270.6 27.3 %collective-permute-start.44 = (bf16[256,1536]{1,0:T(8,128)(2,1)S(1)}, bf16[256,1536]{1,0:T(8,128)(2,1)S(1)}, u32[]{:S(2)}, u32[]{:S(2)}) collective-permute-start(bf16[256,1536]{1,0:T(8,128)(2,1)S(1)} %get-tuple-element.700), channel_id=1, source_target_pairs={{0,1},{1,0},{2,3},{3,2},{4,5},{5,4},{6,7},{7,6},{8,16},{9,17},{10,... | collective-permute-start | bytes 2359304 | tf_op jit(solution)/shard_map/ppermute | solution.py:314
  273.4 39.9 %collective-permute-start.35 = (bf16[160,1536]{1,0:T(8,128)(2,1)}, bf16[160,1536]{1,0:T(8,128)(2,1)}, u32[]{:S(2)}, u32[]{:S(2)}) collective-permute-start(bf16[160,1536]{1,0:T(8,128)(2,1)} %convolution_convert_fusion.28), channel_id=1, source_target_pairs={{0,4},{4,0},{8,12},{12,8},{16,20},{20,16},{24,28},{28,24},{1,5},{5... | collective-permute-start | bytes 1474568 | tf_op jit(solution)/shard_map/ppermute | solution.py:299
  275.3 22.6 %collective-permute-start.36 = (bf16[160,1536]{1,0:T(8,128)(2,1)S(1)}, bf16[160,1536]{1,0:T(8,128)(2,1)S(1)}, u32[]{:S(2)}, u32[]{:S(2)}) collective-permute-start(bf16[160,1536]{1,0:T(8,128)(2,1)S(1)} %copy-done.105), channel_id=1, source_target_pairs={{0,4},{4,0},{8,12},{12,8},{16,20},{20,16},{24,28},{28,24},{1,5},{5... | collective-permute-start | bytes 1474568 | tf_op jit(solution)/shard_map/ppermute | solution.py:299
  315.2 23.9 %collective-permute-start.46 = (bf16[160,1536]{1,0:T(8,128)(2,1)}, bf16[160,1536]{1,0:T(8,128)(2,1)}, u32[]{:S(2)}, u32[]{:S(2)}) collective-permute-start(bf16[160,1536]{1,0:T(8,128)(2,1)} %convolution_convert_fusion.26), channel_id=1, source_target_pairs={{0,4},{4,0},{8,12},{12,8},{16,20},{20,16},{24,28},{28,24},{1,5},{5... | collective-permute-start | bytes 1474568 | tf_op jit(solution)/shard_map/ppermute | solution.py:299
  339.1 19.8 %collective-permute-start.48 = (bf16[256,1536]{1,0:T(8,128)(2,1)S(1)}, bf16[256,1536]{1,0:T(8,128)(2,1)}, u32[]{:S(2)}, u32[]{:S(2)}) collective-permute-start(bf16[256,1536]{1,0:T(8,128)(2,1)S(1)} %multiply_convert_fusion.2), channel_id=1, source_target_pairs={{0,8},{4,12},{8,0},{12,4},{16,24},{20,28},{24,16},{28,20},{1,9},{5... | collective-permute-start | bytes 2359304 | tf_op jit(solution)/shard_map/ppermute | solution.py:302
  339.5 19.4 %collective-permute-start.49 = (bf16[256,1536]{1,0:T(8,128)(2,1)S(1)}, bf16[256,1536]{1,0:T(8,128)(2,1)}, u32[]{:S(2)}, u32[]{:S(2)}) collective-permute-start(bf16[256,1536]{1,0:T(8,128)(2,1)S(1)} %multiply_convert_fusion.2), channel_id=1, source_target_pairs={{0,1},{1,0},{2,3},{3,2},{4,5},{5,4},{6,7},{7,6},{8,16},{9,17},{10,... | collective-permute-start | bytes 2359304 | tf_op jit(solution)/shard_map/ppermute | solution.py:314
  358.9 19.1 %collective-permute-start.51 = (bf16[256,1536]{1,0:T(8,128)(2,1)}, bf16[256,1536]{1,0:T(8,128)(2,1)S(1)}, u32[]{:S(2)}, u32[]{:S(2)}) collective-permute-start(bf16[256,1536]{1,0:T(8,128)(2,1)} %collective-permute-done.49), channel_id=1, source_target_pairs={{0,8},{4,12},{8,0},{12,4},{16,24},{20,28},{24,16},{28,20},{1,9},{5... | collective-permute-start | bytes 2359304 | tf_op jit(solution)/shard_map/ppermute | solution.py:302
  424.8 27.9 %collective-permute-start.60 = (bf16[160,1536]{1,0:T(8,128)(2,1)}, bf16[160,1536]{1,0:T(8,128)(2,1)}, u32[]{:S(2)}, u32[]{:S(2)}) collective-permute-start(bf16[160,1536]{1,0:T(8,128)(2,1)} %get-tuple-element.671), channel_id=1, source_target_pairs={{0,4},{4,0},{8,12},{12,8},{16,20},{20,16},{24,28},{28,24},{1,5},{5... | collective-permute-start | bytes 1474568 | tf_op jit(solution)/shard_map/ppermute | solution.py:299
  469.5 479.8 %all-gather.17.cloned.1.call-start = ((), (), s32[]{:S(2)}) async-start(), calls=%async_computation.11 | async-start | bytes 1966080 | tf_op jit(solution)/shard_map/all_gather | solution.py:677
  508.7 555.2 %reduce-scatter.11.cloned.1.call-start = ((), (), s32[]{:S(2)}) async-start(), calls=%async_computation.15 | async-start | bytes 2949120 | tf_op jit(solution)/shard_map/reduce_scatter | solution.py:738
  511.2 62.8 %collective-permute-start.59 = (bf16[160,1536]{1,0:T(8,128)(2,1)}, bf16[160,1536]{1,0:T(8,128)(2,1)S(1)}, u32[]{:S(2)}, u32[]{:S(2)}) collective-permute-start(bf16[160,1536]{1,0:T(8,128)(2,1)} %get-tuple-element.672), channel_id=1, source_target_pairs={{0,4},{4,0},{8,12},{12,8},{16,20},{20,16},{24,28},{28,24},{1,5},{5... | collective-permute-start | bytes 1474568 | tf_op jit(solution)/shard_map/ppermute | solution.py:299
  526.3 20.5 %collective-permute-start.71 = (bf16[256,1536]{1,0:T(8,128)(2,1)S(1)}, bf16[256,1536]{1,0:T(8,128)(2,1)S(1)}, u32[]{:S(2)}, u32[]{:S(2)}) collective-permute-start(bf16[256,1536]{1,0:T(8,128)(2,1)S(1)} %get-tuple-element.695), channel_id=1, source_target_pairs={{0,8},{4,12},{8,0},{12,4},{16,24},{20,28},{24,16},{28,20},{1,9},{5... | collective-permute-start | bytes 2359304 | tf_op jit(solution)/shard_map/ppermute | solution.py:302
  526.4 20.5 %collective-permute-start.72 = (bf16[256,1536]{1,0:T(8,128)(2,1)S(1)}, bf16[256,1536]{1,0:T(8,128)(2,1)S(1)}, u32[]{:S(2)}, u32[]{:S(2)}) collective-permute-start(bf16[256,1536]{1,0:T(8,128)(2,1)S(1)} %get-tuple-element.694), channel_id=1, source_target_pairs={{0,1},{1,0},{2,3},{3,2},{4,5},{5,4},{6,7},{7,6},{8,16},{9,17},{10,... | collective-permute-start | bytes 2359304 | tf_op jit(solution)/shard_map/ppermute | solution.py:314
  531.6 42.5 %collective-permute-start.62 = (bf16[256,1536]{1,0:T(8,128)(2,1)S(1)}, bf16[256,1536]{1,0:T(8,128)(2,1)S(1)}, u32[]{:S(2)}, u32[]{:S(2)}) collective-permute-start(bf16[256,1536]{1,0:T(8,128)(2,1)S(1)} %get-tuple-element.699), channel_id=1, source_target_pairs={{0,8},{4,12},{8,0},{12,4},{16,24},{20,28},{24,16},{28,20},{1,9},{5... | collective-permute-start | bytes 2359304 | tf_op jit(solution)/shard_map/ppermute | solution.py:302
  543.7 30.3 %collective-permute-start.63 = (bf16[256,1536]{1,0:T(8,128)(2,1)S(1)}, bf16[256,1536]{1,0:T(8,128)(2,1)S(1)}, u32[]{:S(2)}, u32[]{:S(2)}) collective-permute-start(bf16[256,1536]{1,0:T(8,128)(2,1)S(1)} %get-tuple-element.698), channel_id=1, source_target_pairs={{0,1},{1,0},{2,3},{3,2},{4,5},{5,4},{6,7},{7,6},{8,16},{9,17},{10,... | collective-permute-start | bytes 2359304 | tf_op jit(solution)/shard_map/ppermute | solution.py:314
  583.9 19.7 %collective-permute-start.73 = (bf16[256,1536]{1,0:T(8,128)(2,1)S(1)}, bf16[256,1536]{1,0:T(8,128)(2,1)S(1)}, u32[]{:S(2)}, u32[]{:S(2)}) collective-permute-start(bf16[256,1536]{1,0:T(8,128)(2,1)S(1)} %get-tuple-element.693), channel_id=1, source_target_pairs={{0,8},{4,12},{8,0},{12,4},{16,24},{20,28},{24,16},{28,20},{1,9},{5... | collective-permute-start | bytes 2359304 | tf_op jit(solution)/shard_map/ppermute | solution.py:302
  606.8 19.0 %collective-permute-start.83 = (bf16[256,1536]{1,0:T(8,128)(2,1)S(1)}, bf16[256,1536]{1,0:T(8,128)(2,1)S(1)}, u32[]{:S(2)}, u32[]{:S(2)}) collective-permute-start(bf16[256,1536]{1,0:T(8,128)(2,1)S(1)} %convert_element_type.647), channel_id=1, source_target_pairs={{0,8},{4,12},{8,0},{12,4},{16,24},{20,28},{24,16},{28,20},{1,9},{5... | collective-permute-start | bytes 2359304 | tf_op jit(solution)/shard_map/ppermute | solution.py:302
  627.5 26.8 %collective-permute-start.90 = (bf16[512,1536]{1,0:T(8,128)(2,1)}, bf16[512,1536]{1,0:T(8,128)(2,1)}, u32[]{:S(2)}, u32[]{:S(2)}) collective-permute-start(bf16[512,1536]{1,0:T(8,128)(2,1)} %pad_maximum_fusion.8), channel_id=1, source_target_pairs={{0,1},{1,0},{2,3},{3,2},{4,5},{5,4},{6,7},{7,6},{8,9},{9,8},{10,11... | collective-permute-start | bytes 4718600 | tf_op jit(solution)/shard_map/ppermute | solution.py:385
  629.5 21.0 %collective-permute-start.91 = (bf16[256,1536]{1,0:T(8,128)(2,1)S(1)}, bf16[256,1536]{1,0:T(8,128)(2,1)S(1)}, u32[]{:S(2)}, u32[]{:S(2)}) collective-permute-start(bf16[256,1536]{1,0:T(8,128)(2,1)S(1)} %get-tuple-element.451), channel_id=1, source_target_pairs={{0,2},{1,3},{2,0},{3,1},{4,6},{5,7},{6,4},{7,5},{8,10},{9,11},{10,... | collective-permute-start | bytes 2359304 | tf_op jit(solution)/shard_map/ppermute | solution.py:389
  631.1 27.2 %collective-permute-start.87 = (bf16[256,1536]{1,0:T(8,128)(2,1)}, bf16[256,1536]{1,0:T(8,128)(2,1)}, u32[]{:S(2)}, u32[]{:S(2)}) collective-permute-start(bf16[256,1536]{1,0:T(8,128)(2,1)} %copy-done.87), channel_id=1, source_target_pairs={{0,8},{4,12},{8,0},{12,4},{16,24},{20,28},{24,16},{28,20},{1,9},{5... | collective-permute-start | bytes 2359304 | tf_op jit(solution)/shard_map/ppermute | solution.py:302
  632.6 27.6 %collective-permute-start.88 = (bf16[256,1536]{1,0:T(8,128)(2,1)}, bf16[256,1536]{1,0:T(8,128)(2,1)}, u32[]{:S(2)}, u32[]{:S(2)}) collective-permute-start(bf16[256,1536]{1,0:T(8,128)(2,1)} %copy-done.64), channel_id=1, source_target_pairs={{0,1},{1,0},{2,3},{3,2},{4,5},{5,4},{6,7},{7,6},{8,16},{9,17},{10,... | collective-permute-start | bytes 2359304 | tf_op jit(solution)/shard_map/ppermute | solution.py:314
  634.6 19.6 %collective-permute-start.89 = (bf16[160,1536]{1,0:T(8,128)(2,1)S(1)}, bf16[160,1536]{1,0:T(8,128)(2,1)S(1)}, u32[]{:S(2)}, u32[]{:S(2)}) collective-permute-start(bf16[160,1536]{1,0:T(8,128)(2,1)S(1)} %convolution_convert_fusion.14), channel_id=1, source_target_pairs={{0,4},{4,0},{8,12},{12,8},{16,20},{20,16},{24,28},{28,24},{1,5},{5... | collective-permute-start | bytes 1474568 | tf_op jit(solution)/shard_map/ppermute | solution.py:299
  658.2 36.5 %collective-permute-start.80 = (bf16[256,384]{1,0:T(8,128)(2,1)}, bf16[256,384]{1,0:T(8,128)(2,1)}, u32[]{:S(2)}, u32[]{:S(2)}) collective-permute-start(bf16[256,384]{1,0:T(8,128)(2,1)} %get-tuple-element.726), channel_id=1, source_target_pairs={{0,2},{1,3},{2,0},{3,1},{4,6},{5,7},{6,4},{7,5},{8,10},{9,11},{10,... | collective-permute-start | bytes 589832 | tf_op jit(solution)/shard_map/ppermute | solution.py:438
  662.4 21.0 %collective-permute-start.94 = (bf16[512,1536]{1,0:T(8,128)(2,1)}, bf16[512,1536]{1,0:T(8,128)(2,1)}, u32[]{:S(2)}, u32[]{:S(2)}) collective-permute-start(bf16[512,1536]{1,0:T(8,128)(2,1)} %pad_maximum_fusion.9), channel_id=1, source_target_pairs={{0,1},{1,0},{2,3},{3,2},{4,5},{5,4},{6,7},{7,6},{8,9},{9,8},{10,11... | collective-permute-start | bytes 4718600 | tf_op jit(solution)/shard_map/ppermute | solution.py:385
  671.9 19.4 %collective-permute-start.92 = (bf16[256,1536]{1,0:T(8,128)(2,1)}, bf16[256,1536]{1,0:T(8,128)(2,1)S(1)}, u32[]{:S(2)}, u32[]{:S(2)}) collective-permute-start(bf16[256,1536]{1,0:T(8,128)(2,1)} %collective-permute-done.88), channel_id=1, source_target_pairs={{0,8},{4,12},{8,0},{12,4},{16,24},{20,28},{24,16},{28,20},{1,9},{5... | collective-permute-start | bytes 2359304 | tf_op jit(solution)/shard_map/ppermute | solution.py:302
  724.4 32.9 %collective-permute-start.104 = (bf16[192,3712]{1,0:T(8,128)(2,1)S(1)}, bf16[192,3712]{1,0:T(8,128)(2,1)S(1)}, u32[]{:S(2)}, u32[]{:S(2)}) collective-permute-start(bf16[192,3712]{1,0:T(8,128)(2,1)S(1)} %constant_dynamic-slice_fusion.8), channel_id=1, source_target_pairs={{0,4},{4,0},{8,12},{12,8},{16,20},{20,16},{24,28},{28,24},{1,5},{5... | collective-permute-start | bytes 4276232 | tf_op jit(solution)/shard_map/ppermute | solution.py:299
  763.9 19.8 %all-to-all-start.1 = ((f32[8,1,256]{2,1,0:T(1,128)}), f32[8,1,256]{2,1,0:T(1,128)S(1)}, u32[]{:S(2)}, u32[]{:S(2)}) async-start(f32[8,1,256]{2,1,0:T(1,128)} %constant_dynamic-update-slice_fusion), calls=%async_computation.1 | async-start | bytes 16384 | tf_op jit(solution)/shard_map/all_to_all | solution.py:710
  769.0 294.9 %reduce-scatter.9.cloned.1.call-start = ((), (), s32[]{:S(2)}) async-start(), calls=%async_computation.14 | async-start | bytes 2949120 | tf_op jit(solution)/shard_map/reduce_scatter | solution.py:738
  806.1 278.8 %reduce-scatter.7.cloned.1.call-start = ((), (), s32[]{:S(2)}) async-start(), calls=%async_computation.13 | async-start | bytes 5898240 | tf_op jit(solution)/shard_map/reduce_scatter | solution.py:738
  806.8 278.1 %reduce-scatter.5.cloned.1.call-start = ((), (), s32[]{:S(2)}) async-start(), calls=%async_computation.12 | async-start | bytes 5898240 | tf_op jit(solution)/shard_map/reduce_scatter | solution.py:738
  833.9 99.4 %collective-permute-start.77 = (bf16[256,384]{1,0:T(8,128)(2,1)}, bf16[256,384]{1,0:T(8,128)(2,1)}, u32[]{:S(2)}, u32[]{:S(2)}) collective-permute-start(bf16[256,384]{1,0:T(8,128)(2,1)} %get-tuple-element.718), channel_id=1, source_target_pairs={{0,2},{1,3},{2,0},{3,1},{4,6},{5,7},{6,4},{7,5},{8,10},{9,11},{10,... | collective-permute-start | bytes 589832 | tf_op jit(solution)/shard_map/ppermute | solution.py:438
  856.2 27.8 %collective-permute-start.117 = (bf16[256,1536]{1,0:T(8,128)(2,1)S(1)}, bf16[256,1536]{1,0:T(8,128)(2,1)S(1)}, u32[]{:S(2)}, u32[]{:S(2)}) collective-permute-start(bf16[256,1536]{1,0:T(8,128)(2,1)S(1)} %get-tuple-element.642), channel_id=1, source_target_pairs={{0,2},{1,3},{2,0},{3,1},{4,6},{5,7},{6,4},{7,5},{8,10},{9,11},{10,... | collective-permute-start | bytes 2359304 | tf_op jit(solution)/shard_map/ppermute | solution.py:389
  885.3 30.4 %collective-permute-start.118 = (bf16[512,1536]{1,0:T(8,128)(2,1)}, bf16[512,1536]{1,0:T(8,128)(2,1)}, u32[]{:S(2)}, u32[]{:S(2)}) collective-permute-start(bf16[512,1536]{1,0:T(8,128)(2,1)} %pad_maximum_fusion.10), channel_id=1, source_target_pairs={{0,1},{1,0},{2,3},{3,2},{4,5},{5,4},{6,7},{7,6},{8,9},{9,8},{10,11... | collective-permute-start | bytes 4718600 | tf_op jit(solution)/shard_map/ppermute | solution.py:385
  886.3 32.8 %collective-permute-start.105 = (bf16[48,3712]{1,0:T(8,128)(2,1)}, bf16[48,3712]{1,0:T(8,128)(2,1)}, u32[]{:S(2)}, u32[]{:S(2)}) collective-permute-start(bf16[48,3712]{1,0:T(8,128)(2,1)} %get-tuple-element.706), channel_id=1, source_target_pairs={{0,8},{4,12},{8,16},{12,20},{16,24},{20,28},{24,0},{28,4},{1,9},{5... | collective-permute-start | bytes 1069064 | tf_op jit(solution)/shard_map/ppermute | solution.py:381
  887.6 33.1 %collective-permute-start.106 = (bf16[48,3712]{1,0:T(8,128)(2,1)}, bf16[48,3712]{1,0:T(8,128)(2,1)}, u32[]{:S(2)}, u32[]{:S(2)}) collective-permute-start(bf16[48,3712]{1,0:T(8,128)(2,1)} %get-tuple-element.705), channel_id=1, source_target_pairs={{0,16},{4,20},{8,24},{12,28},{16,0},{20,4},{24,8},{28,12},{1,17},{... | collective-permute-start | bytes 1069064 | tf_op jit(solution)/shard_map/ppermute | solution.py:381
  889.1 31.5 %collective-permute-start.107 = (bf16[48,3712]{1,0:T(8,128)(2,1)}, bf16[48,3712]{1,0:T(8,128)(2,1)}, u32[]{:S(2)}, u32[]{:S(2)}) collective-permute-start(bf16[48,3712]{1,0:T(8,128)(2,1)} %get-tuple-element.704), channel_id=1, source_target_pairs={{0,24},{4,28},{8,0},{12,4},{16,8},{20,12},{24,16},{28,20},{1,25},{... | collective-permute-start | bytes 1069064 | tf_op jit(solution)/shard_map/ppermute | solution.py:381
  924.5 52.1 %collective-permute-start.120 = (bf16[48,3712]{1,0:T(8,128)(2,1)}, bf16[48,3712]{1,0:T(8,128)(2,1)}, u32[]{:S(2)}, u32[]{:S(2)}) collective-permute-start(bf16[48,3712]{1,0:T(8,128)(2,1)} %get-tuple-element.641), channel_id=1, source_target_pairs={{0,24},{4,28},{8,0},{12,4},{16,8},{20,12},{24,16},{28,20},{1,25},{... | collective-permute-start | bytes 1069064 | tf_op jit(solution)/shard_map/ppermute | solution.py:381
  931.7 44.9 %collective-permute-start.121 = (bf16[48,3712]{1,0:T(8,128)(2,1)}, bf16[48,3712]{1,0:T(8,128)(2,1)}, u32[]{:S(2)}, u32[]{:S(2)}) collective-permute-start(bf16[48,3712]{1,0:T(8,128)(2,1)} %get-tuple-element.641), channel_id=1, source_target_pairs={{0,16},{4,20},{8,24},{12,28},{16,0},{20,4},{24,8},{28,12},{1,17},{... | collective-permute-start | bytes 1069064 | tf_op jit(solution)/shard_map/ppermute | solution.py:381
  933.2 44.6 %collective-permute-start.122 = (bf16[48,3712]{1,0:T(8,128)(2,1)}, bf16[48,3712]{1,0:T(8,128)(2,1)}, u32[]{:S(2)}, u32[]{:S(2)}) collective-permute-start(bf16[48,3712]{1,0:T(8,128)(2,1)} %get-tuple-element.641), channel_id=1, source_target_pairs={{0,8},{4,12},{8,16},{12,20},{16,24},{20,28},{24,0},{28,4},{1,9},{5... | collective-permute-start | bytes 1069064 | tf_op jit(solution)/shard_map/ppermute | solution.py:381
  937.4 40.5 %collective-permute-start.119 = (bf16[192,1536]{1,0:T(8,128)(2,1)S(1)}, bf16[192,1536]{1,0:T(8,128)(2,1)}, u32[]{:S(2)}, u32[]{:S(2)}) collective-permute-start(bf16[192,1536]{1,0:T(8,128)(2,1)S(1)} %dynamic-slice_convert_fusion.1), channel_id=1, source_target_pairs={{0,4},{4,0},{8,12},{12,8},{16,20},{20,16},{24,28},{28,24},{1,5},{5... | collective-permute-start | bytes 1769480 | tf_op jit(solution)/shard_map/ppermute | solution.py:299
  948.3 26.1 %collective-permute-start.124 = (bf16[256,1536]{1,0:T(8,128)(2,1)S(1)}, bf16[256,1536]{1,0:T(8,128)(2,1)}, u32[]{:S(2)}, u32[]{:S(2)}) collective-permute-start(bf16[256,1536]{1,0:T(8,128)(2,1)S(1)} %get-tuple-element.503), channel_id=1, source_target_pairs={{0,2},{1,3},{2,0},{3,1},{4,6},{5,7},{6,4},{7,5},{8,10},{9,11},{10,... | collective-permute-start | bytes 2359304 | tf_op jit(solution)/shard_map/ppermute | solution.py:389
  991.1 45.1 %collective-permute-start.143 = (bf16[192,3712]{1,0:T(8,128)(2,1)}, bf16[192,3712]{1,0:T(8,128)(2,1)}, u32[]{:S(2)}, u32[]{:S(2)}) collective-permute-start(bf16[192,3712]{1,0:T(8,128)(2,1)} %bitcast.86), channel_id=1, source_target_pairs={{0,4},{4,0},{8,12},{12,8},{16,20},{20,16},{24,28},{28,24},{1,5},{5... | collective-permute-start | bytes 4276232 | tf_op jit(solution)/shard_map/ppermute | solution.py:299
  1010.4 30.2 %collective-permute-start.142 = (bf16[192,640]{1,0:T(8,128)(2,1)}, bf16[192,640]{1,0:T(8,128)(2,1)S(1)}, u32[]{:S(2)}, u32[]{:S(2)}) collective-permute-start(bf16[192,640]{1,0:T(8,128)(2,1)} %fusion.141), channel_id=1, source_target_pairs={{0,4},{4,0},{8,12},{12,8},{16,20},{20,16},{24,28},{28,24},{1,5},{5... | collective-permute-start | bytes 737288 | tf_op jit(solution)/shard_map/ppermute | solution.py:299
  1012.8 23.4 %collective-permute-start.138 = (bf16[48,1536]{1,0:T(8,128)(2,1)}, bf16[48,1536]{1,0:T(8,128)(2,1)}, u32[]{:S(2)}, u32[]{:S(2)}) collective-permute-start(bf16[48,1536]{1,0:T(8,128)(2,1)} %get-tuple-element.737), channel_id=1, source_target_pairs={{0,8},{4,12},{8,16},{12,20},{16,24},{20,28},{24,0},{28,4},{1,9},{5... | collective-permute-start | bytes 442376 | tf_op jit(solution)/shard_map/ppermute | solution.py:381
  1015.4 20.8 %collective-permute-start.139 = (bf16[48,1536]{1,0:T(8,128)(2,1)}, bf16[48,1536]{1,0:T(8,128)(2,1)}, u32[]{:S(2)}, u32[]{:S(2)}) collective-permute-start(bf16[48,1536]{1,0:T(8,128)(2,1)} %get-tuple-element.736), channel_id=1, source_target_pairs={{0,16},{4,20},{8,24},{12,28},{16,0},{20,4},{24,8},{28,12},{1,17},{... | collective-permute-start | bytes 442376 | tf_op jit(solution)/shard_map/ppermute | solution.py:381
  1016.6 19.6 %collective-permute-start.140 = (bf16[48,1536]{1,0:T(8,128)(2,1)}, bf16[48,1536]{1,0:T(8,128)(2,1)}, u32[]{:S(2)}, u32[]{:S(2)}) collective-permute-start(bf16[48,1536]{1,0:T(8,128)(2,1)} %get-tuple-element.735), channel_id=1, source_target_pairs={{0,24},{4,28},{8,0},{12,4},{16,8},{20,12},{24,16},{28,20},{1,25},{... | collective-permute-start | bytes 442376 | tf_op jit(solution)/shard_map/ppermute | solution.py:381
  1042.4 20.6 %collective-permute-start.150 = (bf16[48,1536]{1,0:T(8,128)(2,1)}, bf16[48,1536]{1,0:T(8,128)(2,1)S(1)}, u32[]{:S(2)}, u32[]{:S(2)}) collective-permute-start(bf16[48,1536]{1,0:T(8,128)(2,1)} %get-tuple-element.637), channel_id=1, source_target_pairs={{0,24},{4,28},{8,0},{12,4},{16,8},{20,12},{24,16},{28,20},{1,25},{... | collective-permute-start | bytes 442376 | tf_op jit(solution)/shard_map/ppermute | solution.py:381
  1044.1 22.5 %collective-permute-start.151 = (bf16[48,1536]{1,0:T(8,128)(2,1)}, bf16[48,1536]{1,0:T(8,128)(2,1)S(1)}, u32[]{:S(2)}, u32[]{:S(2)}) collective-permute-start(bf16[48,1536]{1,0:T(8,128)(2,1)} %get-tuple-element.637), channel_id=1, source_target_pairs={{0,16},{4,20},{8,24},{12,28},{16,0},{20,4},{24,8},{28,12},{1,17},{... | collective-permute-start | bytes 442376 | tf_op jit(solution)/shard_map/ppermute | solution.py:381
  1077.2 26.5 %collective-permute-start.153 = (bf16[192,1536]{1,0:T(8,128)(2,1)S(1)}, bf16[192,1536]{1,0:T(8,128)(2,1)S(1)}, u32[]{:S(2)}, u32[]{:S(2)}) collective-permute-start(bf16[192,1536]{1,0:T(8,128)(2,1)S(1)} %bitcast.566), channel_id=1, source_target_pairs={{0,4},{4,0},{8,12},{12,8},{16,20},{20,16},{24,28},{28,24},{1,5},{5... | collective-permute-start | bytes 1769480 | tf_op jit(solution)/shard_map/ppermute | solution.py:299
  (296 other events, 3543.0 us)
Sparse Core Ops, SparseCore 0:
  51.9 43.8 all-gather.6
  97.3 20.8 all-gather.8
  120.3 37.4 all-gather.10
  220.4 37.3 all-gather.12
  339.7 36.5 all-gather.14
  508.8 19.8 all-gather.16
  629.6 36.3 reduce-scatter.10
  806.2 33.3 reduce-scatter.8
  842.7 56.8 reduce-scatter.6
  902.7 63.1 reduce-scatter.4

commit v3 on v2

--- a/solution.py
+++ b/solution.py
@@ -1,3 +1,5 @@
+import math
+
 import jax
 import jax.numpy as jnp
 from jax import lax
@@ -62,27 +64,43 @@
     return pltpu.CompilerParams(vmem_limit_bytes=40 * 1024 * 1024)
 
 
-def project_kv(hidden, w_kv, tables):
-    rows, width = hidden.shape[0], w_kv.shape[1]
-
-    def kernel(hidden_ref, w_ref, cos_ref, sin_ref, out_ref):
-        value = jnp.dot(hidden_ref[...], w_ref[...], preferred_element_type=f32)
+def project(parts, weights, tables=None):
+    rows, width = parts[0].shape[0], weights[0].shape[1]
+    tile = width if tables else width // 3
+    count = len(parts)
+
+    def kernel(*refs):
+        out_ref = refs[-1]
+        value = mm(refs[0][...], refs[count][...])
+        for k in range(1, count):
+            value = value + mm(refs[k][...], refs[count + k][...])
+        if tables is None:
+            out_ref[...] = value
+            return
         for at in range(0, width, HEAD_SIZE):
             part = value[:, at : at + HEAD_SIZE]
             if at // HEAD_SIZE % 2 == 0:
-                part = turned(part, cos_ref[...], sin_ref[...])
+                part = turned(part, refs[2 * count][...], refs[2 * count + 1][...])
             out_ref[:, at : at + HEAD_SIZE] = part.astype(bf16)
 
+    fixed = lambda x: pl.BlockSpec(x.shape, lambda t: (0, 0))
+    columns = lambda x: pl.BlockSpec((x.shape[0], tile), lambda t: (0, t))
+    extra = list(tables) if tables else []
     return pl.pallas_call(
         kernel,
-        out_shape=jax.ShapeDtypeStruct((rows, width), bf16),
+        grid=(width // tile,),
+        in_specs=[fixed(x) for x in parts]
+        + [columns(x) for x in weights]
+        + [fixed(x) for x in extra],
+        out_specs=pl.BlockSpec((rows, tile), lambda t: (0, t)),
+        out_shape=jax.ShapeDtypeStruct((rows, width), bf16 if tables else f32),
         compiler_params=kernel_params(),
         cost_estimate=pl.CostEstimate(
-            flops=2 * rows * width * hidden.shape[1],
-            bytes_accessed=2 * hidden.size + 2 * w_kv.size,
+            flops=2 * rows * width * sum(x.shape[0] for x in weights),
+            bytes_accessed=2 * sum(x.size for x in parts + weights),
             transcendentals=0,
         ),
-    )(hidden, w_kv, *tables)
+    )(*parts, *weights, *extra)
 
 
 def turn_kv_back(first, second, tables):
@@ -154,10 +172,8 @@
         q_pre,
         kv_all,
         *tables,
-        query_marks[0][:, None],
-        query_marks[1][:, None],
-        key_marks[0][None, :],
-        key_marks[1][None, :],
+        *query_marks,
+        *key_marks,
     )
 
 
@@ -247,6 +263,134 @@
     )
 
 
+gelu_scale = (2.0 / math.pi) ** 0.5
+gelu_cube = 0.044715
+
+
+def weight_block(weight, layer):
+    return pl.BlockSpec((None, None) + weight.shape[2:], lambda t: (layer, 0, 0, 0))
+
+
+def expert_forward(layer, part, arrived, router, chosen, own, weights, into=None):
+    rows, width = arrived.shape
+    hidden = weights[0].shape[3]
+    tile = rows // 4
+    kept = () if into is None else tuple(into)
+
+    def kernel(
+        x_ref, router_ref, chosen_ref, own_ref, wg_ref, wu_ref, wd_ref, *others
+    ):
+        out_ref, pre_ref, up_ref, gated_ref, gate_ref = others[len(kept) :]
+        x = x_ref[...]
+        logits = mm_nt(x, router_ref[...])
+        among = chosen_ref[...] > 0.5
+        weight = jnp.exp(
+            jnp.where(among, logits, masked_score)
+            - jnp.max(jnp.where(among, logits, masked_score), axis=1, keepdims=True)
+        )
+        weight = jnp.where(among, weight, 0.0)
+        total = jnp.sum(weight, axis=1, keepdims=True)
+        gate = jnp.sum(weight * own_ref[...], axis=1, keepdims=True)
+        gate = gate / jnp.where(total > 0.0, total, 1.0)
+        gate_ref[...] = gate
+        for at in range(0, hidden, 256):
+            part = slice(at, at + 256)
+            gate_pre = mm(x, wg_ref[:, part])
+            up_pre = mm(x, wu_ref[:, part])
+            turn = jnp.tanh(gelu_scale * gate_pre * (1.0 + gelu_cube * gate_pre * gate_pre))
+            active = 0.5 * gate_pre * (1.0 + turn) * up_pre
+            gated_ref[:, part] = (gate * active).astype(bf16)
+            pre_ref[:, part] = gate_pre
+            up_ref[:, part] = up_pre
+        out_ref[...] = mm(gated_ref[...], wd_ref[...]).astype(bf16)
+
+    by_row = lambda columns: pl.BlockSpec((tile, columns), lambda t: (2 * part + t, 0))
+    fixed = lambda x: pl.BlockSpec(x.shape, lambda t: (0, 0))
+    produced, *results = pl.pallas_call(
+        kernel,
+        grid=(2,),
+        in_specs=[by_row(width), fixed(router), by_row(chosen.shape[1]), fixed(own)]
+        + [weight_block(w, layer) for w in weights]
+        + [pl.BlockSpec(memory_space=pl.ANY)] * len(kept),
+        out_specs=[pl.BlockSpec((tile, width), lambda t: (t, 0))]
+        + [by_row(hidden), by_row(hidden), by_row(hidden), by_row(1)],
+        out_shape=[
+            jax.ShapeDtypeStruct((rows // 2, width), bf16),
+            jax.ShapeDtypeStruct((rows, hidden), f32),
+            jax.ShapeDtypeStruct((rows, hidden), f32),
+            jax.ShapeDtypeStruct((rows, hidden), bf16),
+            jax.ShapeDtypeStruct((rows, 1), f32),
+        ],
+        input_output_aliases={7 + k: 1 + k for k in range(len(kept))},
+        compiler_params=kernel_params(),
+        cost_estimate=pl.CostEstimate(
+            flops=3 * rows * width * hidden,
+            bytes_accessed=2 * rows * width + 6 * rows * hidden + 6 * width * hidden,
+            transcendentals=rows * hidden // 2,
+        ),
+    )(arrived, router, chosen, own, *weights, *kept)
+    return produced, results
+
+
+def expert_backward(layer, part, d_arrived, gate_pre, up_pre, gate, marks, weights, into=None):
+    rows, width = d_arrived.shape
+    hidden = weights[0].shape[3]
+    tile = rows // 4
+    kept = () if into is None else (into,)
+
+    def kernel(
+        d_ref, pre_ref, up_ref, gate_ref, marks_ref, wg_ref, wu_ref, wd_ref, *others
+    ):
+        rows_ref, both_ref = others[len(kept) :]
+        d_rows, gate = d_ref[...], gate_ref[...]
+        d_gate_sum = jnp.zeros((tile, 1), f32)
+        for at in range(0, hidden, 256):
+            part = slice(at, at + 256)
+            du = mm_nt(d_rows, wd_ref[part, :])
+            v, up_value = pre_ref[:, part], up_ref[:, part]
+            square = v * v
+            turn = jnp.tanh(gelu_scale * v * (1.0 + gelu_cube * square))
+            half = 0.5 * (1.0 + turn)
+            unit = v * half
+            slope = half + 0.5 * v * (1.0 - turn * turn) * (
+                gelu_scale * (1.0 + 3.0 * gelu_cube * square)
+            )
+            d_gate_sum += jnp.sum(du * unit * up_value, axis=1, keepdims=True)
+            d_active = (gate * du).astype(bf16).astype(f32)
+            both_ref[:, part] = (d_active * slope * up_value).astype(bf16)
+            both_ref[:, hidden + at : hidden + at + 256] = (d_active * unit).astype(bf16)
+        coarse = d_gate_sum.astype(bf16).astype(f32)
+        beside = coarse * marks_ref[0:1, :] + (d_gate_sum - coarse) * marks_ref[1:2, :]
+        rows_ref[:, width:] = beside.astype(bf16)
+        d_pre = mm_nt(both_ref[:, :hidden], wg_ref[...]) + mm_nt(both_ref[:, hidden:], wu_ref[...])
+        rows_ref[:, :width] = d_pre.astype(bf16)
+
+    by_row = lambda columns: pl.BlockSpec((tile, columns), lambda t: (2 * part + t, 0))
+    return pl.pallas_call(
+        kernel,
+        grid=(2,),
+        in_specs=[by_row(width), by_row(hidden), by_row(hidden), by_row(1)]
+        + [pl.BlockSpec(marks.shape, lambda t: (0, 0))]
+        + [weight_block(w, layer) for w in weights]
+        + [pl.BlockSpec(memory_space=pl.ANY)] * len(kept),
+        out_specs=[
+            pl.BlockSpec((tile, width + marks.shape[1]), lambda t: (t, 0)),
+            by_row(2 * hidden),
+        ],
+        out_shape=[
+            jax.ShapeDtypeStruct((rows // 2, width + marks.shape[1]), bf16),
+            jax.ShapeDtypeStruct((rows, 2 * hidden), bf16),
+        ],
+        input_output_aliases={8 + k: 1 + k for k in range(len(kept))},
+        compiler_params=kernel_params(),
+        cost_estimate=pl.CostEstimate(
+            flops=3 * rows * width * hidden,
+            bytes_accessed=2 * rows * width + 6 * rows * hidden + 6 * width * hidden,
+            transcendentals=rows * hidden // 2,
+        ),
+    )(d_arrived, gate_pre, up_pre, gate, marks, *weights, *kept)
+
+
 def documents(lengths_row, position):
     doc_ends = jnp.cumsum(lengths_row)
     doc_starts = doc_ends - lengths_row
@@ -398,12 +542,15 @@
     return units
 
 
-def ordered_columns(values, units):
+def column_parts(values, units):
     width = values.shape[1] // 8
-    return jnp.concatenate(
-        [lax.dynamic_slice(values, (0, unit * width), (values.shape[0], width)) for unit in units],
-        axis=1,
-    )
+    rows = values.shape[0]
+    parts = [
+        lax.dynamic_slice(values, (0, units[at] * width), (rows, 2 * width)) for at in (0, 2)
+    ]
+    return parts + [
+        lax.dynamic_slice(values, (0, units[at] * width), (rows, width)) for at in range(4, 8)
+    ]
 
 
 def ordered_small(blocks):
@@ -440,6 +587,39 @@
 
 def own_columns(values):
     return jnp.concatenate(exchange_blocks(split_columns(values)), axis=0)
+
+
+class ShardSummed:
+    def __init__(self, columns, right):
+        self.columns, self.right = columns, right
+        self.width = columns[0].shape[1]
+        self.moving = ()
+
+    @property
+    def value(self):
+        return self.moving, self.columns, self.right
+
+    @value.setter
+    def value(self, value):
+        self.moving, self.columns, self.right = value
+
+    def product(self, k):
+        return mm_tn(self.columns[k], self.right)
+
+    def core(self):
+        sent = [self.product(k).astype(bf16) for k in (3, 1)]
+        self.moving = core_swap(jnp.concatenate(sent, axis=0))
+
+    def row(self):
+        self.came = self.moving
+        across = self.product(2) + self.came[: self.width].astype(f32)
+        self.moving = row_swap(across.astype(bf16))
+
+    def keep(self):
+        self.kept = self.product(0) + self.came[self.width :].astype(f32)
+
+    def total(self):
+        return self.kept + self.moving.astype(f32)
 
 
 class Summed:
@@ -478,19 +658,37 @@
             self.lines.turn(self.kept, -steps) for steps in range(1, self.lines.count)
         )
 
-    def join(self):
-        lines = self.lines
-        blocks = jnp.zeros((lines.count,) + self.kept.shape, bf16)
+    def assembled(self):
+        blocks = jnp.zeros((self.lines.count,) + self.kept.shape, bf16)
         for steps, block in enumerate((self.kept,) + self.value):
             blocks = lax.dynamic_update_slice(blocks, block[None], (self.place(steps), 0, 0))
-        self.kept = blocks.reshape(-1, self.kept.shape[1])
-        self.value = lines.swap(self.kept)
-
-    def whole(self):
+        return blocks.reshape(-1, self.kept.shape[1])
+
+
+def merged(sums):
+    one = Summed(sums[0].lines, None)
+    one.kept = jnp.concatenate([s.kept for s in sums], axis=1)
+    one.value = jnp.concatenate([s.value for s in sums], axis=1)
+    return one
+
+
+class Joined:
+    def __init__(self, lines, kept):
+        self.lines, self.kept = lines, kept
+        self.value = lines.swap(kept)
+
+    def whole(self, take):
         low = self.lines.side == 0
-        first = jnp.where(low, self.kept, self.value)
-        second = jnp.where(low, self.value, self.kept)
-        return jnp.concatenate([first, second], axis=0).astype(f32)
+        kept, value = take(self.kept), take(self.value)
+        pair = (jnp.where(low, kept, value), jnp.where(low, value, kept))
+        return jnp.concatenate(pair, axis=0).astype(f32)
+
+    def put(self, whole, layer, take=lambda x: x):
+        half = self.kept.shape[0]
+        for rows, side in ((self.kept, self.lines.side), (self.value, 1 - self.lines.side)):
+            block = take(rows).astype(f32)[None]
+            whole = lax.dynamic_update_slice(whole, block, (layer, side * half, 0))
+        return whole
 
 
 class Sent:
@@ -499,15 +697,15 @@
         self.held = [(values, values)]
         rows = 2 * routing.lines.count * routing.capacity
         self.buffer = jnp.zeros((rows, values.shape[1]), values.dtype)
-        self.far = None
+        self.fars, self.ready = {}, {}
 
     @property
     def value(self):
-        return self.held[-1], self.buffer, self.far
+        return self.held[-1], self.buffer, self.fars, self.ready
 
     @value.setter
     def value(self, value):
-        self.held[-1], self.buffer, self.far = value
+        self.held[-1], self.buffer, self.fars, self.ready = value
 
     def step(self):
         self.held = self.routing.lines.step_gather(self.held)
@@ -516,48 +714,81 @@
         at = block * self.routing.capacity
         self.buffer = lax.dynamic_update_slice(self.buffer, rows, (at, 0))
 
-    def pack(self, j):
-        routing = self.routing
-        block = routing.lines.slot(self.held, j)
-        arrived = self.far
-        self.far = routing.lines.swap(mm(routing.mate_hot[j], block).astype(bf16))
-        if arrived is not None:
-            self.put(arrived, routing.lines.count + j - 1)
-        self.put(mm(routing.own_hot[j], block).astype(bf16), j)
+    def prepare(self, j):
+        block = self.routing.lines.slot(self.held, j)
+        self.ready[j] = mm(self.routing.mate_hot[j], block).astype(bf16)
+
+    def send(self, j):
+        if j not in self.ready:
+            self.prepare(j)
+        self.fars[j] = self.routing.lines.swap(self.ready.pop(j))
+
+    def place(self, j):
+        block = self.routing.lines.slot(self.held, j)
+        self.put(mm(self.routing.own_hot[j], block).astype(bf16), j)
+
+    def take(self, j):
+        self.put(self.fars.pop(j), self.routing.lines.count + j)
+
+    def round(self, j):
+        if j < self.routing.lines.count - 1:
+            self.step()
+        self.send(j)
+        if j > 0:
+            self.take(j - 1)
+        self.place(j)
 
     def total(self):
-        if self.far is not None:
-            self.put(self.far, 2 * self.routing.lines.count - 1)
-            self.far = None
+        for j in list(self.fars):
+            self.take(j)
         return self.buffer
 
 
 class Returned:
-    def __init__(self, routing, rows):
+    def __init__(self, routing, far):
         self.routing = routing
-        count, capacity = routing.lines.count, routing.capacity
-        self.blocks = [rows[i * capacity : (i + 1) * capacity] for i in range(2 * count)]
+        count = routing.lines.count
+        self.blocks = [None] * count + self.cut(far)
         self.parts = [None] * count
-        self.round = 0
-        self.value = (None, None)
+        self.steps = 0
+        self.came, self.arrived = {}, None
+
+    @property
+    def value(self):
+        return self.came, self.arrived, self.blocks
+
+    @value.setter
+    def value(self, value):
+        self.came, self.arrived, self.blocks = value
+
+    def cut(self, rows):
+        capacity = self.routing.capacity
+        return [rows[at : at + capacity] for at in range(0, rows.shape[0], capacity)]
+
+    def near(self, rows):
+        self.blocks = self.cut(rows) + self.blocks[self.routing.lines.count :]
+
+    def swap(self, j):
+        lines = self.routing.lines
+        self.came[j] = lines.swap(self.blocks[lines.count + j])
 
     def spread(self, j):
         own, far = self.routing.own_hot[j], self.routing.mate_hot[j]
-        self.parts[j] = mm_tn(own, self.blocks[j]) + mm_tn(far, self.value[0])
-
-    def advance(self):
+        self.parts[j] = mm_tn(own, self.blocks[j]) + mm_tn(far, self.came.pop(j))
+
+    def step(self):
         lines = self.routing.lines
-        j = lines.count - 1 - self.round
-        arrived = self.value[1]
-        if self.round > 0:
-            self.spread(j + 1)
-            arrived = lines.step_reduce(self.round - 1, self.parts, arrived)
-        self.value = (lines.swap(self.blocks[lines.count + j]), arrived)
-        self.round += 1
+        self.spread(lines.count - 1 - self.steps)
+        self.arrived = lines.step_reduce(self.steps, self.parts, self.arrived)
+        self.steps += 1
+
+    def advance(self, stage):
+        self.step()
+        self.swap(self.routing.lines.count - 1 - stage)
 
     def total(self):
         self.spread(0)
-        from_even, from_odd = self.routing.lines.inward(self.value[1])
+        from_even, from_odd = self.routing.lines.inward(self.arrived)
         return self.parts[0] + from_even + from_odd
 
 
@@ -617,7 +848,6 @@
             parts += [key_matrix[i, :, at : at + HEAD_SIZE], value_matrix[i, :, at : at + HEAD_SIZE]]
         return jnp.concatenate(parts, axis=1)
 
-    kv_shards = [paired(i) for i in range(layer_count)]
     small = jnp.concatenate(
         [router_weight.transpose(0, 2, 1), attn_gain[:, None, :], ffn_gain[:, None, :]], axis=1
     )
@@ -626,25 +856,30 @@
     late = Sent(routing, cotangent)
     units = column_units(lines)
 
-    def side_half(shard):
-        half = shard.shape[0] // 2
-        return lax.dynamic_slice(shard, (lines.side * half, 0), (half, shard.shape[1]))
-
-    def joined(shard, beside, across, crossed):
-        far = jnp.concatenate([across, crossed], axis=0)
-        return jnp.concatenate([shard, beside, far, core_swap(far)], axis=0)
-
+    def side_half(shards, layer):
+        half = shards.shape[1] // 2
+        return lax.dynamic_slice(
+            shards, (layer, lines.side * half, 0), (1, half, shards.shape[2])
+        )[0]
+
+    kv_first = paired(0)
     small_across, small_beside = row_swap(small), core_swap(small)
-    kv_across, kv_beside = row_swap(side_half(kv_shards[0])), core_swap(kv_shards[0])
+    kv_across, kv_beside = row_swap(side_half(kv_first[None], 0)), core_swap(kv_first)
+    query_half = side_half(q_weight, 0)
+    small_across, small_beside, kv_across, kv_beside, query_half, q_gated = sync(
+        small_across, small_beside, kv_across, kv_beside, query_half, q_weight
+    )
+    slot_code = jnp.arange(1, capacity + 1, dtype=jnp.int32).astype(f32)[:, None]
+    query_rows = tuple(mark[:, None] for mark in query_marks)
+    key_rows = tuple(mark[None, :] for mark in key_marks)
+
+    query_across = row_swap(query_half)
+    query_own = q_gated[0]
+    query_beside = core_swap(query_own)
+    kv_crossed = lines.swap(kv_across)
+    kv_across_beside = core_swap(kv_across)
+    late.step()
     own_table = slot_table(routes, slot_order[0], experts, capacity)
-    first_query = q_weight[0]
-    small_across, small_beside, kv_across, kv_beside, own_table, first_query = sync(
-        small_across, small_beside, kv_across, kv_beside, own_table, first_query
-    )
-
-    query_across, query_beside = row_swap(side_half(first_query)), core_swap(first_query)
-    kv_crossed = lines.swap(kv_across)
-    late.step()
     small_diagonal = core_swap(small_across)
     small = ordered_small({0: small, 1: small_beside, 2: small_across, 3: small_diagonal})
     routers = [small[i, :experts] for i in range(layer_count)]
@@ -653,89 +888,52 @@
     stream = tokens.astype(f32)
     normed, attn_inverse = norm_forward(stream, attn_gains[0])
     hidden = normed.astype(bf16)
-    matched = ordered_columns(hidden, units)
-    first_out = out_weight[0]
-    query_across, query_beside, kv_crossed, matched, own_table, first_out = settle(
-        [late], query_across, query_beside, kv_crossed, matched, own_table, first_out
+    matched = column_parts(hidden, units)
+    query_across, query_beside, kv_crossed, kv_across_beside, matched, own_table, later = settle(
+        [late], query_across, query_beside, kv_crossed, kv_across_beside, matched, own_table,
+        (out_weight, key_matrix, value_matrix),
     )
+    every = lambda part: lax.all_gather(part, "shard", axis=0, tiled=True)
+    gathered = [(None, None, every(later[0][0]))]
+    tables, query_rows, key_rows, slot_code = sync(tables, query_rows, key_rows, slot_code)
 
     query_crossed = lines.swap(query_across)
-    first_kv = joined(kv_shards[0], kv_beside, kv_across, kv_crossed)
-    first_pair = shard_rows_of(project_kv(matched, first_kv, tables))
+    query_across_beside = core_swap(query_across)
+    kv_pieces = [kv_first, kv_beside, kv_across, kv_crossed, kv_across_beside]
+    kv_pieces.append(core_swap(kv_crossed))
+    first_pair = shard_rows_of(project(matched, kv_pieces, tables))
     held_tables = [(own_table, own_table)]
     for _ in range(lines.count - 1):
         held_tables = lines.step_gather(held_tables)
+    query_crossed, query_across_beside, first_pair, q_gated, later = settle(
+        [late], query_crossed, query_across_beside, first_pair, q_gated, later
+    )
     near_tables = jnp.stack([lines.slot(held_tables, j) for j in range(lines.count)], axis=0)
-    later = [q_weight[0], kv_shards[0]]
-    for i in range(1, layer_count):
-        later += [kv_shards[i], q_weight[i], out_weight[i]]
-    query_crossed, first_pair, near_tables, later = sync(
-        query_crossed, first_pair, near_tables, later
-    )
-    first_query = joined(first_query, query_beside, query_across, query_crossed)
-
-    whole = [lax.all_gather(part, "shard", axis=0, tiled=True) for part in [first_out] + later]
-    gathered = [(whole[1], whole[2], whole[0])]
-    for i in range(1, layer_count):
-        gathered.append((whole[3 * i + 1], whole[3 * i], whole[3 * i + 2]))
-
-    chosen_here = own_table.T != 0.0
-    far_tables = lines.swap(near_tables)
-    slot_code = jnp.arange(1, capacity + 1, dtype=jnp.int32).astype(f32)[:, None]
-
-    def hot_rows(codes, expert):
-        code = lax.dynamic_index_in_dim(codes, expert, 1, keepdims=True)
-        return (code == slot_code).astype(bf16)
-
-    routing.own_hot = hot_rows(near_tables, lines.index)
-    routing.mate_hot = hot_rows(near_tables, lines.index ^ 1)
-    all_hot = jnp.concatenate([routing.own_hot, hot_rows(far_tables, lines.index)], axis=0)
-    all_tables = jnp.concatenate([near_tables, far_tables], axis=0)
-    row_chosen = jnp.einsum(
-        "sct,set->sce", all_hot, (all_tables != 0.0).astype(bf16), preferred_element_type=f32
-    ).reshape(2 * lines.count * capacity, experts)
-    row_chosen = row_chosen > 0.5
-    sources = [
-        lines.source(slot) * 2 + (lines.side ^ column)
-        for column in range(2)
-        for slot in range(lines.count)
-    ]
-
-    def gate_grads_back(row_values):
-        blocks = row_values.reshape(2 * lines.count, capacity)
-        spread = jnp.zeros((experts, token_rows), f32)
-        rows = jnp.sum(all_hot.astype(f32) * blocks[:, :, None], axis=1)
-        for i, source in enumerate(sources):
-            spread = lax.dynamic_update_slice(spread, rows[i : i + 1], (source, 0))
-        return lax.all_to_all(spread, "expert", split_axis=0, concat_axis=0, tiled=True).T
-
-    def expert_forward(i, arrived):
-        gates = chosen_softmax(mm_nt(arrived, routers[i]), row_chosen)
-        own_gate = lax.dynamic_slice(gates, (0, lines.index), (gates.shape[0], 1))
-        gate_pre = mm(arrived, gate_weight[i, 0])
-        up_pre = mm(arrived, up_weight[i, 0])
-        active = jax.nn.gelu(gate_pre, approximate=True) * up_pre
-        gated = (own_gate * active).astype(bf16)
-        produced = mm(gated, down_weight[i, 0]).astype(bf16)
-        return produced, dict(gate=own_gate, gate_pre=gate_pre, up_pre=up_pre, gated=gated)
-
-    def expert_backward(i, kept, d_arrived):
-        du = mm_nt(d_arrived, down_weight[i, 0])
-        unit, pull = jax.vjp(
-            lambda a, b: jax.nn.gelu(a, approximate=True) * b, kept["gate_pre"], kept["up_pre"]
-        )
-        d_gate_rows = jnp.sum(du * unit, axis=1)
-        d_active = (kept["gate"] * du).astype(bf16).astype(f32)
-        d_gate_pre, d_up_pre = pull(d_active)
-        d_both = jnp.concatenate([d_gate_pre.astype(bf16), d_up_pre.astype(bf16)], axis=1)
-        return d_gate_rows, d_both
-
-    def expert_rows(i, d_both):
-        d_rows = mm_nt(d_both[:, :hidden_units], gate_weight[i, 0])
-        return (d_rows + mm_nt(d_both[:, hidden_units:], up_weight[i, 0])).astype(bf16)
-
-    def shard_sum(part):
-        return lax.psum_scatter(part, "shard", scatter_dimension=0, tiled=True)
+    query_pieces = [query_own, query_beside, query_across, query_crossed, query_across_beside]
+    query_pieces.append(core_swap(query_crossed))
+
+    def prepare_routing(near_tables, own_table):
+        far_tables = lines.swap(near_tables)
+
+        def hot_rows(codes, expert):
+            code = lax.dynamic_index_in_dim(codes, expert, 1, keepdims=True)
+            return (code == slot_code).astype(bf16)
+
+        routing.own_hot = hot_rows(near_tables, lines.index)
+        routing.mate_hot = hot_rows(near_tables, lines.index ^ 1)
+        all_hot = jnp.concatenate([routing.own_hot, hot_rows(far_tables, lines.index)], axis=0)
+        all_tables = jnp.concatenate([near_tables, far_tables], axis=0)
+        row_chosen = jnp.einsum(
+            "sct,set->sce", all_hot, (all_tables != 0.0).astype(bf16), preferred_element_type=f32
+        ).reshape(2 * lines.count * capacity, experts)
+        return own_table.T != 0.0, row_chosen
+
+    own_expert = (jnp.arange(experts) == lines.index).astype(f32)[None, :]
+    assert experts <= 64
+    gate_marks = jnp.arange(128)[None, :] == lines.index + 64 * jnp.arange(2)[:, None]
+    gate_marks = gate_marks.astype(f32)
+
+    weights = (gate_weight, up_weight, down_weight)
 
     def small_sum(part):
         own = sum(exchange_blocks(split_columns(part)))
@@ -747,42 +945,71 @@
         w_query, w_kv, w_out = gathered[i]
         if i == 0:
             late.step()
-            late.pack(0)
             kv_pair = first_pair
-            q_pre = mm(matched, first_query)
+            q_pre = project(matched, query_pieces)
         else:
             if i == last:
-                late.pack(2)
+                late.send(2)
             normed, attn_inverse = norm_forward(stream, attn_gains[i])
             hidden = normed.astype(bf16)
-            kv_pair = shard_rows_of(project_kv(hidden, w_kv, tables))
+            kv_pair = shard_rows_of(project([hidden], [w_kv], tables))
             q_pre = mm(hidden, w_query)
             kv_pair, q_pre = settle([late], kv_pair, q_pre)
             if i == last:
-                late.pack(3)
+                late.send(3)
+                for k in range(4, lines.count):
+                    late.step()
+                    late.send(k)
         kv_all = shard_rows_all(kv_pair)
-        query, mixed = attend(q_pre, kv_all, tables, query_marks, key_marks)
+        query, mixed = attend(q_pre, kv_all, tables, query_rows, key_rows)
         stream_mid = stream + mm(mixed, w_out)
         normed_ffn, ffn_inverse = norm_forward(stream_mid, ffn_gains[i])
         routed = normed_ffn.astype(bf16)
-        (routed,) = settle([late], routed)
+        if i == last:
+            (routed, gathered[0]) = settle([late], routed, gathered[0])
+        else:
+            routed, q_gated, later, near_tables = settle(
+                [late], routed, q_gated, later, near_tables
+            )
+            chosen_here, row_chosen = prepare_routing(near_tables, own_table)
+        if i == 0:
+
+            def paired_of(k):
+                parts = []
+                for at in range(0, kv_width, HEAD_SIZE):
+                    parts += [later[m][k, :, at : at + HEAD_SIZE] for m in (1, 2)]
+                return jnp.concatenate(parts, axis=1)
+
+            for k in range(1, layer_count):
+                gathered.append((every(q_gated[k]), every(paired_of(k)), every(later[0][k])))
+            gathered[0] = (every(q_gated[0]), every(paired_of(0)), w_out)
         gates = chosen_softmax(mm_nt(routed, routers[i]), chosen_here)
         sent = Sent(routing, routed)
         for j in range(lines.count):
-            if j < lines.count - 1:
-                sent.step()
-            sent.pack(j)
-            if i == last and j == 0:
-                late.total()
+            sent.round(j)
+            if i == 0 and j < 2:
+                late.prepare(j)
+            if i == last:
+                late.place(j)
+                late.take(j)
             hidden, mixed = settle([sent, late], hidden, mixed)
         columns = [own_columns(hidden), own_columns(mixed)]
         arrived = sent.total()
         if i == 0:
             (arrived,) = settle([late], arrived)
+        shared = (arrived, routers[i], row_chosen, own_expert, weights)
+        produced, kept = expert_forward(i, 1, *shared)
+        if i == 0:
             late.step()
-            late.pack(1)
-        produced, kept = expert_forward(i, arrived)
-        produced, kept = settle([late], produced, kept)
+            late.send(0)
+        produced, kept = sync(produced, kept)
+        back = Returned(routing, produced)
+        back.swap(lines.count - 1)
+        produced, kept = expert_forward(i, 0, *shared, into=kept)
+        if i == 0:
+            late.send(1)
+        produced, kept = settle([late, back], produced, kept)
+        back.near(produced)
         stored.append(
             dict(
                 stream=stream,
@@ -799,81 +1026,127 @@
                 kept=kept,
             )
         )
-        back = Returned(routing, produced)
         if i < last:
-            for _ in range(lines.count):
-                back.advance()
-                settle([back])
+            for j in range(1, lines.count):
+                back.advance(j)
+                if i == last - 1 and j in (1, 2):
+                    late.prepare(j + 1)
+                settle([back, late])
             stream = stream_mid + back.total()
 
+    own_width = model_width // shard_count
+    results = dict(
+        query=jnp.full((layer_count, own_width, model_width), 0.0, f32),
+        out=jnp.full((layer_count, own_width, model_width), 1.0, f32),
+        key=jnp.full((layer_count, own_width, kv_width), 0.0, f32),
+        value=jnp.full((layer_count, own_width, kv_width), 1.0, f32),
+        gate=jnp.full((layer_count, own_width, hidden_units), 0.0, f32),
+        up=jnp.full((layer_count, own_width, hidden_units), 1.0, f32),
+        down=jnp.full((layer_count, hidden_units // shard_count, model_width), 0.0, f32),
+    )
+
+    small_results = [None] * layer_count
+
+    def put_experts(layer, both, down):
+        for name, block in (
+            ("gate", both[:, :hidden_units]),
+            ("up", both[:, hidden_units:]),
+            ("down", down),
+        ):
+            results[name] = lax.dynamic_update_slice(
+                results[name], block.astype(f32)[None], (layer, 0, 0)
+            )
+
+    def put_kv(layer, joined, take):
+        heads = lambda first: lambda x: jnp.concatenate(
+            [take(x)[:, at : at + HEAD_SIZE] for at in range(first, 2 * kv_width, 2 * HEAD_SIZE)],
+            axis=1,
+        )
+        results["key"] = joined.put(results["key"], layer, heads(0))
+        results["value"] = joined.put(results["value"], layer, heads(HEAD_SIZE))
+        rest = lambda x: take(x)[:, 2 * kv_width :]
+        small_results[layer] = joined.whole(rest)
+
     output_back = back
-    output_back.advance()
+    top = lines.count - 1
     d_arrived = late.total()
     upstream = cotangent.astype(f32)
-    grads = [None] * layer_count
     for i in reversed(range(layer_count)):
         w_query, w_kv, w_out = gathered[i]
         saved = stored[i]
         if i < last:
             sent = Sent(routing, upstream.astype(bf16))
-            above = stored[i + 1]
-            d_branch, d_query, d_kv_low = waiting
+            columns = stored[i + 1]["hidden_columns"]
+            out_above, d_query, d_kv_low, small_grad = waiting
+            small_part = small_grad
             for j in range(lines.count):
-                if j < lines.count - 1:
-                    sent.step()
-                sent.pack(j)
+                sent.round(j)
+                moving = []
                 if j == 0:
-                    d_branch = shard_rows_of(d_branch)
+                    d_kv_low = shard_rows_of(d_kv_low)
+                if j == 1:
+                    d_query = shard_rows_all(d_query)
+                    d_kv_low = shard_rows_all(d_kv_low)
                     small_part = small_sum(small_grad)
+                if j == 2:
+                    query_above = Summed(lines, mm_tn(columns, d_query))
+                    query_above.side()
+                if j == 3:
+                    kv_above = mm_tn(columns, d_kv_low)
+                    kv_above = Summed(lines, jnp.concatenate([kv_above, small_part], axis=1))
+                    kv_above.side()
+                    moving = [query_above, kv_above]
+                d_query, d_kv_low, small_part = settle(
+                    [sent] + moving, d_query, d_kv_low, small_part
+                )
                 if j == 1:
-                    d_query = shard_rows_of(d_query)
-                    d_branch = shard_rows_all(d_branch)
-                if j == 2:
-                    out_part = mm_tn(above["mixed_columns"], d_branch).astype(bf16)
-                    d_kv_low = shard_rows_of(d_kv_low)
-                    d_query = shard_rows_all(d_query)
-                if j == 3:
-                    d_kv_low = shard_rows_all(d_kv_low)
-                    q_part = mm_tn(above["hidden_columns"], d_query).astype(bf16)
-                d_branch, d_query, d_kv_low = settle([sent], d_branch, d_query, d_kv_low)
-            kv_part = mm_tn(above["hidden_columns"], d_kv_low).astype(bf16)
-            part = jnp.concatenate([q_part, out_part, kv_part, small_part.astype(bf16)], axis=1)
-            last_sum = Summed(lines, part)
-            last_sum.side()
-            last_experts = expert_grads
+                    results, d_query = sync(results, d_query)
+                if j == lines.count - 1:
+                    d_query, both_grad, down_grad = sync(d_query, both_grad, down_grad)
+            put_experts(last, both_grad, down_grad)
             d_arrived = sent.total()
-        d_gate_rows, d_both = expert_backward(i, saved["kept"], d_arrived)
+            above = merged([out_above, kv_above, query_above])
+            above.scatter()
+        gate_pre, up_pre, gated, own_gate = saved["kept"]
+        shared = (d_arrived, gate_pre, up_pre, own_gate, gate_marks, weights)
         if i == last:
-            d_gate_rows, d_both = settle([output_back], d_gate_rows, d_both)
-            output_back.advance()
-            d_rows = expert_rows(i, d_both)
-            d_rows, d_gate_rows, d_both = settle([output_back], d_rows, d_gate_rows, d_both)
-        else:
-            d_rows = expert_rows(i, d_both)
-            d_rows, d_gate_rows, d_both = settle([last_sum], d_rows, d_gate_rows, d_both)
-        d_gates = gate_grads_back(d_gate_rows)
+            output_back.step()
+        d_rows, d_both = expert_backward(i, 1, *shared)
+        d_rows, d_both = sync(d_rows, d_both)
         back = Returned(routing, d_rows)
-        arrived, gated = saved["arrived"], saved["kept"]["gated"]
-        for j in range(lines.count):
-            back.advance()
-            extra = ()
-            if j == 0:
-                extra = mm_tn(arrived, d_both).astype(bf16)
+        back.swap(top)
+        d_rows, d_both = expert_backward(i, 0, *shared, into=d_both)
+        moving = [back, output_back if i == last else above]
+        d_rows, d_both = settle(moving, d_rows, d_both)
+        back.near(d_rows)
+        both = ShardSummed(split_columns(saved["arrived"]), d_both)
+        down = ShardSummed(split_columns(gated), d_arrived)
+        for j in range(1, lines.count):
+            back.advance(j)
+            moving = [back, both, down]
             if j == 1:
-                extra = mm_tn(gated, d_arrived).astype(bf16)
-            extra, d_gates, arrived, gated, d_both, d_arrived = settle(
-                [back], extra, d_gates, arrived, gated, d_both, d_arrived
-            )
-            if j == 0:
-                both_grad = shard_sum(extra).astype(f32)
-            if j == 1:
-                down_grad = shard_sum(extra).astype(f32)
-        expert_grads = (both_grad, down_grad)
+                both.core()
+            if j == 2:
+                both.row()
+                down.core()
+                if i == last:
+                    for k in reversed(range(2, top)):
+                        output_back.swap(k)
+                    moving.append(output_back)
+            if j == 3:
+                both.keep()
+                down.row()
+                moving = [back, both] + ([output_back] if i == last else [])
+            settle(moving)
+        down.keep()
+        returned = back.total()
+        d_gates = returned[:, model_width : model_width + experts]
+        d_gates = d_gates + returned[:, model_width + 64 : model_width + 64 + experts]
         gates = saved["gates"]
         d_logits = gates * (d_gates - jnp.sum(gates * d_gates, axis=1, keepdims=True))
         d_logits = d_logits.astype(bf16)
         router_grad = mm_tn(d_logits, saved["routed"])
-        d_routed = back.total() + mm(d_logits, routers[i])
+        d_routed = returned[:, :model_width] + mm(d_logits, routers[i])
         d_stream, ffn_gain_grad = norm_backward(
             saved["stream_mid"], saved["ffn_inverse"], ffn_gains[i], d_routed
         )
@@ -881,32 +1154,42 @@
         d_branch = upstream.astype(bf16)
         d_mixed = mm_nt(d_branch, w_out).astype(bf16)
         if i == last:
-            output_back.advance()
+            while output_back.steps < top - 1:
+                output_back.step()
+            output_back.swap(1)
+            output_back.swap(0)
             moving = [output_back]
-            d_branch_all = ()
         else:
-            last_sum.scatter()
-            moving = [last_sum]
-            d_branch_all = shard_rows_all(shard_rows_of(d_branch))
+            above.spread()
+            moving = []
+        d_branch_crossed = row_swap(d_branch)
         d_query, d_kv = attend_back(
             saved["query"], saved["kv_all"], d_mixed, tables, query_marks, key_marks
         )
-        d_query, d_kv, d_branch_all = settle(moving, d_query, d_kv, d_branch_all)
-        if i == last:
-            output_back.advance()
-            sums = [output_back]
-        else:
-            out_sum = Summed(lines, mm_tn(saved["mixed_columns"], d_branch_all))
-            out_sum.side()
-            last_sum.spread()
-            sums = [out_sum, last_sum]
+        d_query, d_kv, d_branch_crossed = settle(
+            moving + [down], d_query, d_kv, d_branch_crossed
+        )
+        d_branch_pair = jnp.concatenate([d_branch, d_branch_crossed], axis=0)
+        both_grad, down_grad = both.total(), down.total()
         pair_rows = 2 * token_rows
         d_kv_pair = d_kv[:pair_rows].astype(f32) + core_swap(d_kv[pair_rows:]).astype(f32)
+        d_branch_all = shard_rows_all(d_branch_pair)
+        d_kv_pair, d_branch_all, d_query = sync(d_kv_pair, d_branch_all, d_query)
+        d_kv_crossed = row_swap(d_kv_pair[token_rows:].astype(bf16))
         d_hidden = mm_nt(d_query, w_query)
-        d_kv_pair, d_hidden, d_query = sync(d_kv_pair, d_hidden, d_query)
-        d_kv_crossed = row_swap(d_kv_pair[token_rows:].astype(bf16))
-        if i < last:
-            d_query_pair = shard_rows_of(d_query)
+        out_part = mm_tn(saved["mixed_columns"], d_branch_all)
+        d_kv_crossed, d_query, d_hidden, out_part = sync(
+            d_kv_crossed, d_query, d_hidden, out_part
+        )
+        out_sum = Summed(lines, out_part)
+        out_sum.side()
+        moving = [out_sum]
+        if i == last:
+            output_back.step()
+            moving.append(output_back)
+        else:
+            moving.append(above)
+        d_query_pair = shard_rows_of(d_query)
         d_kv_low = turn_kv_back(d_kv_pair[:token_rows], d_kv_crossed, tables)
         d_hidden = d_hidden + mm_nt(d_kv_low, w_kv)
         d_stream, attn_gain_grad = norm_backward(
@@ -916,56 +1199,59 @@
         small_grad = jnp.concatenate(
             [router_grad, attn_gain_grad[None, :], ffn_gain_grad[None, :]], axis=0
         )
+        upstream, d_kv_low, small_grad = settle(moving, upstream, d_kv_low, small_grad)
         if i == last:
-            upstream, d_kv_low, small_grad = settle(sums, upstream, d_kv_low, small_grad)
             output = (saved["stream_mid"] + output_back.total()).astype(bf16)
-            waiting = (d_branch, d_query, d_kv_low)
-            upstream, output, waiting = sync(upstream, output, waiting)
-        else:
-            d_query_pair, d_kv_low, small_grad, upstream = settle(
-                sums, d_query_pair, d_kv_low, small_grad, upstream
-            )
-            out_sum.scatter()
-            d_kv_pair = shard_rows_of(d_kv_low)
-            small_part = small_sum(small_grad)
-            hidden_columns = saved["hidden_columns"]
-            q_sum = Summed(lines, mm_tn(hidden_columns, shard_rows_all(d_query_pair)))
-            q_sum.side()
-            d_kv_pair, small_part = settle([q_sum, out_sum], d_kv_pair, small_part)
-            kv_part = mm_tn(hidden_columns, shard_rows_all(d_kv_pair))
-            kv_sum = Summed(lines, jnp.concatenate([kv_part, small_part], axis=1))
-            for sends in (
-                (q_sum.scatter, kv_sum.side, last_sum.join),
-                (q_sum.spread, kv_sum.scatter, out_sum.spread),
-                (q_sum.join, kv_sum.spread, out_sum.join),
-                (kv_sum.join,),
-            ):
-                for send in sends:
-                    send()
-                settle([q_sum, kv_sum, out_sum, last_sum])
-            grads[i] = (q_sum.whole(), kv_sum.whole(), out_sum.whole()) + expert_grads
-            above = last_sum.whole()
-            width = model_width
-            grads[last] = (above[:, :width], above[:, 2 * width :], above[:, width : 2 * width])
-            grads[last] += last_experts
-    input_grad = upstream.astype(bf16)
-    stacked = [jnp.stack([grads[i][k] for i in range(layer_count)], axis=0) for k in range(5)]
-    q_grad, kv_grad, out_grad, both_grad, down_grad = stacked
-    kv_parts = [kv_grad[:, :, at : at + HEAD_SIZE] for at in range(0, 2 * kv_width, HEAD_SIZE)]
-    small_grad = kv_grad[:, :, 2 * kv_width :]
+            out_above = out_sum
+            waiting = (out_above, d_query_pair, d_kv_low, small_grad)
+
+    hidden_columns = stored[0]["hidden_columns"]
+    out_sum.scatter()
+    d_kv_pair = shard_rows_of(d_kv_low)
+    small_part = small_sum(small_grad)
+    q_sum = Summed(lines, mm_tn(hidden_columns, shard_rows_all(d_query_pair)))
+    q_sum.side()
+    d_kv_pair, small_part = settle([q_sum, out_sum], d_kv_pair, small_part)
+    q_sum.scatter()
+    kv_part = mm_tn(hidden_columns, shard_rows_all(d_kv_pair))
+    kv_sum = Summed(lines, jnp.concatenate([kv_part, small_part], axis=1))
+    kv_sum.side()
+    half_result = above.assembled()
+    split = half_result.shape[1] - model_width
+    above_first = Joined(lines, half_result[:, :split])
+    out_sum.spread()
+    above_second_rows = half_result[:, split:]
+    (above_second_rows,) = settle([q_sum, kv_sum, out_sum], above_second_rows)
+    q_sum.spread()
+    kv_sum.scatter()
+    out_join = Joined(lines, out_sum.assembled())
+    above_second = Joined(lines, above_second_rows)
+    put_experts(0, both_grad, down_grad)
+    (results,) = settle([q_sum, kv_sum, out_join, above_first], results)
+    q_join = Joined(lines, q_sum.assembled())
+    kv_sum.spread()
+    results["out"] = above_first.put(results["out"], last, lambda x: x[:, :model_width])
+    put_kv(last, above_first, lambda x: x[:, model_width:])
+    results["out"] = out_join.put(results["out"], 0)
+    (results,) = settle([q_join, kv_sum, above_second], results)
+    kv_join = Joined(lines, kv_sum.assembled())
+    results["query"] = above_second.put(results["query"], last)
+    results["query"] = q_join.put(results["query"], 0)
+    put_kv(0, kv_join, lambda x: x)
+    small_result = jnp.stack(small_results, axis=0)
     return (
         output,
-        input_grad,
-        q_grad,
-        jnp.concatenate(kv_parts[0::2], axis=2),
-        jnp.concatenate(kv_parts[1::2], axis=2),
-        out_grad,
-        small_grad[:, :, :experts],
-        small_grad[:, :, experts],
-        small_grad[:, :, experts + 1],
-        both_grad[:, None, :, :hidden_units],
-        both_grad[:, None, :, hidden_units:],
-        down_grad[:, None],
+        upstream.astype(bf16),
+        results["query"],
+        results["key"],
+        results["value"],
+        results["out"],
+        small_result[:, :, :experts],
+        small_result[:, :, experts],
+        small_result[:, :, experts + 1],
+        results["gate"][:, None],
+        results["up"][:, None],
+        results["down"][:, None],
     )
 
 

time: 1150 us -> 1040 us (0.904)
  matrix products: 255 us -> 160 us
  Pallas kernels: 66.1 us -> 153 us
  waiting for transfers between devices: 453 us -> 379 us
  other arithmetic: 75.3 us -> 34.5 us
    pallas_call x2 -> x11, Pallas kernels: 1.28 us -> 88.8 us  [the longest x4 45 us: expert_backward(): pl.pallas_call(kernel, grid=(2,), in_specs=[by_row(width), by_row(hidden)...]
    ppermute x13 -> x17, waiting for transfers between devices: 107 us -> 36.6 us  [row_swap(): lax.ppermute(values, 'shard', [(i, i ^ 2) for i in range(lax.axis_size('s...]
    dot_general x16 -> x8, matrix products: 64 us -> 14.2 us  [mm_nt(): lax.dot_general(left, right, (((1,), (1,)), ((), ())), preferred_element_...]
    dot_general x45 -> x38, matrix products: 84.9 us -> 61.2 us  [mm(): return jnp.dot(left, right, preferred_element_type=f32)]
    ppermute x43 -> x46, waiting for transfers between devices: 254 us -> 232 us  [swap(): lax.ppermute(values, 'expert', [(i, i ^ 1) for i in range(self.experts)])]
    dot_general x45 -> x57, matrix products: 105 us -> 84.6 us  [mm_tn(): lax.dot_general(left, right, (((0,), (0,)), ((), ())), preferred_element_...]
    ppermute x24, waiting for transfers between devices: 23.7 us -> 38.5 us  [turn(): return lax.ppermute(values, 'expert', pairs)]
    unnamed x395 -> x481, local copies, waits for them, and re-layouts: 32.3 us -> 45.3 us
  transfers between devices with their start and end apart: 171 -> 178, of which waited for: 67 -> 77; matrix products, arithmetic and copies ran while one was open for 34% -> 22% of each run, Pallas kernels for 6% -> 12%
where the time goes in v3:
time: 1040 us; the launch traced here: 1030 us
  waiting for transfers between devices  379 us (36%)
  starting transfers between devices  178 us (17%)
  matrix products  160 us (15%)
  Pallas kernels  153 us (15%)
  local copies, waits for them, and re-layouts  104 us (10%)
  other arithmetic  34.5 us (3%)
  between operations  19.1 us (2%)
    ppermute x46, waiting for transfers between devices, swap(): lax.ppermute(values, 'expert', [(i, i ^ 1) for i in range(self.experts)])  232 us
    dot_general x57, matrix products, mm_tn(): lax.dot_general(left, right, (((0,), (0,)), ((), ())), preferred_element_...  84.6 us
    ppermute x27, waiting for transfers between devices, even(): lax.ppermute(values, 'expert', [(i, i ^ 2) for i in range(self.experts)])  62.3 us
    dot_general x38, matrix products, mm(): return jnp.dot(left, right, preferred_element_type=f32)  61.2 us
    ppermute x46, starting transfers between devices, swap(): lax.ppermute(values, 'expert', [(i, i ^ 1) for i in range(self.experts)])  52.2 us
    ppermute x27, starting transfers between devices, even(): lax.ppermute(values, 'expert', [(i, i ^ 2) for i in range(self.experts)])  49.3 us
    unnamed x481, local copies, waits for them, and re-layouts  45.3 us
    pallas_call x4, Pallas kernels, expert_backward(): pl.pallas_call(kernel, grid=(2,), in_specs=[by_row(width), by_row(hidden)...  45 us
  transfers between devices with their start and end apart: 178, of which 77 were waited for; matrix products, arithmetic and copies ran while one was open for 22% of the time, Pallas kernels for 12%

profile of v3, /device:TPU:0, one launch (start us, length us, event | category | flops | bytes accessed | tf_op | source)
XLA Modules:
  0.0 1027.7 jit_solution(10023592950719303491)
XLA Ops:
  30.3 4.6 collective-permute-done.8.refs_9_
  49.9 5.2 collective-permute-start.20
  55.1 4.0 collective-permute-done.20
  79.3 3.9 shard_map.518.q_ref
  83.2 10.9 %shard_map.519 = (bf16[256,1536]{1,0:T(8,128)(2,1)S(1)}, bf16[256,1536]{1,0:T(8,128)(2,1)S(1)}) custom-call(f32[256,1536]{1,0:T(8,128)S(1)} %shard_map.518.q_ref, bf16[1024,512]{1,0:T(8,128)(2,1)S(1)} %constant_dynamic-update-slice_fusion.20.kv_ref, f32[256,128]{1,0:T(8,128)S(1)} %get-tuple-element.491.refs_12_.cos_ref.refs_2_, ...), custom_call_target="tpu_custom_call" | custom-call | flops 3221225472 | bytes 3145728 | tf_op jit(solution)/shard_map/pallas_call | solution.py:149
  94.2 4.6 multiply_reduce_fusion.8
  119.3 6.6 collective-permute-done.26
  131.6 12.1 %collective-permute-done.29 = bf16[160,1536]{1,0:T(8,128)(2,1)S(1)} collective-permute-done((bf16[160,1536]{1,0:T(8,128)(2,1)S(1)}, bf16[160,1536]{1,0:T(8,128)(2,1)S(1)}, u32[]{:S(2)}, u32[]{:S(2)}) %collective-permute-start.29) | collective-permute-done | bytes 491552 | tf_op jit(solution)/shard_map/ppermute | solution.py:443
  150.4 9.6 collective-permute-done.31
  160.1 4.2 collective-permute-done.30
  167.0 9.2 collective-permute-done.32
  179.4 9.6 shard_map.520
  198.2 9.6 shard_map.521
  219.9 6.4 collective-permute-done.38
  236.7 9.3 collective-permute-done.40
  252.7 12.1 %collective-permute-done.43 = bf16[160,1536]{1,0:T(8,128)(2,1)S(1)} collective-permute-done((bf16[160,1536]{1,0:T(8,128)(2,1)S(1)}, bf16[160,1536]{1,0:T(8,128)(2,1)S(1)}, u32[]{:S(2)}, u32[]{:S(2)}) %collective-permute-start.43) | collective-permute-done | bytes 491552 | tf_op jit(solution)/shard_map/ppermute | solution.py:443
  264.8 4.7 collective-permute-done.44
  276.9 4.5 collective-permute-done.47
  289.4 11.1 %shard_map.523 = (bf16[256,1536]{1,0:T(8,128)(2,1)S(1)}, bf16[256,1536]{1,0:T(8,128)(2,1)S(1)}) custom-call(f32[256,1536]{1,0:T(8,128)S(1)} %fusion.6.q_ref, bf16[1024,512]{1,0:T(8,128)(2,1)S(1)} %constant_dynamic-update-slice_fusion.22.kv_ref, f32[256,128]{1,0:T(8,128)S(1)} %get-tuple-element.491.refs_12_.cos_ref.refs_2_, f32[256,128]{1,0:T(8,128)S(1)} %copy-done.30, ...), custom_call_target="tpu_custom_call" | custom-call | flops 3221225472 | bytes 3145728 | tf_op jit(solution)/shard_map/pallas_call | solution.py:149
  301.4 4.6 multiply_reduce_fusion.6
  317.3 8.1 collective-permute-done.52
  336.6 8.2 collective-permute-done.55
  354.6 6.7 collective-permute-done.57
  361.3 4.0 collective-permute-done.56
  372.1 5.2 collective-permute-done.58
  379.2 9.6 shard_map.524
  393.5 9.8 shard_map.525
  412.5 10.9 %shard_map.526 = (bf16[640,1664]{1,0:T(8,128)(2,1)S(1)}, bf16[1280,1536]{1,0:T(8,128)(2,1)S(1)}) custom-call(bf16[1280,1536]{1,0:T(8,128)(2,1)S(1)} %constant_dynamic-update-slice_fusion.5.d_ref, f32[1280,768]{1,0:T(8,128)S(1)} %copy-done.15, f32[1280,768]{1,0:T(8,128)} %copy-done.16, f32[1280,1]{1,0:T(8,128)S(1)} %copy-done.26, f32[2,128]{1,0:T(2,128)S(1)} %copy-done.56, ...), custom_call_target="tpu_custom_call" | custom-call | flops 4529848320 | bytes 16908288 | tf_op jit(solution)/shard_map/pallas_call | solution.py:369
  429.3 11.4 %shard_map.527 = (bf16[640,1664]{1,0:T(8,128)(2,1)S(1)}, bf16[1280,1536]{1,0:T(8,128)(2,1)S(1)}) custom-call(bf16[1280,1536]{1,0:T(8,128)(2,1)S(1)} %constant_dynamic-update-slice_fusion.5.d_ref, f32[1280,768]{1,0:T(8,128)S(1)} %copy-done.15, f32[1280,768]{1,0:T(8,128)} %copy-done.16, f32[1280,1]{1,0:T(8,128)S(1)} %copy-done.26, ...), custom_call_target="tpu_custom_call", output_to_operand_aliasing={{1}: (8, {})} | custom-call | flops 4529848320 | bytes 16908288 | tf_op jit(solution)/shard_map/pallas_call | solution.py:369
  458.8 9.8 collective-permute-done.62
  468.6 5.6 collective-permute-done.63
  475.6 4.2 fusion.19
  487.8 4.1 constant_dynamic-slice_fusion.16
  493.6 7.5 collective-permute-done.65
  501.1 5.0 collective-permute-done.66
  518.1 9.4 collective-permute-done.71
  527.5 3.9 collective-permute-done.72
  544.3 20.8 %shard_map.528 = (bf16[256,1536]{1,0:T(8,128)(2,1)S(1)}, bf16[1024,512]{1,0:T(8,128)(2,1)S(1)}) custom-call(bf16[256,1536]{1,0:T(8,128)(2,1)S(1)} %copy-done.68, bf16[1024,512]{1,0:T(8,128)(2,1)S(1)} %copy-done.45, bf16[256,1536]{1,0:T(8,128)(2,1)S(1)} %fusion.35.dm_ref, f32[256,128]{1,0:T(8,128)S(1)} %copy-done.28, f32[256,128]{1,0:T(8,128)S(1)} %copy-done.31, ...), custom_call_target="tpu_custom_call" | custom-call | flops 8053063680 | bytes 3145728 | tf_op jit(solution)/shard_map/pallas_call | solution.py:228
  582.0 5.9 collective-permute-done.82.second_ref
  593.9 9.1 collective-permute-done.86
  610.6 4.3 collective-permute-done.93
  617.3 4.2 collective-permute-done.89
  636.3 7.1 collective-permute-done.96
  656.7 6.0 collective-permute-done.103
  675.5 12.7 %collective-permute-done.109 = bf16[192,640]{1,0:T(8,128)(2,1)S(1)} collective-permute-done((bf16[192,640]{1,0:T(8,128)(2,1)S(1)}, bf16[192,640]{1,0:T(8,128)(2,1)S(1)}, u32[]{:S(2)}, u32[]{:S(2)}) %collective-permute-start.109) | collective-permute-done | bytes 245792 | tf_op jit(solution)/shard_map/ppermute | solution.py:443
  690.0 11.2 %shard_map.530 = (bf16[640,1664]{1,0:T(8,128)(2,1)S(1)}, bf16[1280,1536]{1,0:T(8,128)(2,1)S(1)}) custom-call(bf16[1280,1536]{1,0:T(8,128)(2,1)} %constant_dynamic-update-slice_fusion.d_ref, f32[1280,768]{1,0:T(8,128)S(1)} %copy-done.10, f32[1280,768]{1,0:T(8,128)} %copy-done.13, f32[1280,1]{1,0:T(8,128)S(1)} %copy-done.24, f32[2,128]{1,0:T(2,128)S(1)} %copy-done.57, ...), custom_call_target="tpu_custom_call" | custom-call | flops 4529848320 | bytes 16908288 | tf_op jit(solution)/shard_map/pallas_call | solution.py:369
  710.3 11.4 %shard_map.531 = (bf16[640,1664]{1,0:T(8,128)(2,1)S(1)}, bf16[1280,1536]{1,0:T(8,128)(2,1)S(1)}) custom-call(bf16[1280,1536]{1,0:T(8,128)(2,1)} %constant_dynamic-update-slice_fusion.d_ref, f32[1280,768]{1,0:T(8,128)S(1)} %copy-done.10, f32[1280,768]{1,0:T(8,128)} %copy-done.13, f32[1280,1]{1,0:T(8,128)S(1)} %copy-done.24, ...), custom_call_target="tpu_custom_call", output_to_operand_aliasing={{1}: (8, {})} | custom-call | flops 4529848320 | bytes 16908288 | tf_op jit(solution)/shard_map/pallas_call | solution.py:369
  721.7 9.0 collective-permute-done.112
  739.6 7.3 collective-permute-start.115
  751.8 12.0 %collective-permute-done.114 = bf16[160,1664]{1,0:T(8,128)(2,1)S(1)} collective-permute-done((bf16[160,1664]{1,0:T(8,128)(2,1)S(1)}, bf16[160,1664]{1,0:T(8,128)(2,1)S(1)}, u32[]{:S(2)}, u32[]{:S(2)}) %collective-permute-start.114) | collective-permute-done | bytes 532512 | tf_op jit(solution)/shard_map/ppermute | solution.py:443
  783.6 11.0 %collective-permute-done.117 = bf16[160,1664]{1,0:T(8,128)(2,1)S(1)} collective-permute-done((bf16[160,1664]{1,0:T(8,128)(2,1)S(1)}, bf16[160,1664]{1,0:T(8,128)(2,1)S(1)}, u32[]{:S(2)}, u32[]{:S(2)}) %collective-permute-start.117) | collective-permute-done | bytes 532512 | tf_op jit(solution)/shard_map/ppermute | solution.py:443
  807.0 9.5 collective-permute-done.123
  828.7 20.8 %shard_map.532 = (bf16[256,1536]{1,0:T(8,128)(2,1)S(1)}, bf16[1024,512]{1,0:T(8,128)(2,1)S(1)}) custom-call(bf16[256,1536]{1,0:T(8,128)(2,1)S(1)} %copy-done.66, bf16[1024,512]{1,0:T(8,128)(2,1)S(1)} %copy-done.43, bf16[256,1536]{1,0:T(8,128)(2,1)S(1)} %convolution_convert_fusion.4.dm_ref, f32[256,128]{1,0:T(8,128)S(1)} %copy-done.28, ...), custom_call_target="tpu_custom_call" | custom-call | flops 8053063680 | bytes 3145728 | tf_op jit(solution)/shard_map/pallas_call | solution.py:228
  864.2 3.8 fusion.201
  871.9 4.4 collective-permute-done.129.second_ref
  881.2 14.0 %collective-permute-done.135 = bf16[48,3712]{1,0:T(8,128)(2,1)S(1)} collective-permute-done((bf16[48,3712]{1,0:T(8,128)(2,1)}, bf16[48,3712]{1,0:T(8,128)(2,1)S(1)}, u32[]{:S(2)}, u32[]{:S(2)}) %collective-permute-start.135) | collective-permute-done | bytes 356384 | tf_op jit(solution)/shard_map/ppermute | solution.py:525
  913.8 5.8 collective-permute-done.146
  939.7 6.7 collective-permute-done.151
  951.5 3.8 collective-permute-done.154
  967.0 6.2 collective-permute-done.165
  986.3 5.5 collective-permute-start.167
  995.0 6.3 collective-permute-done.170
  1001.3 9.0 collective-permute-done.166
  1012.5 4.8 collective-permute-done.171
  (1131 shorter events, 506.0 us)
Async XLA Ops:
  7.2 87.0 %all-gather.15.cloned.1.call-start = ((), (), s32[]{:S(2)}) async-start(), calls=%async_computation.2 | async-start | bytes 5898240 | tf_op jit(solution)/shard_map/all_gather | solution.py:896
  12.4 24.6 %collective-permute-start = (bf16[256,1536]{1,0:T(8,128)(2,1)}, bf16[256,1536]{1,0:T(8,128)(2,1)}, u32[]{:S(2)}, u32[]{:S(2)}) collective-permute-start(bf16[256,1536]{1,0:T(8,128)(2,1)} %param.50), channel_id=1, source_target_pairs={{0,8},{4,12},{8,0},{12,4},{16,24},{20,28},{24,16},{28,20},{1,9},{5... | collective-permute-start | bytes 2359304 | tf_op jit(solution)/shard_map/ppermute | solution.py:446
  40.2 231.8 %all-gather.11.cloned.1.call-start = ((), (), s32[]{:S(2)}) async-start(), calls=%async_computation | async-start | bytes 1966080 | tf_op jit(solution)/shard_map/all_gather | solution.py:896
  41.3 25.5 %collective-permute-start.11 = (bf16[192,1536]{1,0:T(8,128)(2,1)}, bf16[192,1536]{1,0:T(8,128)(2,1)}, u32[]{:S(2)}, u32[]{:S(2)}) collective-permute-start(bf16[192,1536]{1,0:T(8,128)(2,1)} %collective-permute-done.6.refs_8_), channel_id=1, source_target_pairs={{0,4},{4,0},{8,12},{12,8},{16,20},{20,16},{24,28},{28,24},{1,5},{5... | collective-permute-start | bytes 1769480 | tf_op jit(solution)/shard_map/ppermute | solution.py:443
  42.8 23.9 %collective-permute-start.12 = (bf16[192,1536]{1,0:T(8,128)(2,1)}, bf16[192,1536]{1,0:T(8,128)(2,1)}, u32[]{:S(2)}, u32[]{:S(2)}) collective-permute-start(bf16[192,1536]{1,0:T(8,128)(2,1)} %collective-permute-done.6.refs_8_), channel_id=1, source_target_pairs={{0,1},{1,0},{2,3},{3,2},{4,5},{5,4},{6,7},{7,6},{8,9},{9,8},{10,11... | collective-permute-start | bytes 1769480 | tf_op jit(solution)/shard_map/ppermute | solution.py:529
  72.9 26.2 %collective-permute-start.17 = (bf16[256,1536]{1,0:T(8,128)(2,1)}, bf16[256,1536]{1,0:T(8,128)(2,1)}, u32[]{:S(2)}, u32[]{:S(2)}) collective-permute-start(bf16[256,1536]{1,0:T(8,128)(2,1)} %copy-done.143), channel_id=1, source_target_pairs={{0,8},{4,12},{8,0},{12,4},{16,24},{20,28},{24,16},{28,20},{1,9},{5... | collective-permute-start | bytes 2359304 | tf_op jit(solution)/shard_map/ppermute | solution.py:446
  75.2 23.9 %collective-permute-start.18 = (bf16[256,1536]{1,0:T(8,128)(2,1)}, bf16[256,1536]{1,0:T(8,128)(2,1)}, u32[]{:S(2)}, u32[]{:S(2)}) collective-permute-start(bf16[256,1536]{1,0:T(8,128)(2,1)} %collective-permute-done), channel_id=1, source_target_pairs={{0,1},{1,0},{2,3},{3,2},{4,5},{5,4},{6,7},{7,6},{8,16},{9,17},{10,... | collective-permute-start | bytes 2359304 | tf_op jit(solution)/shard_map/ppermute | solution.py:458
  101.5 180.0 %all-gather.17.cloned.1.call-start = ((), (), s32[]{:S(2)}) async-start(), calls=%async_computation.3 | async-start | bytes 5898240 | tf_op jit(solution)/shard_map/all_gather | solution.py:896
  104.7 196.7 %all-gather.19.cloned.1.call-start = ((), (), s32[]{:S(2)}) async-start(), calls=%async_computation.4 | async-start | bytes 5898240 | tf_op jit(solution)/shard_map/all_gather | solution.py:896
  107.2 200.5 %all-gather.13.cloned.1.call-start = ((), (), s32[]{:S(2)}) async-start(), calls=%async_computation.1 | async-start | bytes 1966080 | tf_op jit(solution)/shard_map/all_gather | solution.py:896
  107.3 19.8 %collective-permute-start.24 = (bf16[256,1536]{1,0:T(8,128)(2,1)S(1)}, bf16[256,1536]{1,0:T(8,128)(2,1)S(1)}, u32[]{:S(2)}, u32[]{:S(2)}) collective-permute-start(bf16[256,1536]{1,0:T(8,128)(2,1)S(1)} %multiply_convert_fusion.2), channel_id=1, source_target_pairs={{0,8},{4,12},{8,0},{12,4},{16,24},{20,28},{24,16},{28,20},{1,9},{5... | collective-permute-start | bytes 2359304 | tf_op jit(solution)/shard_map/ppermute | solution.py:446
  109.4 198.3 %all-gather.21.cloned.1.call-start = ((), (), s32[]{:S(2)}) async-start(), calls=%async_computation.5 | async-start | bytes 5898240 | tf_op jit(solution)/shard_map/all_gather | solution.py:896
  176.3 33.4 %collective-permute-start.33 = (bf16[256,1536]{1,0:T(8,128)(2,1)}, bf16[256,1536]{1,0:T(8,128)(2,1)}, u32[]{:S(2)}, u32[]{:S(2)}) collective-permute-start(bf16[256,1536]{1,0:T(8,128)(2,1)} %collective-permute-done.18), channel_id=1, source_target_pairs={{0,8},{4,12},{8,0},{12,4},{16,24},{20,28},{24,16},{28,20},{1,9},{5... | collective-permute-start | bytes 2359304 | tf_op jit(solution)/shard_map/ppermute | solution.py:446
  177.3 32.3 %collective-permute-start.34 = (bf16[160,1536]{1,0:T(8,128)(2,1)}, bf16[160,1536]{1,0:T(8,128)(2,1)}, u32[]{:S(2)}, u32[]{:S(2)}) collective-permute-start(bf16[160,1536]{1,0:T(8,128)(2,1)} %convolution_convert_fusion.38), channel_id=1, source_target_pairs={{0,4},{4,0},{8,12},{12,8},{16,20},{20,16},{24,28},{28,24},{1,5},{5... | collective-permute-start | bytes 1474568 | tf_op jit(solution)/shard_map/ppermute | solution.py:443
  177.8 31.9 %collective-permute-start.35 = (bf16[160,1536]{1,0:T(8,128)(2,1)}, bf16[160,1536]{1,0:T(8,128)(2,1)}, u32[]{:S(2)}, u32[]{:S(2)}) collective-permute-start(bf16[160,1536]{1,0:T(8,128)(2,1)} %convolution_convert_fusion.35), channel_id=1, source_target_pairs={{0,4},{4,0},{8,12},{12,8},{16,20},{20,16},{24,28},{28,24},{1,5},{5... | collective-permute-start | bytes 1474568 | tf_op jit(solution)/shard_map/ppermute | solution.py:443
  287.6 20.1 %collective-permute-start.49 = (bf16[160,1536]{1,0:T(8,128)(2,1)}, bf16[160,1536]{1,0:T(8,128)(2,1)}, u32[]{:S(2)}, u32[]{:S(2)}) collective-permute-start(bf16[160,1536]{1,0:T(8,128)(2,1)} %convolution_convert_fusion.29), channel_id=1, source_target_pairs={{0,4},{4,0},{8,12},{12,8},{16,20},{20,16},{24,28},{28,24},{1,5},{5... | collective-permute-start | bytes 1474568 | tf_op jit(solution)/shard_map/ppermute | solution.py:443
  307.7 20.5 %collective-permute-start.50 = (bf16[256,1536]{1,0:T(8,128)(2,1)}, bf16[256,1536]{1,0:T(8,128)(2,1)S(1)}, u32[]{:S(2)}, u32[]{:S(2)}) collective-permute-start(bf16[256,1536]{1,0:T(8,128)(2,1)} %multiply_convert_fusion), channel_id=1, source_target_pairs={{0,8},{4,12},{8,0},{12,4},{16,24},{20,28},{24,16},{28,20},{1,9},{5... | collective-permute-start | bytes 2359304 | tf_op jit(solution)/shard_map/ppermute | solution.py:446
  450.1 24.0 %collective-permute-start.64 = (bf16[768,1536]{1,0:T(8,128)(2,1)}, bf16[768,1536]{1,0:T(8,128)(2,1)}, u32[]{:S(2)}, u32[]{:S(2)}) collective-permute-start(bf16[768,1536]{1,0:T(8,128)(2,1)} %pad_maximum_fusion.3), channel_id=1, source_target_pairs={{0,1},{1,0},{2,3},{3,2},{4,5},{5,4},{6,7},{7,6},{8,9},{9,8},{10,11... | collective-permute-start | bytes 7077896 | tf_op jit(solution)/shard_map/ppermute | solution.py:529
  452.6 21.6 %collective-permute-start.63 = (bf16[256,1664]{1,0:T(8,128)(2,1)}, bf16[256,1664]{1,0:T(8,128)(2,1)S(1)}, u32[]{:S(2)}, u32[]{:S(2)}) collective-permute-start(bf16[256,1664]{1,0:T(8,128)(2,1)} %get-tuple-element.1188), channel_id=1, source_target_pairs={{0,8},{4,12},{8,0},{12,4},{16,24},{20,28},{24,16},{28,20},{1,9},{5... | collective-permute-start | bytes 2555912 | tf_op jit(solution)/shard_map/ppermute | solution.py:446
  457.2 29.1 %collective-permute-start.70 = (bf16[160,1536]{1,0:T(8,128)(2,1)}, bf16[160,1536]{1,0:T(8,128)(2,1)}, u32[]{:S(2)}, u32[]{:S(2)}) collective-permute-start(bf16[160,1536]{1,0:T(8,128)(2,1)} %get-tuple-element.713), channel_id=1, source_target_pairs={{0,4},{4,0},{8,12},{12,8},{16,20},{20,16},{24,28},{28,24},{1,5},{5... | collective-permute-start | bytes 1474568 | tf_op jit(solution)/shard_map/ppermute | solution.py:443
  479.8 28.0 %collective-permute-start.68 = (bf16[384,1536]{1,0:T(8,128)(2,1)}, bf16[384,1536]{1,0:T(8,128)(2,1)}, u32[]{:S(2)}, u32[]{:S(2)}) collective-permute-start(bf16[384,1536]{1,0:T(8,128)(2,1)} %fusion.19), channel_id=1, source_target_pairs={{0,2},{1,3},{2,0},{3,1},{4,6},{5,7},{6,4},{7,5},{8,10},{9,11},{10,... | collective-permute-start | bytes 3538952 | tf_op jit(solution)/shard_map/ppermute | solution.py:533
  482.8 25.0 %collective-permute-start.69 = (bf16[384,1536]{1,0:T(8,128)(2,1)}, bf16[384,1536]{1,0:T(8,128)(2,1)}, u32[]{:S(2)}, u32[]{:S(2)}) collective-permute-start(bf16[384,1536]{1,0:T(8,128)(2,1)} %pad_maximum_fusion.9), channel_id=1, source_target_pairs={{0,1},{1,0},{2,3},{3,2},{4,5},{5,4},{6,7},{7,6},{8,9},{9,8},{10,11... | collective-permute-start | bytes 3538952 | tf_op jit(solution)/shard_map/ppermute | solution.py:529
  484.9 21.1 %collective-permute-start.66 = (bf16[256,1664]{1,0:T(8,128)(2,1)}, bf16[256,1664]{1,0:T(8,128)(2,1)S(1)}, u32[]{:S(2)}, u32[]{:S(2)}) collective-permute-start(bf16[256,1664]{1,0:T(8,128)(2,1)} %get-tuple-element.1085), channel_id=1, source_target_pairs={{0,8},{4,12},{8,0},{12,4},{16,24},{20,28},{24,16},{28,20},{1,9},{5... | collective-permute-start | bytes 2555912 | tf_op jit(solution)/shard_map/ppermute | solution.py:446
  485.8 20.3 %collective-permute-start.67 = (bf16[256,1664]{1,0:T(8,128)(2,1)}, bf16[256,1664]{1,0:T(8,128)(2,1)}, u32[]{:S(2)}, u32[]{:S(2)}) collective-permute-start(bf16[256,1664]{1,0:T(8,128)(2,1)} %get-tuple-element.1084), channel_id=1, source_target_pairs={{0,1},{1,0},{2,3},{3,2},{4,5},{5,4},{6,7},{7,6},{8,16},{9,17},{10,... | collective-permute-start | bytes 2555912 | tf_op jit(solution)/shard_map/ppermute | solution.py:458
  511.6 19.9 %collective-permute-start.72 = (bf16[256,1664]{1,0:T(8,128)(2,1)S(1)}, bf16[256,1664]{1,0:T(8,128)(2,1)S(1)}, u32[]{:S(2)}, u32[]{:S(2)}) collective-permute-start(bf16[256,1664]{1,0:T(8,128)(2,1)S(1)} %get-tuple-element.1083), channel_id=1, source_target_pairs={{0,8},{4,12},{8,0},{12,4},{16,24},{20,28},{24,16},{28,20},{1,9},{5... | collective-permute-start | bytes 2555912 | tf_op jit(solution)/shard_map/ppermute | solution.py:446
  516.7 26.7 %collective-permute-start.78 = (bf16[192,1536]{1,0:T(8,128)(2,1)S(1)}, bf16[192,1536]{1,0:T(8,128)(2,1)S(1)}, u32[]{:S(2)}, u32[]{:S(2)}) collective-permute-start(bf16[192,1536]{1,0:T(8,128)(2,1)S(1)} %fusion.42), channel_id=1, source_target_pairs={{0,2},{1,3},{2,0},{3,1},{4,6},{5,7},{6,4},{7,5},{8,10},{9,11},{10,... | collective-permute-start | bytes 1769480 | tf_op jit(solution)/shard_map/ppermute | solution.py:533
  531.4 33.7 %collective-permute-start.74 = (bf16[160,1536]{1,0:T(8,128)(2,1)S(1)}, bf16[160,1536]{1,0:T(8,128)(2,1)S(1)}, u32[]{:S(2)}, u32[]{:S(2)}) collective-permute-start(bf16[160,1536]{1,0:T(8,128)(2,1)S(1)} %copy-done.166), channel_id=1, source_target_pairs={{0,4},{4,0},{8,12},{12,8},{16,20},{20,16},{24,28},{28,24},{1,5},{5... | collective-permute-start | bytes 1474568 | tf_op jit(solution)/shard_map/ppermute | solution.py:443
  534.8 30.3 %collective-permute-start.76 = (bf16[256,1536]{1,0:T(8,128)(2,1)S(1)}, bf16[256,1536]{1,0:T(8,128)(2,1)S(1)}, u32[]{:S(2)}, u32[]{:S(2)}) collective-permute-start(bf16[256,1536]{1,0:T(8,128)(2,1)S(1)} %get-tuple-element.1089), channel_id=1, source_target_pairs={{0,8},{4,12},{8,0},{12,4},{16,24},{20,28},{24,16},{28,20},{1,9},{5... | collective-permute-start | bytes 2359304 | tf_op jit(solution)/shard_map/ppermute | solution.py:446
  536.6 28.5 %collective-permute-start.77 = (bf16[256,1536]{1,0:T(8,128)(2,1)S(1)}, bf16[256,1536]{1,0:T(8,128)(2,1)S(1)}, u32[]{:S(2)}, u32[]{:S(2)}) collective-permute-start(bf16[256,1536]{1,0:T(8,128)(2,1)S(1)} %get-tuple-element.1088), channel_id=1, source_target_pairs={{0,1},{1,0},{2,3},{3,2},{4,5},{5,4},{6,7},{7,6},{8,16},{9,17},{10,... | collective-permute-start | bytes 2359304 | tf_op jit(solution)/shard_map/ppermute | solution.py:458
  541.2 24.0 %collective-permute-start.79 = (bf16[256,1536]{1,0:T(8,128)(2,1)S(1)}, bf16[256,1536]{1,0:T(8,128)(2,1)S(1)}, u32[]{:S(2)}, u32[]{:S(2)}) collective-permute-start(bf16[256,1536]{1,0:T(8,128)(2,1)S(1)} %fusion.180), channel_id=1, source_target_pairs={{0,2},{1,3},{2,0},{3,1},{4,6},{5,7},{6,4},{7,5},{8,10},{9,11},{10,... | collective-permute-start | bytes 2359304 | tf_op jit(solution)/shard_map/ppermute | solution.py:533
  543.4 21.7 %collective-permute-start.75 = (bf16[160,1536]{1,0:T(8,128)(2,1)S(1)}, bf16[160,1536]{1,0:T(8,128)(2,1)S(1)}, u32[]{:S(2)}, u32[]{:S(2)}) collective-permute-start(bf16[160,1536]{1,0:T(8,128)(2,1)S(1)} %copy-done.165), channel_id=1, source_target_pairs={{0,4},{4,0},{8,12},{12,8},{16,20},{20,16},{24,28},{28,24},{1,5},{5... | collective-permute-start | bytes 1474568 | tf_op jit(solution)/shard_map/ppermute | solution.py:443
  574.0 19.8 %collective-permute-start.87 = (bf16[256,1536]{1,0:T(8,128)(2,1)S(1)}, bf16[256,1536]{1,0:T(8,128)(2,1)S(1)}, u32[]{:S(2)}, u32[]{:S(2)}) collective-permute-start(bf16[256,1536]{1,0:T(8,128)(2,1)S(1)} %get-tuple-element.1087), channel_id=1, source_target_pairs={{0,8},{4,12},{8,0},{12,4},{16,24},{20,28},{24,16},{28,20},{1,9},{5... | collective-permute-start | bytes 2359304 | tf_op jit(solution)/shard_map/ppermute | solution.py:446
  590.4 20.1 %collective-permute-start.92 = (bf16[256,1536]{1,0:T(8,128)(2,1)S(1)}, bf16[256,1536]{1,0:T(8,128)(2,1)S(1)}, u32[]{:S(2)}, u32[]{:S(2)}) collective-permute-start(bf16[256,1536]{1,0:T(8,128)(2,1)S(1)} %get-tuple-element.775), channel_id=1, source_target_pairs={{0,2},{1,3},{2,0},{3,1},{4,6},{5,7},{6,4},{7,5},{8,10},{9,11},{10,... | collective-permute-start | bytes 2359304 | tf_op jit(solution)/shard_map/ppermute | solution.py:533
  652.2 23.2 %collective-permute-start.108 = (bf16[192,1536]{1,0:T(8,128)(2,1)}, bf16[192,1536]{1,0:T(8,128)(2,1)}, u32[]{:S(2)}, u32[]{:S(2)}) collective-permute-start(bf16[192,1536]{1,0:T(8,128)(2,1)} %dynamic-slice_convert_fusion.2), channel_id=1, source_target_pairs={{0,4},{4,0},{8,12},{12,8},{16,20},{20,16},{24,28},{28,24},{1,5},{5... | collective-permute-start | bytes 1769480 | tf_op jit(solution)/shard_map/ppermute | solution.py:443
  665.3 22.8 %collective-permute-start.104 = (bf16[160,1536]{1,0:T(8,128)(2,1)}, bf16[160,1536]{1,0:T(8,128)(2,1)}, u32[]{:S(2)}, u32[]{:S(2)}) collective-permute-start(bf16[160,1536]{1,0:T(8,128)(2,1)} %convolution_convert_fusion.9), channel_id=1, source_target_pairs={{0,4},{4,0},{8,12},{12,8},{16,20},{20,16},{24,28},{28,24},{1,5},{5... | collective-permute-start | bytes 1474568 | tf_op jit(solution)/shard_map/ppermute | solution.py:443
  701.4 29.4 %collective-permute-start.110 = (bf16[160,1664]{1,0:T(8,128)(2,1)S(1)}, bf16[160,1664]{1,0:T(8,128)(2,1)S(1)}, u32[]{:S(2)}, u32[]{:S(2)}) collective-permute-start(bf16[160,1664]{1,0:T(8,128)(2,1)S(1)} %get-tuple-element.1048), channel_id=1, source_target_pairs={{0,4},{4,0},{8,12},{12,8},{16,20},{20,16},{24,28},{28,24},{1,5},{5... | collective-permute-start | bytes 1597448 | tf_op jit(solution)/shard_map/ppermute | solution.py:443
  706.4 24.4 %collective-permute-start.112 = (bf16[48,3712]{1,0:T(8,128)(2,1)S(1)}, bf16[48,3712]{1,0:T(8,128)(2,1)S(1)}, u32[]{:S(2)}, u32[]{:S(2)}) collective-permute-start(bf16[48,3712]{1,0:T(8,128)(2,1)S(1)} %get-tuple-element.1099), channel_id=1, source_target_pairs={{0,16},{4,20},{8,24},{12,28},{16,0},{20,4},{24,8},{28,12},{1,17},{... | collective-permute-start | bytes 1069064 | tf_op jit(solution)/shard_map/ppermute | solution.py:525
  709.1 21.7 %collective-permute-start.113 = (bf16[48,3712]{1,0:T(8,128)(2,1)S(1)}, bf16[48,3712]{1,0:T(8,128)(2,1)S(1)}, u32[]{:S(2)}, u32[]{:S(2)}) collective-permute-start(bf16[48,3712]{1,0:T(8,128)(2,1)S(1)} %get-tuple-element.1098), channel_id=1, source_target_pairs={{0,24},{4,28},{8,0},{12,4},{16,8},{20,12},{24,16},{28,20},{1,25},{... | collective-permute-start | bytes 1069064 | tf_op jit(solution)/shard_map/ppermute | solution.py:525
  734.5 31.1 %collective-permute-start.116 = (bf16[768,1536]{1,0:T(8,128)(2,1)S(1)}, bf16[768,1536]{1,0:T(8,128)(2,1)S(1)}, u32[]{:S(2)}, u32[]{:S(2)}) collective-permute-start(bf16[768,1536]{1,0:T(8,128)(2,1)S(1)} %pad_maximum_fusion.4), channel_id=1, source_target_pairs={{0,1},{1,0},{2,3},{3,2},{4,5},{5,4},{6,7},{7,6},{8,9},{9,8},{10,11... | collective-permute-start | bytes 7077896 | tf_op jit(solution)/shard_map/ppermute | solution.py:529
  739.6 26.0 %collective-permute-start.115 = (bf16[256,1664]{1,0:T(8,128)(2,1)S(1)}, bf16[256,1664]{1,0:T(8,128)(2,1)S(1)}, u32[]{:S(2)}, u32[]{:S(2)}) collective-permute-start(bf16[256,1664]{1,0:T(8,128)(2,1)S(1)} %get-tuple-element.1194), channel_id=1, source_target_pairs={{0,8},{4,12},{8,0},{12,4},{16,24},{20,28},{24,16},{28,20},{1,9},{5... | collective-permute-start | bytes 2555912 | tf_op jit(solution)/shard_map/ppermute | solution.py:446
  767.8 29.6 %collective-permute-start.120 = (bf16[384,1536]{1,0:T(8,128)(2,1)S(1)}, bf16[384,1536]{1,0:T(8,128)(2,1)S(1)}, u32[]{:S(2)}, u32[]{:S(2)}) collective-permute-start(bf16[384,1536]{1,0:T(8,128)(2,1)S(1)} %fusion.20), channel_id=1, source_target_pairs={{0,2},{1,3},{2,0},{3,1},{4,6},{5,7},{6,4},{7,5},{8,10},{9,11},{10,... | collective-permute-start | bytes 3538952 | tf_op jit(solution)/shard_map/ppermute | solution.py:533
  775.4 22.0 %collective-permute-start.121 = (bf16[384,1536]{1,0:T(8,128)(2,1)S(1)}, bf16[384,1536]{1,0:T(8,128)(2,1)S(1)}, u32[]{:S(2)}, u32[]{:S(2)}) collective-permute-start(bf16[384,1536]{1,0:T(8,128)(2,1)S(1)} %pad_maximum_fusion.10), channel_id=1, source_target_pairs={{0,1},{1,0},{2,3},{3,2},{4,5},{5,4},{6,7},{7,6},{8,9},{9,8},{10,11... | collective-permute-start | bytes 3538952 | tf_op jit(solution)/shard_map/ppermute | solution.py:529
  776.0 21.4 %collective-permute-start.118 = (bf16[256,1664]{1,0:T(8,128)(2,1)S(1)}, bf16[256,1664]{1,0:T(8,128)(2,1)S(1)}, u32[]{:S(2)}, u32[]{:S(2)}) collective-permute-start(bf16[256,1664]{1,0:T(8,128)(2,1)S(1)} %get-tuple-element.1081), channel_id=1, source_target_pairs={{0,8},{4,12},{8,0},{12,4},{16,24},{20,28},{24,16},{28,20},{1,9},{5... | collective-permute-start | bytes 2555912 | tf_op jit(solution)/shard_map/ppermute | solution.py:446
  794.6 73.6 %collective-permute-start.132 = (bf16[256,384]{1,0:T(8,128)(2,1)}, bf16[256,384]{1,0:T(8,128)(2,1)}, u32[]{:S(2)}, u32[]{:S(2)}) collective-permute-start(bf16[256,384]{1,0:T(8,128)(2,1)} %get-tuple-element.1110), channel_id=1, source_target_pairs={{0,3},{1,2},{2,1},{3,0},{4,7},{5,6},{6,5},{7,4},{8,11},{9,10},{10,... | collective-permute-start | bytes 589832 | tf_op jit(solution)/shard_map/ppermute | solution.py:585
  797.4 71.1 %collective-permute-start.131 = (bf16[256,384]{1,0:T(8,128)(2,1)}, bf16[256,384]{1,0:T(8,128)(2,1)}, u32[]{:S(2)}, u32[]{:S(2)}) collective-permute-start(bf16[256,384]{1,0:T(8,128)(2,1)} %get-tuple-element.1111), channel_id=1, source_target_pairs={{0,1},{1,0},{2,3},{3,2},{4,5},{5,4},{6,7},{7,6},{8,9},{9,8},{10,11... | collective-permute-start | bytes 589832 | tf_op jit(solution)/shard_map/ppermute | solution.py:585
  799.7 21.4 %collective-permute-start.124 = (bf16[256,1664]{1,0:T(8,128)(2,1)S(1)}, bf16[256,1664]{1,0:T(8,128)(2,1)S(1)}, u32[]{:S(2)}, u32[]{:S(2)}) collective-permute-start(bf16[256,1664]{1,0:T(8,128)(2,1)S(1)} %get-tuple-element.1079), channel_id=1, source_target_pairs={{0,8},{4,12},{8,0},{12,4},{16,24},{20,28},{24,16},{28,20},{1,9},{5... | collective-permute-start | bytes 2555912 | tf_op jit(solution)/shard_map/ppermute | solution.py:446
  801.5 20.4 %collective-permute-start.125 = (bf16[256,1664]{1,0:T(8,128)(2,1)S(1)}, bf16[256,1664]{1,0:T(8,128)(2,1)S(1)}, u32[]{:S(2)}, u32[]{:S(2)}) collective-permute-start(bf16[256,1664]{1,0:T(8,128)(2,1)S(1)} %get-tuple-element.1078), channel_id=1, source_target_pairs={{0,1},{1,0},{2,3},{3,2},{4,5},{5,4},{6,7},{7,6},{8,16},{9,17},{10,... | collective-permute-start | bytes 2555912 | tf_op jit(solution)/shard_map/ppermute | solution.py:458
  816.5 52.9 %collective-permute-start.130 = (bf16[256,384]{1,0:T(8,128)(2,1)S(1)}, bf16[256,384]{1,0:T(8,128)(2,1)}, u32[]{:S(2)}, u32[]{:S(2)}) collective-permute-start(bf16[256,384]{1,0:T(8,128)(2,1)S(1)} %copy-done.186), channel_id=1, source_target_pairs={{0,2},{1,3},{2,0},{3,1},{4,6},{5,7},{6,4},{7,5},{8,10},{9,11},{10,... | collective-permute-start | bytes 589832 | tf_op jit(solution)/shard_map/ppermute | solution.py:585
  821.1 28.4 %collective-permute-start.122 = (bf16[192,1536]{1,0:T(8,128)(2,1)S(1)}, bf16[192,1536]{1,0:T(8,128)(2,1)S(1)}, u32[]{:S(2)}, u32[]{:S(2)}) collective-permute-start(bf16[192,1536]{1,0:T(8,128)(2,1)S(1)} %fusion.43), channel_id=1, source_target_pairs={{0,2},{1,3},{2,0},{3,1},{4,6},{5,7},{6,4},{7,5},{8,10},{9,11},{10,... | collective-permute-start | bytes 1769480 | tf_op jit(solution)/shard_map/ppermute | solution.py:533
  825.9 27.1 %collective-permute-start.126 = (bf16[256,1536]{1,0:T(8,128)(2,1)S(1)}, bf16[256,1536]{1,0:T(8,128)(2,1)S(1)}, u32[]{:S(2)}, u32[]{:S(2)}) collective-permute-start(bf16[256,1536]{1,0:T(8,128)(2,1)S(1)} %get-tuple-element.1020), channel_id=1, source_target_pairs={{0,2},{1,3},{2,0},{3,1},{4,6},{5,7},{6,4},{7,5},{8,10},{9,11},{10,... | collective-permute-start | bytes 2359304 | tf_op jit(solution)/shard_map/ppermute | solution.py:533
  860.6 20.5 %collective-permute-start.134 = (bf16[48,3712]{1,0:T(8,128)(2,1)}, bf16[48,3712]{1,0:T(8,128)(2,1)S(1)}, u32[]{:S(2)}, u32[]{:S(2)}) collective-permute-start(bf16[48,3712]{1,0:T(8,128)(2,1)} %get-tuple-element.1019), channel_id=1, source_target_pairs={{0,24},{4,28},{8,0},{12,4},{16,8},{20,12},{24,16},{28,20},{1,25},{... | collective-permute-start | bytes 1069064 | tf_op jit(solution)/shard_map/ppermute | solution.py:525
  862.7 32.5 %collective-permute-start.135 = (bf16[48,3712]{1,0:T(8,128)(2,1)}, bf16[48,3712]{1,0:T(8,128)(2,1)S(1)}, u32[]{:S(2)}, u32[]{:S(2)}) collective-permute-start(bf16[48,3712]{1,0:T(8,128)(2,1)} %get-tuple-element.1019), channel_id=1, source_target_pairs={{0,16},{4,20},{8,24},{12,28},{16,0},{20,4},{24,8},{28,12},{1,17},{... | collective-permute-start | bytes 1069064 | tf_op jit(solution)/shard_map/ppermute | solution.py:525
  868.1 27.1 %collective-permute-start.136 = (bf16[48,3712]{1,0:T(8,128)(2,1)}, bf16[48,3712]{1,0:T(8,128)(2,1)S(1)}, u32[]{:S(2)}, u32[]{:S(2)}) collective-permute-start(bf16[48,3712]{1,0:T(8,128)(2,1)} %get-tuple-element.1019), channel_id=1, source_target_pairs={{0,8},{4,12},{8,16},{12,20},{16,24},{20,28},{24,0},{28,4},{1,9},{5... | collective-permute-start | bytes 1069064 | tf_op jit(solution)/shard_map/ppermute | solution.py:525
  876.4 19.7 %collective-permute-start.133 = (bf16[192,1536]{1,0:T(8,128)(2,1)S(1)}, bf16[192,1536]{1,0:T(8,128)(2,1)S(1)}, u32[]{:S(2)}, u32[]{:S(2)}) collective-permute-start(bf16[192,1536]{1,0:T(8,128)(2,1)S(1)} %dynamic-slice_convert_fusion.1), channel_id=1, source_target_pairs={{0,4},{4,0},{8,12},{12,8},{16,20},{20,16},{24,28},{28,24},{1,5},{5... | collective-permute-start | bytes 1769480 | tf_op jit(solution)/shard_map/ppermute | solution.py:443
  878.8 20.4 %collective-permute-start.140 = (bf16[256,1536]{1,0:T(8,128)(2,1)S(1)}, bf16[256,1536]{1,0:T(8,128)(2,1)S(1)}, u32[]{:S(2)}, u32[]{:S(2)}) collective-permute-start(bf16[256,1536]{1,0:T(8,128)(2,1)S(1)} %get-tuple-element.871), channel_id=1, source_target_pairs={{0,2},{1,3},{2,0},{3,1},{4,6},{5,7},{6,4},{7,5},{8,10},{9,11},{10,... | collective-permute-start | bytes 2359304 | tf_op jit(solution)/shard_map/ppermute | solution.py:533
  881.2 20.7 %collective-permute-start.139 = (bf16[256,384]{1,0:T(8,128)(2,1)S(1)}, bf16[256,384]{1,0:T(8,128)(2,1)S(1)}, u32[]{:S(2)}, u32[]{:S(2)}) collective-permute-start(bf16[256,384]{1,0:T(8,128)(2,1)S(1)} %copy-done.190), channel_id=1, source_target_pairs={{0,3},{1,2},{2,1},{3,0},{4,7},{5,6},{6,5},{7,4},{8,11},{9,10},{10,... | collective-permute-start | bytes 589832 | tf_op jit(solution)/shard_map/ppermute | solution.py:585
  899.7 19.9 %collective-permute-start.143 = (bf16[48,1536]{1,0:T(8,128)(2,1)S(1)}, bf16[48,1536]{1,0:T(8,128)(2,1)S(1)}, u32[]{:S(2)}, u32[]{:S(2)}) collective-permute-start(bf16[48,1536]{1,0:T(8,128)(2,1)S(1)} %get-tuple-element.1132), channel_id=1, source_target_pairs={{0,8},{4,12},{8,16},{12,20},{16,24},{20,28},{24,0},{28,4},{1,9},{5... | collective-permute-start | bytes 442376 | tf_op jit(solution)/shard_map/ppermute | solution.py:525
  922.4 29.2 %collective-permute-start.155 = (bf16[48,1536]{1,0:T(8,128)(2,1)}, bf16[48,1536]{1,0:T(8,128)(2,1)}, u32[]{:S(2)}, u32[]{:S(2)}) collective-permute-start(bf16[48,1536]{1,0:T(8,128)(2,1)} %get-tuple-element.1015), channel_id=1, source_target_pairs={{0,24},{4,28},{8,0},{12,4},{16,8},{20,12},{24,16},{28,20},{1,25},{... | collective-permute-start | bytes 442376 | tf_op jit(solution)/shard_map/ppermute | solution.py:525
  925.5 26.0 %collective-permute-start.156 = (bf16[48,1536]{1,0:T(8,128)(2,1)}, bf16[48,1536]{1,0:T(8,128)(2,1)}, u32[]{:S(2)}, u32[]{:S(2)}) collective-permute-start(bf16[48,1536]{1,0:T(8,128)(2,1)} %get-tuple-element.1015), channel_id=1, source_target_pairs={{0,16},{4,20},{8,24},{12,28},{16,0},{20,4},{24,8},{28,12},{1,17},{... | collective-permute-start | bytes 442376 | tf_op jit(solution)/shard_map/ppermute | solution.py:525
  925.5 26.0 %collective-permute-start.157 = (bf16[48,1536]{1,0:T(8,128)(2,1)}, bf16[48,1536]{1,0:T(8,128)(2,1)}, u32[]{:S(2)}, u32[]{:S(2)}) collective-permute-start(bf16[48,1536]{1,0:T(8,128)(2,1)} %get-tuple-element.1015), channel_id=1, source_target_pairs={{0,8},{4,12},{8,16},{12,20},{16,24},{20,28},{24,0},{28,4},{1,9},{5... | collective-permute-start | bytes 442376 | tf_op jit(solution)/shard_map/ppermute | solution.py:525
  950.5 22.7 %collective-permute-start.165 = (bf16[192,2176]{1,0:T(8,128)(2,1)S(1)}, bf16[192,2176]{1,0:T(8,128)(2,1)S(1)}, u32[]{:S(2)}, u32[]{:S(2)}) collective-permute-start(bf16[192,2176]{1,0:T(8,128)(2,1)S(1)} %slice.567), channel_id=1, source_target_pairs={{0,4},{4,0},{8,12},{12,8},{16,20},{20,16},{24,28},{28,24},{1,5},{5... | collective-permute-start | bytes 2506760 | tf_op jit(solution)/shard_map/ppermute | solution.py:443
  955.5 20.5 %collective-permute-start.161 = (bf16[48,640]{1,0:T(8,128)(2,1)S(1)}, bf16[48,640]{1,0:T(8,128)(2,1)S(1)}, u32[]{:S(2)}, u32[]{:S(2)}) collective-permute-start(bf16[48,640]{1,0:T(8,128)(2,1)S(1)} %get-tuple-element.1157), channel_id=1, source_target_pairs={{0,8},{4,12},{8,16},{12,20},{16,24},{20,28},{24,0},{28,4},{1,9},{5... | collective-permute-start | bytes 184328 | tf_op jit(solution)/shard_map/ppermute | solution.py:525
  958.6 21.0 %collective-permute-start.162 = (bf16[48,640]{1,0:T(8,128)(2,1)S(1)}, bf16[48,640]{1,0:T(8,128)(2,1)S(1)}, u32[]{:S(2)}, u32[]{:S(2)}) collective-permute-start(bf16[48,640]{1,0:T(8,128)(2,1)S(1)} %get-tuple-element.1156), channel_id=1, source_target_pairs={{0,16},{4,20},{8,24},{12,28},{16,0},{20,4},{24,8},{28,12},{1,17},{... | collective-permute-start | bytes 184328 | tf_op jit(solution)/shard_map/ppermute | solution.py:525
  964.7 21.5 %collective-permute-start.164 = (bf16[192,1536]{1,0:T(8,128)(2,1)S(1)}, bf16[192,1536]{1,0:T(8,128)(2,1)S(1)}, u32[]{:S(2)}, u32[]{:S(2)}) collective-permute-start(bf16[192,1536]{1,0:T(8,128)(2,1)S(1)} %bitcast.551), channel_id=1, source_target_pairs={{0,4},{4,0},{8,12},{12,8},{16,20},{20,16},{24,28},{28,24},{1,5},{5... | collective-permute-start | bytes 1769480 | tf_op jit(solution)/shard_map/ppermute | solution.py:443
  (351 other events, 3403.2 us)
Sparse Core Ops, SparseCore 0:
  40.3 43.5 all-gather.14
  101.6 17.9 all-gather.10
  121.2 37.4 all-gather.16
  160.1 37.4 all-gather.18
  199.0 19.6 all-gather.12
  220.6 37.4 all-gather.20

commit v4 on v3

--- a/solution.py
+++ b/solution.py
@@ -126,6 +126,7 @@
     keys = kv_all.shape[0]
     heads = width // HEAD_SIZE
     group = heads // KEY_VALUE_HEADS
+    together = 3 if group % 3 == 0 else 1
     scale = HEAD_SIZE ** (-0.5)
 
     def kernel(
@@ -136,22 +137,24 @@
             seen = (qd_ref[...] == kd_ref[...]) & (kp_ref[...] <= qp_ref[...])
             bias[...] = jnp.where(seen, 0.0, masked_score)
 
-        query = turned(q_ref[...], cos_ref[...], sin_ref[...]).astype(bf16)
-        turned_ref[...] = query
-        scores = mm_nt(query, kv_ref[:, :HEAD_SIZE]) * scale + bias[...]
-        weight = jnp.exp(scores - jnp.max(scores, axis=1, keepdims=True))
-        total = jnp.sum(weight, axis=1, keepdims=True)
-        probs = (weight * (1.0 / total)).astype(bf16)
-        out_ref[...] = mm(probs, kv_ref[:, HEAD_SIZE:]).astype(bf16)
+        for at in range(0, together * HEAD_SIZE, HEAD_SIZE):
+            head = slice(at, at + HEAD_SIZE)
+            query = turned(q_ref[:, head], cos_ref[...], sin_ref[...]).astype(bf16)
+            turned_ref[:, head] = query
+            scores = mm_nt(query, kv_ref[:, :HEAD_SIZE]) * scale + bias[...]
+            weight = jnp.exp(scores - jnp.max(scores, axis=1, keepdims=True))
+            total = jnp.sum(weight, axis=1, keepdims=True)
+            probs = (weight * (1.0 / total)).astype(bf16)
+            out_ref[:, head] = mm(probs, kv_ref[:, HEAD_SIZE:]).astype(bf16)
 
     fixed = lambda shape: pl.BlockSpec(shape, lambda h: (0, 0))
-    by_head = pl.BlockSpec((rows, HEAD_SIZE), lambda h: (0, h))
+    by_head = pl.BlockSpec((rows, together * HEAD_SIZE), lambda h: (0, h))
     return pl.pallas_call(
         kernel,
-        grid=(heads,),
+        grid=(heads // together,),
         in_specs=[
             by_head,
-            pl.BlockSpec((keys, 2 * HEAD_SIZE), lambda h: (0, h // group)),
+            pl.BlockSpec((keys, 2 * HEAD_SIZE), lambda h: (0, h * together // group)),
             fixed((rows, HEAD_SIZE)),
             fixed((rows, HEAD_SIZE)),
             fixed((rows, 1)),
@@ -182,6 +185,8 @@
     keys = kv_all.shape[0]
     heads = width // HEAD_SIZE
     group = heads // KEY_VALUE_HEADS
+    together = 3 if group % 3 == 0 else 1
+    steps = group // together
     scale = HEAD_SIZE ** (-0.5)
 
     def kernel(
@@ -195,39 +200,42 @@
             seen = (qd_ref[...] == kd_ref[...]) & (kp_ref[...] <= qp_ref[...])
             bias[...] = jnp.where(seen, 0.0, masked_score)
 
-        query, key, value = q_ref[...], kv_ref[:, :HEAD_SIZE], kv_ref[:, HEAD_SIZE:]
-        d_out = dm_ref[...]
-        scores = mm_nt(key, query) * scale + bias[...]
-        weight = jnp.exp(scores - jnp.max(scores, axis=0, keepdims=True))
-        probs = weight * (1.0 / jnp.sum(weight, axis=0, keepdims=True))
-        d_probs = mm_nt(value, d_out)
-        mean = jnp.sum(probs * d_probs, axis=0, keepdims=True)
-        d_scores = (probs * (d_probs - mean)).astype(bf16)
-        d_value = mm(probs.astype(bf16), d_out)
-        d_key = mm(d_scores, query) * scale
-        d_query = mm_tn(d_scores, key) * scale
-        dq_ref[...] = turned(d_query, cos_ref[...], -sin_ref[...]).astype(bf16)
-
-        @pl.when(head % group == 0)
+        key, value = kv_ref[:, :HEAD_SIZE], kv_ref[:, HEAD_SIZE:]
+        d_key = d_value = 0.0
+        for at in range(0, together * HEAD_SIZE, HEAD_SIZE):
+            own = slice(at, at + HEAD_SIZE)
+            query, d_out = q_ref[:, own], dm_ref[:, own]
+            scores = mm_nt(key, query) * scale + bias[...]
+            weight = jnp.exp(scores - jnp.max(scores, axis=0, keepdims=True))
+            probs = weight * (1.0 / jnp.sum(weight, axis=0, keepdims=True))
+            d_probs = mm_nt(value, d_out)
+            mean = jnp.sum(probs * d_probs, axis=0, keepdims=True)
+            d_scores = (probs * (d_probs - mean)).astype(bf16)
+            d_value = d_value + mm(probs.astype(bf16), d_out)
+            d_key = d_key + mm(d_scores, query) * scale
+            d_query = mm_tn(d_scores, key) * scale
+            dq_ref[:, own] = turned(d_query, cos_ref[...], -sin_ref[...]).astype(bf16)
+
+        @pl.when(head % steps == 0)
         def _():
             dkv[:, :HEAD_SIZE] = d_key
             dkv[:, HEAD_SIZE:] = d_value
 
-        @pl.when(head % group != 0)
+        @pl.when(head % steps != 0)
         def _():
             dkv[:, :HEAD_SIZE] += d_key
             dkv[:, HEAD_SIZE:] += d_value
 
-        @pl.when(head % group == group - 1)
+        @pl.when(head % steps == steps - 1)
         def _():
             dkv_ref[...] = dkv[...].astype(bf16)
 
     fixed = lambda shape: pl.BlockSpec(shape, lambda h: (0, 0))
-    by_head = pl.BlockSpec((rows, HEAD_SIZE), lambda h: (0, h))
-    by_group = pl.BlockSpec((keys, 2 * HEAD_SIZE), lambda h: (0, h // group))
+    by_head = pl.BlockSpec((rows, together * HEAD_SIZE), lambda h: (0, h))
+    by_group = pl.BlockSpec((keys, 2 * HEAD_SIZE), lambda h: (0, h // steps))
     return pl.pallas_call(
         kernel,
-        grid=(heads,),
+        grid=(heads // together,),
         in_specs=[
             by_head,
             by_group,
@@ -300,8 +308,8 @@
             turn = jnp.tanh(gelu_scale * gate_pre * (1.0 + gelu_cube * gate_pre * gate_pre))
             active = 0.5 * gate_pre * (1.0 + turn) * up_pre
             gated_ref[:, part] = (gate * active).astype(bf16)
-            pre_ref[:, part] = gate_pre
-            up_ref[:, part] = up_pre
+            pre_ref[:, part] = gate_pre.astype(bf16)
+            up_ref[:, part] = up_pre.astype(bf16)
         out_ref[...] = mm(gated_ref[...], wd_ref[...]).astype(bf16)
 
     by_row = lambda columns: pl.BlockSpec((tile, columns), lambda t: (2 * part + t, 0))
@@ -316,8 +324,8 @@
         + [by_row(hidden), by_row(hidden), by_row(hidden), by_row(1)],
         out_shape=[
             jax.ShapeDtypeStruct((rows // 2, width), bf16),
-            jax.ShapeDtypeStruct((rows, hidden), f32),
-            jax.ShapeDtypeStruct((rows, hidden), f32),
+            jax.ShapeDtypeStruct((rows, hidden), bf16),
+            jax.ShapeDtypeStruct((rows, hidden), bf16),
             jax.ShapeDtypeStruct((rows, hidden), bf16),
             jax.ShapeDtypeStruct((rows, 1), f32),
         ],
@@ -347,7 +355,7 @@
         for at in range(0, hidden, 256):
             part = slice(at, at + 256)
             du = mm_nt(d_rows, wd_ref[part, :])
-            v, up_value = pre_ref[:, part], up_ref[:, part]
+            v, up_value = pre_ref[:, part].astype(f32), up_ref[:, part].astype(f32)
             square = v * v
             turn = jnp.tanh(gelu_scale * v * (1.0 + gelu_cube * square))
             half = 0.5 * (1.0 + turn)
@@ -952,9 +960,11 @@
                 late.send(2)
             normed, attn_inverse = norm_forward(stream, attn_gains[i])
             hidden = normed.astype(bf16)
-            kv_pair = shard_rows_of(project([hidden], [w_kv], tables))
+            kv_own = project([hidden], [w_kv], tables)
+            kv_crossed = row_swap(kv_own)
             q_pre = mm(hidden, w_query)
-            kv_pair, q_pre = settle([late], kv_pair, q_pre)
+            kv_own, kv_crossed, q_pre = settle([late], kv_own, kv_crossed, q_pre)
+            kv_pair = jnp.concatenate([kv_own, kv_crossed], axis=0)
             if i == last:
                 late.send(3)
                 for k in range(4, lines.count):
@@ -1207,11 +1217,12 @@
 
     hidden_columns = stored[0]["hidden_columns"]
     out_sum.scatter()
-    d_kv_pair = shard_rows_of(d_kv_low)
+    d_kv_crossed = row_swap(d_kv_low)
     small_part = small_sum(small_grad)
     q_sum = Summed(lines, mm_tn(hidden_columns, shard_rows_all(d_query_pair)))
     q_sum.side()
-    d_kv_pair, small_part = settle([q_sum, out_sum], d_kv_pair, small_part)
+    d_kv_crossed, small_part = settle([q_sum, out_sum], d_kv_crossed, small_part)
+    d_kv_pair = jnp.concatenate([d_kv_low, d_kv_crossed], axis=0)
     q_sum.scatter()
     kv_part = mm_tn(hidden_columns, shard_rows_all(d_kv_pair))
     kv_sum = Summed(lines, jnp.concatenate([kv_part, small_part], axis=1))

time: 1040 us -> 1020 us (0.981)
  Pallas kernels: 153 us -> 141 us
    pallas_call x4, Pallas kernels: 63.7 us -> 53 us  [the longest x2 34.8 us: attend_back(): pl.pallas_call(kernel, grid=(heads // together,), in_specs=[by_head, by_g...]
    unnamed x481 -> x474, local copies, waits for them, and re-layouts: 45.3 us -> 40.4 us
  transfers between devices with their start and end apart: 178 -> 178, of which waited for: 77 -> 79; matrix products, arithmetic and copies ran while one was open for 22% -> 23% of each run, Pallas kernels for 12% -> 11%
where the time goes in v4:
time: 1020 us; the launch traced here: 1010 us
  waiting for transfers between devices  382 us (37%)
  starting transfers between devices  170 us (17%)
  matrix products  155 us (15%)
  Pallas kernels  141 us (14%)
  local copies, waits for them, and re-layouts  109 us (11%)
  other arithmetic  34.9 us (3%)
  between operations  18.6 us (2%)
    ppermute x46, waiting for transfers between devices, swap(): lax.ppermute(values, 'expert', [(i, i ^ 1) for i in range(self.experts)])  231 us
    dot_general x57, matrix products, mm_tn(): lax.dot_general(left, right, (((0,), (0,)), ((), ())), preferred_element_...  85.6 us
    ppermute x27, waiting for transfers between devices, even(): lax.ppermute(values, 'expert', [(i, i ^ 2) for i in range(self.experts)])  62.4 us
    dot_general x38, matrix products, mm(): return jnp.dot(left, right, preferred_element_type=f32)  58.5 us
    ppermute x27, starting transfers between devices, even(): lax.ppermute(values, 'expert', [(i, i ^ 2) for i in range(self.experts)])  49.7 us
    ppermute x24, waiting for transfers between devices, turn(): return lax.ppermute(values, 'expert', pairs)  48.1 us
    pallas_call x4, Pallas kernels, expert_backward(): pl.pallas_call(kernel, grid=(2,), in_specs=[by_row(width), by_row(hidden)...  44.2 us
    ppermute x46, starting transfers between devices, swap(): lax.ppermute(values, 'expert', [(i, i ^ 1) for i in range(self.experts)])  43.4 us
  transfers between devices with their start and end apart: 178, of which 79 were waited for; matrix products, arithmetic and copies ran while one was open for 23% of the time, Pallas kernels for 11%

profile of v4, /device:TPU:0, one launch (start us, length us, event | category | flops | bytes accessed | tf_op | source)
XLA Modules:
  0.0 1010.1 jit_solution(2442417234418830042)
XLA Ops:
  30.3 4.6 collective-permute-done.8.refs_9_
  50.2 5.2 collective-permute-start.20
  55.4 3.9 collective-permute-done.20
  80.1 3.9 shard_map.518.q_ref
  84.0 9.0 shard_map.519
  93.1 4.6 multiply_reduce_fusion.8
  119.6 6.6 collective-permute-done.26
  130.9 12.2 %collective-permute-done.29 = bf16[160,1536]{1,0:T(8,128)(2,1)S(1)} collective-permute-done((bf16[160,1536]{1,0:T(8,128)(2,1)S(1)}, bf16[160,1536]{1,0:T(8,128)(2,1)S(1)}, u32[]{:S(2)}, u32[]{:S(2)}) %collective-permute-start.29) | collective-permute-done | bytes 491552 | tf_op jit(solution)/shard_map/ppermute | solution.py:451
  150.0 10.0 collective-permute-done.31
  160.0 4.4 collective-permute-done.30
  166.9 9.7 collective-permute-done.32
  179.7 9.7 shard_map.520
  197.8 9.2 shard_map.521
  218.2 6.9 collective-permute-done.38
  234.8 10.0 collective-permute-done.40
  251.0 12.8 %collective-permute-done.43 = bf16[160,1536]{1,0:T(8,128)(2,1)S(1)} collective-permute-done((bf16[160,1536]{1,0:T(8,128)(2,1)S(1)}, bf16[160,1536]{1,0:T(8,128)(2,1)S(1)}, u32[]{:S(2)}, u32[]{:S(2)}) %collective-permute-start.43) | collective-permute-done | bytes 491552 | tf_op jit(solution)/shard_map/ppermute | solution.py:451
  263.8 4.4 collective-permute-done.44
  288.9 9.2 shard_map.523
  300.8 4.5 multiply_reduce_fusion.6
  316.4 7.9 collective-permute-done.52
  335.4 8.6 collective-permute-done.55
  354.2 6.0 collective-permute-done.57
  360.2 4.1 collective-permute-done.56
  370.4 5.5 collective-permute-done.58
  376.0 9.2 shard_map.524
  389.0 9.4 shard_map.525
  405.3 10.7 %shard_map.526 = (bf16[640,1664]{1,0:T(8,128)(2,1)S(1)}, bf16[1280,1536]{1,0:T(8,128)(2,1)S(1)}) custom-call(bf16[1280,1536]{1,0:T(8,128)(2,1)S(1)} %constant_dynamic-update-slice_fusion.5.d_ref, bf16[1280,768]{1,0:T(8,128)(2,1)S(1)} %copy-done.14, bf16[1280,768]{1,0:T(8,128)(2,1)S(1)} %copy-done.16, f32[1280,1]{1,0:T(8,128)S(1)} %get-tuple-element.682.gate_ref, ...), custom_call_target="tpu_custom_call" | custom-call | flops 4529848320 | bytes 16908288 | tf_op jit(solution)/shard_map/pallas_call | solution.py:377
  421.6 11.1 %shard_map.527 = (bf16[640,1664]{1,0:T(8,128)(2,1)S(1)}, bf16[1280,1536]{1,0:T(8,128)(2,1)S(1)}) custom-call(bf16[1280,1536]{1,0:T(8,128)(2,1)S(1)} %constant_dynamic-update-slice_fusion.5.d_ref, bf16[1280,768]{1,0:T(8,128)(2,1)S(1)} %copy-done.14, bf16[1280,768]{1,0:T(8,128)(2,1)S(1)} %copy-done.16, ...), custom_call_target="tpu_custom_call", output_to_operand_aliasing={{1}: (8, {})} | custom-call | flops 4529848320 | bytes 16908288 | tf_op jit(solution)/shard_map/pallas_call | solution.py:377
  445.3 4.4 constant_dynamic-slice_fusion.34
  451.9 7.6 collective-permute-done.62
  459.5 5.6 collective-permute-done.63
  466.4 4.2 fusion.19
  480.7 4.1 constant_dynamic-slice_fusion.16
  486.3 7.9 collective-permute-done.65
  494.2 4.7 collective-permute-done.66
  509.7 9.9 collective-permute-done.71
  536.6 17.3 %shard_map.528 = (bf16[256,1536]{1,0:T(8,128)(2,1)S(1)}, bf16[1024,512]{1,0:T(8,128)(2,1)S(1)}) custom-call(bf16[256,1536]{1,0:T(8,128)(2,1)S(1)} %copy-done.60, bf16[1024,512]{1,0:T(8,128)(2,1)S(1)} %copy-done.54, bf16[256,1536]{1,0:T(8,128)(2,1)S(1)} %fusion.35.dm_ref, f32[256,128]{1,0:T(8,128)S(1)} %get-tuple-element.492.refs_12_.cos_ref.refs_2_, ...), custom_call_target="tpu_custom_call" | custom-call | flops 8053063680 | bytes 3145728 | tf_op jit(solution)/shard_map/pallas_call | solution.py:236
  569.2 4.5 collective-permute-done.82.second_ref
  581.8 6.7 collective-permute-done.86
  593.7 4.0 collective-permute-done.92
  622.1 7.0 collective-permute-done.96
  642.2 6.1 collective-permute-done.103
  661.1 13.1 %collective-permute-done.109 = bf16[192,640]{1,0:T(8,128)(2,1)S(1)} collective-permute-done((bf16[192,640]{1,0:T(8,128)(2,1)S(1)}, bf16[192,640]{1,0:T(8,128)(2,1)S(1)}, u32[]{:S(2)}, u32[]{:S(2)}) %collective-permute-start.109) | collective-permute-done | bytes 245792 | tf_op jit(solution)/shard_map/ppermute | solution.py:451
  676.0 11.0 %shard_map.530 = (bf16[640,1664]{1,0:T(8,128)(2,1)S(1)}, bf16[1280,1536]{1,0:T(8,128)(2,1)S(1)}) custom-call(bf16[1280,1536]{1,0:T(8,128)(2,1)} %constant_dynamic-update-slice_fusion.d_ref, bf16[1280,768]{1,0:T(8,128)(2,1)S(1)} %get-tuple-element.802.pre_ref, bf16[1280,768]{1,0:T(8,128)(2,1)S(1)} %copy-done.12, f32[1280,1]{1,0:T(8,128)S(1)} %copy-done.25, ...), custom_call_target="tpu_custom_call" | custom-call | flops 4529848320 | bytes 16908288 | tf_op jit(solution)/shard_map/pallas_call | solution.py:377
  695.0 11.3 %shard_map.531 = (bf16[640,1664]{1,0:T(8,128)(2,1)S(1)}, bf16[1280,1536]{1,0:T(8,128)(2,1)S(1)}) custom-call(bf16[1280,1536]{1,0:T(8,128)(2,1)} %constant_dynamic-update-slice_fusion.d_ref, bf16[1280,768]{1,0:T(8,128)(2,1)S(1)} %get-tuple-element.802.pre_ref, bf16[1280,768]{1,0:T(8,128)(2,1)S(1)} %copy-done.12, ...), custom_call_target="tpu_custom_call", output_to_operand_aliasing={{1}: (8, {})} | custom-call | flops 4529848320 | bytes 16908288 | tf_op jit(solution)/shard_map/pallas_call | solution.py:377
  706.3 9.7 collective-permute-done.112
  725.7 7.1 collective-permute-start.115
  737.5 12.3 %collective-permute-done.114 = bf16[160,1664]{1,0:T(8,128)(2,1)S(1)} collective-permute-done((bf16[160,1664]{1,0:T(8,128)(2,1)S(1)}, bf16[160,1664]{1,0:T(8,128)(2,1)S(1)}, u32[]{:S(2)}, u32[]{:S(2)}) %collective-permute-start.114) | collective-permute-done | bytes 532512 | tf_op jit(solution)/shard_map/ppermute | solution.py:451
  769.2 11.3 %collective-permute-done.117 = bf16[160,1664]{1,0:T(8,128)(2,1)S(1)} collective-permute-done((bf16[160,1664]{1,0:T(8,128)(2,1)S(1)}, bf16[160,1664]{1,0:T(8,128)(2,1)S(1)}, u32[]{:S(2)}, u32[]{:S(2)}) %collective-permute-start.117) | collective-permute-done | bytes 532512 | tf_op jit(solution)/shard_map/ppermute | solution.py:451
  793.3 9.8 collective-permute-done.123
  814.6 17.5 %shard_map.532 = (bf16[256,1536]{1,0:T(8,128)(2,1)S(1)}, bf16[1024,512]{1,0:T(8,128)(2,1)S(1)}) custom-call(bf16[256,1536]{1,0:T(8,128)(2,1)S(1)} %copy-done.58, bf16[1024,512]{1,0:T(8,128)(2,1)S(1)} %copy-done.41, bf16[256,1536]{1,0:T(8,128)(2,1)S(1)} %convolution_convert_fusion.4.dm_ref, f32[256,128]{1,0:T(8,128)S(1)} %get-tuple-element.492.refs_12_.cos_ref.refs_2_, ...), custom_call_target="tpu_custom_call" | custom-call | flops 8053063680 | bytes 3145728 | tf_op jit(solution)/shard_map/pallas_call | solution.py:236
  832.1 7.1 collective-permute-done.126
  854.1 4.6 collective-permute-done.129.second_ref
  863.2 16.6 %collective-permute-done.135 = bf16[48,3712]{1,0:T(8,128)(2,1)S(1)} collective-permute-done((bf16[48,3712]{1,0:T(8,128)(2,1)}, bf16[48,3712]{1,0:T(8,128)(2,1)S(1)}, u32[]{:S(2)}, u32[]{:S(2)}) %collective-permute-start.135) | collective-permute-done | bytes 356384 | tf_op jit(solution)/shard_map/ppermute | solution.py:533
  896.9 4.0 collective-permute-done.144
  915.9 5.7 collective-permute-done.150
  922.0 6.9 collective-permute-done.151
  936.8 4.1 collective-permute-start.161
  949.0 5.6 collective-permute-done.165
  957.7 4.2 collective-permute-start.160
  968.8 5.3 collective-permute-start.167
  977.1 6.8 collective-permute-done.170
  983.9 9.0 collective-permute-done.166
  994.5 5.5 collective-permute-done.171
  (1126 shorter events, 495.4 us)
Async XLA Ops:
  7.2 85.9 %all-gather.15.cloned.1.call-start = ((), (), s32[]{:S(2)}) async-start(), calls=%async_computation.2 | async-start | bytes 5898240 | tf_op jit(solution)/shard_map/all_gather | solution.py:904
  12.4 24.6 %collective-permute-start = (bf16[256,1536]{1,0:T(8,128)(2,1)}, bf16[256,1536]{1,0:T(8,128)(2,1)}, u32[]{:S(2)}, u32[]{:S(2)}) collective-permute-start(bf16[256,1536]{1,0:T(8,128)(2,1)} %param.50), channel_id=1, source_target_pairs={{0,8},{4,12},{8,0},{12,4},{16,24},{20,28},{24,16},{28,20},{1,9},{5... | collective-permute-start | bytes 2359304 | tf_op jit(solution)/shard_map/ppermute | solution.py:454
  40.2 233.6 %all-gather.11.cloned.1.call-start = ((), (), s32[]{:S(2)}) async-start(), calls=%async_computation | async-start | bytes 1966080 | tf_op jit(solution)/shard_map/all_gather | solution.py:904
  41.5 25.4 %collective-permute-start.11 = (bf16[192,1536]{1,0:T(8,128)(2,1)}, bf16[192,1536]{1,0:T(8,128)(2,1)}, u32[]{:S(2)}, u32[]{:S(2)}) collective-permute-start(bf16[192,1536]{1,0:T(8,128)(2,1)} %collective-permute-done.6.refs_8_), channel_id=1, source_target_pairs={{0,4},{4,0},{8,12},{12,8},{16,20},{20,16},{24,28},{28,24},{1,5},{5... | collective-permute-start | bytes 1769480 | tf_op jit(solution)/shard_map/ppermute | solution.py:451
  43.1 23.8 %collective-permute-start.12 = (bf16[192,1536]{1,0:T(8,128)(2,1)}, bf16[192,1536]{1,0:T(8,128)(2,1)}, u32[]{:S(2)}, u32[]{:S(2)}) collective-permute-start(bf16[192,1536]{1,0:T(8,128)(2,1)} %collective-permute-done.6.refs_8_), channel_id=1, source_target_pairs={{0,1},{1,0},{2,3},{3,2},{4,5},{5,4},{6,7},{7,6},{8,9},{9,8},{10,11... | collective-permute-start | bytes 1769480 | tf_op jit(solution)/shard_map/ppermute | solution.py:537
  74.6 23.4 %collective-permute-start.17 = (bf16[256,1536]{1,0:T(8,128)(2,1)}, bf16[256,1536]{1,0:T(8,128)(2,1)}, u32[]{:S(2)}, u32[]{:S(2)}) collective-permute-start(bf16[256,1536]{1,0:T(8,128)(2,1)} %copy-done.135), channel_id=1, source_target_pairs={{0,8},{4,12},{8,0},{12,4},{16,24},{20,28},{24,16},{28,20},{1,9},{5... | collective-permute-start | bytes 2359304 | tf_op jit(solution)/shard_map/ppermute | solution.py:454
  76.2 22.0 %collective-permute-start.18 = (bf16[256,1536]{1,0:T(8,128)(2,1)}, bf16[256,1536]{1,0:T(8,128)(2,1)}, u32[]{:S(2)}, u32[]{:S(2)}) collective-permute-start(bf16[256,1536]{1,0:T(8,128)(2,1)} %collective-permute-done), channel_id=1, source_target_pairs={{0,1},{1,0},{2,3},{3,2},{4,5},{5,4},{6,7},{7,6},{8,16},{9,17},{10,... | collective-permute-start | bytes 2359304 | tf_op jit(solution)/shard_map/ppermute | solution.py:466
  101.3 176.9 %all-gather.17.cloned.1.call-start = ((), (), s32[]{:S(2)}) async-start(), calls=%async_computation.3 | async-start | bytes 5898240 | tf_op jit(solution)/shard_map/all_gather | solution.py:904
  104.7 196.1 %all-gather.19.cloned.1.call-start = ((), (), s32[]{:S(2)}) async-start(), calls=%async_computation.4 | async-start | bytes 5898240 | tf_op jit(solution)/shard_map/all_gather | solution.py:904
  105.9 201.7 %all-gather.13.cloned.1.call-start = ((), (), s32[]{:S(2)}) async-start(), calls=%async_computation.1 | async-start | bytes 1966080 | tf_op jit(solution)/shard_map/all_gather | solution.py:904
  106.6 20.0 %collective-permute-start.24 = (bf16[256,1536]{1,0:T(8,128)(2,1)S(1)}, bf16[256,1536]{1,0:T(8,128)(2,1)S(1)}, u32[]{:S(2)}, u32[]{:S(2)}) collective-permute-start(bf16[256,1536]{1,0:T(8,128)(2,1)S(1)} %multiply_convert_fusion.2), channel_id=1, source_target_pairs={{0,8},{4,12},{8,0},{12,4},{16,24},{20,28},{24,16},{28,20},{1,9},{5... | collective-permute-start | bytes 2359304 | tf_op jit(solution)/shard_map/ppermute | solution.py:454
  110.7 196.9 %all-gather.21.cloned.1.call-start = ((), (), s32[]{:S(2)}) async-start(), calls=%async_computation.5 | async-start | bytes 5898240 | tf_op jit(solution)/shard_map/all_gather | solution.py:904
  126.6 19.4 %collective-permute-start.27 = (bf16[256,1536]{1,0:T(8,128)(2,1)}, bf16[256,1536]{1,0:T(8,128)(2,1)S(1)}, u32[]{:S(2)}, u32[]{:S(2)}) collective-permute-start(bf16[256,1536]{1,0:T(8,128)(2,1)} %collective-permute-done.25), channel_id=1, source_target_pairs={{0,8},{4,12},{8,0},{12,4},{16,24},{20,28},{24,16},{28,20},{1,9},{5... | collective-permute-start | bytes 2359304 | tf_op jit(solution)/shard_map/ppermute | solution.py:454
  176.7 32.1 %collective-permute-start.33 = (bf16[256,1536]{1,0:T(8,128)(2,1)}, bf16[256,1536]{1,0:T(8,128)(2,1)}, u32[]{:S(2)}, u32[]{:S(2)}) collective-permute-start(bf16[256,1536]{1,0:T(8,128)(2,1)} %collective-permute-done.18), channel_id=1, source_target_pairs={{0,8},{4,12},{8,0},{12,4},{16,24},{20,28},{24,16},{28,20},{1,9},{5... | collective-permute-start | bytes 2359304 | tf_op jit(solution)/shard_map/ppermute | solution.py:454
  177.6 29.4 %collective-permute-start.34 = (bf16[160,1536]{1,0:T(8,128)(2,1)}, bf16[160,1536]{1,0:T(8,128)(2,1)}, u32[]{:S(2)}, u32[]{:S(2)}) collective-permute-start(bf16[160,1536]{1,0:T(8,128)(2,1)} %convolution_convert_fusion.38), channel_id=1, source_target_pairs={{0,4},{4,0},{8,12},{12,8},{16,20},{20,16},{24,28},{28,24},{1,5},{5... | collective-permute-start | bytes 1474568 | tf_op jit(solution)/shard_map/ppermute | solution.py:451
  178.1 28.9 %collective-permute-start.35 = (bf16[160,1536]{1,0:T(8,128)(2,1)}, bf16[160,1536]{1,0:T(8,128)(2,1)}, u32[]{:S(2)}, u32[]{:S(2)}) collective-permute-start(bf16[160,1536]{1,0:T(8,128)(2,1)} %convolution_convert_fusion.35), channel_id=1, source_target_pairs={{0,4},{4,0},{8,12},{12,8},{16,20},{20,16},{24,28},{28,24},{1,5},{5... | collective-permute-start | bytes 1474568 | tf_op jit(solution)/shard_map/ppermute | solution.py:451
  285.7 21.9 %collective-permute-start.49 = (bf16[160,1536]{1,0:T(8,128)(2,1)}, bf16[160,1536]{1,0:T(8,128)(2,1)}, u32[]{:S(2)}, u32[]{:S(2)}) collective-permute-start(bf16[160,1536]{1,0:T(8,128)(2,1)} %convolution_convert_fusion.29), channel_id=1, source_target_pairs={{0,4},{4,0},{8,12},{12,8},{16,20},{20,16},{24,28},{28,24},{1,5},{5... | collective-permute-start | bytes 1474568 | tf_op jit(solution)/shard_map/ppermute | solution.py:451
  307.6 19.9 %collective-permute-start.50 = (bf16[256,1536]{1,0:T(8,128)(2,1)}, bf16[256,1536]{1,0:T(8,128)(2,1)S(1)}, u32[]{:S(2)}, u32[]{:S(2)}) collective-permute-start(bf16[256,1536]{1,0:T(8,128)(2,1)} %multiply_convert_fusion), channel_id=1, source_target_pairs={{0,8},{4,12},{8,0},{12,4},{16,24},{20,28},{24,16},{28,20},{1,9},{5... | collective-permute-start | bytes 2359304 | tf_op jit(solution)/shard_map/ppermute | solution.py:454
  441.0 24.2 %collective-permute-start.64 = (bf16[768,1536]{1,0:T(8,128)(2,1)}, bf16[768,1536]{1,0:T(8,128)(2,1)}, u32[]{:S(2)}, u32[]{:S(2)}) collective-permute-start(bf16[768,1536]{1,0:T(8,128)(2,1)} %pad_maximum_fusion.3), channel_id=1, source_target_pairs={{0,1},{1,0},{2,3},{3,2},{4,5},{5,4},{6,7},{7,6},{8,9},{9,8},{10,11... | collective-permute-start | bytes 7077896 | tf_op jit(solution)/shard_map/ppermute | solution.py:537
  443.5 21.7 %collective-permute-start.63 = (bf16[256,1664]{1,0:T(8,128)(2,1)}, bf16[256,1664]{1,0:T(8,128)(2,1)}, u32[]{:S(2)}, u32[]{:S(2)}) collective-permute-start(bf16[256,1664]{1,0:T(8,128)(2,1)} %get-tuple-element.1190), channel_id=1, source_target_pairs={{0,8},{4,12},{8,0},{12,4},{16,24},{20,28},{24,16},{28,20},{1,9},{5... | collective-permute-start | bytes 2555912 | tf_op jit(solution)/shard_map/ppermute | solution.py:454
  449.8 29.9 %collective-permute-start.70 = (bf16[160,1536]{1,0:T(8,128)(2,1)}, bf16[160,1536]{1,0:T(8,128)(2,1)}, u32[]{:S(2)}, u32[]{:S(2)}) collective-permute-start(bf16[160,1536]{1,0:T(8,128)(2,1)} %get-tuple-element.715), channel_id=1, source_target_pairs={{0,4},{4,0},{8,12},{12,8},{16,20},{20,16},{24,28},{28,24},{1,5},{5... | collective-permute-start | bytes 1474568 | tf_op jit(solution)/shard_map/ppermute | solution.py:451
  470.6 28.4 %collective-permute-start.68 = (bf16[384,1536]{1,0:T(8,128)(2,1)}, bf16[384,1536]{1,0:T(8,128)(2,1)}, u32[]{:S(2)}, u32[]{:S(2)}) collective-permute-start(bf16[384,1536]{1,0:T(8,128)(2,1)} %fusion.19), channel_id=1, source_target_pairs={{0,2},{1,3},{2,0},{3,1},{4,6},{5,7},{6,4},{7,5},{8,10},{9,11},{10,... | collective-permute-start | bytes 3538952 | tf_op jit(solution)/shard_map/ppermute | solution.py:541
  474.3 24.7 %collective-permute-start.69 = (bf16[384,1536]{1,0:T(8,128)(2,1)}, bf16[384,1536]{1,0:T(8,128)(2,1)}, u32[]{:S(2)}, u32[]{:S(2)}) collective-permute-start(bf16[384,1536]{1,0:T(8,128)(2,1)} %pad_maximum_fusion.9), channel_id=1, source_target_pairs={{0,1},{1,0},{2,3},{3,2},{4,5},{5,4},{6,7},{7,6},{8,9},{9,8},{10,11... | collective-permute-start | bytes 3538952 | tf_op jit(solution)/shard_map/ppermute | solution.py:537
  477.3 21.7 %collective-permute-start.66 = (bf16[256,1664]{1,0:T(8,128)(2,1)}, bf16[256,1664]{1,0:T(8,128)(2,1)}, u32[]{:S(2)}, u32[]{:S(2)}) collective-permute-start(bf16[256,1664]{1,0:T(8,128)(2,1)} %get-tuple-element.1087), channel_id=1, source_target_pairs={{0,8},{4,12},{8,0},{12,4},{16,24},{20,28},{24,16},{28,20},{1,9},{5... | collective-permute-start | bytes 2555912 | tf_op jit(solution)/shard_map/ppermute | solution.py:454
  478.2 20.8 %collective-permute-start.67 = (bf16[256,1664]{1,0:T(8,128)(2,1)}, bf16[256,1664]{1,0:T(8,128)(2,1)}, u32[]{:S(2)}, u32[]{:S(2)}) collective-permute-start(bf16[256,1664]{1,0:T(8,128)(2,1)} %get-tuple-element.1086), channel_id=1, source_target_pairs={{0,1},{1,0},{2,3},{3,2},{4,5},{5,4},{6,7},{7,6},{8,16},{9,17},{10,... | collective-permute-start | bytes 2555912 | tf_op jit(solution)/shard_map/ppermute | solution.py:466
  502.7 20.6 %collective-permute-start.72 = (bf16[256,1664]{1,0:T(8,128)(2,1)S(1)}, bf16[256,1664]{1,0:T(8,128)(2,1)S(1)}, u32[]{:S(2)}, u32[]{:S(2)}) collective-permute-start(bf16[256,1664]{1,0:T(8,128)(2,1)S(1)} %get-tuple-element.1085), channel_id=1, source_target_pairs={{0,8},{4,12},{8,0},{12,4},{16,24},{20,28},{24,16},{28,20},{1,9},{5... | collective-permute-start | bytes 2555912 | tf_op jit(solution)/shard_map/ppermute | solution.py:454
  508.3 27.1 %collective-permute-start.78 = (bf16[192,1536]{1,0:T(8,128)(2,1)S(1)}, bf16[192,1536]{1,0:T(8,128)(2,1)S(1)}, u32[]{:S(2)}, u32[]{:S(2)}) collective-permute-start(bf16[192,1536]{1,0:T(8,128)(2,1)S(1)} %fusion.42), channel_id=1, source_target_pairs={{0,2},{1,3},{2,0},{3,1},{4,6},{5,7},{6,4},{7,5},{8,10},{9,11},{10,... | collective-permute-start | bytes 1769480 | tf_op jit(solution)/shard_map/ppermute | solution.py:541
  523.4 30.5 %collective-permute-start.74 = (bf16[160,1536]{1,0:T(8,128)(2,1)S(1)}, bf16[160,1536]{1,0:T(8,128)(2,1)S(1)}, u32[]{:S(2)}, u32[]{:S(2)}) collective-permute-start(bf16[160,1536]{1,0:T(8,128)(2,1)S(1)} %copy-done.163), channel_id=1, source_target_pairs={{0,4},{4,0},{8,12},{12,8},{16,20},{20,16},{24,28},{28,24},{1,5},{5... | collective-permute-start | bytes 1474568 | tf_op jit(solution)/shard_map/ppermute | solution.py:451
  526.3 27.7 %collective-permute-start.76 = (bf16[256,1536]{1,0:T(8,128)(2,1)S(1)}, bf16[256,1536]{1,0:T(8,128)(2,1)S(1)}, u32[]{:S(2)}, u32[]{:S(2)}) collective-permute-start(bf16[256,1536]{1,0:T(8,128)(2,1)S(1)} %get-tuple-element.1091), channel_id=1, source_target_pairs={{0,8},{4,12},{8,0},{12,4},{16,24},{20,28},{24,16},{28,20},{1,9},{5... | collective-permute-start | bytes 2359304 | tf_op jit(solution)/shard_map/ppermute | solution.py:454
  528.1 25.9 %collective-permute-start.77 = (bf16[256,1536]{1,0:T(8,128)(2,1)S(1)}, bf16[256,1536]{1,0:T(8,128)(2,1)S(1)}, u32[]{:S(2)}, u32[]{:S(2)}) collective-permute-start(bf16[256,1536]{1,0:T(8,128)(2,1)S(1)} %get-tuple-element.1090), channel_id=1, source_target_pairs={{0,1},{1,0},{2,3},{3,2},{4,5},{5,4},{6,7},{7,6},{8,16},{9,17},{10,... | collective-permute-start | bytes 2359304 | tf_op jit(solution)/shard_map/ppermute | solution.py:466
  532.6 21.4 %collective-permute-start.79 = (bf16[256,1536]{1,0:T(8,128)(2,1)S(1)}, bf16[256,1536]{1,0:T(8,128)(2,1)S(1)}, u32[]{:S(2)}, u32[]{:S(2)}) collective-permute-start(bf16[256,1536]{1,0:T(8,128)(2,1)S(1)} %fusion.182), channel_id=1, source_target_pairs={{0,2},{1,3},{2,0},{3,1},{4,6},{5,7},{6,4},{7,5},{8,10},{9,11},{10,... | collective-permute-start | bytes 2359304 | tf_op jit(solution)/shard_map/ppermute | solution.py:541
  562.4 19.4 %collective-permute-start.87 = (bf16[256,1536]{1,0:T(8,128)(2,1)S(1)}, bf16[256,1536]{1,0:T(8,128)(2,1)S(1)}, u32[]{:S(2)}, u32[]{:S(2)}) collective-permute-start(bf16[256,1536]{1,0:T(8,128)(2,1)S(1)} %get-tuple-element.1089), channel_id=1, source_target_pairs={{0,8},{4,12},{8,0},{12,4},{16,24},{20,28},{24,16},{28,20},{1,9},{5... | collective-permute-start | bytes 2359304 | tf_op jit(solution)/shard_map/ppermute | solution.py:454
  577.2 20.5 %collective-permute-start.92 = (bf16[256,1536]{1,0:T(8,128)(2,1)S(1)}, bf16[256,1536]{1,0:T(8,128)(2,1)S(1)}, u32[]{:S(2)}, u32[]{:S(2)}) collective-permute-start(bf16[256,1536]{1,0:T(8,128)(2,1)S(1)} %get-tuple-element.777), channel_id=1, source_target_pairs={{0,2},{1,3},{2,0},{3,1},{4,6},{5,7},{6,4},{7,5},{8,10},{9,11},{10,... | collective-permute-start | bytes 2359304 | tf_op jit(solution)/shard_map/ppermute | solution.py:541
  637.5 23.6 %collective-permute-start.108 = (bf16[192,1536]{1,0:T(8,128)(2,1)}, bf16[192,1536]{1,0:T(8,128)(2,1)}, u32[]{:S(2)}, u32[]{:S(2)}) collective-permute-start(bf16[192,1536]{1,0:T(8,128)(2,1)} %dynamic-slice_convert_fusion.2), channel_id=1, source_target_pairs={{0,4},{4,0},{8,12},{12,8},{16,20},{20,16},{24,28},{28,24},{1,5},{5... | collective-permute-start | bytes 1769480 | tf_op jit(solution)/shard_map/ppermute | solution.py:451
  651.3 22.8 %collective-permute-start.104 = (bf16[160,1536]{1,0:T(8,128)(2,1)}, bf16[160,1536]{1,0:T(8,128)(2,1)}, u32[]{:S(2)}, u32[]{:S(2)}) collective-permute-start(bf16[160,1536]{1,0:T(8,128)(2,1)} %convolution_convert_fusion.9), channel_id=1, source_target_pairs={{0,4},{4,0},{8,12},{12,8},{16,20},{20,16},{24,28},{28,24},{1,5},{5... | collective-permute-start | bytes 1474568 | tf_op jit(solution)/shard_map/ppermute | solution.py:451
  688.3 27.8 %collective-permute-start.110 = (bf16[160,1664]{1,0:T(8,128)(2,1)S(1)}, bf16[160,1664]{1,0:T(8,128)(2,1)S(1)}, u32[]{:S(2)}, u32[]{:S(2)}) collective-permute-start(bf16[160,1664]{1,0:T(8,128)(2,1)S(1)} %get-tuple-element.1050), channel_id=1, source_target_pairs={{0,4},{4,0},{8,12},{12,8},{16,20},{20,16},{24,28},{28,24},{1,5},{5... | collective-permute-start | bytes 1597448 | tf_op jit(solution)/shard_map/ppermute | solution.py:451
  691.2 24.8 %collective-permute-start.112 = (bf16[48,3712]{1,0:T(8,128)(2,1)S(1)}, bf16[48,3712]{1,0:T(8,128)(2,1)S(1)}, u32[]{:S(2)}, u32[]{:S(2)}) collective-permute-start(bf16[48,3712]{1,0:T(8,128)(2,1)S(1)} %get-tuple-element.1101), channel_id=1, source_target_pairs={{0,16},{4,20},{8,24},{12,28},{16,0},{20,4},{24,8},{28,12},{1,17},{... | collective-permute-start | bytes 1069064 | tf_op jit(solution)/shard_map/ppermute | solution.py:533
  693.8 22.2 %collective-permute-start.113 = (bf16[48,3712]{1,0:T(8,128)(2,1)S(1)}, bf16[48,3712]{1,0:T(8,128)(2,1)S(1)}, u32[]{:S(2)}, u32[]{:S(2)}) collective-permute-start(bf16[48,3712]{1,0:T(8,128)(2,1)S(1)} %get-tuple-element.1100), channel_id=1, source_target_pairs={{0,24},{4,28},{8,0},{12,4},{16,8},{20,12},{24,16},{28,20},{1,25},{... | collective-permute-start | bytes 1069064 | tf_op jit(solution)/shard_map/ppermute | solution.py:533
  720.6 31.0 %collective-permute-start.116 = (bf16[768,1536]{1,0:T(8,128)(2,1)S(1)}, bf16[768,1536]{1,0:T(8,128)(2,1)S(1)}, u32[]{:S(2)}, u32[]{:S(2)}) collective-permute-start(bf16[768,1536]{1,0:T(8,128)(2,1)S(1)} %pad_maximum_fusion.4), channel_id=1, source_target_pairs={{0,1},{1,0},{2,3},{3,2},{4,5},{5,4},{6,7},{7,6},{8,9},{9,8},{10,11... | collective-permute-start | bytes 7077896 | tf_op jit(solution)/shard_map/ppermute | solution.py:537
  725.7 25.9 %collective-permute-start.115 = (bf16[256,1664]{1,0:T(8,128)(2,1)S(1)}, bf16[256,1664]{1,0:T(8,128)(2,1)S(1)}, u32[]{:S(2)}, u32[]{:S(2)}) collective-permute-start(bf16[256,1664]{1,0:T(8,128)(2,1)S(1)} %get-tuple-element.1196), channel_id=1, source_target_pairs={{0,8},{4,12},{8,0},{12,4},{16,24},{20,28},{24,16},{28,20},{1,9},{5... | collective-permute-start | bytes 2555912 | tf_op jit(solution)/shard_map/ppermute | solution.py:454
  753.8 29.5 %collective-permute-start.120 = (bf16[384,1536]{1,0:T(8,128)(2,1)S(1)}, bf16[384,1536]{1,0:T(8,128)(2,1)S(1)}, u32[]{:S(2)}, u32[]{:S(2)}) collective-permute-start(bf16[384,1536]{1,0:T(8,128)(2,1)S(1)} %fusion.20), channel_id=1, source_target_pairs={{0,2},{1,3},{2,0},{3,1},{4,6},{5,7},{6,4},{7,5},{8,10},{9,11},{10,... | collective-permute-start | bytes 3538952 | tf_op jit(solution)/shard_map/ppermute | solution.py:541
  761.3 22.0 %collective-permute-start.121 = (bf16[384,1536]{1,0:T(8,128)(2,1)S(1)}, bf16[384,1536]{1,0:T(8,128)(2,1)S(1)}, u32[]{:S(2)}, u32[]{:S(2)}) collective-permute-start(bf16[384,1536]{1,0:T(8,128)(2,1)S(1)} %pad_maximum_fusion.10), channel_id=1, source_target_pairs={{0,1},{1,0},{2,3},{3,2},{4,5},{5,4},{6,7},{7,6},{8,9},{9,8},{10,11... | collective-permute-start | bytes 3538952 | tf_op jit(solution)/shard_map/ppermute | solution.py:537
  761.9 21.4 %collective-permute-start.118 = (bf16[256,1664]{1,0:T(8,128)(2,1)S(1)}, bf16[256,1664]{1,0:T(8,128)(2,1)S(1)}, u32[]{:S(2)}, u32[]{:S(2)}) collective-permute-start(bf16[256,1664]{1,0:T(8,128)(2,1)S(1)} %get-tuple-element.1083), channel_id=1, source_target_pairs={{0,8},{4,12},{8,0},{12,4},{16,24},{20,28},{24,16},{28,20},{1,9},{5... | collective-permute-start | bytes 2555912 | tf_op jit(solution)/shard_map/ppermute | solution.py:454
  763.7 19.6 %collective-permute-start.119 = (bf16[256,1664]{1,0:T(8,128)(2,1)S(1)}, bf16[256,1664]{1,0:T(8,128)(2,1)S(1)}, u32[]{:S(2)}, u32[]{:S(2)}) collective-permute-start(bf16[256,1664]{1,0:T(8,128)(2,1)S(1)} %get-tuple-element.1082), channel_id=1, source_target_pairs={{0,1},{1,0},{2,3},{3,2},{4,5},{5,4},{6,7},{7,6},{8,16},{9,17},{10,... | collective-permute-start | bytes 2555912 | tf_op jit(solution)/shard_map/ppermute | solution.py:466
  780.5 69.6 %collective-permute-start.132 = (bf16[256,384]{1,0:T(8,128)(2,1)}, bf16[256,384]{1,0:T(8,128)(2,1)}, u32[]{:S(2)}, u32[]{:S(2)}) collective-permute-start(bf16[256,384]{1,0:T(8,128)(2,1)} %get-tuple-element.1112), channel_id=1, source_target_pairs={{0,3},{1,2},{2,1},{3,0},{4,7},{5,6},{6,5},{7,4},{8,11},{9,10},{10,... | collective-permute-start | bytes 589832 | tf_op jit(solution)/shard_map/ppermute | solution.py:593
  783.3 67.4 %collective-permute-start.131 = (bf16[256,384]{1,0:T(8,128)(2,1)}, bf16[256,384]{1,0:T(8,128)(2,1)}, u32[]{:S(2)}, u32[]{:S(2)}) collective-permute-start(bf16[256,384]{1,0:T(8,128)(2,1)} %get-tuple-element.1113), channel_id=1, source_target_pairs={{0,1},{1,0},{2,3},{3,2},{4,5},{5,4},{6,7},{7,6},{8,9},{9,8},{10,11... | collective-permute-start | bytes 589832 | tf_op jit(solution)/shard_map/ppermute | solution.py:593
  785.4 21.4 %collective-permute-start.124 = (bf16[256,1664]{1,0:T(8,128)(2,1)S(1)}, bf16[256,1664]{1,0:T(8,128)(2,1)S(1)}, u32[]{:S(2)}, u32[]{:S(2)}) collective-permute-start(bf16[256,1664]{1,0:T(8,128)(2,1)S(1)} %get-tuple-element.1081), channel_id=1, source_target_pairs={{0,8},{4,12},{8,0},{12,4},{16,24},{20,28},{24,16},{28,20},{1,9},{5... | collective-permute-start | bytes 2555912 | tf_op jit(solution)/shard_map/ppermute | solution.py:454
  787.3 20.4 %collective-permute-start.125 = (bf16[256,1664]{1,0:T(8,128)(2,1)S(1)}, bf16[256,1664]{1,0:T(8,128)(2,1)S(1)}, u32[]{:S(2)}, u32[]{:S(2)}) collective-permute-start(bf16[256,1664]{1,0:T(8,128)(2,1)S(1)} %get-tuple-element.1080), channel_id=1, source_target_pairs={{0,1},{1,0},{2,3},{3,2},{4,5},{5,4},{6,7},{7,6},{8,16},{9,17},{10,... | collective-permute-start | bytes 2555912 | tf_op jit(solution)/shard_map/ppermute | solution.py:466
  803.1 48.5 %collective-permute-start.130 = (bf16[256,384]{1,0:T(8,128)(2,1)}, bf16[256,384]{1,0:T(8,128)(2,1)}, u32[]{:S(2)}, u32[]{:S(2)}) collective-permute-start(bf16[256,384]{1,0:T(8,128)(2,1)} %get-tuple-element.1114), channel_id=1, source_target_pairs={{0,2},{1,3},{2,0},{3,1},{4,6},{5,7},{6,4},{7,5},{8,10},{9,11},{10,... | collective-permute-start | bytes 589832 | tf_op jit(solution)/shard_map/ppermute | solution.py:593
  806.8 25.3 %collective-permute-start.122 = (bf16[192,1536]{1,0:T(8,128)(2,1)S(1)}, bf16[192,1536]{1,0:T(8,128)(2,1)S(1)}, u32[]{:S(2)}, u32[]{:S(2)}) collective-permute-start(bf16[192,1536]{1,0:T(8,128)(2,1)S(1)} %fusion.43), channel_id=1, source_target_pairs={{0,2},{1,3},{2,0},{3,1},{4,6},{5,7},{6,4},{7,5},{8,10},{9,11},{10,... | collective-permute-start | bytes 1769480 | tf_op jit(solution)/shard_map/ppermute | solution.py:541
  811.9 27.2 %collective-permute-start.126 = (bf16[256,1536]{1,0:T(8,128)(2,1)S(1)}, bf16[256,1536]{1,0:T(8,128)(2,1)S(1)}, u32[]{:S(2)}, u32[]{:S(2)}) collective-permute-start(bf16[256,1536]{1,0:T(8,128)(2,1)S(1)} %get-tuple-element.1022), channel_id=1, source_target_pairs={{0,2},{1,3},{2,0},{3,1},{4,6},{5,7},{6,4},{7,5},{8,10},{9,11},{10,... | collective-permute-start | bytes 2359304 | tf_op jit(solution)/shard_map/ppermute | solution.py:541
  847.9 31.9 %collective-permute-start.135 = (bf16[48,3712]{1,0:T(8,128)(2,1)}, bf16[48,3712]{1,0:T(8,128)(2,1)S(1)}, u32[]{:S(2)}, u32[]{:S(2)}) collective-permute-start(bf16[48,3712]{1,0:T(8,128)(2,1)} %get-tuple-element.1021), channel_id=1, source_target_pairs={{0,16},{4,20},{8,24},{12,28},{16,0},{20,4},{24,8},{28,12},{1,17},{... | collective-permute-start | bytes 1069064 | tf_op jit(solution)/shard_map/ppermute | solution.py:533
  850.1 29.7 %collective-permute-start.136 = (bf16[48,3712]{1,0:T(8,128)(2,1)}, bf16[48,3712]{1,0:T(8,128)(2,1)S(1)}, u32[]{:S(2)}, u32[]{:S(2)}) collective-permute-start(bf16[48,3712]{1,0:T(8,128)(2,1)} %get-tuple-element.1021), channel_id=1, source_target_pairs={{0,8},{4,12},{8,16},{12,20},{16,24},{20,28},{24,0},{28,4},{1,9},{5... | collective-permute-start | bytes 1069064 | tf_op jit(solution)/shard_map/ppermute | solution.py:533
  858.8 22.0 %collective-permute-start.133 = (bf16[192,1536]{1,0:T(8,128)(2,1)S(1)}, bf16[192,1536]{1,0:T(8,128)(2,1)S(1)}, u32[]{:S(2)}, u32[]{:S(2)}) collective-permute-start(bf16[192,1536]{1,0:T(8,128)(2,1)S(1)} %dynamic-slice_convert_fusion.1), channel_id=1, source_target_pairs={{0,4},{4,0},{8,12},{12,8},{16,20},{20,16},{24,28},{28,24},{1,5},{5... | collective-permute-start | bytes 1769480 | tf_op jit(solution)/shard_map/ppermute | solution.py:451
  860.9 20.3 %collective-permute-start.140 = (bf16[256,1536]{1,0:T(8,128)(2,1)S(1)}, bf16[256,1536]{1,0:T(8,128)(2,1)S(1)}, u32[]{:S(2)}, u32[]{:S(2)}) collective-permute-start(bf16[256,1536]{1,0:T(8,128)(2,1)S(1)} %get-tuple-element.873), channel_id=1, source_target_pairs={{0,2},{1,3},{2,0},{3,1},{4,6},{5,7},{6,4},{7,5},{8,10},{9,11},{10,... | collective-permute-start | bytes 2359304 | tf_op jit(solution)/shard_map/ppermute | solution.py:541
  863.2 21.1 %collective-permute-start.139 = (bf16[256,384]{1,0:T(8,128)(2,1)S(1)}, bf16[256,384]{1,0:T(8,128)(2,1)S(1)}, u32[]{:S(2)}, u32[]{:S(2)}) collective-permute-start(bf16[256,384]{1,0:T(8,128)(2,1)S(1)} %copy-done.183), channel_id=1, source_target_pairs={{0,3},{1,2},{2,1},{3,0},{4,7},{5,6},{6,5},{7,4},{8,11},{9,10},{10,... | collective-permute-start | bytes 589832 | tf_op jit(solution)/shard_map/ppermute | solution.py:593
  905.5 27.8 %collective-permute-start.155 = (bf16[48,1536]{1,0:T(8,128)(2,1)}, bf16[48,1536]{1,0:T(8,128)(2,1)}, u32[]{:S(2)}, u32[]{:S(2)}) collective-permute-start(bf16[48,1536]{1,0:T(8,128)(2,1)} %get-tuple-element.1017), channel_id=1, source_target_pairs={{0,24},{4,28},{8,0},{12,4},{16,8},{20,12},{24,16},{28,20},{1,25},{... | collective-permute-start | bytes 442376 | tf_op jit(solution)/shard_map/ppermute | solution.py:533
  907.3 26.0 %collective-permute-start.156 = (bf16[48,1536]{1,0:T(8,128)(2,1)}, bf16[48,1536]{1,0:T(8,128)(2,1)}, u32[]{:S(2)}, u32[]{:S(2)}) collective-permute-start(bf16[48,1536]{1,0:T(8,128)(2,1)} %get-tuple-element.1017), channel_id=1, source_target_pairs={{0,16},{4,20},{8,24},{12,28},{16,0},{20,4},{24,8},{28,12},{1,17},{... | collective-permute-start | bytes 442376 | tf_op jit(solution)/shard_map/ppermute | solution.py:533
  908.0 25.3 %collective-permute-start.157 = (bf16[48,1536]{1,0:T(8,128)(2,1)}, bf16[48,1536]{1,0:T(8,128)(2,1)}, u32[]{:S(2)}, u32[]{:S(2)}) collective-permute-start(bf16[48,1536]{1,0:T(8,128)(2,1)} %get-tuple-element.1017), channel_id=1, source_target_pairs={{0,8},{4,12},{8,16},{12,20},{16,24},{20,28},{24,0},{28,4},{1,9},{5... | collective-permute-start | bytes 442376 | tf_op jit(solution)/shard_map/ppermute | solution.py:533
  932.4 22.2 %collective-permute-start.165 = (bf16[192,2176]{1,0:T(8,128)(2,1)S(1)}, bf16[192,2176]{1,0:T(8,128)(2,1)S(1)}, u32[]{:S(2)}, u32[]{:S(2)}) collective-permute-start(bf16[192,2176]{1,0:T(8,128)(2,1)S(1)} %slice.567), channel_id=1, source_target_pairs={{0,4},{4,0},{8,12},{12,8},{16,20},{20,16},{24,28},{28,24},{1,5},{5... | collective-permute-start | bytes 2506760 | tf_op jit(solution)/shard_map/ppermute | solution.py:451
  936.8 20.9 %collective-permute-start.161 = (bf16[48,640]{1,0:T(8,128)(2,1)S(1)}, bf16[48,640]{1,0:T(8,128)(2,1)S(1)}, u32[]{:S(2)}, u32[]{:S(2)}) collective-permute-start(bf16[48,640]{1,0:T(8,128)(2,1)S(1)} %get-tuple-element.1159), channel_id=1, source_target_pairs={{0,8},{4,12},{8,16},{12,20},{16,24},{20,28},{24,0},{28,4},{1,9},{5... | collective-permute-start | bytes 184328 | tf_op jit(solution)/shard_map/ppermute | solution.py:533
  940.9 21.0 %collective-permute-start.162 = (bf16[48,640]{1,0:T(8,128)(2,1)S(1)}, bf16[48,640]{1,0:T(8,128)(2,1)S(1)}, u32[]{:S(2)}, u32[]{:S(2)}) collective-permute-start(bf16[48,640]{1,0:T(8,128)(2,1)S(1)} %get-tuple-element.1158), channel_id=1, source_target_pairs={{0,16},{4,20},{8,24},{12,28},{16,0},{20,4},{24,8},{28,12},{1,17},{... | collective-permute-start | bytes 184328 | tf_op jit(solution)/shard_map/ppermute | solution.py:533
  947.0 21.7 %collective-permute-start.164 = (bf16[192,1536]{1,0:T(8,128)(2,1)S(1)}, bf16[192,1536]{1,0:T(8,128)(2,1)S(1)}, u32[]{:S(2)}, u32[]{:S(2)}) collective-permute-start(bf16[192,1536]{1,0:T(8,128)(2,1)S(1)} %bitcast.551), channel_id=1, source_target_pairs={{0,4},{4,0},{8,12},{12,8},{16,20},{20,16},{24,28},{28,24},{1,5},{5... | collective-permute-start | bytes 1769480 | tf_op jit(solution)/shard_map/ppermute | solution.py:451
  948.9 19.8 %collective-permute-start.158 = (bf16[48,1536]{1,0:T(8,128)(2,1)S(1)}, bf16[48,1536]{1,0:T(8,128)(2,1)S(1)}, u32[]{:S(2)}, u32[]{:S(2)}) collective-permute-start(bf16[48,1536]{1,0:T(8,128)(2,1)S(1)} %get-tuple-element.1019), channel_id=1, source_target_pairs={{0,24},{4,28},{8,0},{12,4},{16,8},{20,12},{24,16},{28,20},{1,25},{... | collective-permute-start | bytes 442376 | tf_op jit(solution)/shard_map/ppermute | solution.py:533
  (347 other events, 3041.9 us)
Sparse Core Ops, SparseCore 0:
  40.3 43.8 all-gather.14
  101.4 17.2 all-gather.10
  120.3 37.4 all-gather.16
  159.1 37.4 all-gather.18
  198.1 19.6 all-gather.12
  219.7 37.4 all-gather.20

commit v5 on v4

--- a/solution.py
+++ b/solution.py
@@ -978,9 +978,7 @@
         if i == last:
             (routed, gathered[0]) = settle([late], routed, gathered[0])
         else:
-            routed, q_gated, later, near_tables = settle(
-                [late], routed, q_gated, later, near_tables
-            )
+            routed, near_tables = settle([late], routed, near_tables)
             chosen_here, row_chosen = prepare_routing(near_tables, own_table)
         if i == 0:
 
@@ -989,10 +987,6 @@
                 for at in range(0, kv_width, HEAD_SIZE):
                     parts += [later[m][k, :, at : at + HEAD_SIZE] for m in (1, 2)]
                 return jnp.concatenate(parts, axis=1)
-
-            for k in range(1, layer_count):
-                gathered.append((every(q_gated[k]), every(paired_of(k)), every(later[0][k])))
-            gathered[0] = (every(q_gated[0]), every(paired_of(0)), w_out)
         gates = chosen_softmax(mm_nt(routed, routers[i]), chosen_here)
         sent = Sent(routing, routed)
         for j in range(lines.count):
@@ -1002,7 +996,11 @@
             if i == last:
                 late.place(j)
                 late.take(j)
-            hidden, mixed = settle([sent, late], hidden, mixed)
+            hidden, mixed, q_gated, later = settle([sent, late], hidden, mixed, q_gated, later)
+            if i == 0 and j == 0:
+                for k in range(1, layer_count):
+                    gathered.append((every(q_gated[k]), every(paired_of(k)), every(later[0][k])))
+                gathered[0] = (every(q_gated[0]), every(paired_of(0)), w_out)
         columns = [own_columns(hidden), own_columns(mixed)]
         arrived = sent.total()
         if i == 0:
@@ -1041,7 +1039,13 @@
                 back.advance(j)
                 if i == last - 1 and j in (1, 2):
                     late.prepare(j + 1)
-                settle([back, late])
+                if j == 1:
+                    stored[i]["arrived_parts"] = split_columns(arrived)
+                if j == 2:
+                    stored[i]["gated_parts"] = split_columns(kept[2])
+                parts = [stored[i].get(n, ()) for n in ("arrived_parts", "gated_parts")]
+                parts = settle([back, late], parts)[0]
+                stored[i].update(zip(("arrived_parts", "gated_parts"), parts))
             stream = stream_mid + back.total()
 
     own_width = model_width // shard_count
@@ -1111,6 +1115,11 @@
                 )
                 if j == 1:
                     results, d_query = sync(results, d_query)
+                if j == 2:
+                    names = ("hidden_columns", "mixed_columns")
+                    first = [stored[0][name] for name in names]
+                    first, d_query = sync(first, d_query)
+                    stored[0].update(zip(names, first))
                 if j == lines.count - 1:
                     d_query, both_grad, down_grad = sync(d_query, both_grad, down_grad)
             put_experts(last, both_grad, down_grad)
@@ -1129,8 +1138,12 @@
         moving = [back, output_back if i == last else above]
         d_rows, d_both = settle(moving, d_rows, d_both)
         back.near(d_rows)
-        both = ShardSummed(split_columns(saved["arrived"]), d_both)
-        down = ShardSummed(split_columns(gated), d_arrived)
+        if i == last:
+            both = ShardSummed(split_columns(saved["arrived"]), d_both)
+            down = ShardSummed(split_columns(gated), d_arrived)
+        else:
+            both = ShardSummed(saved["arrived_parts"], d_both)
+            down = ShardSummed(saved["gated_parts"], d_arrived)
         for j in range(1, lines.count):
             back.advance(j)
             moving = [back, both, down]

time: 1020 us -> 1010 us (level)
  local copies, waits for them, and re-layouts: 109 us -> 90.2 us
    unnamed x474 -> x484, local copies, waits for them, and re-layouts: 40.4 us -> 28.4 us
  transfers between devices with their start and end apart: 178 -> 178, of which waited for: 79 -> 84; matrix products, arithmetic and copies ran while one was open for 23% -> 23% of each run, Pallas kernels for 11% -> 12%
where the time goes in v5:
time: 1010 us; the launch traced here: 998 us
  waiting for transfers between devices  379 us (38%)
  starting transfers between devices  177 us (18%)
  matrix products  152 us (15%)
  Pallas kernels  141 us (14%)
  local copies, waits for them, and re-layouts  90.2 us (9%)
  other arithmetic  39.6 us (4%)
  between operations  18.9 us (2%)
    ppermute x46, waiting for transfers between devices, swap(): lax.ppermute(values, 'expert', [(i, i ^ 1) for i in range(self.experts)])  229 us
    dot_general x57, matrix products, mm_tn(): lax.dot_general(left, right, (((0,), (0,)), ((), ())), preferred_element_...  80.5 us
    ppermute x27, waiting for transfers between devices, even(): lax.ppermute(values, 'expert', [(i, i ^ 2) for i in range(self.experts)])  64 us
    dot_general x38, matrix products, mm(): return jnp.dot(left, right, preferred_element_type=f32)  62.5 us
    ppermute x46, starting transfers between devices, swap(): lax.ppermute(values, 'expert', [(i, i ^ 1) for i in range(self.experts)])  47.9 us
    ppermute x27, starting transfers between devices, even(): lax.ppermute(values, 'expert', [(i, i ^ 2) for i in range(self.experts)])  47.4 us
    pallas_call x4, Pallas kernels, expert_backward(): pl.pallas_call(kernel, grid=(2,), in_specs=[by_row(width), by_row(hidden)...  44.5 us
    ppermute x24, starting transfers between devices, turn(): return lax.ppermute(values, 'expert', pairs)  42.7 us
  transfers between devices with their start and end apart: 178, of which 84 were waited for; matrix products, arithmetic and copies ran while one was open for 23% of the time, Pallas kernels for 12%

profile of v5, /device:TPU:0, one launch (start us, length us, event | category | flops | bytes accessed | tf_op | source)
XLA Modules:
  0.0 998.3 jit_solution(14222626366897732754)
XLA Ops:
  31.0 3.8 collective-permute-done.8.refs_9_
  50.8 5.2 collective-permute-start.20
  56.0 4.0 collective-permute-done.20
  78.8 3.9 shard_map.518.q_ref
  82.7 9.1 shard_map.519
  91.9 4.3 multiply_reduce_fusion.8
  108.9 7.5 collective-permute-done.26
  134.0 9.7 collective-permute-done.29
  156.5 6.1 collective-permute-done.31
  170.3 7.6 collective-permute-done.32
  184.3 10.1 %shard_map.520 = (bf16[640,1536]{1,0:T(8,128)(2,1)S(1)}, bf16[1280,768]{1,0:T(8,128)(2,1)S(1)}, bf16[1280,768]{1,0:T(8,128)(2,1)S(1)}, bf16[1280,768]{1,0:T(8,128)(2,1)S(1)}, f32[1280,1]{1,0:T(8,128)S(1)}) custom-call(bf16[1280,1536]{1,0:T(8,128)(2,1)S(1)} %copy-done.7, bf16[8,1536]{1,0:T(8,128)(2,1)S(1)} %get-tuple-element.1213.router_ref, ...), custom_call_target="tpu_custom_call" | custom-call | flops 4529848320 | bytes 16908288 | tf_op jit(solution)/shard_map/pallas_call | solution.py:317
  198.1 9.8 shard_map.521
  219.7 6.9 collective-permute-done.38
  238.1 7.9 collective-permute-done.40
  252.2 12.1 %collective-permute-done.43 = bf16[160,1536]{1,0:T(8,128)(2,1)S(1)} collective-permute-done((bf16[160,1536]{1,0:T(8,128)(2,1)S(1)}, bf16[160,1536]{1,0:T(8,128)(2,1)S(1)}, u32[]{:S(2)}, u32[]{:S(2)}) %collective-permute-start.43) | collective-permute-done | bytes 491552 | tf_op jit(solution)/shard_map/ppermute | solution.py:451
  264.2 4.5 collective-permute-done.44
  275.2 3.7 fusion.6.q_ref
  283.8 9.2 shard_map.523
  294.9 4.6 multiply_reduce_fusion.6
  305.2 10.1 %collective-permute-done.52 = bf16[160,1536]{1,0:T(8,128)(2,1)S(1)} collective-permute-done((bf16[160,1536]{1,0:T(8,128)(2,1)S(1)}, bf16[160,1536]{1,0:T(8,128)(2,1)S(1)}, u32[]{:S(2)}, u32[]{:S(2)}) %collective-permute-start.52) | collective-permute-done | bytes 491552 | tf_op jit(solution)/shard_map/ppermute | solution.py:451
  315.3 4.1 collective-permute-done.50
  326.8 9.1 collective-permute-done.55
  346.6 5.4 collective-permute-done.57
  352.0 4.0 collective-permute-done.56
  361.7 6.1 collective-permute-done.58
  367.8 9.2 shard_map.524
  381.1 9.2 shard_map.525
  390.3 11.0 %shard_map.526 = (bf16[640,1664]{1,0:T(8,128)(2,1)S(1)}, bf16[1280,1536]{1,0:T(8,128)(2,1)S(1)}) custom-call(bf16[1280,1536]{1,0:T(8,128)(2,1)S(1)} %constant_dynamic-update-slice_fusion.5.d_ref, bf16[1280,768]{1,0:T(8,128)(2,1)S(1)} %get-tuple-element.715.pre_ref, bf16[1280,768]{1,0:T(8,128)(2,1)S(1)} %get-tuple-element.716.up_ref, ...), custom_call_target="tpu_custom_call" | custom-call | flops 4529848320 | bytes 16908288 | tf_op jit(solution)/shard_map/pallas_call | solution.py:377
  406.6 11.2 %shard_map.527 = (bf16[640,1664]{1,0:T(8,128)(2,1)S(1)}, bf16[1280,1536]{1,0:T(8,128)(2,1)S(1)}) custom-call(bf16[1280,1536]{1,0:T(8,128)(2,1)S(1)} %constant_dynamic-update-slice_fusion.5.d_ref, bf16[1280,768]{1,0:T(8,128)(2,1)S(1)} %get-tuple-element.715.pre_ref, bf16[1280,768]{1,0:T(8,128)(2,1)S(1)} %get-tuple-element.716.up_ref, ...), custom_call_target="tpu_custom_call", output_to_operand_aliasing={{1}: (8, {})} | custom-call | flops 4529848320 | bytes 16908288 | tf_op jit(solution)/shard_map/pallas_call | solution.py:377
  433.8 9.7 collective-permute-done.62
  443.5 4.6 collective-permute-done.63
  461.4 11.7 %collective-permute-done.65 = bf16[160,1664]{1,0:T(8,128)(2,1)S(1)} collective-permute-done((bf16[160,1664]{1,0:T(8,128)(2,1)}, bf16[160,1664]{1,0:T(8,128)(2,1)S(1)}, u32[]{:S(2)}, u32[]{:S(2)}) %collective-permute-start.65) | collective-permute-done | bytes 532512 | tf_op jit(solution)/shard_map/ppermute | solution.py:451
  473.0 6.0 collective-permute-done.66
  489.7 10.2 %collective-permute-done.71 = bf16[160,1664]{1,0:T(8,128)(2,1)S(1)} collective-permute-done((bf16[160,1664]{1,0:T(8,128)(2,1)S(1)}, bf16[160,1664]{1,0:T(8,128)(2,1)S(1)}, u32[]{:S(2)}, u32[]{:S(2)}) %collective-permute-start.71) | collective-permute-done | bytes 532512 | tf_op jit(solution)/shard_map/ppermute | solution.py:451
  500.0 3.8 collective-permute-done.72
  516.8 17.3 %shard_map.528 = (bf16[256,1536]{1,0:T(8,128)(2,1)S(1)}, bf16[1024,512]{1,0:T(8,128)(2,1)S(1)}) custom-call(bf16[256,1536]{1,0:T(8,128)(2,1)S(1)} %copy-done.52, bf16[1024,512]{1,0:T(8,128)(2,1)S(1)} %copy-done.44, bf16[256,1536]{1,0:T(8,128)(2,1)S(1)} %fusion.35.dm_ref, f32[256,128]{1,0:T(8,128)S(1)} %get-tuple-element.514.refs_12_.cos_ref.refs_2_, ...), custom_call_target="tpu_custom_call" | custom-call | flops 8053063680 | bytes 3145728 | tf_op jit(solution)/shard_map/pallas_call | solution.py:236
  549.4 4.8 collective-permute-done.82.second_ref
  562.3 7.1 collective-permute-done.86
  576.6 4.3 collective-permute-done.93
  583.6 4.4 collective-permute-done.89
  603.4 6.6 collective-permute-done.96
  623.9 6.1 collective-permute-done.103
  642.7 12.5 %collective-permute-done.109 = bf16[192,640]{1,0:T(8,128)(2,1)S(1)} collective-permute-done((bf16[192,640]{1,0:T(8,128)(2,1)S(1)}, bf16[192,640]{1,0:T(8,128)(2,1)S(1)}, u32[]{:S(2)}, u32[]{:S(2)}) %collective-permute-start.109) | collective-permute-done | bytes 245792 | tf_op jit(solution)/shard_map/ppermute | solution.py:451
  657.1 11.1 %shard_map.530 = (bf16[640,1664]{1,0:T(8,128)(2,1)S(1)}, bf16[1280,1536]{1,0:T(8,128)(2,1)S(1)}) custom-call(bf16[1280,1536]{1,0:T(8,128)(2,1)} %constant_dynamic-update-slice_fusion.d_ref, bf16[1280,768]{1,0:T(8,128)(2,1)S(1)} %copy-done.9, bf16[1280,768]{1,0:T(8,128)(2,1)S(1)} %copy-done.11, f32[1280,1]{1,0:T(8,128)S(1)} %copy-done.19, ...), custom_call_target="tpu_custom_call" | custom-call | flops 4529848320 | bytes 16908288 | tf_op jit(solution)/shard_map/pallas_call | solution.py:377
  677.2 11.3 %shard_map.531 = (bf16[640,1664]{1,0:T(8,128)(2,1)S(1)}, bf16[1280,1536]{1,0:T(8,128)(2,1)S(1)}) custom-call(bf16[1280,1536]{1,0:T(8,128)(2,1)} %constant_dynamic-update-slice_fusion.d_ref, bf16[1280,768]{1,0:T(8,128)(2,1)S(1)} %copy-done.9, bf16[1280,768]{1,0:T(8,128)(2,1)S(1)} %copy-done.11, ...), custom_call_target="tpu_custom_call", output_to_operand_aliasing={{1}: (8, {})} | custom-call | flops 4529848320 | bytes 16908288 | tf_op jit(solution)/shard_map/pallas_call | solution.py:377
  688.7 9.1 collective-permute-done.112
  711.8 4.9 collective-permute-done.133
  719.9 6.1 collective-permute-start.115
  730.5 11.9 %collective-permute-done.114 = bf16[160,1664]{1,0:T(8,128)(2,1)S(1)} collective-permute-done((bf16[160,1664]{1,0:T(8,128)(2,1)S(1)}, bf16[160,1664]{1,0:T(8,128)(2,1)S(1)}, u32[]{:S(2)}, u32[]{:S(2)}) %collective-permute-start.114) | collective-permute-done | bytes 532512 | tf_op jit(solution)/shard_map/ppermute | solution.py:451
  763.8 11.1 %collective-permute-done.117 = bf16[160,1664]{1,0:T(8,128)(2,1)S(1)} collective-permute-done((bf16[160,1664]{1,0:T(8,128)(2,1)S(1)}, bf16[160,1664]{1,0:T(8,128)(2,1)S(1)}, u32[]{:S(2)}, u32[]{:S(2)}) %collective-permute-start.117) | collective-permute-done | bytes 532512 | tf_op jit(solution)/shard_map/ppermute | solution.py:451
  789.8 7.8 collective-permute-done.123
  807.1 17.1 %shard_map.532 = (bf16[256,1536]{1,0:T(8,128)(2,1)S(1)}, bf16[1024,512]{1,0:T(8,128)(2,1)S(1)}) custom-call(bf16[256,1536]{1,0:T(8,128)(2,1)S(1)} %copy-done.50, bf16[1024,512]{1,0:T(8,128)(2,1)S(1)} %copy-done.33, bf16[256,1536]{1,0:T(8,128)(2,1)S(1)} %convolution_convert_fusion.4.dm_ref, f32[256,128]{1,0:T(8,128)S(1)} %get-tuple-element.514.refs_12_.cos_ref.refs_2_, ...), custom_call_target="tpu_custom_call" | custom-call | flops 8053063680 | bytes 3145728 | tf_op jit(solution)/shard_map/pallas_call | solution.py:236
  844.0 4.3 collective-permute-done.129.second_ref
  852.9 9.9 collective-permute-done.138
  863.3 6.2 collective-permute-done.140
  881.8 5.7 collective-permute-done.144
  904.0 4.6 collective-permute-done.150
  910.4 5.9 collective-permute-done.151
  925.4 4.0 collective-permute-start.161
  937.9 5.2 collective-permute-done.165
  957.2 5.3 collective-permute-start.167
  966.1 6.0 collective-permute-done.170
  972.1 9.0 collective-permute-done.166
  983.7 4.5 collective-permute-done.171
  (1138 shorter events, 499.8 us)
Async XLA Ops:
  7.2 84.6 %all-gather.15.cloned.1.call-start = ((), (), s32[]{:S(2)}) async-start(), calls=%async_computation.2 | async-start | bytes 5898240 | tf_op jit(solution)/shard_map/all_gather | solution.py:904
  12.4 24.6 %collective-permute-start = (bf16[256,1536]{1,0:T(8,128)(2,1)}, bf16[256,1536]{1,0:T(8,128)(2,1)}, u32[]{:S(2)}, u32[]{:S(2)}) collective-permute-start(bf16[256,1536]{1,0:T(8,128)(2,1)} %param.50), channel_id=1, source_target_pairs={{0,8},{4,12},{8,0},{12,4},{16,24},{20,28},{24,16},{28,20},{1,9},{5... | collective-permute-start | bytes 2359304 | tf_op jit(solution)/shard_map/ppermute | solution.py:454
  40.2 231.5 %all-gather.11.cloned.1.call-start = ((), (), s32[]{:S(2)}) async-start(), calls=%async_computation | async-start | bytes 1966080 | tf_op jit(solution)/shard_map/all_gather | solution.py:904
  42.2 25.4 %collective-permute-start.11 = (bf16[192,1536]{1,0:T(8,128)(2,1)}, bf16[192,1536]{1,0:T(8,128)(2,1)}, u32[]{:S(2)}, u32[]{:S(2)}) collective-permute-start(bf16[192,1536]{1,0:T(8,128)(2,1)} %collective-permute-done.6.refs_8_), channel_id=1, source_target_pairs={{0,4},{4,0},{8,12},{12,8},{16,20},{20,16},{24,28},{28,24},{1,5},{5... | collective-permute-start | bytes 1769480 | tf_op jit(solution)/shard_map/ppermute | solution.py:451
  43.7 23.9 %collective-permute-start.12 = (bf16[192,1536]{1,0:T(8,128)(2,1)}, bf16[192,1536]{1,0:T(8,128)(2,1)}, u32[]{:S(2)}, u32[]{:S(2)}) collective-permute-start(bf16[192,1536]{1,0:T(8,128)(2,1)} %collective-permute-done.6.refs_8_), channel_id=1, source_target_pairs={{0,1},{1,0},{2,3},{3,2},{4,5},{5,4},{6,7},{7,6},{8,9},{9,8},{10,11... | collective-permute-start | bytes 1769480 | tf_op jit(solution)/shard_map/ppermute | solution.py:537
  73.1 23.3 %collective-permute-start.17 = (bf16[256,1536]{1,0:T(8,128)(2,1)}, bf16[256,1536]{1,0:T(8,128)(2,1)}, u32[]{:S(2)}, u32[]{:S(2)}) collective-permute-start(bf16[256,1536]{1,0:T(8,128)(2,1)} %copy-done.126), channel_id=1, source_target_pairs={{0,8},{4,12},{8,0},{12,4},{16,24},{20,28},{24,16},{28,20},{1,9},{5... | collective-permute-start | bytes 2359304 | tf_op jit(solution)/shard_map/ppermute | solution.py:454
  74.9 21.5 %collective-permute-start.18 = (bf16[256,1536]{1,0:T(8,128)(2,1)}, bf16[256,1536]{1,0:T(8,128)(2,1)}, u32[]{:S(2)}, u32[]{:S(2)}) collective-permute-start(bf16[256,1536]{1,0:T(8,128)(2,1)} %collective-permute-done), channel_id=1, source_target_pairs={{0,1},{1,0},{2,3},{3,2},{4,5},{5,4},{6,7},{7,6},{8,16},{9,17},{10,... | collective-permute-start | bytes 2359304 | tf_op jit(solution)/shard_map/ppermute | solution.py:466
  96.5 20.0 %collective-permute-start.24 = (bf16[256,1536]{1,0:T(8,128)(2,1)S(1)}, bf16[256,1536]{1,0:T(8,128)(2,1)S(1)}, u32[]{:S(2)}, u32[]{:S(2)}) collective-permute-start(bf16[256,1536]{1,0:T(8,128)(2,1)S(1)} %multiply_convert_fusion.2), channel_id=1, source_target_pairs={{0,8},{4,12},{8,0},{12,4},{16,24},{20,28},{24,16},{28,20},{1,9},{5... | collective-permute-start | bytes 2359304 | tf_op jit(solution)/shard_map/ppermute | solution.py:454
  119.1 156.1 %all-gather.17.cloned.1.call-start = ((), (), s32[]{:S(2)}) async-start(), calls=%async_computation.3 | async-start | bytes 5898240 | tf_op jit(solution)/shard_map/all_gather | solution.py:904
  120.8 174.1 %all-gather.19.cloned.1.call-start = ((), (), s32[]{:S(2)}) async-start(), calls=%async_computation.4 | async-start | bytes 5898240 | tf_op jit(solution)/shard_map/all_gather | solution.py:904
  123.3 176.5 %all-gather.13.cloned.1.call-start = ((), (), s32[]{:S(2)}) async-start(), calls=%async_computation.1 | async-start | bytes 1966080 | tf_op jit(solution)/shard_map/all_gather | solution.py:904
  124.2 175.6 %all-gather.21.cloned.1.call-start = ((), (), s32[]{:S(2)}) async-start(), calls=%async_computation.5 | async-start | bytes 5898240 | tf_op jit(solution)/shard_map/all_gather | solution.py:904
  127.9 19.5 %collective-permute-start.27 = (bf16[256,1536]{1,0:T(8,128)(2,1)}, bf16[256,1536]{1,0:T(8,128)(2,1)}, u32[]{:S(2)}, u32[]{:S(2)}) collective-permute-start(bf16[256,1536]{1,0:T(8,128)(2,1)} %collective-permute-done.25), channel_id=1, source_target_pairs={{0,8},{4,12},{8,0},{12,4},{16,24},{20,28},{24,16},{28,20},{1,9},{5... | collective-permute-start | bytes 2359304 | tf_op jit(solution)/shard_map/ppermute | solution.py:454
  127.9 19.5 %collective-permute-start.28 = (bf16[256,1536]{1,0:T(8,128)(2,1)S(1)}, bf16[256,1536]{1,0:T(8,128)(2,1)S(1)}, u32[]{:S(2)}, u32[]{:S(2)}) collective-permute-start(bf16[256,1536]{1,0:T(8,128)(2,1)S(1)} %copy-done.95), channel_id=1, source_target_pairs={{0,1},{1,0},{2,3},{3,2},{4,5},{5,4},{6,7},{7,6},{8,16},{9,17},{10,... | collective-permute-start | bytes 2359304 | tf_op jit(solution)/shard_map/ppermute | solution.py:466
  178.7 31.8 %collective-permute-start.33 = (bf16[256,1536]{1,0:T(8,128)(2,1)}, bf16[256,1536]{1,0:T(8,128)(2,1)S(1)}, u32[]{:S(2)}, u32[]{:S(2)}) collective-permute-start(bf16[256,1536]{1,0:T(8,128)(2,1)} %collective-permute-done.18), channel_id=1, source_target_pairs={{0,8},{4,12},{8,0},{12,4},{16,24},{20,28},{24,16},{28,20},{1,9},{5... | collective-permute-start | bytes 2359304 | tf_op jit(solution)/shard_map/ppermute | solution.py:454
  179.7 28.2 %collective-permute-start.34 = (bf16[160,1536]{1,0:T(8,128)(2,1)S(1)}, bf16[160,1536]{1,0:T(8,128)(2,1)S(1)}, u32[]{:S(2)}, u32[]{:S(2)}) collective-permute-start(bf16[160,1536]{1,0:T(8,128)(2,1)S(1)} %copy-done.172), channel_id=1, source_target_pairs={{0,4},{4,0},{8,12},{12,8},{16,20},{20,16},{24,28},{28,24},{1,5},{5... | collective-permute-start | bytes 1474568 | tf_op jit(solution)/shard_map/ppermute | solution.py:451
  180.6 27.3 %collective-permute-start.35 = (bf16[160,1536]{1,0:T(8,128)(2,1)S(1)}, bf16[160,1536]{1,0:T(8,128)(2,1)S(1)}, u32[]{:S(2)}, u32[]{:S(2)}) collective-permute-start(bf16[160,1536]{1,0:T(8,128)(2,1)S(1)} %copy-done.175), channel_id=1, source_target_pairs={{0,4},{4,0},{8,12},{12,8},{16,20},{20,16},{24,28},{28,24},{1,5},{5... | collective-permute-start | bytes 1474568 | tf_op jit(solution)/shard_map/ppermute | solution.py:451
  249.4 19.3 %collective-permute-start.44 = (bf16[256,1536]{1,0:T(8,128)(2,1)S(1)}, bf16[256,1536]{1,0:T(8,128)(2,1)S(1)}, u32[]{:S(2)}, u32[]{:S(2)}) collective-permute-start(bf16[256,1536]{1,0:T(8,128)(2,1)S(1)} %get-tuple-element.1137), channel_id=1, source_target_pairs={{0,8},{4,12},{8,0},{12,4},{16,24},{20,28},{24,16},{28,20},{1,9},{5... | collective-permute-start | bytes 2359304 | tf_op jit(solution)/shard_map/ppermute | solution.py:454
  299.8 19.6 %collective-permute-start.50 = (bf16[256,1536]{1,0:T(8,128)(2,1)S(1)}, bf16[256,1536]{1,0:T(8,128)(2,1)S(1)}, u32[]{:S(2)}, u32[]{:S(2)}) collective-permute-start(bf16[256,1536]{1,0:T(8,128)(2,1)S(1)} %multiply_convert_fusion), channel_id=1, source_target_pairs={{0,8},{4,12},{8,0},{12,4},{16,24},{20,28},{24,16},{28,20},{1,9},{5... | collective-permute-start | bytes 2359304 | tf_op jit(solution)/shard_map/ppermute | solution.py:454
  424.5 23.6 %collective-permute-start.64 = (bf16[768,1536]{1,0:T(8,128)(2,1)S(1)}, bf16[768,1536]{1,0:T(8,128)(2,1)S(1)}, u32[]{:S(2)}, u32[]{:S(2)}) collective-permute-start(bf16[768,1536]{1,0:T(8,128)(2,1)S(1)} %pad_maximum_fusion.3), channel_id=1, source_target_pairs={{0,1},{1,0},{2,3},{3,2},{4,5},{5,4},{6,7},{7,6},{8,9},{9,8},{10,11... | collective-permute-start | bytes 7077896 | tf_op jit(solution)/shard_map/ppermute | solution.py:537
  427.6 20.6 %collective-permute-start.63 = (bf16[256,1664]{1,0:T(8,128)(2,1)S(1)}, bf16[256,1664]{1,0:T(8,128)(2,1)S(1)}, u32[]{:S(2)}, u32[]{:S(2)}) collective-permute-start(bf16[256,1664]{1,0:T(8,128)(2,1)S(1)} %get-tuple-element.1234), channel_id=1, source_target_pairs={{0,8},{4,12},{8,0},{12,4},{16,24},{20,28},{24,16},{28,20},{1,9},{5... | collective-permute-start | bytes 2555912 | tf_op jit(solution)/shard_map/ppermute | solution.py:454
  432.0 26.5 %collective-permute-start.70 = (bf16[160,1536]{1,0:T(8,128)(2,1)S(1)}, bf16[160,1536]{1,0:T(8,128)(2,1)}, u32[]{:S(2)}, u32[]{:S(2)}) collective-permute-start(bf16[160,1536]{1,0:T(8,128)(2,1)S(1)} %copy-done.174), channel_id=1, source_target_pairs={{0,4},{4,0},{8,12},{12,8},{16,20},{20,16},{24,28},{28,24},{1,5},{5... | collective-permute-start | bytes 1474568 | tf_op jit(solution)/shard_map/ppermute | solution.py:451
  451.4 27.7 %collective-permute-start.68 = (bf16[384,1536]{1,0:T(8,128)(2,1)}, bf16[384,1536]{1,0:T(8,128)(2,1)}, u32[]{:S(2)}, u32[]{:S(2)}) collective-permute-start(bf16[384,1536]{1,0:T(8,128)(2,1)} %fusion.19), channel_id=1, source_target_pairs={{0,2},{1,3},{2,0},{3,1},{4,6},{5,7},{6,4},{7,5},{8,10},{9,11},{10,... | collective-permute-start | bytes 3538952 | tf_op jit(solution)/shard_map/ppermute | solution.py:541
  455.6 23.5 %collective-permute-start.69 = (bf16[384,1536]{1,0:T(8,128)(2,1)}, bf16[384,1536]{1,0:T(8,128)(2,1)}, u32[]{:S(2)}, u32[]{:S(2)}) collective-permute-start(bf16[384,1536]{1,0:T(8,128)(2,1)} %pad_maximum_fusion.9), channel_id=1, source_target_pairs={{0,1},{1,0},{2,3},{3,2},{4,5},{5,4},{6,7},{7,6},{8,9},{9,8},{10,11... | collective-permute-start | bytes 3538952 | tf_op jit(solution)/shard_map/ppermute | solution.py:537
  457.4 21.7 %collective-permute-start.66 = (bf16[256,1664]{1,0:T(8,128)(2,1)}, bf16[256,1664]{1,0:T(8,128)(2,1)}, u32[]{:S(2)}, u32[]{:S(2)}) collective-permute-start(bf16[256,1664]{1,0:T(8,128)(2,1)} %get-tuple-element.1131), channel_id=1, source_target_pairs={{0,8},{4,12},{8,0},{12,4},{16,24},{20,28},{24,16},{28,20},{1,9},{5... | collective-permute-start | bytes 2555912 | tf_op jit(solution)/shard_map/ppermute | solution.py:454
  458.3 20.8 %collective-permute-start.67 = (bf16[256,1664]{1,0:T(8,128)(2,1)}, bf16[256,1664]{1,0:T(8,128)(2,1)}, u32[]{:S(2)}, u32[]{:S(2)}) collective-permute-start(bf16[256,1664]{1,0:T(8,128)(2,1)} %get-tuple-element.1130), channel_id=1, source_target_pairs={{0,1},{1,0},{2,3},{3,2},{4,5},{5,4},{6,7},{7,6},{8,16},{9,17},{10,... | collective-permute-start | bytes 2555912 | tf_op jit(solution)/shard_map/ppermute | solution.py:466
  483.1 20.6 %collective-permute-start.72 = (bf16[256,1664]{1,0:T(8,128)(2,1)S(1)}, bf16[256,1664]{1,0:T(8,128)(2,1)S(1)}, u32[]{:S(2)}, u32[]{:S(2)}) collective-permute-start(bf16[256,1664]{1,0:T(8,128)(2,1)S(1)} %get-tuple-element.1129), channel_id=1, source_target_pairs={{0,8},{4,12},{8,0},{12,4},{16,24},{20,28},{24,16},{28,20},{1,9},{5... | collective-permute-start | bytes 2555912 | tf_op jit(solution)/shard_map/ppermute | solution.py:454
  484.9 18.8 %collective-permute-start.73 = (bf16[256,1664]{1,0:T(8,128)(2,1)S(1)}, bf16[256,1664]{1,0:T(8,128)(2,1)S(1)}, u32[]{:S(2)}, u32[]{:S(2)}) collective-permute-start(bf16[256,1664]{1,0:T(8,128)(2,1)S(1)} %get-tuple-element.1128), channel_id=1, source_target_pairs={{0,1},{1,0},{2,3},{3,2},{4,5},{5,4},{6,7},{7,6},{8,16},{9,17},{10,... | collective-permute-start | bytes 2555912 | tf_op jit(solution)/shard_map/ppermute | solution.py:466
  488.4 27.4 %collective-permute-start.78 = (bf16[192,1536]{1,0:T(8,128)(2,1)S(1)}, bf16[192,1536]{1,0:T(8,128)(2,1)S(1)}, u32[]{:S(2)}, u32[]{:S(2)}) collective-permute-start(bf16[192,1536]{1,0:T(8,128)(2,1)S(1)} %fusion.42), channel_id=1, source_target_pairs={{0,2},{1,3},{2,0},{3,1},{4,6},{5,7},{6,4},{7,5},{8,10},{9,11},{10,... | collective-permute-start | bytes 1769480 | tf_op jit(solution)/shard_map/ppermute | solution.py:541
  503.8 30.4 %collective-permute-start.74 = (bf16[160,1536]{1,0:T(8,128)(2,1)S(1)}, bf16[160,1536]{1,0:T(8,128)(2,1)S(1)}, u32[]{:S(2)}, u32[]{:S(2)}) collective-permute-start(bf16[160,1536]{1,0:T(8,128)(2,1)S(1)} %copy-done.167), channel_id=1, source_target_pairs={{0,4},{4,0},{8,12},{12,8},{16,20},{20,16},{24,28},{28,24},{1,5},{5... | collective-permute-start | bytes 1474568 | tf_op jit(solution)/shard_map/ppermute | solution.py:451
  506.7 27.5 %collective-permute-start.76 = (bf16[256,1536]{1,0:T(8,128)(2,1)S(1)}, bf16[256,1536]{1,0:T(8,128)(2,1)S(1)}, u32[]{:S(2)}, u32[]{:S(2)}) collective-permute-start(bf16[256,1536]{1,0:T(8,128)(2,1)S(1)} %get-tuple-element.1135), channel_id=1, source_target_pairs={{0,8},{4,12},{8,0},{12,4},{16,24},{20,28},{24,16},{28,20},{1,9},{5... | collective-permute-start | bytes 2359304 | tf_op jit(solution)/shard_map/ppermute | solution.py:454
  508.5 25.7 %collective-permute-start.77 = (bf16[256,1536]{1,0:T(8,128)(2,1)S(1)}, bf16[256,1536]{1,0:T(8,128)(2,1)S(1)}, u32[]{:S(2)}, u32[]{:S(2)}) collective-permute-start(bf16[256,1536]{1,0:T(8,128)(2,1)S(1)} %get-tuple-element.1134), channel_id=1, source_target_pairs={{0,1},{1,0},{2,3},{3,2},{4,5},{5,4},{6,7},{7,6},{8,16},{9,17},{10,... | collective-permute-start | bytes 2359304 | tf_op jit(solution)/shard_map/ppermute | solution.py:466
  513.0 21.1 %collective-permute-start.79 = (bf16[256,1536]{1,0:T(8,128)(2,1)S(1)}, bf16[256,1536]{1,0:T(8,128)(2,1)S(1)}, u32[]{:S(2)}, u32[]{:S(2)}) collective-permute-start(bf16[256,1536]{1,0:T(8,128)(2,1)S(1)} %fusion.173), channel_id=1, source_target_pairs={{0,2},{1,3},{2,0},{3,1},{4,6},{5,7},{6,4},{7,5},{8,10},{9,11},{10,... | collective-permute-start | bytes 2359304 | tf_op jit(solution)/shard_map/ppermute | solution.py:541
  542.0 19.3 %collective-permute-start.87 = (bf16[256,1536]{1,0:T(8,128)(2,1)S(1)}, bf16[256,1536]{1,0:T(8,128)(2,1)S(1)}, u32[]{:S(2)}, u32[]{:S(2)}) collective-permute-start(bf16[256,1536]{1,0:T(8,128)(2,1)S(1)} %get-tuple-element.1133), channel_id=1, source_target_pairs={{0,8},{4,12},{8,0},{12,4},{16,24},{20,28},{24,16},{28,20},{1,9},{5... | collective-permute-start | bytes 2359304 | tf_op jit(solution)/shard_map/ppermute | solution.py:454
  556.2 20.3 %collective-permute-start.92 = (bf16[256,1536]{1,0:T(8,128)(2,1)S(1)}, bf16[256,1536]{1,0:T(8,128)(2,1)S(1)}, u32[]{:S(2)}, u32[]{:S(2)}) collective-permute-start(bf16[256,1536]{1,0:T(8,128)(2,1)S(1)} %get-tuple-element.812), channel_id=1, source_target_pairs={{0,2},{1,3},{2,0},{3,1},{4,6},{5,7},{6,4},{7,5},{8,10},{9,11},{10,... | collective-permute-start | bytes 2359304 | tf_op jit(solution)/shard_map/ppermute | solution.py:541
  593.5 18.8 %collective-permute-start.94 = (bf16[256,1536]{1,0:T(8,128)(2,1)S(1)}, bf16[256,1536]{1,0:T(8,128)(2,1)S(1)}, u32[]{:S(2)}, u32[]{:S(2)}) collective-permute-start(bf16[256,1536]{1,0:T(8,128)(2,1)S(1)} %collective-permute-done.90), channel_id=1, source_target_pairs={{0,8},{4,12},{8,0},{12,4},{16,24},{20,28},{24,16},{28,20},{1,9},{5... | collective-permute-start | bytes 2359304 | tf_op jit(solution)/shard_map/ppermute | solution.py:454
  600.4 105.5 %collective-permute-start.132 = (bf16[256,384]{1,0:T(8,128)(2,1)}, bf16[256,384]{1,0:T(8,128)(2,1)}, u32[]{:S(2)}, u32[]{:S(2)}) collective-permute-start(bf16[256,384]{1,0:T(8,128)(2,1)} %get-tuple-element.1156), channel_id=1, source_target_pairs={{0,3},{1,2},{2,1},{3,0},{4,7},{5,6},{6,5},{7,4},{8,11},{9,10},{10,... | collective-permute-start | bytes 589832 | tf_op jit(solution)/shard_map/ppermute | solution.py:593
  620.3 22.4 %collective-permute-start.108 = (bf16[192,1536]{1,0:T(8,128)(2,1)}, bf16[192,1536]{1,0:T(8,128)(2,1)}, u32[]{:S(2)}, u32[]{:S(2)}) collective-permute-start(bf16[192,1536]{1,0:T(8,128)(2,1)} %dynamic-slice_convert_fusion.2), channel_id=1, source_target_pairs={{0,4},{4,0},{8,12},{12,8},{16,20},{20,16},{24,28},{28,24},{1,5},{5... | collective-permute-start | bytes 1769480 | tf_op jit(solution)/shard_map/ppermute | solution.py:451
  632.4 22.8 %collective-permute-start.104 = (bf16[160,1536]{1,0:T(8,128)(2,1)}, bf16[160,1536]{1,0:T(8,128)(2,1)}, u32[]{:S(2)}, u32[]{:S(2)}) collective-permute-start(bf16[160,1536]{1,0:T(8,128)(2,1)} %convolution_convert_fusion.9), channel_id=1, source_target_pairs={{0,4},{4,0},{8,12},{12,8},{16,20},{20,16},{24,28},{28,24},{1,5},{5... | collective-permute-start | bytes 1474568 | tf_op jit(solution)/shard_map/ppermute | solution.py:451
  635.9 19.4 %collective-permute-start.109 = (bf16[192,640]{1,0:T(8,128)(2,1)S(1)}, bf16[192,640]{1,0:T(8,128)(2,1)S(1)}, u32[]{:S(2)}, u32[]{:S(2)}) collective-permute-start(bf16[192,640]{1,0:T(8,128)(2,1)S(1)} %fusion.100), channel_id=1, source_target_pairs={{0,4},{4,0},{8,12},{12,8},{16,20},{20,16},{24,28},{28,24},{1,5},{5... | collective-permute-start | bytes 737288 | tf_op jit(solution)/shard_map/ppermute | solution.py:451
  669.4 29.4 %collective-permute-start.110 = (bf16[160,1664]{1,0:T(8,128)(2,1)S(1)}, bf16[160,1664]{1,0:T(8,128)(2,1)S(1)}, u32[]{:S(2)}, u32[]{:S(2)}) collective-permute-start(bf16[160,1664]{1,0:T(8,128)(2,1)S(1)} %get-tuple-element.1094), channel_id=1, source_target_pairs={{0,4},{4,0},{8,12},{12,8},{16,20},{20,16},{24,28},{28,24},{1,5},{5... | collective-permute-start | bytes 1597448 | tf_op jit(solution)/shard_map/ppermute | solution.py:451
  673.7 24.0 %collective-permute-start.112 = (bf16[48,3712]{1,0:T(8,128)(2,1)S(1)}, bf16[48,3712]{1,0:T(8,128)(2,1)S(1)}, u32[]{:S(2)}, u32[]{:S(2)}) collective-permute-start(bf16[48,3712]{1,0:T(8,128)(2,1)S(1)} %get-tuple-element.1145), channel_id=1, source_target_pairs={{0,16},{4,20},{8,24},{12,28},{16,0},{20,4},{24,8},{28,12},{1,17},{... | collective-permute-start | bytes 1069064 | tf_op jit(solution)/shard_map/ppermute | solution.py:533
  675.7 23.1 %collective-permute-start.113 = (bf16[48,3712]{1,0:T(8,128)(2,1)S(1)}, bf16[48,3712]{1,0:T(8,128)(2,1)S(1)}, u32[]{:S(2)}, u32[]{:S(2)}) collective-permute-start(bf16[48,3712]{1,0:T(8,128)(2,1)S(1)} %get-tuple-element.1144), channel_id=1, source_target_pairs={{0,24},{4,28},{8,0},{12,4},{16,8},{20,12},{24,16},{28,20},{1,25},{... | collective-permute-start | bytes 1069064 | tf_op jit(solution)/shard_map/ppermute | solution.py:533
  704.0 40.6 %collective-permute-start.116 = (bf16[768,1536]{1,0:T(8,128)(2,1)}, bf16[768,1536]{1,0:T(8,128)(2,1)}, u32[]{:S(2)}, u32[]{:S(2)}) collective-permute-start(bf16[768,1536]{1,0:T(8,128)(2,1)} %pad_maximum_fusion.4), channel_id=1, source_target_pairs={{0,1},{1,0},{2,3},{3,2},{4,5},{5,4},{6,7},{7,6},{8,9},{9,8},{10,11... | collective-permute-start | bytes 7077896 | tf_op jit(solution)/shard_map/ppermute | solution.py:537
  719.9 24.7 %collective-permute-start.115 = (bf16[256,1664]{1,0:T(8,128)(2,1)S(1)}, bf16[256,1664]{1,0:T(8,128)(2,1)S(1)}, u32[]{:S(2)}, u32[]{:S(2)}) collective-permute-start(bf16[256,1664]{1,0:T(8,128)(2,1)S(1)} %get-tuple-element.1240), channel_id=1, source_target_pairs={{0,8},{4,12},{8,0},{12,4},{16,24},{20,28},{24,16},{28,20},{1,9},{5... | collective-permute-start | bytes 2555912 | tf_op jit(solution)/shard_map/ppermute | solution.py:454
  748.2 29.5 %collective-permute-start.120 = (bf16[384,1536]{1,0:T(8,128)(2,1)S(1)}, bf16[384,1536]{1,0:T(8,128)(2,1)S(1)}, u32[]{:S(2)}, u32[]{:S(2)}) collective-permute-start(bf16[384,1536]{1,0:T(8,128)(2,1)S(1)} %fusion.20), channel_id=1, source_target_pairs={{0,2},{1,3},{2,0},{3,1},{4,6},{5,7},{6,4},{7,5},{8,10},{9,11},{10,... | collective-permute-start | bytes 3538952 | tf_op jit(solution)/shard_map/ppermute | solution.py:541
  755.7 22.0 %collective-permute-start.121 = (bf16[384,1536]{1,0:T(8,128)(2,1)S(1)}, bf16[384,1536]{1,0:T(8,128)(2,1)S(1)}, u32[]{:S(2)}, u32[]{:S(2)}) collective-permute-start(bf16[384,1536]{1,0:T(8,128)(2,1)S(1)} %pad_maximum_fusion.10), channel_id=1, source_target_pairs={{0,1},{1,0},{2,3},{3,2},{4,5},{5,4},{6,7},{7,6},{8,9},{9,8},{10,11... | collective-permute-start | bytes 3538952 | tf_op jit(solution)/shard_map/ppermute | solution.py:537
  756.3 21.4 %collective-permute-start.118 = (bf16[256,1664]{1,0:T(8,128)(2,1)S(1)}, bf16[256,1664]{1,0:T(8,128)(2,1)S(1)}, u32[]{:S(2)}, u32[]{:S(2)}) collective-permute-start(bf16[256,1664]{1,0:T(8,128)(2,1)S(1)} %get-tuple-element.1127), channel_id=1, source_target_pairs={{0,8},{4,12},{8,0},{12,4},{16,24},{20,28},{24,16},{28,20},{1,9},{5... | collective-permute-start | bytes 2555912 | tf_op jit(solution)/shard_map/ppermute | solution.py:454
  758.1 19.6 %collective-permute-start.119 = (bf16[256,1664]{1,0:T(8,128)(2,1)S(1)}, bf16[256,1664]{1,0:T(8,128)(2,1)S(1)}, u32[]{:S(2)}, u32[]{:S(2)}) collective-permute-start(bf16[256,1664]{1,0:T(8,128)(2,1)S(1)} %get-tuple-element.1126), channel_id=1, source_target_pairs={{0,1},{1,0},{2,3},{3,2},{4,5},{5,4},{6,7},{7,6},{8,16},{9,17},{10,... | collective-permute-start | bytes 2555912 | tf_op jit(solution)/shard_map/ppermute | solution.py:466
  779.9 20.6 %collective-permute-start.124 = (bf16[256,1664]{1,0:T(8,128)(2,1)S(1)}, bf16[256,1664]{1,0:T(8,128)(2,1)S(1)}, u32[]{:S(2)}, u32[]{:S(2)}) collective-permute-start(bf16[256,1664]{1,0:T(8,128)(2,1)S(1)} %get-tuple-element.1125), channel_id=1, source_target_pairs={{0,8},{4,12},{8,0},{12,4},{16,24},{20,28},{24,16},{28,20},{1,9},{5... | collective-permute-start | bytes 2555912 | tf_op jit(solution)/shard_map/ppermute | solution.py:454
  788.8 35.4 %collective-permute-start.122 = (bf16[192,1536]{1,0:T(8,128)(2,1)S(1)}, bf16[192,1536]{1,0:T(8,128)(2,1)S(1)}, u32[]{:S(2)}, u32[]{:S(2)}) collective-permute-start(bf16[192,1536]{1,0:T(8,128)(2,1)S(1)} %fusion.43), channel_id=1, source_target_pairs={{0,2},{1,3},{2,0},{3,1},{4,6},{5,7},{6,4},{7,5},{8,10},{9,11},{10,... | collective-permute-start | bytes 1769480 | tf_op jit(solution)/shard_map/ppermute | solution.py:541
  804.7 19.6 %collective-permute-start.126 = (bf16[256,1536]{1,0:T(8,128)(2,1)S(1)}, bf16[256,1536]{1,0:T(8,128)(2,1)S(1)}, u32[]{:S(2)}, u32[]{:S(2)}) collective-permute-start(bf16[256,1536]{1,0:T(8,128)(2,1)S(1)} %get-tuple-element.1066), channel_id=1, source_target_pairs={{0,2},{1,3},{2,0},{3,1},{4,6},{5,7},{6,4},{7,5},{8,10},{9,11},{10,... | collective-permute-start | bytes 2359304 | tf_op jit(solution)/shard_map/ppermute | solution.py:541
  828.3 24.5 %collective-permute-start.137 = (bf16[48,3712]{1,0:T(8,128)(2,1)}, bf16[48,3712]{1,0:T(8,128)(2,1)}, u32[]{:S(2)}, u32[]{:S(2)}) collective-permute-start(bf16[48,3712]{1,0:T(8,128)(2,1)} %get-tuple-element.1065), channel_id=1, source_target_pairs={{0,24},{4,28},{8,0},{12,4},{16,8},{20,12},{24,16},{28,20},{1,25},{... | collective-permute-start | bytes 1069064 | tf_op jit(solution)/shard_map/ppermute | solution.py:533
  830.8 32.0 %collective-permute-start.138 = (bf16[48,3712]{1,0:T(8,128)(2,1)}, bf16[48,3712]{1,0:T(8,128)(2,1)}, u32[]{:S(2)}, u32[]{:S(2)}) collective-permute-start(bf16[48,3712]{1,0:T(8,128)(2,1)} %get-tuple-element.1065), channel_id=1, source_target_pairs={{0,16},{4,20},{8,24},{12,28},{16,0},{20,4},{24,8},{28,12},{1,17},{... | collective-permute-start | bytes 1069064 | tf_op jit(solution)/shard_map/ppermute | solution.py:533
  831.6 31.1 %collective-permute-start.139 = (bf16[48,3712]{1,0:T(8,128)(2,1)}, bf16[48,3712]{1,0:T(8,128)(2,1)S(1)}, u32[]{:S(2)}, u32[]{:S(2)}) collective-permute-start(bf16[48,3712]{1,0:T(8,128)(2,1)} %get-tuple-element.1065), channel_id=1, source_target_pairs={{0,8},{4,12},{8,16},{12,20},{16,24},{20,28},{24,0},{28,4},{1,9},{5... | collective-permute-start | bytes 1069064 | tf_op jit(solution)/shard_map/ppermute | solution.py:533
  850.6 18.9 %collective-permute-start.140 = (bf16[256,1536]{1,0:T(8,128)(2,1)S(1)}, bf16[256,1536]{1,0:T(8,128)(2,1)S(1)}, u32[]{:S(2)}, u32[]{:S(2)}) collective-permute-start(bf16[256,1536]{1,0:T(8,128)(2,1)S(1)} %get-tuple-element.917), channel_id=1, source_target_pairs={{0,2},{1,3},{2,0},{3,1},{4,6},{5,7},{6,4},{7,5},{8,10},{9,11},{10,... | collective-permute-start | bytes 2359304 | tf_op jit(solution)/shard_map/ppermute | solution.py:541
  892.0 30.4 %collective-permute-start.155 = (bf16[48,1536]{1,0:T(8,128)(2,1)}, bf16[48,1536]{1,0:T(8,128)(2,1)}, u32[]{:S(2)}, u32[]{:S(2)}) collective-permute-start(bf16[48,1536]{1,0:T(8,128)(2,1)} %get-tuple-element.1061), channel_id=1, source_target_pairs={{0,24},{4,28},{8,0},{12,4},{16,8},{20,12},{24,16},{28,20},{1,25},{... | collective-permute-start | bytes 442376 | tf_op jit(solution)/shard_map/ppermute | solution.py:533
  894.6 27.9 %collective-permute-start.156 = (bf16[48,1536]{1,0:T(8,128)(2,1)}, bf16[48,1536]{1,0:T(8,128)(2,1)}, u32[]{:S(2)}, u32[]{:S(2)}) collective-permute-start(bf16[48,1536]{1,0:T(8,128)(2,1)} %get-tuple-element.1061), channel_id=1, source_target_pairs={{0,16},{4,20},{8,24},{12,28},{16,0},{20,4},{24,8},{28,12},{1,17},{... | collective-permute-start | bytes 442376 | tf_op jit(solution)/shard_map/ppermute | solution.py:533
  894.6 27.9 %collective-permute-start.157 = (bf16[48,1536]{1,0:T(8,128)(2,1)}, bf16[48,1536]{1,0:T(8,128)(2,1)}, u32[]{:S(2)}, u32[]{:S(2)}) collective-permute-start(bf16[48,1536]{1,0:T(8,128)(2,1)} %get-tuple-element.1061), channel_id=1, source_target_pairs={{0,8},{4,12},{8,16},{12,20},{16,24},{20,28},{24,0},{28,4},{1,9},{5... | collective-permute-start | bytes 442376 | tf_op jit(solution)/shard_map/ppermute | solution.py:533
  921.2 21.9 %collective-permute-start.165 = (bf16[192,2176]{1,0:T(8,128)(2,1)S(1)}, bf16[192,2176]{1,0:T(8,128)(2,1)S(1)}, u32[]{:S(2)}, u32[]{:S(2)}) collective-permute-start(bf16[192,2176]{1,0:T(8,128)(2,1)S(1)} %slice.567), channel_id=1, source_target_pairs={{0,4},{4,0},{8,12},{12,8},{16,20},{20,16},{24,28},{28,24},{1,5},{5... | collective-permute-start | bytes 2506760 | tf_op jit(solution)/shard_map/ppermute | solution.py:451
  925.4 21.3 %collective-permute-start.161 = (bf16[48,640]{1,0:T(8,128)(2,1)S(1)}, bf16[48,640]{1,0:T(8,128)(2,1)S(1)}, u32[]{:S(2)}, u32[]{:S(2)}) collective-permute-start(bf16[48,640]{1,0:T(8,128)(2,1)S(1)} %get-tuple-element.1203), channel_id=1, source_target_pairs={{0,8},{4,12},{8,16},{12,20},{16,24},{20,28},{24,0},{28,4},{1,9},{5... | collective-permute-start | bytes 184328 | tf_op jit(solution)/shard_map/ppermute | solution.py:533
  929.4 21.0 %collective-permute-start.162 = (bf16[48,640]{1,0:T(8,128)(2,1)S(1)}, bf16[48,640]{1,0:T(8,128)(2,1)S(1)}, u32[]{:S(2)}, u32[]{:S(2)}) collective-permute-start(bf16[48,640]{1,0:T(8,128)(2,1)S(1)} %get-tuple-element.1202), channel_id=1, source_target_pairs={{0,16},{4,20},{8,24},{12,28},{16,0},{20,4},{24,8},{28,12},{1,17},{... | collective-permute-start | bytes 184328 | tf_op jit(solution)/shard_map/ppermute | solution.py:533
  935.4 21.7 %collective-permute-start.164 = (bf16[192,1536]{1,0:T(8,128)(2,1)S(1)}, bf16[192,1536]{1,0:T(8,128)(2,1)S(1)}, u32[]{:S(2)}, u32[]{:S(2)}) collective-permute-start(bf16[192,1536]{1,0:T(8,128)(2,1)S(1)} %bitcast.554), channel_id=1, source_target_pairs={{0,4},{4,0},{8,12},{12,8},{16,20},{20,16},{24,28},{28,24},{1,5},{5... | collective-permute-start | bytes 1769480 | tf_op jit(solution)/shard_map/ppermute | solution.py:451
  937.8 19.3 %collective-permute-start.158 = (bf16[48,1536]{1,0:T(8,128)(2,1)S(1)}, bf16[48,1536]{1,0:T(8,128)(2,1)S(1)}, u32[]{:S(2)}, u32[]{:S(2)}) collective-permute-start(bf16[48,1536]{1,0:T(8,128)(2,1)S(1)} %get-tuple-element.1063), channel_id=1, source_target_pairs={{0,24},{4,28},{8,0},{12,4},{16,8},{20,12},{24,16},{28,20},{1,25},{... | collective-permute-start | bytes 442376 | tf_op jit(solution)/shard_map/ppermute | solution.py:533
  (352 other events, 4330.7 us)
Sparse Core Ops, SparseCore 0:
  40.3 44.5 all-gather.14
  119.2 17.1 all-gather.10
  138.0 37.4 all-gather.16
  176.9 37.4 all-gather.18
  215.8 19.6 all-gather.12
  237.5 37.4 all-gather.20

commit v6 on v5

--- a/solution.py
+++ b/solution.py
@@ -909,13 +909,15 @@
     query_across_beside = core_swap(query_across)
     kv_pieces = [kv_first, kv_beside, kv_across, kv_crossed, kv_across_beside]
     kv_pieces.append(core_swap(kv_crossed))
-    first_pair = shard_rows_of(project(matched, kv_pieces, tables))
+    first_own = project(matched, kv_pieces, tables)
+    first_crossed = row_swap(first_own)
     held_tables = [(own_table, own_table)]
     for _ in range(lines.count - 1):
         held_tables = lines.step_gather(held_tables)
-    query_crossed, query_across_beside, first_pair, q_gated, later = settle(
-        [late], query_crossed, query_across_beside, first_pair, q_gated, later
+    query_crossed, query_across_beside, first_own, first_crossed, q_gated, later = settle(
+        [late], query_crossed, query_across_beside, first_own, first_crossed, q_gated, later
     )
+    first_pair = jnp.concatenate([first_own, first_crossed], axis=0)
     near_tables = jnp.stack([lines.slot(held_tables, j) for j in range(lines.count)], axis=0)
     query_pieces = [query_own, query_beside, query_across, query_crossed, query_across_beside]
     query_pieces.append(core_swap(query_crossed))

time: 1010 us -> 1010 us (level)
  waiting for transfers between devices: 379 us -> 396 us
  starting transfers between devices: 177 us -> 162 us
    ppermute x46, starting transfers between devices: 47.9 us -> 37 us  [swap(): lax.ppermute(values, 'expert', [(i, i ^ 1) for i in range(self.experts)])]
    ppermute x46, waiting for transfers between devices: 229 us -> 239 us  [swap(): lax.ppermute(values, 'expert', [(i, i ^ 1) for i in range(self.experts)])]
    unnamed x484 -> x467, local copies, waits for them, and re-layouts: 28.4 us -> 22.9 us
  transfers between devices with their start and end apart: 178 -> 178, of which waited for: 84 -> 80; matrix products, arithmetic and copies ran while one was open for 23% -> 24% of each run, Pallas kernels for 12% -> 12%
where the time goes in v6:
time: 1010 us; the launch traced here: 1000 us
  waiting for transfers between devices  396 us (39%)
  starting transfers between devices  162 us (16%)
  matrix products  156 us (15%)
  Pallas kernels  142 us (14%)
  local copies, waits for them, and re-layouts  87 us (9%)
  other arithmetic  41.6 us (4%)
  between operations  18.9 us (2%)
    ppermute x46, waiting for transfers between devices, swap(): lax.ppermute(values, 'expert', [(i, i ^ 1) for i in range(self.experts)])  239 us
    dot_general x57, matrix products, mm_tn(): lax.dot_general(left, right, (((0,), (0,)), ((), ())), preferred_element_...  82.8 us
    ppermute x27, waiting for transfers between devices, even(): lax.ppermute(values, 'expert', [(i, i ^ 2) for i in range(self.experts)])  64 us
    dot_general x38, matrix products, mm(): return jnp.dot(left, right, preferred_element_type=f32)  61.8 us
    ppermute x27, starting transfers between devices, even(): lax.ppermute(values, 'expert', [(i, i ^ 2) for i in range(self.experts)])  45.8 us
    pallas_call x4, Pallas kernels, expert_backward(): pl.pallas_call(kernel, grid=(2,), in_specs=[by_row(width), by_row(hidden)...  44.4 us
    ppermute x24, waiting for transfers between devices, turn(): return lax.ppermute(values, 'expert', pairs)  41.7 us
    ppermute x24, starting transfers between devices, turn(): return lax.ppermute(values, 'expert', pairs)  41.6 us
  transfers between devices with their start and end apart: 178, of which 80 were waited for; matrix products, arithmetic and copies ran while one was open for 24% of the time, Pallas kernels for 12%

profile of v6, /device:TPU:0, one launch (start us, length us, event | category | flops | bytes accessed | tf_op | source)
XLA Modules:
  0.0 1003.3 jit_solution(10054823617940419266)
XLA Ops:
  43.8 6.9 collective-permute-start.20
  67.3 7.7 collective-permute-done.14
  81.3 4.4 shard_map.518.q_ref
  85.7 9.0 shard_map.519
  95.6 4.3 multiply_reduce_fusion.8
  114.0 7.5 collective-permute-done.26
  138.6 9.8 collective-permute-done.29
  160.2 5.4 collective-permute-done.31
  172.7 7.1 collective-permute-done.32
  185.9 9.7 shard_map.520
  198.7 9.8 shard_map.521
  219.2 7.6 collective-permute-done.38
  237.6 8.8 collective-permute-done.40
  250.2 13.3 %collective-permute-done.43 = bf16[160,1536]{1,0:T(8,128)(2,1)S(1)} collective-permute-done((bf16[160,1536]{1,0:T(8,128)(2,1)S(1)}, bf16[160,1536]{1,0:T(8,128)(2,1)S(1)}, u32[]{:S(2)}, u32[]{:S(2)}) %collective-permute-start.43) | collective-permute-done | bytes 491552 | tf_op jit(solution)/shard_map/ppermute | solution.py:451
  263.5 5.4 collective-permute-done.44
  276.3 3.7 fusion.6.q_ref
  280.0 3.8 collective-permute-done.47
  287.6 9.2 shard_map.523
  296.8 4.8 multiply_reduce_fusion.6
  308.2 10.5 %collective-permute-done.52 = bf16[160,1536]{1,0:T(8,128)(2,1)S(1)} collective-permute-done((bf16[160,1536]{1,0:T(8,128)(2,1)S(1)}, bf16[160,1536]{1,0:T(8,128)(2,1)S(1)}, u32[]{:S(2)}, u32[]{:S(2)}) %collective-permute-start.52) | collective-permute-done | bytes 491552 | tf_op jit(solution)/shard_map/ppermute | solution.py:451
  318.7 4.1 collective-permute-done.50
  330.3 9.7 collective-permute-done.55
  350.0 6.4 collective-permute-done.57
  356.5 4.1 collective-permute-done.56
  365.4 7.2 collective-permute-done.58
  372.7 9.2 shard_map.524
  385.2 9.2 shard_map.525
  394.4 11.0 %shard_map.526 = (bf16[640,1664]{1,0:T(8,128)(2,1)S(1)}, bf16[1280,1536]{1,0:T(8,128)(2,1)S(1)}) custom-call(bf16[1280,1536]{1,0:T(8,128)(2,1)S(1)} %constant_dynamic-update-slice_fusion.5.d_ref, bf16[1280,768]{1,0:T(8,128)(2,1)S(1)} %get-tuple-element.717.pre_ref, bf16[1280,768]{1,0:T(8,128)(2,1)S(1)} %get-tuple-element.718.up_ref, ...), custom_call_target="tpu_custom_call" | custom-call | flops 4529848320 | bytes 16908288 | tf_op jit(solution)/shard_map/pallas_call | solution.py:377
  411.7 11.1 %shard_map.527 = (bf16[640,1664]{1,0:T(8,128)(2,1)S(1)}, bf16[1280,1536]{1,0:T(8,128)(2,1)S(1)}) custom-call(bf16[1280,1536]{1,0:T(8,128)(2,1)S(1)} %constant_dynamic-update-slice_fusion.5.d_ref, bf16[1280,768]{1,0:T(8,128)(2,1)S(1)} %get-tuple-element.717.pre_ref, bf16[1280,768]{1,0:T(8,128)(2,1)S(1)} %get-tuple-element.718.up_ref, ...), custom_call_target="tpu_custom_call", output_to_operand_aliasing={{1}: (8, {})} | custom-call | flops 4529848320 | bytes 16908288 | tf_op jit(solution)/shard_map/pallas_call | solution.py:377
  439.8 9.4 collective-permute-done.62
  449.3 5.6 collective-permute-done.63
  467.1 12.1 %collective-permute-done.65 = bf16[160,1664]{1,0:T(8,128)(2,1)} collective-permute-done((bf16[160,1664]{1,0:T(8,128)(2,1)}, bf16[160,1664]{1,0:T(8,128)(2,1)}, u32[]{:S(2)}, u32[]{:S(2)}) %collective-permute-start.65) | collective-permute-done | bytes 532512 | tf_op jit(solution)/shard_map/ppermute | solution.py:451
  479.2 6.0 collective-permute-done.66
  496.6 10.5 %collective-permute-done.71 = bf16[160,1664]{1,0:T(8,128)(2,1)S(1)} collective-permute-done((bf16[160,1664]{1,0:T(8,128)(2,1)S(1)}, bf16[160,1664]{1,0:T(8,128)(2,1)S(1)}, u32[]{:S(2)}, u32[]{:S(2)}) %collective-permute-start.71) | collective-permute-done | bytes 532512 | tf_op jit(solution)/shard_map/ppermute | solution.py:451
  507.1 3.9 collective-permute-done.72
  524.4 17.2 %shard_map.528 = (bf16[256,1536]{1,0:T(8,128)(2,1)S(1)}, bf16[1024,512]{1,0:T(8,128)(2,1)S(1)}) custom-call(bf16[256,1536]{1,0:T(8,128)(2,1)S(1)} %copy-done.40, bf16[1024,512]{1,0:T(8,128)(2,1)S(1)} %constant_dynamic-update-slice_fusion.23.kv_ref, bf16[256,1536]{1,0:T(8,128)(2,1)S(1)} %fusion.35.dm_ref, ...), custom_call_target="tpu_custom_call" | custom-call | flops 8053063680 | bytes 3145728 | tf_op jit(solution)/shard_map/pallas_call | solution.py:236
  557.0 4.5 collective-permute-done.82.second_ref
  568.8 7.8 collective-permute-done.86
  583.3 4.4 collective-permute-done.93
  590.9 4.1 collective-permute-done.89
  609.8 7.1 collective-permute-done.96
  631.4 6.0 collective-permute-done.103
  650.2 12.5 %collective-permute-done.109 = bf16[192,640]{1,0:T(8,128)(2,1)S(1)} collective-permute-done((bf16[192,640]{1,0:T(8,128)(2,1)S(1)}, bf16[192,640]{1,0:T(8,128)(2,1)S(1)}, u32[]{:S(2)}, u32[]{:S(2)}) %collective-permute-start.109) | collective-permute-done | bytes 245792 | tf_op jit(solution)/shard_map/ppermute | solution.py:451
  664.5 11.1 %shard_map.530 = (bf16[640,1664]{1,0:T(8,128)(2,1)S(1)}, bf16[1280,1536]{1,0:T(8,128)(2,1)S(1)}) custom-call(bf16[1280,1536]{1,0:T(8,128)(2,1)} %constant_dynamic-update-slice_fusion.d_ref, bf16[1280,768]{1,0:T(8,128)(2,1)S(1)} %copy-done.9, bf16[1280,768]{1,0:T(8,128)(2,1)S(1)} %copy-done.11, f32[1280,1]{1,0:T(8,128)S(1)} %copy-done.19, ...), custom_call_target="tpu_custom_call" | custom-call | flops 4529848320 | bytes 16908288 | tf_op jit(solution)/shard_map/pallas_call | solution.py:377
  684.6 11.3 %shard_map.531 = (bf16[640,1664]{1,0:T(8,128)(2,1)S(1)}, bf16[1280,1536]{1,0:T(8,128)(2,1)S(1)}) custom-call(bf16[1280,1536]{1,0:T(8,128)(2,1)} %constant_dynamic-update-slice_fusion.d_ref, bf16[1280,768]{1,0:T(8,128)(2,1)S(1)} %copy-done.9, bf16[1280,768]{1,0:T(8,128)(2,1)S(1)} %copy-done.11, ...), custom_call_target="tpu_custom_call", output_to_operand_aliasing={{1}: (8, {})} | custom-call | flops 4529848320 | bytes 16908288 | tf_op jit(solution)/shard_map/pallas_call | solution.py:377
  696.0 9.2 collective-permute-done.112
  719.0 4.8 collective-permute-done.133
  727.0 6.5 collective-permute-start.115
  737.9 12.1 %collective-permute-done.114 = bf16[160,1664]{1,0:T(8,128)(2,1)S(1)} collective-permute-done((bf16[160,1664]{1,0:T(8,128)(2,1)S(1)}, bf16[160,1664]{1,0:T(8,128)(2,1)S(1)}, u32[]{:S(2)}, u32[]{:S(2)}) %collective-permute-start.114) | collective-permute-done | bytes 532512 | tf_op jit(solution)/shard_map/ppermute | solution.py:451
  770.7 11.3 %collective-permute-done.117 = bf16[160,1664]{1,0:T(8,128)(2,1)S(1)} collective-permute-done((bf16[160,1664]{1,0:T(8,128)(2,1)S(1)}, bf16[160,1664]{1,0:T(8,128)(2,1)S(1)}, u32[]{:S(2)}, u32[]{:S(2)}) %collective-permute-start.117) | collective-permute-done | bytes 532512 | tf_op jit(solution)/shard_map/ppermute | solution.py:451
  797.0 8.2 collective-permute-done.123
  814.5 17.1 %shard_map.532 = (bf16[256,1536]{1,0:T(8,128)(2,1)S(1)}, bf16[1024,512]{1,0:T(8,128)(2,1)S(1)}) custom-call(bf16[256,1536]{1,0:T(8,128)(2,1)S(1)} %copy-done.38, bf16[1024,512]{1,0:T(8,128)(2,1)S(1)} %copy-done.36, bf16[256,1536]{1,0:T(8,128)(2,1)S(1)} %convolution_convert_fusion.4.dm_ref, f32[256,128]{1,0:T(8,128)S(1)} %get-tuple-element.515.refs_12_.cos_ref.refs_2_, ...), custom_call_target="tpu_custom_call" | custom-call | flops 8053063680 | bytes 3145728 | tf_op jit(solution)/shard_map/pallas_call | solution.py:236
  847.2 3.7 fusion.194
  859.5 8.9 collective-permute-done.138
  869.8 6.1 collective-permute-done.140
  887.0 5.6 collective-permute-done.144
  908.3 6.0 collective-permute-done.150
  915.4 6.7 collective-permute-done.151
  927.3 3.7 collective-permute-done.154
  942.6 6.3 collective-permute-done.165
  962.1 5.4 collective-permute-start.167
  970.9 6.2 collective-permute-done.170
  977.1 9.0 collective-permute-done.166
  988.4 4.7 collective-permute-done.171
  (1120 shorter events, 488.6 us)
Async XLA Ops:
  7.2 88.4 %all-gather.15.cloned.1.call-start = ((), (), s32[]{:S(2)}) async-start(), calls=%async_computation.2 | async-start | bytes 5898240 | tf_op jit(solution)/shard_map/all_gather | solution.py:904
  12.4 25.2 %collective-permute-start = (bf16[256,1536]{1,0:T(8,128)(2,1)}, bf16[256,1536]{1,0:T(8,128)(2,1)}, u32[]{:S(2)}, u32[]{:S(2)}) collective-permute-start(bf16[256,1536]{1,0:T(8,128)(2,1)} %param.50), channel_id=1, source_target_pairs={{0,8},{4,12},{8,0},{12,4},{16,24},{20,28},{24,16},{28,20},{1,9},{5... | collective-permute-start | bytes 2359304 | tf_op jit(solution)/shard_map/ppermute | solution.py:454
  40.2 231.2 %all-gather.11.cloned.1.call-start = ((), (), s32[]{:S(2)}) async-start(), calls=%async_computation | async-start | bytes 1966080 | tf_op jit(solution)/shard_map/all_gather | solution.py:904
  41.6 33.4 %collective-permute-start.11 = (bf16[192,1536]{1,0:T(8,128)(2,1)}, bf16[192,1536]{1,0:T(8,128)(2,1)}, u32[]{:S(2)}, u32[]{:S(2)}) collective-permute-start(bf16[192,1536]{1,0:T(8,128)(2,1)} %collective-permute-done.6.refs_8_), channel_id=1, source_target_pairs={{0,4},{4,0},{8,12},{12,8},{16,20},{20,16},{24,28},{28,24},{1,5},{5... | collective-permute-start | bytes 1769480 | tf_op jit(solution)/shard_map/ppermute | solution.py:451
  43.2 31.9 %collective-permute-start.12 = (bf16[192,1536]{1,0:T(8,128)(2,1)}, bf16[192,1536]{1,0:T(8,128)(2,1)}, u32[]{:S(2)}, u32[]{:S(2)}) collective-permute-start(bf16[192,1536]{1,0:T(8,128)(2,1)} %collective-permute-done.6.refs_8_), channel_id=1, source_target_pairs={{0,1},{1,0},{2,3},{3,2},{4,5},{5,4},{6,7},{7,6},{8,9},{9,8},{10,11... | collective-permute-start | bytes 1769480 | tf_op jit(solution)/shard_map/ppermute | solution.py:537
  79.5 20.7 %collective-permute-start.17 = (bf16[256,1536]{1,0:T(8,128)(2,1)}, bf16[256,1536]{1,0:T(8,128)(2,1)}, u32[]{:S(2)}, u32[]{:S(2)}) collective-permute-start(bf16[256,1536]{1,0:T(8,128)(2,1)} %copy-done.118), channel_id=1, source_target_pairs={{0,8},{4,12},{8,0},{12,4},{16,24},{20,28},{24,16},{28,20},{1,9},{5... | collective-permute-start | bytes 2359304 | tf_op jit(solution)/shard_map/ppermute | solution.py:454
  80.1 20.1 %collective-permute-start.18 = (bf16[256,1536]{1,0:T(8,128)(2,1)}, bf16[256,1536]{1,0:T(8,128)(2,1)}, u32[]{:S(2)}, u32[]{:S(2)}) collective-permute-start(bf16[256,1536]{1,0:T(8,128)(2,1)} %collective-permute-done), channel_id=1, source_target_pairs={{0,1},{1,0},{2,3},{3,2},{4,5},{5,4},{6,7},{7,6},{8,16},{9,17},{10,... | collective-permute-start | bytes 2359304 | tf_op jit(solution)/shard_map/ppermute | solution.py:466
  100.3 21.2 %collective-permute-start.24 = (bf16[256,1536]{1,0:T(8,128)(2,1)S(1)}, bf16[256,1536]{1,0:T(8,128)(2,1)S(1)}, u32[]{:S(2)}, u32[]{:S(2)}) collective-permute-start(bf16[256,1536]{1,0:T(8,128)(2,1)S(1)} %multiply_convert_fusion.2), channel_id=1, source_target_pairs={{0,8},{4,12},{8,0},{12,4},{16,24},{20,28},{24,16},{28,20},{1,9},{5... | collective-permute-start | bytes 2359304 | tf_op jit(solution)/shard_map/ppermute | solution.py:454
  123.4 152.9 %all-gather.17.cloned.1.call-start = ((), (), s32[]{:S(2)}) async-start(), calls=%async_computation.3 | async-start | bytes 5898240 | tf_op jit(solution)/shard_map/all_gather | solution.py:904
  126.8 170.0 %all-gather.19.cloned.1.call-start = ((), (), s32[]{:S(2)}) async-start(), calls=%async_computation.4 | async-start | bytes 5898240 | tf_op jit(solution)/shard_map/all_gather | solution.py:904
  128.1 175.0 %all-gather.13.cloned.1.call-start = ((), (), s32[]{:S(2)}) async-start(), calls=%async_computation.1 | async-start | bytes 1966080 | tf_op jit(solution)/shard_map/all_gather | solution.py:904
  129.0 174.2 %all-gather.21.cloned.1.call-start = ((), (), s32[]{:S(2)}) async-start(), calls=%async_computation.5 | async-start | bytes 5898240 | tf_op jit(solution)/shard_map/all_gather | solution.py:904
  180.7 31.1 %collective-permute-start.33 = (bf16[256,1536]{1,0:T(8,128)(2,1)}, bf16[256,1536]{1,0:T(8,128)(2,1)S(1)}, u32[]{:S(2)}, u32[]{:S(2)}) collective-permute-start(bf16[256,1536]{1,0:T(8,128)(2,1)} %collective-permute-done.18), channel_id=1, source_target_pairs={{0,8},{4,12},{8,0},{12,4},{16,24},{20,28},{24,16},{28,20},{1,9},{5... | collective-permute-start | bytes 2359304 | tf_op jit(solution)/shard_map/ppermute | solution.py:454
  181.8 26.9 %collective-permute-start.34 = (bf16[160,1536]{1,0:T(8,128)(2,1)S(1)}, bf16[160,1536]{1,0:T(8,128)(2,1)S(1)}, u32[]{:S(2)}, u32[]{:S(2)}) collective-permute-start(bf16[160,1536]{1,0:T(8,128)(2,1)S(1)} %copy-done.161), channel_id=1, source_target_pairs={{0,4},{4,0},{8,12},{12,8},{16,20},{20,16},{24,28},{28,24},{1,5},{5... | collective-permute-start | bytes 1474568 | tf_op jit(solution)/shard_map/ppermute | solution.py:451
  182.1 26.5 %collective-permute-start.35 = (bf16[160,1536]{1,0:T(8,128)(2,1)S(1)}, bf16[160,1536]{1,0:T(8,128)(2,1)S(1)}, u32[]{:S(2)}, u32[]{:S(2)}) collective-permute-start(bf16[160,1536]{1,0:T(8,128)(2,1)S(1)} %copy-done.164), channel_id=1, source_target_pairs={{0,4},{4,0},{8,12},{12,8},{16,20},{20,16},{24,28},{28,24},{1,5},{5... | collective-permute-start | bytes 1474568 | tf_op jit(solution)/shard_map/ppermute | solution.py:451
  249.7 19.2 %collective-permute-start.44 = (bf16[256,1536]{1,0:T(8,128)(2,1)S(1)}, bf16[256,1536]{1,0:T(8,128)(2,1)S(1)}, u32[]{:S(2)}, u32[]{:S(2)}) collective-permute-start(bf16[256,1536]{1,0:T(8,128)(2,1)S(1)} %get-tuple-element.1139), channel_id=1, source_target_pairs={{0,8},{4,12},{8,0},{12,4},{16,24},{20,28},{24,16},{28,20},{1,9},{5... | collective-permute-start | bytes 2359304 | tf_op jit(solution)/shard_map/ppermute | solution.py:454
  249.9 19.0 %collective-permute-start.45 = (bf16[256,1536]{1,0:T(8,128)(2,1)S(1)}, bf16[256,1536]{1,0:T(8,128)(2,1)S(1)}, u32[]{:S(2)}, u32[]{:S(2)}) collective-permute-start(bf16[256,1536]{1,0:T(8,128)(2,1)S(1)} %get-tuple-element.1138), channel_id=1, source_target_pairs={{0,1},{1,0},{2,3},{3,2},{4,5},{5,4},{6,7},{7,6},{8,16},{9,17},{10,... | collective-permute-start | bytes 2359304 | tf_op jit(solution)/shard_map/ppermute | solution.py:466
  303.1 19.7 %collective-permute-start.50 = (bf16[256,1536]{1,0:T(8,128)(2,1)S(1)}, bf16[256,1536]{1,0:T(8,128)(2,1)S(1)}, u32[]{:S(2)}, u32[]{:S(2)}) collective-permute-start(bf16[256,1536]{1,0:T(8,128)(2,1)S(1)} %multiply_convert_fusion), channel_id=1, source_target_pairs={{0,8},{4,12},{8,0},{12,4},{16,24},{20,28},{24,16},{28,20},{1,9},{5... | collective-permute-start | bytes 2359304 | tf_op jit(solution)/shard_map/ppermute | solution.py:454
  322.9 19.5 %collective-permute-start.53 = (bf16[256,1536]{1,0:T(8,128)(2,1)S(1)}, bf16[256,1536]{1,0:T(8,128)(2,1)S(1)}, u32[]{:S(2)}, u32[]{:S(2)}) collective-permute-start(bf16[256,1536]{1,0:T(8,128)(2,1)S(1)} %collective-permute-done.51), channel_id=1, source_target_pairs={{0,8},{4,12},{8,0},{12,4},{16,24},{20,28},{24,16},{28,20},{1,9},{5... | collective-permute-start | bytes 2359304 | tf_op jit(solution)/shard_map/ppermute | solution.py:454
  430.2 24.7 %collective-permute-start.64 = (bf16[768,1536]{1,0:T(8,128)(2,1)S(1)}, bf16[768,1536]{1,0:T(8,128)(2,1)S(1)}, u32[]{:S(2)}, u32[]{:S(2)}) collective-permute-start(bf16[768,1536]{1,0:T(8,128)(2,1)S(1)} %pad_maximum_fusion.3), channel_id=1, source_target_pairs={{0,1},{1,0},{2,3},{3,2},{4,5},{5,4},{6,7},{7,6},{8,9},{9,8},{10,11... | collective-permute-start | bytes 7077896 | tf_op jit(solution)/shard_map/ppermute | solution.py:537
  433.5 21.4 %collective-permute-start.63 = (bf16[256,1664]{1,0:T(8,128)(2,1)S(1)}, bf16[256,1664]{1,0:T(8,128)(2,1)S(1)}, u32[]{:S(2)}, u32[]{:S(2)}) collective-permute-start(bf16[256,1664]{1,0:T(8,128)(2,1)S(1)} %get-tuple-element.1236), channel_id=1, source_target_pairs={{0,8},{4,12},{8,0},{12,4},{16,24},{20,28},{24,16},{28,20},{1,9},{5... | collective-permute-start | bytes 2555912 | tf_op jit(solution)/shard_map/ppermute | solution.py:454
  437.1 27.5 %collective-permute-start.70 = (bf16[160,1536]{1,0:T(8,128)(2,1)S(1)}, bf16[160,1536]{1,0:T(8,128)(2,1)}, u32[]{:S(2)}, u32[]{:S(2)}) collective-permute-start(bf16[160,1536]{1,0:T(8,128)(2,1)S(1)} %copy-done.163), channel_id=1, source_target_pairs={{0,4},{4,0},{8,12},{12,8},{16,20},{20,16},{24,28},{28,24},{1,5},{5... | collective-permute-start | bytes 1474568 | tf_op jit(solution)/shard_map/ppermute | solution.py:451
  458.2 28.0 %collective-permute-start.68 = (bf16[384,1536]{1,0:T(8,128)(2,1)}, bf16[384,1536]{1,0:T(8,128)(2,1)}, u32[]{:S(2)}, u32[]{:S(2)}) collective-permute-start(bf16[384,1536]{1,0:T(8,128)(2,1)} %fusion.19), channel_id=1, source_target_pairs={{0,2},{1,3},{2,0},{3,1},{4,6},{5,7},{6,4},{7,5},{8,10},{9,11},{10,... | collective-permute-start | bytes 3538952 | tf_op jit(solution)/shard_map/ppermute | solution.py:541
  461.8 24.4 %collective-permute-start.69 = (bf16[384,1536]{1,0:T(8,128)(2,1)}, bf16[384,1536]{1,0:T(8,128)(2,1)}, u32[]{:S(2)}, u32[]{:S(2)}) collective-permute-start(bf16[384,1536]{1,0:T(8,128)(2,1)} %pad_maximum_fusion.9), channel_id=1, source_target_pairs={{0,1},{1,0},{2,3},{3,2},{4,5},{5,4},{6,7},{7,6},{8,9},{9,8},{10,11... | collective-permute-start | bytes 3538952 | tf_op jit(solution)/shard_map/ppermute | solution.py:537
  463.5 21.7 %collective-permute-start.66 = (bf16[256,1664]{1,0:T(8,128)(2,1)}, bf16[256,1664]{1,0:T(8,128)(2,1)}, u32[]{:S(2)}, u32[]{:S(2)}) collective-permute-start(bf16[256,1664]{1,0:T(8,128)(2,1)} %get-tuple-element.1133), channel_id=1, source_target_pairs={{0,8},{4,12},{8,0},{12,4},{16,24},{20,28},{24,16},{28,20},{1,9},{5... | collective-permute-start | bytes 2555912 | tf_op jit(solution)/shard_map/ppermute | solution.py:454
  464.4 20.9 %collective-permute-start.67 = (bf16[256,1664]{1,0:T(8,128)(2,1)}, bf16[256,1664]{1,0:T(8,128)(2,1)}, u32[]{:S(2)}, u32[]{:S(2)}) collective-permute-start(bf16[256,1664]{1,0:T(8,128)(2,1)} %get-tuple-element.1132), channel_id=1, source_target_pairs={{0,1},{1,0},{2,3},{3,2},{4,5},{5,4},{6,7},{7,6},{8,16},{9,17},{10,... | collective-permute-start | bytes 2555912 | tf_op jit(solution)/shard_map/ppermute | solution.py:466
  491.2 19.9 %collective-permute-start.72 = (bf16[256,1664]{1,0:T(8,128)(2,1)S(1)}, bf16[256,1664]{1,0:T(8,128)(2,1)S(1)}, u32[]{:S(2)}, u32[]{:S(2)}) collective-permute-start(bf16[256,1664]{1,0:T(8,128)(2,1)S(1)} %get-tuple-element.1131), channel_id=1, source_target_pairs={{0,8},{4,12},{8,0},{12,4},{16,24},{20,28},{24,16},{28,20},{1,9},{5... | collective-permute-start | bytes 2555912 | tf_op jit(solution)/shard_map/ppermute | solution.py:454
  492.1 19.0 %collective-permute-start.73 = (bf16[256,1664]{1,0:T(8,128)(2,1)S(1)}, bf16[256,1664]{1,0:T(8,128)(2,1)S(1)}, u32[]{:S(2)}, u32[]{:S(2)}) collective-permute-start(bf16[256,1664]{1,0:T(8,128)(2,1)S(1)} %get-tuple-element.1130), channel_id=1, source_target_pairs={{0,1},{1,0},{2,3},{3,2},{4,5},{5,4},{6,7},{7,6},{8,16},{9,17},{10,... | collective-permute-start | bytes 2555912 | tf_op jit(solution)/shard_map/ppermute | solution.py:466
  495.2 27.5 %collective-permute-start.78 = (bf16[192,1536]{1,0:T(8,128)(2,1)S(1)}, bf16[192,1536]{1,0:T(8,128)(2,1)S(1)}, u32[]{:S(2)}, u32[]{:S(2)}) collective-permute-start(bf16[192,1536]{1,0:T(8,128)(2,1)S(1)} %fusion.42), channel_id=1, source_target_pairs={{0,2},{1,3},{2,0},{3,1},{4,6},{5,7},{6,4},{7,5},{8,10},{9,11},{10,... | collective-permute-start | bytes 1769480 | tf_op jit(solution)/shard_map/ppermute | solution.py:541
  511.1 30.6 %collective-permute-start.74 = (bf16[160,1536]{1,0:T(8,128)(2,1)S(1)}, bf16[160,1536]{1,0:T(8,128)(2,1)S(1)}, u32[]{:S(2)}, u32[]{:S(2)}) collective-permute-start(bf16[160,1536]{1,0:T(8,128)(2,1)S(1)} %copy-done.156), channel_id=1, source_target_pairs={{0,4},{4,0},{8,12},{12,8},{16,20},{20,16},{24,28},{28,24},{1,5},{5... | collective-permute-start | bytes 1474568 | tf_op jit(solution)/shard_map/ppermute | solution.py:451
  513.6 28.1 %collective-permute-start.76 = (bf16[256,1536]{1,0:T(8,128)(2,1)S(1)}, bf16[256,1536]{1,0:T(8,128)(2,1)S(1)}, u32[]{:S(2)}, u32[]{:S(2)}) collective-permute-start(bf16[256,1536]{1,0:T(8,128)(2,1)S(1)} %get-tuple-element.1137), channel_id=1, source_target_pairs={{0,8},{4,12},{8,0},{12,4},{16,24},{20,28},{24,16},{28,20},{1,9},{5... | collective-permute-start | bytes 2359304 | tf_op jit(solution)/shard_map/ppermute | solution.py:454
  515.4 26.3 %collective-permute-start.77 = (bf16[256,1536]{1,0:T(8,128)(2,1)S(1)}, bf16[256,1536]{1,0:T(8,128)(2,1)S(1)}, u32[]{:S(2)}, u32[]{:S(2)}) collective-permute-start(bf16[256,1536]{1,0:T(8,128)(2,1)S(1)} %get-tuple-element.1136), channel_id=1, source_target_pairs={{0,1},{1,0},{2,3},{3,2},{4,5},{5,4},{6,7},{7,6},{8,16},{9,17},{10,... | collective-permute-start | bytes 2359304 | tf_op jit(solution)/shard_map/ppermute | solution.py:466
  519.9 21.8 %collective-permute-start.79 = (bf16[256,1536]{1,0:T(8,128)(2,1)S(1)}, bf16[256,1536]{1,0:T(8,128)(2,1)S(1)}, u32[]{:S(2)}, u32[]{:S(2)}) collective-permute-start(bf16[256,1536]{1,0:T(8,128)(2,1)S(1)} %fusion.173), channel_id=1, source_target_pairs={{0,2},{1,3},{2,0},{3,1},{4,6},{5,7},{6,4},{7,5},{8,10},{9,11},{10,... | collective-permute-start | bytes 2359304 | tf_op jit(solution)/shard_map/ppermute | solution.py:541
  522.7 19.0 %collective-permute-start.75 = (bf16[160,1536]{1,0:T(8,128)(2,1)S(1)}, bf16[160,1536]{1,0:T(8,128)(2,1)S(1)}, u32[]{:S(2)}, u32[]{:S(2)}) collective-permute-start(bf16[160,1536]{1,0:T(8,128)(2,1)S(1)} %copy-done.155), channel_id=1, source_target_pairs={{0,4},{4,0},{8,12},{12,8},{16,20},{20,16},{24,28},{28,24},{1,5},{5... | collective-permute-start | bytes 1474568 | tf_op jit(solution)/shard_map/ppermute | solution.py:451
  549.6 19.2 %collective-permute-start.87 = (bf16[256,1536]{1,0:T(8,128)(2,1)S(1)}, bf16[256,1536]{1,0:T(8,128)(2,1)S(1)}, u32[]{:S(2)}, u32[]{:S(2)}) collective-permute-start(bf16[256,1536]{1,0:T(8,128)(2,1)S(1)} %get-tuple-element.1135), channel_id=1, source_target_pairs={{0,8},{4,12},{8,0},{12,4},{16,24},{20,28},{24,16},{28,20},{1,9},{5... | collective-permute-start | bytes 2359304 | tf_op jit(solution)/shard_map/ppermute | solution.py:454
  563.1 20.1 %collective-permute-start.92 = (bf16[256,1536]{1,0:T(8,128)(2,1)S(1)}, bf16[256,1536]{1,0:T(8,128)(2,1)S(1)}, u32[]{:S(2)}, u32[]{:S(2)}) collective-permute-start(bf16[256,1536]{1,0:T(8,128)(2,1)S(1)} %get-tuple-element.814), channel_id=1, source_target_pairs={{0,2},{1,3},{2,0},{3,1},{4,6},{5,7},{6,4},{7,5},{8,10},{9,11},{10,... | collective-permute-start | bytes 2359304 | tf_op jit(solution)/shard_map/ppermute | solution.py:541
  606.8 106.6 %collective-permute-start.132 = (bf16[256,384]{1,0:T(8,128)(2,1)}, bf16[256,384]{1,0:T(8,128)(2,1)}, u32[]{:S(2)}, u32[]{:S(2)}) collective-permute-start(bf16[256,384]{1,0:T(8,128)(2,1)} %get-tuple-element.1158), channel_id=1, source_target_pairs={{0,3},{1,2},{2,1},{3,0},{4,7},{5,6},{6,5},{7,4},{8,11},{9,10},{10,... | collective-permute-start | bytes 589832 | tf_op jit(solution)/shard_map/ppermute | solution.py:593
  627.3 22.9 %collective-permute-start.108 = (bf16[192,1536]{1,0:T(8,128)(2,1)}, bf16[192,1536]{1,0:T(8,128)(2,1)}, u32[]{:S(2)}, u32[]{:S(2)}) collective-permute-start(bf16[192,1536]{1,0:T(8,128)(2,1)} %dynamic-slice_convert_fusion.2), channel_id=1, source_target_pairs={{0,4},{4,0},{8,12},{12,8},{16,20},{20,16},{24,28},{28,24},{1,5},{5... | collective-permute-start | bytes 1769480 | tf_op jit(solution)/shard_map/ppermute | solution.py:451
  639.8 22.8 %collective-permute-start.104 = (bf16[160,1536]{1,0:T(8,128)(2,1)}, bf16[160,1536]{1,0:T(8,128)(2,1)}, u32[]{:S(2)}, u32[]{:S(2)}) collective-permute-start(bf16[160,1536]{1,0:T(8,128)(2,1)} %convolution_convert_fusion.9), channel_id=1, source_target_pairs={{0,4},{4,0},{8,12},{12,8},{16,20},{20,16},{24,28},{28,24},{1,5},{5... | collective-permute-start | bytes 1474568 | tf_op jit(solution)/shard_map/ppermute | solution.py:451
  643.6 19.0 %collective-permute-start.109 = (bf16[192,640]{1,0:T(8,128)(2,1)S(1)}, bf16[192,640]{1,0:T(8,128)(2,1)S(1)}, u32[]{:S(2)}, u32[]{:S(2)}) collective-permute-start(bf16[192,640]{1,0:T(8,128)(2,1)S(1)} %fusion.100), channel_id=1, source_target_pairs={{0,4},{4,0},{8,12},{12,8},{16,20},{20,16},{24,28},{28,24},{1,5},{5... | collective-permute-start | bytes 737288 | tf_op jit(solution)/shard_map/ppermute | solution.py:451
  676.8 29.2 %collective-permute-start.110 = (bf16[160,1664]{1,0:T(8,128)(2,1)S(1)}, bf16[160,1664]{1,0:T(8,128)(2,1)S(1)}, u32[]{:S(2)}, u32[]{:S(2)}) collective-permute-start(bf16[160,1664]{1,0:T(8,128)(2,1)S(1)} %get-tuple-element.1096), channel_id=1, source_target_pairs={{0,4},{4,0},{8,12},{12,8},{16,20},{20,16},{24,28},{28,24},{1,5},{5... | collective-permute-start | bytes 1597448 | tf_op jit(solution)/shard_map/ppermute | solution.py:451
  681.0 24.2 %collective-permute-start.112 = (bf16[48,3712]{1,0:T(8,128)(2,1)S(1)}, bf16[48,3712]{1,0:T(8,128)(2,1)S(1)}, u32[]{:S(2)}, u32[]{:S(2)}) collective-permute-start(bf16[48,3712]{1,0:T(8,128)(2,1)S(1)} %get-tuple-element.1147), channel_id=1, source_target_pairs={{0,16},{4,20},{8,24},{12,28},{16,0},{20,4},{24,8},{28,12},{1,17},{... | collective-permute-start | bytes 1069064 | tf_op jit(solution)/shard_map/ppermute | solution.py:533
  683.4 22.6 %collective-permute-start.113 = (bf16[48,3712]{1,0:T(8,128)(2,1)S(1)}, bf16[48,3712]{1,0:T(8,128)(2,1)S(1)}, u32[]{:S(2)}, u32[]{:S(2)}) collective-permute-start(bf16[48,3712]{1,0:T(8,128)(2,1)S(1)} %get-tuple-element.1146), channel_id=1, source_target_pairs={{0,24},{4,28},{8,0},{12,4},{16,8},{20,12},{24,16},{28,20},{1,25},{... | collective-permute-start | bytes 1069064 | tf_op jit(solution)/shard_map/ppermute | solution.py:533
  711.1 41.0 %collective-permute-start.116 = (bf16[768,1536]{1,0:T(8,128)(2,1)}, bf16[768,1536]{1,0:T(8,128)(2,1)}, u32[]{:S(2)}, u32[]{:S(2)}) collective-permute-start(bf16[768,1536]{1,0:T(8,128)(2,1)} %pad_maximum_fusion.4), channel_id=1, source_target_pairs={{0,1},{1,0},{2,3},{3,2},{4,5},{5,4},{6,7},{7,6},{8,9},{9,8},{10,11... | collective-permute-start | bytes 7077896 | tf_op jit(solution)/shard_map/ppermute | solution.py:537
  727.0 25.1 %collective-permute-start.115 = (bf16[256,1664]{1,0:T(8,128)(2,1)S(1)}, bf16[256,1664]{1,0:T(8,128)(2,1)S(1)}, u32[]{:S(2)}, u32[]{:S(2)}) collective-permute-start(bf16[256,1664]{1,0:T(8,128)(2,1)S(1)} %get-tuple-element.1242), channel_id=1, source_target_pairs={{0,8},{4,12},{8,0},{12,4},{16,24},{20,28},{24,16},{28,20},{1,9},{5... | collective-permute-start | bytes 2555912 | tf_op jit(solution)/shard_map/ppermute | solution.py:454
  755.7 29.1 %collective-permute-start.120 = (bf16[384,1536]{1,0:T(8,128)(2,1)S(1)}, bf16[384,1536]{1,0:T(8,128)(2,1)S(1)}, u32[]{:S(2)}, u32[]{:S(2)}) collective-permute-start(bf16[384,1536]{1,0:T(8,128)(2,1)S(1)} %fusion.20), channel_id=1, source_target_pairs={{0,2},{1,3},{2,0},{3,1},{4,6},{5,7},{6,4},{7,5},{8,10},{9,11},{10,... | collective-permute-start | bytes 3538952 | tf_op jit(solution)/shard_map/ppermute | solution.py:541
  762.8 22.0 %collective-permute-start.121 = (bf16[384,1536]{1,0:T(8,128)(2,1)S(1)}, bf16[384,1536]{1,0:T(8,128)(2,1)S(1)}, u32[]{:S(2)}, u32[]{:S(2)}) collective-permute-start(bf16[384,1536]{1,0:T(8,128)(2,1)S(1)} %pad_maximum_fusion.10), channel_id=1, source_target_pairs={{0,1},{1,0},{2,3},{3,2},{4,5},{5,4},{6,7},{7,6},{8,9},{9,8},{10,11... | collective-permute-start | bytes 3538952 | tf_op jit(solution)/shard_map/ppermute | solution.py:537
  763.4 21.4 %collective-permute-start.118 = (bf16[256,1664]{1,0:T(8,128)(2,1)S(1)}, bf16[256,1664]{1,0:T(8,128)(2,1)S(1)}, u32[]{:S(2)}, u32[]{:S(2)}) collective-permute-start(bf16[256,1664]{1,0:T(8,128)(2,1)S(1)} %get-tuple-element.1129), channel_id=1, source_target_pairs={{0,8},{4,12},{8,0},{12,4},{16,24},{20,28},{24,16},{28,20},{1,9},{5... | collective-permute-start | bytes 2555912 | tf_op jit(solution)/shard_map/ppermute | solution.py:454
  765.2 19.6 %collective-permute-start.119 = (bf16[256,1664]{1,0:T(8,128)(2,1)S(1)}, bf16[256,1664]{1,0:T(8,128)(2,1)S(1)}, u32[]{:S(2)}, u32[]{:S(2)}) collective-permute-start(bf16[256,1664]{1,0:T(8,128)(2,1)S(1)} %get-tuple-element.1128), channel_id=1, source_target_pairs={{0,1},{1,0},{2,3},{3,2},{4,5},{5,4},{6,7},{7,6},{8,16},{9,17},{10,... | collective-permute-start | bytes 2555912 | tf_op jit(solution)/shard_map/ppermute | solution.py:466
  786.9 21.3 %collective-permute-start.124 = (bf16[256,1664]{1,0:T(8,128)(2,1)S(1)}, bf16[256,1664]{1,0:T(8,128)(2,1)S(1)}, u32[]{:S(2)}, u32[]{:S(2)}) collective-permute-start(bf16[256,1664]{1,0:T(8,128)(2,1)S(1)} %get-tuple-element.1127), channel_id=1, source_target_pairs={{0,8},{4,12},{8,0},{12,4},{16,24},{20,28},{24,16},{28,20},{1,9},{5... | collective-permute-start | bytes 2555912 | tf_op jit(solution)/shard_map/ppermute | solution.py:454
  796.2 35.4 %collective-permute-start.122 = (bf16[192,1536]{1,0:T(8,128)(2,1)S(1)}, bf16[192,1536]{1,0:T(8,128)(2,1)S(1)}, u32[]{:S(2)}, u32[]{:S(2)}) collective-permute-start(bf16[192,1536]{1,0:T(8,128)(2,1)S(1)} %fusion.43), channel_id=1, source_target_pairs={{0,2},{1,3},{2,0},{3,1},{4,6},{5,7},{6,4},{7,5},{8,10},{9,11},{10,... | collective-permute-start | bytes 1769480 | tf_op jit(solution)/shard_map/ppermute | solution.py:541
  812.4 19.2 %collective-permute-start.126 = (bf16[256,1536]{1,0:T(8,128)(2,1)S(1)}, bf16[256,1536]{1,0:T(8,128)(2,1)S(1)}, u32[]{:S(2)}, u32[]{:S(2)}) collective-permute-start(bf16[256,1536]{1,0:T(8,128)(2,1)S(1)} %get-tuple-element.1068), channel_id=1, source_target_pairs={{0,2},{1,3},{2,0},{3,1},{4,6},{5,7},{6,4},{7,5},{8,10},{9,11},{10,... | collective-permute-start | bytes 2359304 | tf_op jit(solution)/shard_map/ppermute | solution.py:541
  834.4 25.2 %collective-permute-start.137 = (bf16[48,3712]{1,0:T(8,128)(2,1)S(1)}, bf16[48,3712]{1,0:T(8,128)(2,1)S(1)}, u32[]{:S(2)}, u32[]{:S(2)}) collective-permute-start(bf16[48,3712]{1,0:T(8,128)(2,1)S(1)} %get-tuple-element.1067), channel_id=1, source_target_pairs={{0,24},{4,28},{8,0},{12,4},{16,8},{20,12},{24,16},{28,20},{1,25},{... | collective-permute-start | bytes 1069064 | tf_op jit(solution)/shard_map/ppermute | solution.py:533
  837.2 31.3 %collective-permute-start.138 = (bf16[48,3712]{1,0:T(8,128)(2,1)S(1)}, bf16[48,3712]{1,0:T(8,128)(2,1)S(1)}, u32[]{:S(2)}, u32[]{:S(2)}) collective-permute-start(bf16[48,3712]{1,0:T(8,128)(2,1)S(1)} %get-tuple-element.1067), channel_id=1, source_target_pairs={{0,16},{4,20},{8,24},{12,28},{16,0},{20,4},{24,8},{28,12},{1,17},{... | collective-permute-start | bytes 1069064 | tf_op jit(solution)/shard_map/ppermute | solution.py:533
  837.8 30.7 %collective-permute-start.139 = (bf16[48,3712]{1,0:T(8,128)(2,1)S(1)}, bf16[48,3712]{1,0:T(8,128)(2,1)S(1)}, u32[]{:S(2)}, u32[]{:S(2)}) collective-permute-start(bf16[48,3712]{1,0:T(8,128)(2,1)S(1)} %get-tuple-element.1067), channel_id=1, source_target_pairs={{0,8},{4,12},{8,16},{12,20},{16,24},{20,28},{24,0},{28,4},{1,9},{5... | collective-permute-start | bytes 1069064 | tf_op jit(solution)/shard_map/ppermute | solution.py:533
  856.9 18.9 %collective-permute-start.140 = (bf16[256,1536]{1,0:T(8,128)(2,1)S(1)}, bf16[256,1536]{1,0:T(8,128)(2,1)S(1)}, u32[]{:S(2)}, u32[]{:S(2)}) collective-permute-start(bf16[256,1536]{1,0:T(8,128)(2,1)S(1)} %get-tuple-element.919), channel_id=1, source_target_pairs={{0,2},{1,3},{2,0},{3,1},{4,6},{5,7},{6,4},{7,5},{8,10},{9,11},{10,... | collective-permute-start | bytes 2359304 | tf_op jit(solution)/shard_map/ppermute | solution.py:541
  897.2 30.0 %collective-permute-start.155 = (bf16[48,1536]{1,0:T(8,128)(2,1)}, bf16[48,1536]{1,0:T(8,128)(2,1)}, u32[]{:S(2)}, u32[]{:S(2)}) collective-permute-start(bf16[48,1536]{1,0:T(8,128)(2,1)} %get-tuple-element.1063), channel_id=1, source_target_pairs={{0,24},{4,28},{8,0},{12,4},{16,8},{20,12},{24,16},{28,20},{1,25},{... | collective-permute-start | bytes 442376 | tf_op jit(solution)/shard_map/ppermute | solution.py:533
  899.9 27.4 %collective-permute-start.156 = (bf16[48,1536]{1,0:T(8,128)(2,1)}, bf16[48,1536]{1,0:T(8,128)(2,1)}, u32[]{:S(2)}, u32[]{:S(2)}) collective-permute-start(bf16[48,1536]{1,0:T(8,128)(2,1)} %get-tuple-element.1063), channel_id=1, source_target_pairs={{0,16},{4,20},{8,24},{12,28},{16,0},{20,4},{24,8},{28,12},{1,17},{... | collective-permute-start | bytes 442376 | tf_op jit(solution)/shard_map/ppermute | solution.py:533
  899.9 27.4 %collective-permute-start.157 = (bf16[48,1536]{1,0:T(8,128)(2,1)}, bf16[48,1536]{1,0:T(8,128)(2,1)}, u32[]{:S(2)}, u32[]{:S(2)}) collective-permute-start(bf16[48,1536]{1,0:T(8,128)(2,1)} %get-tuple-element.1063), channel_id=1, source_target_pairs={{0,8},{4,12},{8,16},{12,20},{16,24},{20,28},{24,0},{28,4},{1,9},{5... | collective-permute-start | bytes 442376 | tf_op jit(solution)/shard_map/ppermute | solution.py:533
  926.2 22.6 %collective-permute-start.165 = (bf16[192,2176]{1,0:T(8,128)(2,1)S(1)}, bf16[192,2176]{1,0:T(8,128)(2,1)S(1)}, u32[]{:S(2)}, u32[]{:S(2)}) collective-permute-start(bf16[192,2176]{1,0:T(8,128)(2,1)S(1)} %slice.567), channel_id=1, source_target_pairs={{0,4},{4,0},{8,12},{12,8},{16,20},{20,16},{24,28},{28,24},{1,5},{5... | collective-permute-start | bytes 2506760 | tf_op jit(solution)/shard_map/ppermute | solution.py:451
  931.1 20.6 %collective-permute-start.161 = (bf16[48,640]{1,0:T(8,128)(2,1)S(1)}, bf16[48,640]{1,0:T(8,128)(2,1)S(1)}, u32[]{:S(2)}, u32[]{:S(2)}) collective-permute-start(bf16[48,640]{1,0:T(8,128)(2,1)S(1)} %get-tuple-element.1205), channel_id=1, source_target_pairs={{0,8},{4,12},{8,16},{12,20},{16,24},{20,28},{24,0},{28,4},{1,9},{5... | collective-permute-start | bytes 184328 | tf_op jit(solution)/shard_map/ppermute | solution.py:533
  934.3 21.0 %collective-permute-start.162 = (bf16[48,640]{1,0:T(8,128)(2,1)S(1)}, bf16[48,640]{1,0:T(8,128)(2,1)S(1)}, u32[]{:S(2)}, u32[]{:S(2)}) collective-permute-start(bf16[48,640]{1,0:T(8,128)(2,1)S(1)} %get-tuple-element.1204), channel_id=1, source_target_pairs={{0,16},{4,20},{8,24},{12,28},{16,0},{20,4},{24,8},{28,12},{1,17},{... | collective-permute-start | bytes 184328 | tf_op jit(solution)/shard_map/ppermute | solution.py:533
  940.4 21.6 %collective-permute-start.164 = (bf16[192,1536]{1,0:T(8,128)(2,1)S(1)}, bf16[192,1536]{1,0:T(8,128)(2,1)S(1)}, u32[]{:S(2)}, u32[]{:S(2)}) collective-permute-start(bf16[192,1536]{1,0:T(8,128)(2,1)S(1)} %bitcast.554), channel_id=1, source_target_pairs={{0,4},{4,0},{8,12},{12,8},{16,20},{20,16},{24,28},{28,24},{1,5},{5... | collective-permute-start | bytes 1769480 | tf_op jit(solution)/shard_map/ppermute | solution.py:451
  942.5 19.4 %collective-permute-start.158 = (bf16[48,1536]{1,0:T(8,128)(2,1)S(1)}, bf16[48,1536]{1,0:T(8,128)(2,1)S(1)}, u32[]{:S(2)}, u32[]{:S(2)}) collective-permute-start(bf16[48,1536]{1,0:T(8,128)(2,1)S(1)} %get-tuple-element.1065), channel_id=1, source_target_pairs={{0,24},{4,28},{8,0},{12,4},{16,8},{20,12},{24,16},{28,20},{1,25},{... | collective-permute-start | bytes 442376 | tf_op jit(solution)/shard_map/ppermute | solution.py:533
  (343 other events, 3765.5 us)
Sparse Core Ops, SparseCore 0:
  40.3 47.0 all-gather.14
  123.5 17.6 all-gather.10
  142.8 37.4 all-gather.16
  181.7 37.4 all-gather.18
  220.6 19.6 all-gather.12
  242.3 39.3 all-gather.20
